TPU v7x, 32 devices: a whole 2x2x4 slice. The times are simulated.
32 devices in a mesh: dp: 4 (over y, x), ctx: 4 (over z), tp: 2 (over core).
Axes of the slice: x: 2, y: 2, z: 4, core: 2. Of those that a mesh axis runs over, the one named last changes fastest.
Arguments:
- q_proj: bfloat16 [4, 512, 4096], P('dp', 'ctx', 'tp'), may hold values from -6 to 6
- q_bias: bfloat16 [4096], P('tp'), may hold values from -3 to 3
- k_proj: bfloat16 [4, 512, 512], P('dp', 'ctx', 'tp'), may hold values from -6 to 6
- v_proj: bfloat16 [4, 512, 512], P('dp', 'ctx', 'tp'), may hold values from -6 to 6
- v_bias: bfloat16 [512], P('tp'), may hold values from -3 to 3
- dout: bfloat16 [4, 512, 4096], P('dp', 'ctx', 'tp'), may hold values from -6 to 6
- lengths: int32 [4, 8], P('dp'), may hold values from 1 to 384, 512 in all within a row
Outputs:
- attn_out: bfloat16 [4, 512, 4096], P('dp', 'ctx', 'tp')
- q_grad: bfloat16 [4, 512, 4096], P('dp', 'ctx', 'tp')
- k_grad: bfloat16 [4, 512, 512], P('dp', 'ctx', 'tp')
- v_grad: bfloat16 [4, 512, 512], P('dp', 'ctx', 'tp')
- q_bias_grad: float32 [4096], P('tp')
- v_bias_grad: float32 [512], P('tp')
All inputs are finite; a program needn't handle non-finite values.
Results may differ from a plain program's by a relative error of at most 0.035.
Values may be sent and summed in bfloat16 or wider, within the bound.
No kernel may reach another device: no remote copies, remote signals or barrier semaphores. Data moves between devices by JAX's collectives and lax.ppermute only.
A program may use at most 64 MiB of HBM per device.

v0:
```python
import jax
import jax.numpy as jnp
from jax import lax
from jax.sharding import PartitionSpec as P

HEAD_DIM = 128
HEADS = 32
KV_HEADS = 4


def doc_index(positions, ends):
    return jnp.sum((positions[..., None] >= ends).astype(jnp.int32), axis=-1)


def shards(q_proj, q_bias, k_proj, v_proj, v_bias, dout, lengths):
    tok = q_proj.shape[1]
    half = tok // 2
    width = q_proj.shape[2]
    kv_width = k_proj.shape[2]
    kv_heads = kv_width // HEAD_DIM
    group = HEADS // KV_HEADS
    scale = HEAD_DIM ** (-0.5)
    ctx_size = lax.axis_size("ctx")
    ctx_rank = lax.axis_index("ctx")
    total_rows = tok * ctx_size
    queries = (q_proj[0].astype(jnp.float32) + q_bias.astype(jnp.float32)).astype(jnp.bfloat16)
    keys = k_proj[0]
    values = (v_proj[0].astype(jnp.float32) + v_bias.astype(jnp.float32)).astype(jnp.bfloat16)
    grads = dout[0]
    ends = jnp.cumsum(lengths[0])
    offsets = jnp.arange(half, dtype=jnp.int32)
    first_pos = ctx_rank * tok + offsets
    second_pos = ctx_rank * tok + half + offsets
    local_q = queries.reshape(2, half, width)
    local_g = grads.reshape(2, half, width)
    query_pos = jnp.stack([first_pos, second_pos])
    query_doc = doc_index(query_pos, ends)
    q_heads = local_q.reshape(2, half, kv_heads, group, HEAD_DIM)
    g_heads = local_g.reshape(2, half, kv_heads, group, HEAD_DIM).transpose(0, 2, 3, 1, 4)

    def live_of(index, key_pos, key_doc):
        return (key_pos[None, :] <= query_pos[index][:, None]) & (
            key_doc[None, :] == query_doc[index][:, None]
        )

    start_state = (
        jnp.full((2, kv_heads, group, half), -1e30, jnp.float32),
        jnp.zeros((2, kv_heads, group, half), jnp.float32),
        jnp.zeros((2, kv_heads, group, half, HEAD_DIM), jnp.float32),
    )
    block_k = lax.all_gather(keys, "ctx", axis=0, tiled=True)
    block_v = lax.all_gather(values, "ctx", axis=0, tiled=True)
    count = block_k.shape[0]
    key_pos = jnp.arange(count, dtype=jnp.int32)
    key_doc = doc_index(key_pos, ends)
    keys3 = block_k.reshape(count, kv_heads, HEAD_DIM)
    values3 = block_v.reshape(count, kv_heads, HEAD_DIM)
    updated = []
    for index in range(2):
        live = live_of(index, key_pos, key_doc)

        def attend(state, index=index, live=live):
            run_max, run_sum, run_acc = state
            score = (
                jnp.einsum(
                    "tkgd,skd->kgts", q_heads[index], keys3, preferred_element_type=jnp.float32
                )
                * scale
            )
            new_max = jnp.maximum(run_max, jnp.max(jnp.where(live, score, -1e30), axis=-1))
            weights = jnp.where(live, jnp.exp(score - new_max[..., None]), 0.0)
            run_sum = jnp.sum(weights, axis=-1)
            run_acc = jnp.einsum(
                "kgts,skd->kgtd",
                weights.astype(jnp.bfloat16),
                values3,
                preferred_element_type=jnp.float32,
            )
            return (new_max, run_sum, run_acc)

        state = (start_state[0][index], start_state[1][index], start_state[2][index])
        updated.append(lax.cond(jnp.any(live), attend, lambda st: st, state))
    run_max, run_sum, run_acc = tuple((jnp.stack([updated[0][n], updated[1][n]]) for n in range(3)))
    attn = (run_acc / run_sum[..., None]).astype(jnp.bfloat16)
    lse = run_max + jnp.log(run_sum)
    delta = jnp.sum(g_heads.astype(jnp.float32) * attn.astype(jnp.float32), axis=-1)
    q_start = jnp.zeros((2, kv_heads, group, half, HEAD_DIM), jnp.float32)
    q_acc = q_start
    block_k = lax.all_gather(keys, "ctx", axis=0, tiled=True)
    block_v = lax.all_gather(values, "ctx", axis=0, tiled=True)
    count = block_k.shape[0]
    key_pos = jnp.arange(count, dtype=jnp.int32)
    key_doc = doc_index(key_pos, ends)
    grad_keys3 = block_k.reshape(count, kv_heads, HEAD_DIM)
    grad_values3 = block_v.reshape(count, kv_heads, HEAD_DIM)
    key_term = jnp.zeros((count, kv_heads, HEAD_DIM), jnp.float32)
    value_term = jnp.zeros((count, kv_heads, HEAD_DIM), jnp.float32)
    new_q = []
    for index in range(2):
        live = live_of(index, key_pos, key_doc)

        def differentiate(state, index=index, live=live):
            q_part, k_part, v_part = state
            score = (
                jnp.einsum(
                    "tkgd,skd->kgts", q_heads[index], grad_keys3, preferred_element_type=jnp.float32
                )
                * scale
            )
            probs = jnp.where(live, jnp.exp(score - lse[index][..., None]), 0.0)
            v_part = v_part + jnp.einsum(
                "kgts,kgtd->skd",
                probs.astype(jnp.bfloat16),
                g_heads[index],
                preferred_element_type=jnp.float32,
            )
            dprob = jnp.einsum(
                "kgtd,skd->kgts", g_heads[index], grad_values3, preferred_element_type=jnp.float32
            )
            dscore = (probs * (dprob - delta[index][..., None])).astype(jnp.bfloat16)
            q_part = (
                jnp.einsum("kgts,skd->kgtd", dscore, grad_keys3, preferred_element_type=jnp.float32)
                * scale
            )
            k_part = (
                k_part
                + jnp.einsum(
                    "kgts,tkgd->skd", dscore, q_heads[index], preferred_element_type=jnp.float32
                )
                * scale
            )
            return (q_part, k_part, v_part)

        q_part, key_term, value_term = lax.cond(
            jnp.any(live), differentiate, lambda st: st, (q_acc[index], key_term, value_term)
        )
        new_q.append(q_part)
    q_acc = jnp.stack(new_q)
    term = jnp.stack([key_term, value_term], axis=1)
    kv_acc = term
    q_acc, kv_acc = (q_acc, kv_acc)
    shares = lax.psum_scatter(
        kv_acc.reshape(total_rows, 2 * kv_width).astype(jnp.bfloat16),
        "ctx",
        scatter_dimension=0,
        tiled=True,
    ).astype(jnp.float32)
    key_grad = shares[:, :kv_width].astype(jnp.bfloat16)
    value_full = shares[:, kv_width:]
    value_grad = value_full.astype(jnp.bfloat16)
    q_rows = q_acc.transpose(0, 3, 1, 2, 4).reshape(2, half, width)
    out_rows = attn.transpose(0, 3, 1, 2, 4).reshape(2, half, width)
    q_sum = jnp.sum(q_rows, axis=(0, 1))
    v_sum = jnp.sum(value_full, axis=0)
    q_rounded = q_rows.astype(jnp.bfloat16)
    attn_full = out_rows.reshape(tok, width)
    q_full = q_rounded.reshape(tok, width)
    totals = lax.psum((q_sum, v_sum), ("dp", "ctx"))
    batches = lax.axis_size("dp")
    return (
        attn_full[None],
        q_full[None],
        key_grad[None],
        value_grad[None],
        totals[0] / batches,
        totals[1] / batches,
    )


def solution(mesh):
    placed = (
        P("dp", "ctx", "tp"),
        P("tp"),
        P("dp", "ctx", "tp"),
        P("dp", "ctx", "tp"),
        P("tp"),
        P("dp", "ctx", "tp"),
        P("dp", None),
    )
    return jax.shard_map(
        shards,
        mesh=mesh,
        in_specs=placed,
        out_specs=(
            P("dp", "ctx", "tp"),
            P("dp", "ctx", "tp"),
            P("dp", "ctx", "tp"),
            P("dp", "ctx", "tp"),
            P("tp"),
            P("tp"),
        ),
        check_vma=False,
    )
```

profile of v0, /device:TPU:0, one launch (start us, length us, event | category | flops | bytes accessed | tf_op | source)
XLA Modules:
  0.0 128.2 jit_solution(6881178783650228419)
XLA Ops:
  7.2 0.0 reduce-scatter.2.cloned.1.call-start
  7.3 0.7 convert_element_type.94
  8.0 0.8 reduce-window.8
  8.8 0.1 convert_reduce_fusion.1
  8.9 0.1 convert_reduce_fusion.2
  9.0 0.7 bitcast_convert_fusion
  9.7 0.8 fusion.59
  11.7 1.0 copy.60
  12.7 1.0 copy.61
  13.7 0.1 fusion.55
  13.8 14.5 %all_gather.9 = bf16[512,256]{0,1:T(8,128)(2,1)S(1)} all-gather(bf16[128,256]{0,1:T(8,128)(2,1)S(1)} %fusion.55), channel_id=1, replica_groups=mesh['dp'=4,'ctx'=4,'tp'=2] {'ctx'}, dimensions={0}, use_global_device_ids=true | all-gather | bytes 327680 | tf_op jit(solution)/shard_map/all_gather | solution.py:52
  28.2 12.8 %all-gather = bf16[1,512,256]{1,2,0:T(8,128)(2,1)S(1)} all-gather(bf16[1,128,256]{1,2,0:T(8,128)(2,1)S(1)} %copy.60), channel_id=2, replica_groups=mesh['dp'=4,'ctx'=4,'tp'=2] {'ctx'}, dimensions={1}, use_global_device_ids=true | all-gather | bytes 327680 | tf_op jit(solution)/shard_map/all_gather | solution.py:51
  41.0 1.1 copy.116
  42.2 0.1 convert_bitcast_fusion
  42.3 0.2 copy.115
  42.5 0.1 add_convert_fusion
  42.6 2.3 %conditional.4 = (f32[1,2,8,64]{3,2,1,0:T(8,128)S(1)}, f32[1,2,8,64]{3,2,1,0:T(8,128)S(1)}, f32[1,2,8,64,128]{4,2,1,3,0:T(8,128)S(1)}) conditional(s32[]{:T(128)} %convert_element_type.88, () %tuple.56, (pred[64,512]{1,0:T(8,128)(4,1)S(1)}, bf16[2,64,2,8,128]{4,3,2,1,0:T(8,128)(2,1)S(1)}, bf16[512,2,128]{0,2,1:T(8,128)(2,1)S(1)}, ...), branch_computations={%region_4.5_spmd, %region_5.8_spmd} | conditional | flops 274201600 | bytes 9826328 | solution.py:82
  42.6 0.1 copy.62
  42.7 0.5 fusion
  43.3 0.7 fusion.4
  43.9 0.6 convolution_bitcast_fusion
  44.5 0.3 copy.112
  44.8 2.3 %conditional.5 = (f32[1,2,8,64]{3,2,1,0:T(8,128)S(1)}, f32[1,2,8,64]{3,2,1,0:T(8,128)S(1)}, f32[1,2,8,64,128]{4,2,1,3,0:T(8,128)S(1)}) conditional(s32[]{:T(128)} %convert_element_type.96, () %tuple.58, (pred[64,512]{1,0:T(8,128)(4,1)S(1)}, bf16[2,64,2,8,128]{4,3,2,1,0:T(8,128)(2,1)S(1)}, bf16[512,2,128]{0,2,1:T(8,128)(2,1)S(1)}, ...), branch_computations={%region_9.10_spmd, %region_10.13_spmd} | conditional | flops 274201600 | bytes 9826328 | solution.py:82
  44.9 0.1 copy.65
  45.0 0.5 fusion.16
  45.5 0.7 fusion.20
  46.2 0.6 convolution_bitcast_fusion.1
  46.8 0.3 copy.114
  47.1 0.1 copy.70
  47.3 1.4 %multiply_reduce_fusion = (f32[2,2,8,64]{2,1,3,0:T(2,128)S(1)}, bf16[2,2,8,64,128]{4,2,1,3,0:T(8,128)(2,1)}) fusion(bf16[2,64,2,8,128]{4,3,2,1,0:T(8,128)(2,1)S(1)} %bitcast.220, f32[2,2,8,64]{2,1,3,0:T(2,128)S(1)} %copy.70, f32[1,2,8,64,128]{4,2,1,3,0:T(8,128)S(1)} %get-tuple-element.189, f32[1,2,8,64,128]{4,2,1,3,0:T(8,128)S(1)} %get-tuple-element.188), kind=kLoop, calls=%fused_computation.82 | loop fusion | flops 1832960 | bytes 2113536 | tf_op jit(solution)/shard_map/reduce_sum | solution.py:86
  48.7 3.0 %conditional.6 = (f32[512,2,128]{2,0,1:T(8,128)S(1)}, f32[512,2,128]{2,0,1:T(8,128)S(1)}, f32[1,2,8,64,128]{4,3,2,1,0:T(8,128)S(1)}) conditional(s32[]{:T(128)} %convert_element_type.88, () %tuple.60, (pred[64,512]{1,0:T(8,128)(4,1)S(1)}, bf16[2,64,2,8,128]{4,3,2,1,0:T(8,128)(2,1)S(1)}, bf16[512,2,128]{0,2,1:T(8,128)(2,1)S(1)}, ...), branch_computations={%region_14.15_spmd, %region_15.16_spmd} | conditional | flops 675020800 | bytes 15024152 | solution.py:134
  48.7 0.1 copy.75
  48.8 0.2 copy.73
  48.9 0.1 copy.71
  49.1 0.6 fusion.33
  49.7 0.5 convolution_bitcast_fusion.2
  50.2 0.4 multiply_convert_fusion
  50.6 0.5 fusion.36
  51.2 0.4 fusion.34
  51.6 3.1 %conditional.7 = (f32[512,2,128]{2,0,1:T(8,128)S(1)}, f32[512,2,128]{2,0,1:T(8,128)S(1)}, f32[1,2,8,64,128]{4,3,2,1,0:T(8,128)S(1)}) conditional(s32[]{:T(128)} %convert_element_type.96, (f32[512,2,128]{2,0,1:T(8,128)S(1)}, f32[512,2,128]{2,0,1:T(8,128)S(1)}) %tuple.62, (pred[64,512]{1,0:T(8,128)(4,1)S(1)}, ...), branch_computations={%region_16.17_spmd, %region_17.18_spmd} | conditional | flops 675282944 | bytes 16072728 | solution.py:134
  51.7 0.1 copy.80
  51.7 0.2 copy.78
  51.9 0.1 copy.76
  52.1 0.6 fusion.42
  52.6 0.6 fusion.47
  53.3 0.4 multiply_convert_fusion.1
  53.7 0.6 fusion.46
  54.3 0.4 fusion.43
  54.8 0.0 copy-start
  54.9 0.1 pad_maximum_fusion
  54.9 0.5 copy.82
  55.5 1.0 convert_element_type.102
  56.5 0.0 reduce-scatter.2.cloned.1.call-update
  56.5 1.0 broadcast_in_dim_reshape_reshape.3
  57.5 0.1 fusion.54
  57.6 0.3 copy.81
  57.9 1.0 convert_element_type.101
  59.0 0.1 fusion.53
  59.0 18.6 %reduce-scatter.2.cloned.1.call-done = bf16[128,512]{1,0:T(8,128)(2,1)} async-done(((bf16[512,512]{1,0:T(8,128)(2,1)}), bf16[128,512]{1,0:T(8,128)(2,1)}) %reduce-scatter.2.cloned.1.call-update) | async-done | bytes 131088 | tf_op jit(solution)/shard_map/reduce_scatter | solution.py:142
  77.6 0.9 convert_reduce_fusion
  78.5 40.2 %all-reduce = (f32[2048]{0:T(1024)S(1)}, f32[256]{0:T(256)S(1)}) all-reduce(f32[2048]{0:T(1024)S(1)} %bitcast.234, f32[256]{0:T(256)S(1)} %convert_reduce_fusion), channel_id=1, replica_groups=mesh['dp'=4,'ctx'=4,'tp'=2] {'dp','ctx'}, use_global_device_ids=true, to_apply=%region_20.21 | all-reduce | flops 2304 | bytes 18432 | tf_op jit(solution)/shard_map/psum | solution.py:158
  118.7 0.6 broadcast_multiply_fusion
  119.3 0.6 broadcast_multiply_fusion.1
  119.8 1.5 %slice_bitcast_fusion.21 = (bf16[1,128,256]{2,1,0:T(8,128)(2,1)}, bf16[1,128,256]{2,1,0:T(8,128)(2,1)}) fusion(bf16[128,512]{1,0:T(8,128)(2,1)} %reduce-scatter.2.cloned.1.call-done), kind=kLoop, calls=%fused_computation.97 | loop fusion | bytes 262144 | tf_op jit(solution)/shard_map/broadcast_in_dim | solution.py:164
  (18 shorter events, 0.1 us)
Async XLA Ops:
  7.2 35.0 %copy-start.1 = (bf16[1,128,2048]{2,1,0:T(8,128)(2,1)S(1)}, bf16[1,128,2048]{2,1,0:T(8,128)(2,1)}, u32[]{:S(2)}) copy-start(bf16[1,128,2048]{2,1,0:T(8,128)(2,1)} %param.15) | copy-start | bytes 1572868
  7.2 70.4 %reduce-scatter.2.cloned.1.call-start = ((), (), s32[]{:S(2)}) async-start(), calls=%async_computation.1 | async-start | bytes 655360 | tf_op jit(solution)/shard_map/reduce_scatter | solution.py:142
  54.8 1.7 %copy-start = (bf16[2,2,8,64,128]{4,2,1,3,0:T(8,128)(2,1)S(1)}, bf16[2,2,8,64,128]{4,2,1,3,0:T(8,128)(2,1)}, u32[]{:S(2)}) copy-start(bf16[2,2,8,64,128]{4,2,1,3,0:T(8,128)(2,1)} %get-tuple-element.195) | copy-start | bytes 1572868
Sparse Core Ops, SparseCore 0:
  56.6 20.9 reduce-scatter.1
where the time goes:
time: 129 us; the launch traced here: 128 us
  blocking collectives  67.4 us (52%)
  waiting for transfers between devices  18.6 us (14%)
  between operations  15.5 us (12%)
  local copies, waits for them, and re-layouts  10.4 us (8%)
  other arithmetic  8.54 us (7%)
  matrix products  7.43 us (6%)
    psum x1, blocking collectives, shards(): totals = lax.psum((q_sum, v_sum), ('dp', 'ctx'))  40.2 us
    reduce_scatter x1, waiting for transfers between devices, shards(): lax.psum_scatter(kv_acc.reshape(total_rows, 2 * kv_width).astype(jnp.bflo...  18.6 us
    all_gather x1, blocking collectives, shards(): block_v = lax.all_gather(values, 'ctx', axis=0, tiled=True)  14.5 us
    all_gather x1, blocking collectives, shards(): block_k = lax.all_gather(keys, 'ctx', axis=0, tiled=True)  12.8 us
    unnamed x9, local copies, waits for them, and re-layouts  3.25 us
  transfers between devices with their start and end apart: 1, of which 1 were waited for; matrix products, arithmetic and copies ran while one was open for 2% of the time, Pallas kernels for 0%

commit v1 on v0

v1 whole, which is shorter than its diff:
```python
import functools

import jax
import jax.numpy as jnp
from jax import lax
from jax.experimental import pallas as pl
from jax.experimental.pallas import tpu as pltpu
from jax.sharding import PartitionSpec as P

HEAD_DIM = 128
HEADS = 32
KV_HEADS = 4
GROUP = HEADS // KV_HEADS
PAIR = 2
SCALE = HEAD_DIM ** (-0.5)
LOG2E = 1.4426950408889634
NEGATIVE = -1e30


def dot(left, right, left_dim, right_dim):
    return lax.dot_general(
        left, right, (((left_dim,), (right_dim,)), ((), ())), preferred_element_type=jnp.float32
    )


def attention_kernel(slots, *refs):
    len_ref, q_ref, qb_ref, vb_ref, g_ref, k_ref, v_ref = refs[:7]
    got_refs = refs[7 : 7 + slots - 1]
    refs = refs[7 + slots - 1 :]
    attn_ref, qg_ref, own_ref, sums_ref = refs[:4]
    out_refs = refs[4 : 4 + slots - 1]
    keys_ref, values_ref, live_ref = refs[4 + slots - 1 :]
    tok, width = q_ref.shape
    kv_width = k_ref.shape[1]
    kv_heads = kv_width // HEAD_DIM
    rank = lax.axis_index("ctx")

    query_pos = rank * tok + lax.broadcasted_iota(jnp.int32, (1, tok), 1)
    start = jnp.zeros((1, tok), jnp.int32)
    end = jnp.int32(0)
    for doc in range(len_ref.shape[1]):
        length = len_ref[0, doc]
        end = end + length
        start = start + jnp.where(query_pos >= end, length, 0)
    offsets = lax.broadcasted_iota(jnp.int32, (tok, tok), 0)
    bias = vb_ref[...].astype(jnp.float32)
    for slot in range(slots):
        rows = pl.ds(slot * tok, tok)
        key_pos = (rank - slot) * tok + offsets
        live = (key_pos >= start) & (key_pos <= query_pos)
        live_ref[rows, :] = jnp.where(live, 0.0, NEGATIVE)
        if slot == 0:
            keys, values = k_ref[...], v_ref[...]
        else:
            got = got_refs[slot - 1][...]
            keys, values = got[:, :kv_width], got[:, kv_width:]
        keys_ref[rows, :] = keys
        values_ref[rows, :] = (values.astype(jnp.float32) + bias).astype(jnp.bfloat16)

    for kv_head in range(kv_heads):
        kv_cols = slice(kv_head * HEAD_DIM, (kv_head + 1) * HEAD_DIM)
        keys = keys_ref[:, kv_cols]
        values = values_ref[:, kv_cols]
        keys_t = keys.T
        values_t = values.T
        key_term = jnp.zeros((slots * tok, HEAD_DIM), jnp.float32)
        value_term = jnp.zeros((slots * tok, HEAD_DIM), jnp.float32)
        for pair in range(GROUP // PAIR):
            first = kv_head * GROUP + pair * PAIR
            cols = [slice((first + n) * HEAD_DIM, (first + n + 1) * HEAD_DIM) for n in range(PAIR)]
            queries = jnp.concatenate(
                [
                    (q_ref[:, col].astype(jnp.float32) + qb_ref[:, col].astype(jnp.float32)).astype(
                        jnp.bfloat16
                    )
                    for col in cols
                ],
                axis=0,
            )
            grads = jnp.concatenate([g_ref[:, col] for col in cols], axis=0)
            live = jnp.concatenate([live_ref[...]] * PAIR, axis=1)
            score = dot(keys, queries, 1, 1) * (SCALE * LOG2E) + live
            row_max = jnp.max(score, axis=0, keepdims=True)
            weights = jnp.exp2(score - row_max)
            inverse = 1.0 / jnp.sum(weights, axis=0, keepdims=True)
            attn = dot(values_t, weights.astype(jnp.bfloat16), 1, 0) * inverse
            probs = weights * inverse
            dprob = dot(values, grads, 1, 1)
            delta = jnp.sum(probs * dprob, axis=0, keepdims=True)
            dscore = (probs * (dprob - delta)).astype(jnp.bfloat16)
            value_term = value_term + dot(probs.astype(jnp.bfloat16), grads, 1, 0)
            key_term = key_term + dot(dscore, queries, 1, 0)
            query_grad = dot(keys_t, dscore, 1, 0) * SCALE
            attn = attn.T
            query_grad = query_grad.T
            for n, col in enumerate(cols):
                rows = slice(n * tok, (n + 1) * tok)
                attn_ref[:, col] = attn[rows].astype(jnp.bfloat16)
                qg_ref[:, col] = query_grad[rows].astype(jnp.bfloat16)
                sums_ref[:, col] = jnp.sum(query_grad[rows], axis=0, keepdims=True)
        key_term = key_term * SCALE
        sum_cols = slice(width + kv_head * HEAD_DIM, width + (kv_head + 1) * HEAD_DIM)
        sums_ref[:, sum_cols] = jnp.sum(value_term, axis=0, keepdims=True)
        value_cols = slice(kv_width + kv_head * HEAD_DIM, kv_width + (kv_head + 1) * HEAD_DIM)
        own_ref[:, kv_cols] = key_term[:tok]
        own_ref[:, value_cols] = value_term[:tok]
        for slot in range(1, slots):
            rows = slice(slot * tok, (slot + 1) * tok)
            out_refs[slot - 1][:, kv_cols] = key_term[rows].astype(jnp.bfloat16)
            out_refs[slot - 1][:, value_cols] = value_term[rows].astype(jnp.bfloat16)


def attention(slots, lengths, q_proj, q_bias, v_bias, dout, k_proj, v_proj, got):
    tok, width = q_proj.shape
    kv_width = k_proj.shape[1]
    rows = slots * tok
    vmem = pl.BlockSpec(memory_space=pltpu.VMEM)
    shape = jax.ShapeDtypeStruct
    return pl.pallas_call(
        functools.partial(attention_kernel, slots),
        out_shape=[
            shape((tok, width), jnp.bfloat16),
            shape((tok, width), jnp.bfloat16),
            shape((tok, 2 * kv_width), jnp.float32),
            shape((1, width + kv_width), jnp.float32),
        ]
        + [shape((tok, 2 * kv_width), jnp.bfloat16)] * (slots - 1),
        in_specs=[pl.BlockSpec(memory_space=pltpu.SMEM)] + [vmem] * (6 + slots - 1),
        out_specs=[vmem] * (4 + slots - 1),
        scratch_shapes=[
            pltpu.VMEM((rows, kv_width), jnp.bfloat16),
            pltpu.VMEM((rows, kv_width), jnp.bfloat16),
            pltpu.VMEM((rows, tok), jnp.float32),
        ],
        compiler_params=pltpu.CompilerParams(vmem_limit_bytes=48 * 1024 * 1024),
        cost_estimate=pl.CostEstimate(
            flops=12 * rows * tok * width,
            bytes_accessed=8 * tok * width + 8 * rows * kv_width,
            transcendentals=rows * tok * width // HEAD_DIM,
        ),
        name="attention",
    )(lengths, q_proj, q_bias, v_bias, dout, k_proj, v_proj, *got)


def sum_over(axis, part):
    size = lax.axis_size(axis)
    terms = [
        lax.ppermute(part, axis, [(i, (i + shift) % size) for i in range(size)])
        for shift in range(1, size)
    ]
    return functools.reduce(lambda left, right: left + right, terms, part)


def shards(q_proj, q_bias, k_proj, v_proj, v_bias, dout, lengths):
    width = q_proj.shape[2]
    kv_width = k_proj.shape[2]
    ctx = lax.axis_size("ctx")
    batches = lax.axis_size("dp")
    pair = jnp.concatenate([k_proj[0], v_proj[0]], axis=1)
    got = [
        lax.ppermute(pair, "ctx", [(i, i + shift) for i in range(ctx - shift)])
        for shift in range(1, ctx)
    ]
    attn, q_grad, own, sums, *terms = attention(
        ctx, lengths, q_proj[0], q_bias[None], v_bias[None], dout[0], k_proj[0], v_proj[0], got
    )
    back = [
        lax.ppermute(term, "ctx", [(i, i - shift) for i in range(shift, ctx)])
        for shift, term in enumerate(terms, 1)
    ]
    sums = sum_over("dp", sum_over("ctx", sums)) / batches
    kv_grad = own
    for term in back:
        kv_grad = kv_grad + term.astype(jnp.float32)
    kv_grad = kv_grad.astype(jnp.bfloat16)
    return (
        attn[None],
        q_grad[None],
        kv_grad[None, :, :kv_width],
        kv_grad[None, :, kv_width:],
        sums[0, :width],
        sums[0, width:],
    )


def solution(mesh):
    tokens = P("dp", "ctx", "tp")
    return jax.shard_map(
        shards,
        mesh=mesh,
        in_specs=(tokens, P("tp"), tokens, tokens, P("tp"), tokens, P("dp", None)),
        out_specs=(tokens, tokens, tokens, tokens, P("tp"), P("tp")),
        check_vma=False,
    )
```

time: 129 us -> 58.4 us (0.45)
  blocking collectives: 67.4 us -> 0 us
  starting transfers between devices: 0.04 us -> 26.4 us
  between operations: 15.5 us -> 0.78 us
  Pallas kernels: 0 us -> 8.09 us
  other arithmetic: 8.54 us -> 1.03 us
  matrix products: 7.43 us -> 0 us
  local copies, waits for them, and re-layouts: 10.4 us -> 4.59 us
  waiting for transfers between devices: 18.6 us -> 17.1 us
    psum x1 -> x0, blocking collectives: 40.2 us -> none  [shards(): totals = lax.psum((q_sum, v_sum), ('dp', 'ctx'))]
    all_gather x2 -> x0, blocking collectives: 27.2 us -> none  [the longest x1 14.5 us: shards(): block_v = lax.all_gather(values, 'ctx', axis=0, tiled=True)]
    ppermute x0 -> x12, starting transfers between devices: none -> 26.4 us  [the longest x6 11.8 us: sum_over(): lax.ppermute(part, axis, [(i, (i + shift) % size) for i in range(size)])]
    reduce_scatter x1 -> x0, waiting for transfers between devices: 18.6 us -> none  [shards(): lax.psum_scatter(kv_acc.reshape(total_rows, 2 * kv_width).astype(jnp.bflo...]
    ppermute x0 -> x12, waiting for transfers between devices: none -> 17.1 us  [the longest x3 9.09 us: shards(): lax.ppermute(term, 'ctx', [(i, i - shift) for i in range(shift, ctx)])]
    pallas_call x0 -> x1, Pallas kernels: none -> 8.09 us  [attention(): pl.pallas_call(functools.partial(attention_kernel, slots), out_shape=[sha...]
    dot_general x14 -> x0, matrix products: 7.43 us -> none  [the longest x2 1.18 us: attend(): jnp.einsum('kgts,skd->kgtd', weights.astype(jnp.bfloat16), values3, prefe...]
    reduce_sum x7 -> x0, other arithmetic: 3.86 us -> none  [the longest x1 1.41 us: shards(): jnp.sum(g_heads.astype(jnp.float32) * attn.astype(jnp.float32), axis=-1)]
  transfers between devices with their start and end apart: 1 -> 12, of which waited for: 1 -> 8; matrix products, arithmetic and copies ran while one was open for 2% -> 2% of each run, Pallas kernels for 0% -> 0%
where the time goes in v1:
time: 58.4 us; the launch traced here: 58 us
  starting transfers between devices  26.4 us (45%)
  waiting for transfers between devices  17.1 us (29%)
  Pallas kernels  8.09 us (14%)
  local copies, waits for them, and re-layouts  4.59 us (8%)
  other arithmetic  1.03 us (2%)
  between operations  0.78 us (1%)
    ppermute x6, starting transfers between devices, sum_over(): lax.ppermute(part, axis, [(i, (i + shift) % size) for i in range(size)])  11.8 us
    ppermute x3, starting transfers between devices, shards(): lax.ppermute(pair, 'ctx', [(i, i + shift) for i in range(ctx - shift)])  10.7 us
    ppermute x3, waiting for transfers between devices, shards(): lax.ppermute(term, 'ctx', [(i, i - shift) for i in range(shift, ctx)])  9.09 us
    pallas_call x1, Pallas kernels, attention(): pl.pallas_call(functools.partial(attention_kernel, slots), out_shape=[sha...  8.09 us
    ppermute x3, waiting for transfers between devices, shards(): lax.ppermute(pair, 'ctx', [(i, i + shift) for i in range(ctx - shift)])  4.56 us
    ppermute x3, starting transfers between devices, shards(): lax.ppermute(term, 'ctx', [(i, i - shift) for i in range(shift, ctx)])  3.86 us
    ppermute x6, waiting for transfers between devices, sum_over(): lax.ppermute(part, axis, [(i, (i + shift) % size) for i in range(size)])  3.5 us
    unnamed x14, local copies, waits for them, and re-layouts  2.75 us
  transfers between devices with their start and end apart: 12, of which 8 were waited for; matrix products, arithmetic and copies ran while one was open for 2% of the time, Pallas kernels for 0%

profile of v1, /device:TPU:0, one launch (start us, length us, event | category | flops | bytes accessed | tf_op | source)
XLA Modules:
  0.0 58.0 jit_solution(694249677166439055)
XLA Ops:
  0.6 0.0 copy-start.6
  0.6 0.0 copy-start.5
  0.7 0.0 copy-start
  0.7 0.0 copy-start.1
  0.7 0.9 %pad_maximum_fusion = bf16[128,512]{1,0:T(8,128)(2,1)S(1)} fusion(bf16[128,256]{1,0:T(8,128)(2,1)} %bitcast.14, bf16[128,256]{1,0:T(8,128)(2,1)} %bitcast.12), kind=kLoop, calls=%fused_computation.1 | loop fusion | flops 262144 | bytes 262144 | tf_op jit(solution)/shard_map/concatenate | solution.py:159
  1.6 7.0 %collective-permute-start.2 = (bf16[128,512]{1,0:T(8,128)(2,1)S(1)}, bf16[128,512]{1,0:T(8,128)(2,1)S(1)}, u32[]{:S(2)}, u32[]{:S(2)}) collective-permute-start(bf16[128,512]{1,0:T(8,128)(2,1)S(1)} %pad_maximum_fusion), channel_id=1, source_target_pairs={{0,6},{1,7},{8,14},{9,15},{16,22},{17,23},{24,30},{25,31}} | collective-permute-start | bytes 393224 | tf_op jit(solution)/shard_map/ppermute | solution.py:161
  8.6 1.3 %collective-permute-start.1 = (bf16[128,512]{1,0:T(8,128)(2,1)S(1)}, bf16[128,512]{1,0:T(8,128)(2,1)S(1)}, u32[]{:S(2)}, u32[]{:S(2)}) collective-permute-start(bf16[128,512]{1,0:T(8,128)(2,1)S(1)} %pad_maximum_fusion), channel_id=1, source_target_pairs={{0,4},{2,6},{1,5},{3,7},{8,12},{10,14},{9,13},{11,15},{16,20},{18,... | collective-permute-start | bytes 393224 | tf_op jit(solution)/shard_map/ppermute | solution.py:161
  9.9 2.5 %collective-permute-start = (bf16[128,512]{1,0:T(8,128)(2,1)S(1)}, bf16[128,512]{1,0:T(8,128)(2,1)S(1)}, u32[]{:S(2)}, u32[]{:S(2)}) collective-permute-start(bf16[128,512]{1,0:T(8,128)(2,1)S(1)} %pad_maximum_fusion), channel_id=1, source_target_pairs={{0,2},{2,4},{4,6},{1,3},{3,5},{5,7},{8,10},{10,12},{12,14},{9,11},... | collective-permute-start | bytes 393224 | tf_op jit(solution)/shard_map/ppermute | solution.py:161
  12.4 0.0 copy-done.6
  12.4 0.0 copy-done.5
  12.4 0.1 collective-permute-done.2.refs_9_
  12.5 2.8 %collective-permute-done.1.refs_8_ = bf16[128,512]{1,0:T(8,128)(2,1)S(1)} collective-permute-done((bf16[128,512]{1,0:T(8,128)(2,1)S(1)}, bf16[128,512]{1,0:T(8,128)(2,1)S(1)}, u32[]{:S(2)}, u32[]{:S(2)}) %collective-permute-start.1) | collective-permute-done | bytes 131104 | tf_op jit(solution)/shard_map/ppermute | solution.py:161
  15.3 1.7 %collective-permute-done.refs_7_ = bf16[128,512]{1,0:T(8,128)(2,1)S(1)} collective-permute-done((bf16[128,512]{1,0:T(8,128)(2,1)S(1)}, bf16[128,512]{1,0:T(8,128)(2,1)S(1)}, u32[]{:S(2)}, u32[]{:S(2)}) %collective-permute-start) | collective-permute-done | bytes 131104 | tf_op jit(solution)/shard_map/ppermute | solution.py:161
  17.0 0.0 copy-start.4
  17.0 0.0 copy-done
  17.0 0.0 copy-done.1
  17.0 0.6 %copy-done.4 = s32[1,8]{1,0:T(1,128)S(1)} copy-done((s32[1,8]{1,0:T(1,128)S(1)}, s32[1,8]{1,0:T(1,128)}, u32[]{:S(2)}) %copy-start.4) | copy-done | bytes 56
  17.6 0.0 copy-start.2
  17.6 1.0 %copy-done.2 = bf16[1,128,2048]{2,1,0:T(8,128)(2,1)S(1)} copy-done((bf16[1,128,2048]{2,1,0:T(8,128)(2,1)S(1)}, bf16[1,128,2048]{2,1,0:T(8,128)(2,1)}, u32[]{:S(2)}) %copy-start.2) | copy-done | bytes 524312
  18.7 0.0 copy-start.3
  18.7 1.0 %copy-done.3 = bf16[1,128,2048]{2,1,0:T(8,128)(2,1)S(1)} copy-done((bf16[1,128,2048]{2,1,0:T(8,128)(2,1)S(1)}, bf16[1,128,2048]{2,1,0:T(8,128)(2,1)}, u32[]{:S(2)}) %copy-start.3) | copy-done | bytes 524312
  19.7 8.1 %attention.1 = (bf16[128,2048]{1,0:T(8,128)(2,1)}, bf16[128,2048]{1,0:T(8,128)(2,1)}, f32[128,512]{1,0:T(8,128)S(1)}, f32[1,2304]{1,0:T(1,128)S(1)}, bf16[128,51...) custom-call(s32[1,8]{1,0:T(1,128)S(1)} %copy-done.4, ...), custom_call_target="tpu_custom_call" | custom-call | flops 1610612736 | bytes 3145728 | tf_op jit(solution)/shard_map/attention/pallas_call | solution.py:119
  27.8 4.3 %collective-permute-start.8 = (f32[1,2304]{1,0:T(1,128)S(1)}, f32[1,2304]{1,0:T(1,128)S(1)}, u32[]{:S(2)}, u32[]{:S(2)}) collective-permute-start(f32[1,2304]{1,0:T(1,128)S(1)} %get-tuple-element.19), channel_id=1, source_target_pairs={{0,6},{2,0},{4,2},{6,4},{1,7},{3,1},{5,3},{7,5},{8,14},{10,8},{12,... | collective-permute-start | bytes 27656 | tf_op jit(solution)/shard_map/ppermute | solution.py:148
  32.1 1.8 %collective-permute-start.7 = (f32[1,2304]{1,0:T(1,128)S(1)}, f32[1,2304]{1,0:T(1,128)S(1)}, u32[]{:S(2)}, u32[]{:S(2)}) collective-permute-start(f32[1,2304]{1,0:T(1,128)S(1)} %get-tuple-element.19), channel_id=1, source_target_pairs={{0,4},{2,6},{4,0},{6,2},{1,5},{3,7},{5,1},{7,3},{8,12},{10,14},{12... | collective-permute-start | bytes 27656 | tf_op jit(solution)/shard_map/ppermute | solution.py:148
  33.9 2.0 %collective-permute-start.6 = (f32[1,2304]{1,0:T(1,128)S(1)}, f32[1,2304]{1,0:T(1,128)S(1)}, u32[]{:S(2)}, u32[]{:S(2)}) collective-permute-start(f32[1,2304]{1,0:T(1,128)S(1)} %get-tuple-element.19), channel_id=1, source_target_pairs={{0,2},{2,4},{4,6},{6,0},{1,3},{3,5},{5,7},{7,1},{8,10},{10,12},{12... | collective-permute-start | bytes 27656 | tf_op jit(solution)/shard_map/ppermute | solution.py:148
  36.0 0.0 collective-permute-done.8
  36.0 0.7 %collective-permute-done.7 = f32[1,2304]{1,0:T(1,128)S(1)} collective-permute-done((f32[1,2304]{1,0:T(1,128)S(1)}, f32[1,2304]{1,0:T(1,128)S(1)}, u32[]{:S(2)}, u32[]{:S(2)}) %collective-permute-start.7) | collective-permute-done | bytes 9248 | tf_op jit(solution)/shard_map/ppermute | solution.py:148
  36.7 2.7 %collective-permute-done.6 = f32[1,2304]{1,0:T(1,128)S(1)} collective-permute-done((f32[1,2304]{1,0:T(1,128)S(1)}, f32[1,2304]{1,0:T(1,128)S(1)}, u32[]{:S(2)}, u32[]{:S(2)}) %collective-permute-start.6) | collective-permute-done | bytes 9248 | tf_op jit(solution)/shard_map/ppermute | solution.py:148
  39.4 2.5 %collective-permute-start.11 = (f32[1,2304]{1,0:T(1,128)S(1)}, f32[1,2304]{1,0:T(1,128)S(1)}, u32[]{:S(2)}, u32[]{:S(2)}) collective-permute-start(f32[1,2304]{1,0:T(1,128)S(1)} %add_add_fusion), channel_id=1, source_target_pairs={{0,24},{8,0},{16,8},{24,16},{1,25},{9,1},{17,9},{25,17},{2,26},{10... | collective-permute-start | bytes 27656 | tf_op jit(solution)/shard_map/ppermute | solution.py:148
  41.9 0.5 collective-permute-start.10
  42.4 0.6 %collective-permute-start.9 = (f32[1,2304]{1,0:T(1,128)S(1)}, f32[1,2304]{1,0:T(1,128)S(1)}, u32[]{:S(2)}, u32[]{:S(2)}) collective-permute-start(f32[1,2304]{1,0:T(1,128)S(1)} %add_add_fusion), channel_id=1, source_target_pairs={{0,8},{8,16},{16,24},{24,0},{1,9},{9,17},{17,25},{25,1},{2,10},{10... | collective-permute-start | bytes 27656 | tf_op jit(solution)/shard_map/ppermute | solution.py:148
  43.0 1.3 %collective-permute-start.3 = (bf16[128,512]{1,0:T(8,128)(2,1)S(1)}, bf16[128,512]{1,0:T(8,128)(2,1)S(1)}, u32[]{:S(2)}, u32[]{:S(2)}) collective-permute-start(bf16[128,512]{1,0:T(8,128)(2,1)S(1)} %get-tuple-element.16), channel_id=1, source_target_pairs={{2,0},{4,2},{6,4},{3,1},{5,3},{7,5},{10,8},{12,10},{14,12},{11,9},... | collective-permute-start | bytes 393224 | tf_op jit(solution)/shard_map/ppermute | solution.py:168
  44.3 1.3 %collective-permute-start.4 = (bf16[128,512]{1,0:T(8,128)(2,1)S(1)}, bf16[128,512]{1,0:T(8,128)(2,1)S(1)}, u32[]{:S(2)}, u32[]{:S(2)}) collective-permute-start(bf16[128,512]{1,0:T(8,128)(2,1)S(1)} %get-tuple-element.17), channel_id=1, source_target_pairs={{4,0},{6,2},{5,1},{7,3},{12,8},{14,10},{13,9},{15,11},{20,16},{22,... | collective-permute-start | bytes 393224 | tf_op jit(solution)/shard_map/ppermute | solution.py:168
  45.6 0.0 collective-permute-done.11
  45.6 1.3 %collective-permute-start.5 = (bf16[128,512]{1,0:T(8,128)(2,1)S(1)}, bf16[128,512]{1,0:T(8,128)(2,1)S(1)}, u32[]{:S(2)}, u32[]{:S(2)}) collective-permute-start(bf16[128,512]{1,0:T(8,128)(2,1)S(1)} %get-tuple-element.18), channel_id=1, source_target_pairs={{6,0},{7,1},{14,8},{15,9},{22,16},{23,17},{30,24},{31,25}} | collective-permute-start | bytes 393224 | tf_op jit(solution)/shard_map/ppermute | solution.py:168
  46.9 0.0 collective-permute-done.10
  46.9 0.1 collective-permute-done.9
  47.0 0.6 slice.19
  47.6 0.6 %slice.18 = f32[1,2048]{1,0:T(1,128)} slice(f32[1,2304]{1,0:T(1,128)S(1)} %add_multiply_fusion), slice={[0:1], [0:2048]} | slice | bytes 16384 | tf_op jit(solution)/shard_map/slice | solution.py:181
  48.2 2.1 %collective-permute-done.3 = bf16[128,512]{1,0:T(8,128)(2,1)S(1)} collective-permute-done((bf16[128,512]{1,0:T(8,128)(2,1)S(1)}, bf16[128,512]{1,0:T(8,128)(2,1)S(1)}, u32[]{:S(2)}, u32[]{:S(2)}) %collective-permute-start.3) | collective-permute-done | bytes 131104 | tf_op jit(solution)/shard_map/ppermute | solution.py:168
  50.3 7.0 %collective-permute-done.4 = bf16[128,512]{1,0:T(8,128)(2,1)S(1)} collective-permute-done((bf16[128,512]{1,0:T(8,128)(2,1)S(1)}, bf16[128,512]{1,0:T(8,128)(2,1)S(1)}, u32[]{:S(2)}, u32[]{:S(2)}) %collective-permute-start.4) | collective-permute-done | bytes 131104 | tf_op jit(solution)/shard_map/ppermute | solution.py:168
  57.3 0.0 collective-permute-done.5
  57.3 0.1 add_convert_fusion
  57.4 0.7 %slice_bitcast_fusion = (bf16[1,128,256]{2,1,0:T(8,128)(2,1)}, bf16[1,128,256]{2,1,0:T(8,128)(2,1)}) fusion(bf16[128,512]{1,0:T(8,128)(2,1)S(1)} %add_convert_fusion), kind=kLoop, calls=%fused_computation.2 | loop fusion | bytes 262144 | tf_op jit(solution)/shard_map/broadcast_in_dim | solution.py:180
  (4 shorter events, 0.1 us)
Async XLA Ops:
  0.6 11.7 %copy-start.6 = (bf16[256]{0:T(256)(128)(2,1)S(1)}, bf16[256]{0:T(256)(128)(2,1)}, u32[]{:S(2)}) copy-start(bf16[256]{0:T(256)(128)(2,1)} %param.11) | copy-start | bytes 1540
  0.6 11.7 %copy-start.5 = (bf16[2048]{0:T(1024)(128)(2,1)S(1)}, bf16[2048]{0:T(1024)(128)(2,1)}, u32[]{:S(2)}) copy-start(bf16[2048]{0:T(1024)(128)(2,1)} %param.8) | copy-start | bytes 12292
  0.7 16.3 %copy-start = (bf16[1,128,256]{2,1,0:T(8,128)(2,1)S(1)}, bf16[1,128,256]{2,1,0:T(8,128)(2,1)}, u32[]{:S(2)}) copy-start(bf16[1,128,256]{2,1,0:T(8,128)(2,1)} %param.9) | copy-start | bytes 196612
  0.7 16.3 %copy-start.1 = (bf16[1,128,256]{2,1,0:T(8,128)(2,1)S(1)}, bf16[1,128,256]{2,1,0:T(8,128)(2,1)}, u32[]{:S(2)}) copy-start(bf16[1,128,256]{2,1,0:T(8,128)(2,1)} %param.10) | copy-start | bytes 196612
  1.6 10.9 %collective-permute-start.2 = (bf16[128,512]{1,0:T(8,128)(2,1)S(1)}, bf16[128,512]{1,0:T(8,128)(2,1)S(1)}, u32[]{:S(2)}, u32[]{:S(2)}) collective-permute-start(bf16[128,512]{1,0:T(8,128)(2,1)S(1)} %pad_maximum_fusion), channel_id=1, source_target_pairs={{0,6},{1,7},{8,14},{9,15},{16,22},{17,23},{24,30},{25,31}} | collective-permute-start | bytes 393224 | tf_op jit(solution)/shard_map/ppermute | solution.py:161
  8.6 6.7 %collective-permute-start.1 = (bf16[128,512]{1,0:T(8,128)(2,1)S(1)}, bf16[128,512]{1,0:T(8,128)(2,1)S(1)}, u32[]{:S(2)}, u32[]{:S(2)}) collective-permute-start(bf16[128,512]{1,0:T(8,128)(2,1)S(1)} %pad_maximum_fusion), channel_id=1, source_target_pairs={{0,4},{2,6},{1,5},{3,7},{8,12},{10,14},{9,13},{11,15},{16,20},{18,... | collective-permute-start | bytes 393224 | tf_op jit(solution)/shard_map/ppermute | solution.py:161
  9.9 7.1 %collective-permute-start = (bf16[128,512]{1,0:T(8,128)(2,1)S(1)}, bf16[128,512]{1,0:T(8,128)(2,1)S(1)}, u32[]{:S(2)}, u32[]{:S(2)}) collective-permute-start(bf16[128,512]{1,0:T(8,128)(2,1)S(1)} %pad_maximum_fusion), channel_id=1, source_target_pairs={{0,2},{2,4},{4,6},{1,3},{3,5},{5,7},{8,10},{10,12},{12,14},{9,11},... | collective-permute-start | bytes 393224 | tf_op jit(solution)/shard_map/ppermute | solution.py:161
  17.0 0.7 %copy-start.4 = (s32[1,8]{1,0:T(1,128)S(1)}, s32[1,8]{1,0:T(1,128)}, u32[]{:S(2)}) copy-start(s32[1,8]{1,0:T(1,128)} %refs_0_.1) | copy-start | bytes 100
  17.6 1.0 %copy-start.2 = (bf16[1,128,2048]{2,1,0:T(8,128)(2,1)S(1)}, bf16[1,128,2048]{2,1,0:T(8,128)(2,1)}, u32[]{:S(2)}) copy-start(bf16[1,128,2048]{2,1,0:T(8,128)(2,1)} %param.7) | copy-start | bytes 1572868
  18.7 1.0 %copy-start.3 = (bf16[1,128,2048]{2,1,0:T(8,128)(2,1)S(1)}, bf16[1,128,2048]{2,1,0:T(8,128)(2,1)}, u32[]{:S(2)}) copy-start(bf16[1,128,2048]{2,1,0:T(8,128)(2,1)} %param.12) | copy-start | bytes 1572868
  27.8 8.2 %collective-permute-start.8 = (f32[1,2304]{1,0:T(1,128)S(1)}, f32[1,2304]{1,0:T(1,128)S(1)}, u32[]{:S(2)}, u32[]{:S(2)}) collective-permute-start(f32[1,2304]{1,0:T(1,128)S(1)} %get-tuple-element.19), channel_id=1, source_target_pairs={{0,6},{2,0},{4,2},{6,4},{1,7},{3,1},{5,3},{7,5},{8,14},{10,8},{12,... | collective-permute-start | bytes 27656 | tf_op jit(solution)/shard_map/ppermute | solution.py:148
  32.1 4.6 %collective-permute-start.7 = (f32[1,2304]{1,0:T(1,128)S(1)}, f32[1,2304]{1,0:T(1,128)S(1)}, u32[]{:S(2)}, u32[]{:S(2)}) collective-permute-start(f32[1,2304]{1,0:T(1,128)S(1)} %get-tuple-element.19), channel_id=1, source_target_pairs={{0,4},{2,6},{4,0},{6,2},{1,5},{3,7},{5,1},{7,3},{8,12},{10,14},{12... | collective-permute-start | bytes 27656 | tf_op jit(solution)/shard_map/ppermute | solution.py:148
  33.9 5.5 %collective-permute-start.6 = (f32[1,2304]{1,0:T(1,128)S(1)}, f32[1,2304]{1,0:T(1,128)S(1)}, u32[]{:S(2)}, u32[]{:S(2)}) collective-permute-start(f32[1,2304]{1,0:T(1,128)S(1)} %get-tuple-element.19), channel_id=1, source_target_pairs={{0,2},{2,4},{4,6},{6,0},{1,3},{3,5},{5,7},{7,1},{8,10},{10,12},{12... | collective-permute-start | bytes 27656 | tf_op jit(solution)/shard_map/ppermute | solution.py:148
  39.4 6.2 %collective-permute-start.11 = (f32[1,2304]{1,0:T(1,128)S(1)}, f32[1,2304]{1,0:T(1,128)S(1)}, u32[]{:S(2)}, u32[]{:S(2)}) collective-permute-start(f32[1,2304]{1,0:T(1,128)S(1)} %add_add_fusion), channel_id=1, source_target_pairs={{0,24},{8,0},{16,8},{24,16},{1,25},{9,1},{17,9},{25,17},{2,26},{10... | collective-permute-start | bytes 27656 | tf_op jit(solution)/shard_map/ppermute | solution.py:148
  41.9 5.0 %collective-permute-start.10 = (f32[1,2304]{1,0:T(1,128)S(1)}, f32[1,2304]{1,0:T(1,128)S(1)}, u32[]{:S(2)}, u32[]{:S(2)}) collective-permute-start(f32[1,2304]{1,0:T(1,128)S(1)} %add_add_fusion), channel_id=1, source_target_pairs={{0,16},{8,24},{16,0},{24,8},{1,17},{9,25},{17,1},{25,9},{2,18},{10... | collective-permute-start | bytes 27656 | tf_op jit(solution)/shard_map/ppermute | solution.py:148
  42.4 4.6 %collective-permute-start.9 = (f32[1,2304]{1,0:T(1,128)S(1)}, f32[1,2304]{1,0:T(1,128)S(1)}, u32[]{:S(2)}, u32[]{:S(2)}) collective-permute-start(f32[1,2304]{1,0:T(1,128)S(1)} %add_add_fusion), channel_id=1, source_target_pairs={{0,8},{8,16},{16,24},{24,0},{1,9},{9,17},{17,25},{25,1},{2,10},{10... | collective-permute-start | bytes 27656 | tf_op jit(solution)/shard_map/ppermute | solution.py:148
  43.0 7.3 %collective-permute-start.3 = (bf16[128,512]{1,0:T(8,128)(2,1)S(1)}, bf16[128,512]{1,0:T(8,128)(2,1)S(1)}, u32[]{:S(2)}, u32[]{:S(2)}) collective-permute-start(bf16[128,512]{1,0:T(8,128)(2,1)S(1)} %get-tuple-element.16), channel_id=1, source_target_pairs={{2,0},{4,2},{6,4},{3,1},{5,3},{7,5},{10,8},{12,10},{14,12},{11,9},... | collective-permute-start | bytes 393224 | tf_op jit(solution)/shard_map/ppermute | solution.py:168
  44.3 13.0 %collective-permute-start.4 = (bf16[128,512]{1,0:T(8,128)(2,1)S(1)}, bf16[128,512]{1,0:T(8,128)(2,1)S(1)}, u32[]{:S(2)}, u32[]{:S(2)}) collective-permute-start(bf16[128,512]{1,0:T(8,128)(2,1)S(1)} %get-tuple-element.17), channel_id=1, source_target_pairs={{4,0},{6,2},{5,1},{7,3},{12,8},{14,10},{13,9},{15,11},{20,16},{22,... | collective-permute-start | bytes 393224 | tf_op jit(solution)/shard_map/ppermute | solution.py:168
  45.6 11.6 %collective-permute-start.5 = (bf16[128,512]{1,0:T(8,128)(2,1)S(1)}, bf16[128,512]{1,0:T(8,128)(2,1)S(1)}, u32[]{:S(2)}, u32[]{:S(2)}) collective-permute-start(bf16[128,512]{1,0:T(8,128)(2,1)S(1)} %get-tuple-element.18), channel_id=1, source_target_pairs={{6,0},{7,1},{14,8},{15,9},{22,16},{23,17},{30,24},{31,25}} | collective-permute-start | bytes 393224 | tf_op jit(solution)/shard_map/ppermute | solution.py:168

commit v2 on v1

v2 whole, which is shorter than its diff:
```python
import functools

import jax
import jax.numpy as jnp
from jax import lax
from jax.experimental import pallas as pl
from jax.experimental.pallas import tpu as pltpu
from jax.sharding import PartitionSpec as P

HEAD_DIM = 128
HEADS = 32
KV_HEADS = 4
GROUP = HEADS // KV_HEADS
PAIR = 2
SCALE = HEAD_DIM ** (-0.5)
LOG2E = 1.4426950408889634
NEGATIVE = -1e30
VMEM = pl.BlockSpec(memory_space=pltpu.VMEM)
SMEM = pl.BlockSpec(memory_space=pltpu.SMEM)


def dot(left, right, left_dim, right_dim):
    return lax.dot_general(
        left, right, (((left_dim,), (right_dim,)), ((), ())), preferred_element_type=jnp.float32
    )


def head_cols(head):
    return slice(head * HEAD_DIM, (head + 1) * HEAD_DIM)


def shape(dims, dtype):
    return jax.ShapeDtypeStruct(dims, dtype)


def params(mebibytes):
    return pltpu.CompilerParams(vmem_limit_bytes=mebibytes * 1024 * 1024)


def biased(values, bias):
    return (values.astype(jnp.float32) + bias.astype(jnp.float32)).astype(jnp.bfloat16)


def prepare_kernel(
    slots, len_ref, q_ref, qb_ref, vb_ref, g_ref, k_ref, v_ref, bias_ref, keys_ref, values_ref,
    queries_ref, grads_ref, score_ref, dprob_ref, live_ref,
):
    tok, width = q_ref.shape
    kv_heads = k_ref.shape[1] // HEAD_DIM
    rank = lax.axis_index("ctx")
    query_pos = rank * tok + lax.broadcasted_iota(jnp.int32, (1, tok), 1)
    start = jnp.zeros((1, tok), jnp.int32)
    end = jnp.int32(0)
    for doc in range(len_ref.shape[1]):
        length = len_ref[0, doc]
        end = end + length
        start = start + jnp.where(query_pos >= end, length, 0)
    offsets = lax.broadcasted_iota(jnp.int32, (tok, tok), 0)
    for slot in range(slots):
        key_pos = (rank - slot) * tok + offsets
        live = (key_pos >= start) & (key_pos <= query_pos)
        live_ref[slot * tok : (slot + 1) * tok, :] = jnp.where(live, 0.0, NEGATIVE)
    bias_ref[...] = vb_ref[...]
    keys_ref[...] = k_ref[...]
    values_ref[...] = biased(v_ref[...], vb_ref[...])
    for kv_head in range(kv_heads):
        cols = head_cols(kv_head)
        keys = k_ref[:, cols]
        values = values_ref[:, cols]
        for head in range(kv_head * GROUP, (kv_head + 1) * GROUP):
            at = head_cols(head)
            queries_ref[head * tok : (head + 1) * tok, :] = biased(q_ref[:, at], qb_ref[:, at])
            grads_ref[head * tok : (head + 1) * tok, :] = g_ref[:, at]
        rows = slice(kv_head * GROUP * tok, (kv_head + 1) * GROUP * tok)
        score_ref[:, rows] = dot(keys, queries_ref[rows, :], 1, 1)
        dprob_ref[:, rows] = dot(values, grads_ref[rows, :], 1, 1)


def attend_kernel(slots, *refs):
    bias_ref, k_ref, v_ref, queries_ref, grads_ref, score_ref, dprob_ref, live_ref = refs[:8]
    got_refs = refs[8 : 8 + slots - 1]
    refs = refs[8 + slots - 1 :]
    probs_ref, dscore_ref, keys_ref, values_ref, sums_ref, own_ref = refs[:6]
    out_refs = refs[6:]
    tok, kv_width = k_ref.shape
    kv_heads = kv_width // HEAD_DIM
    keys_ref[:tok, :] = k_ref[...]
    values_ref[:tok, :] = v_ref[...]
    for slot in range(1, slots):
        rows = slice(slot * tok, (slot + 1) * tok)
        keys_ref[rows, :] = got_refs[slot - 1][:, :kv_width]
        values_ref[rows, :] = biased(got_refs[slot - 1][:, kv_width:], bias_ref[...])
    for kv_head in range(kv_heads):
        cols = head_cols(kv_head)
        keys = keys_ref[tok:, cols]
        values = values_ref[tok:, cols]
        key_term = jnp.zeros((slots * tok, HEAD_DIM), jnp.float32)
        value_term = jnp.zeros((slots * tok, HEAD_DIM), jnp.float32)
        for pair in range(GROUP // PAIR):
            first = kv_head * GROUP + pair * PAIR
            at = slice(first * tok, (first + PAIR) * tok)
            queries = queries_ref[at, :]
            grads = grads_ref[at, :]
            live = jnp.concatenate([live_ref[...]] * PAIR, axis=1)
            score = jnp.concatenate([score_ref[:, at], dot(keys, queries, 1, 1)], axis=0)
            score = score * (SCALE * LOG2E) + live
            row_max = jnp.max(score, axis=0, keepdims=True)
            weights = jnp.exp2(score - row_max)
            probs = weights * (1.0 / jnp.sum(weights, axis=0, keepdims=True))
            dprob = jnp.concatenate([dprob_ref[:, at], dot(values, grads, 1, 1)], axis=0)
            delta = jnp.sum(probs * dprob, axis=0, keepdims=True)
            dscore = (probs * (dprob - delta)).astype(jnp.bfloat16)
            probs = probs.astype(jnp.bfloat16)
            probs_ref[:, at] = probs
            dscore_ref[:, at] = dscore
            value_term = value_term + dot(probs, grads, 1, 0)
            key_term = key_term + dot(dscore, queries, 1, 0)
        key_term = key_term * SCALE
        sums_ref[kv_head : kv_head + 1, :] = jnp.sum(value_term, axis=0, keepdims=True)
        value_cols = head_cols(kv_heads + kv_head)
        own_ref[:, cols] = key_term[:tok]
        own_ref[:, value_cols] = value_term[:tok]
        for slot in range(1, slots):
            rows = slice(slot * tok, (slot + 1) * tok)
            out_refs[slot - 1][:, cols] = key_term[rows].astype(jnp.bfloat16)
            out_refs[slot - 1][:, value_cols] = value_term[rows].astype(jnp.bfloat16)


def finish_kernel(
    probs_ref, dscore_ref, keys_ref, values_ref, vsums_ref, attn_ref, qg_ref, sums_ref
):
    tok, width = attn_ref.shape
    kv_heads = keys_ref.shape[1] // HEAD_DIM
    heads = width // HEAD_DIM
    copies = sums_ref.shape[0]
    for kv_head in range(kv_heads):
        cols = head_cols(kv_head)
        keys_t = keys_ref[:, cols].T
        values_t = values_ref[:, cols].T
        for pair in range(GROUP // PAIR):
            first = kv_head * GROUP + pair * PAIR
            at = slice(first * tok, (first + PAIR) * tok)
            attn = dot(values_t, probs_ref[:, at], 1, 0).T
            query_grad = (dot(keys_t, dscore_ref[:, at], 1, 0) * SCALE).T
            for n in range(PAIR):
                head = first + n
                rows = slice(n * tok, (n + 1) * tok)
                attn_ref[:, head_cols(head)] = attn[rows].astype(jnp.bfloat16)
                qg_ref[:, head_cols(head)] = query_grad[rows].astype(jnp.bfloat16)
                sums_ref[0, head : head + 1, :] = jnp.sum(query_grad[rows], axis=0, keepdims=True)
    sums_ref[0, heads:, :] = vsums_ref[...]
    sums = sums_ref[0]
    for copy in range(1, copies):
        sums_ref[copy] = sums


def shards(q_proj, q_bias, k_proj, v_proj, v_bias, dout, lengths):
    _, tok, width = q_proj.shape
    kv_width = k_proj.shape[2]
    heads = width // HEAD_DIM
    kv_heads = kv_width // HEAD_DIM
    ctx = lax.axis_size("ctx")
    batches = lax.axis_size("dp")
    rows = ctx * tok
    columns = heads * tok
    keys, values, v_bias = k_proj[0], v_proj[0], v_bias[None]
    pair = jnp.concatenate([keys, values], axis=1)
    got = [
        lax.ppermute(pair, "ctx", [(i, i + shift) for i in range(ctx - shift)])
        for shift in range(1, ctx)
    ]
    prepared = pl.pallas_call(
        functools.partial(prepare_kernel, ctx),
        out_shape=[
            shape((1, kv_width), jnp.bfloat16),
            shape((tok, kv_width), jnp.bfloat16),
            shape((tok, kv_width), jnp.bfloat16),
            shape((columns, HEAD_DIM), jnp.bfloat16),
            shape((columns, HEAD_DIM), jnp.bfloat16),
            shape((tok, columns), jnp.float32),
            shape((tok, columns), jnp.float32),
            shape((rows, tok), jnp.float32),
        ],
        in_specs=[SMEM] + [VMEM] * 6,
        out_specs=[VMEM] * 8,
        compiler_params=params(16),
        cost_estimate=pl.CostEstimate(
            flops=4 * tok * tok * width, bytes_accessed=16 * tok * width, transcendentals=0
        ),
        name="prepare",
    )(lengths, q_proj[0], q_bias[None], v_bias, dout[0], keys, values)
    term = shape((tok, 2 * kv_width), jnp.bfloat16)
    probs, dscore, all_keys, all_values, value_sums, own, *terms = pl.pallas_call(
        functools.partial(attend_kernel, ctx),
        out_shape=[
            shape((rows, columns), jnp.bfloat16),
            shape((rows, columns), jnp.bfloat16),
            shape((rows, kv_width), jnp.bfloat16),
            shape((rows, kv_width), jnp.bfloat16),
            shape((kv_heads, HEAD_DIM), jnp.float32),
            shape((tok, 2 * kv_width), jnp.float32),
        ]
        + [term] * (ctx - 1),
        in_specs=[VMEM] * (8 + ctx - 1),
        out_specs=[VMEM] * (6 + ctx - 1),
        compiler_params=params(40),
        cost_estimate=pl.CostEstimate(
            flops=8 * rows * tok * width,
            bytes_accessed=4 * rows * columns,
            transcendentals=rows * columns,
        ),
        name="attend",
    )(*prepared, *got)
    back = [
        lax.ppermute(term, "ctx", [(i, i - shift) for i in range(shift, ctx)])
        for shift, term in enumerate(terms, 1)
    ]
    attn, q_grad, sums = pl.pallas_call(
        finish_kernel,
        out_shape=[
            shape((tok, width), jnp.bfloat16),
            shape((tok, width), jnp.bfloat16),
            shape((batches * ctx, heads + kv_heads, HEAD_DIM), jnp.float32),
        ],
        in_specs=[VMEM] * 5,
        out_specs=[VMEM] * 3,
        compiler_params=params(24),
        cost_estimate=pl.CostEstimate(
            flops=4 * rows * tok * width, bytes_accessed=4 * rows * columns, transcendentals=0
        ),
        name="finish",
    )(probs, dscore, all_keys, all_values, value_sums)
    sums = lax.all_to_all(sums, ("dp", "ctx"), split_axis=0, concat_axis=0, tiled=True)
    sums = jnp.sum(sums, axis=0) / batches
    kv_grad = own
    for part in back:
        kv_grad = kv_grad + part.astype(jnp.float32)
    kv_grad = kv_grad.astype(jnp.bfloat16)
    return (
        attn[None],
        q_grad[None],
        kv_grad[None, :, :kv_width],
        kv_grad[None, :, kv_width:],
        sums[:heads].reshape(width),
        sums[heads:].reshape(kv_width),
    )


def solution(mesh):
    tokens = P("dp", "ctx", "tp")
    return jax.shard_map(
        shards,
        mesh=mesh,
        in_specs=(tokens, P("tp"), tokens, tokens, P("tp"), tokens, P("dp", None)),
        out_specs=(tokens, tokens, tokens, tokens, P("tp"), P("tp")),
        check_vma=False,
    )
```

time: 58.4 us -> 49.7 us (0.85)
  waiting for transfers between devices: 17.1 us -> 8.33 us
  local copies, waits for them, and re-layouts: 4.59 us -> 7.59 us
  starting transfers between devices: 26.4 us -> 23.8 us
    ppermute x6 -> x0, starting transfers between devices: 11.8 us -> none  [sum_over(): lax.ppermute(part, axis, [(i, (i + shift) % size) for i in range(size)])]
    all_to_all x0 -> x1, starting transfers between devices: none -> 9.23 us  [shards(): lax.all_to_all(sums, ('dp', 'ctx'), split_axis=0, concat_axis=0, tiled=True)]
    ppermute x3, waiting for transfers between devices: 9.09 us -> 2.89 us  [shards(): lax.ppermute(term, 'ctx', [(i, i - shift) for i in range(shift, ctx)])]
    all_to_all x0 -> x1, waiting for transfers between devices: none -> 5.44 us  [shards(): lax.all_to_all(sums, ('dp', 'ctx'), split_axis=0, concat_axis=0, tiled=True)]
    ppermute x3, waiting for transfers between devices: 4.56 us -> 0.01 us  [shards(): lax.ppermute(pair, 'ctx', [(i, i + shift) for i in range(ctx - shift)])]
    ppermute x6 -> x0, waiting for transfers between devices: 3.5 us -> none  [sum_over(): lax.ppermute(part, axis, [(i, (i + shift) % size) for i in range(size)])]
    unnamed x14 -> x10, local copies, waits for them, and re-layouts: 2.75 us -> 4.41 us
    reshape x0 -> x2, local copies, waits for them, and re-layouts: none -> 1.16 us  [the longest x1 0.6 us: shards(): sums[:heads].reshape(width)]
  transfers between devices with their start and end apart: 12 -> 7, of which waited for: 8 -> 2; matrix products, arithmetic and copies ran while one was open for 2% -> 4% of each run, Pallas kernels for 0% -> 6%
where the time goes in v2:
time: 49.7 us; the launch traced here: 49.1 us
  starting transfers between devices  23.8 us (48%)
  waiting for transfers between devices  8.33 us (17%)
  Pallas kernels  7.61 us (15%)
  local copies, waits for them, and re-layouts  7.59 us (15%)
  other arithmetic  0.97 us (2%)
  between operations  0.76 us (2%)
    ppermute x3, starting transfers between devices, shards(): lax.ppermute(pair, 'ctx', [(i, i + shift) for i in range(ctx - shift)])  10.7 us
    all_to_all x1, starting transfers between devices, shards(): lax.all_to_all(sums, ('dp', 'ctx'), split_axis=0, concat_axis=0, tiled=True)  9.23 us
    all_to_all x1, waiting for transfers between devices, shards(): lax.all_to_all(sums, ('dp', 'ctx'), split_axis=0, concat_axis=0, tiled=True)  5.44 us
    pallas_call x1, Pallas kernels, shards(): pl.pallas_call(functools.partial(attend_kernel, ctx), out_shape=[shape((r...  4.62 us
    unnamed x10, local copies, waits for them, and re-layouts  4.41 us
    ppermute x3, starting transfers between devices, shards(): lax.ppermute(term, 'ctx', [(i, i - shift) for i in range(shift, ctx)])  3.88 us
    ppermute x3, waiting for transfers between devices, shards(): lax.ppermute(term, 'ctx', [(i, i - shift) for i in range(shift, ctx)])  2.89 us
    pallas_call x1, Pallas kernels, shards(): pl.pallas_call(finish_kernel, out_shape=[shape((tok, width), jnp.bfloat16...  1.91 us
  transfers between devices with their start and end apart: 7, of which 2 were waited for; matrix products, arithmetic and copies ran while one was open for 4% of the time, Pallas kernels for 6%

profile of v2, /device:TPU:0, one launch (start us, length us, event | category | flops | bytes accessed | tf_op | source)
XLA Modules:
  0.0 49.1 jit_solution(3290425817954094526)
XLA Ops:
  0.6 0.9 %pad_maximum_fusion = bf16[128,512]{1,0:T(8,128)(2,1)S(1)} fusion(bf16[128,256]{1,0:T(8,128)(2,1)} %bitcast.18, bf16[128,256]{1,0:T(8,128)(2,1)} %bitcast.16), kind=kLoop, calls=%fused_computation.1 | loop fusion | flops 262144 | bytes 262144 | tf_op jit(solution)/shard_map/concatenate | solution.py:167
  1.5 7.0 %collective-permute-start.2 = (bf16[128,512]{1,0:T(8,128)(2,1)S(1)}, bf16[128,512]{1,0:T(8,128)(2,1)S(1)}, u32[]{:S(2)}, u32[]{:S(2)}) collective-permute-start(bf16[128,512]{1,0:T(8,128)(2,1)S(1)} %pad_maximum_fusion), channel_id=1, source_target_pairs={{0,6},{1,7},{8,14},{9,15},{16,22},{17,23},{24,30},{25,31}} | collective-permute-start | bytes 393224 | tf_op jit(solution)/shard_map/ppermute | solution.py:169
  8.5 1.3 %collective-permute-start.1 = (bf16[128,512]{1,0:T(8,128)(2,1)S(1)}, bf16[128,512]{1,0:T(8,128)(2,1)S(1)}, u32[]{:S(2)}, u32[]{:S(2)}) collective-permute-start(bf16[128,512]{1,0:T(8,128)(2,1)S(1)} %pad_maximum_fusion), channel_id=1, source_target_pairs={{0,4},{2,6},{1,5},{3,7},{8,12},{10,14},{9,13},{11,15},{16,20},{18,... | collective-permute-start | bytes 393224 | tf_op jit(solution)/shard_map/ppermute | solution.py:169
  9.8 2.5 %collective-permute-start = (bf16[128,512]{1,0:T(8,128)(2,1)S(1)}, bf16[128,512]{1,0:T(8,128)(2,1)S(1)}, u32[]{:S(2)}, u32[]{:S(2)}) collective-permute-start(bf16[128,512]{1,0:T(8,128)(2,1)S(1)} %pad_maximum_fusion), channel_id=1, source_target_pairs={{0,2},{2,4},{4,6},{1,3},{3,5},{5,7},{8,10},{10,12},{12,14},{9,11},... | collective-permute-start | bytes 393224 | tf_op jit(solution)/shard_map/ppermute | solution.py:169
  12.3 0.7 %broadcast_in_dim.19.vb_ref = bf16[1,256]{1,0:T(2,128)(2,1)S(1)} reshape(bf16[256]{0:T(256)(128)(2,1)} %param.11) | data formatting | bytes 1024 | tf_op jit(solution)/shard_map/broadcast_in_dim | solution.py:166
  12.9 0.7 %broadcast_in_dim.18.qb_ref = bf16[1,2048]{1,0:T(2,128)(2,1)S(1)} reshape(bf16[2048]{0:T(1024)(128)(2,1)} %param.8) | data formatting | bytes 8192 | tf_op jit(solution)/shard_map/broadcast_in_dim | solution.py:191
  13.6 0.0 copy-start
  13.6 1.0 %copy-done = bf16[1,128,2048]{2,1,0:T(8,128)(2,1)S(1)} copy-done((bf16[1,128,2048]{2,1,0:T(8,128)(2,1)S(1)}, bf16[1,128,2048]{2,1,0:T(8,128)(2,1)}, u32[]{:S(2)}) %copy-start) | copy-done | bytes 524312
  14.7 0.0 copy-start.1
  14.7 1.0 %copy-done.1 = bf16[1,128,2048]{2,1,0:T(8,128)(2,1)S(1)} copy-done((bf16[1,128,2048]{2,1,0:T(8,128)(2,1)S(1)}, bf16[1,128,2048]{2,1,0:T(8,128)(2,1)}, u32[]{:S(2)}) %copy-start.1) | copy-done | bytes 524312
  15.7 0.0 copy-start.2
  15.7 0.8 %copy-done.2 = bf16[1,128,256]{2,1,0:T(8,128)(2,1)S(1)} copy-done((bf16[1,128,256]{2,1,0:T(8,128)(2,1)S(1)}, bf16[1,128,256]{2,1,0:T(8,128)(2,1)}, u32[]{:S(2)}) %copy-start.2) | copy-done | bytes 65560
  16.5 0.0 copy-start.3
  16.5 0.8 %copy-done.3 = bf16[1,128,256]{2,1,0:T(8,128)(2,1)S(1)} copy-done((bf16[1,128,256]{2,1,0:T(8,128)(2,1)S(1)}, bf16[1,128,256]{2,1,0:T(8,128)(2,1)}, u32[]{:S(2)}) %copy-start.3) | copy-done | bytes 65560
  17.4 0.0 copy-start.4
  17.4 0.7 %copy-done.4 = s32[1,8]{1,0:T(1,128)S(1)} copy-done((s32[1,8]{1,0:T(1,128)S(1)}, s32[1,8]{1,0:T(1,128)}, u32[]{:S(2)}) %copy-start.4) | copy-done | bytes 56
  18.0 1.1 %prepare.1 = (bf16[1,256]{1,0:T(2,128)(2,1)S(1)}, bf16[128,256]{1,0:T(8,128)(2,1)S(1)}, bf16[128,256]{1,0:T(8,128)(2,1)S(1)}, bf16[2048,128]{1,0:T(8,128)(2,1)S(...) custom-call(s32[1,8]{1,0:T(1,128)S(1)} %copy-done.4, ...), custom_call_target="tpu_custom_call" | custom-call | flops 134217728 | bytes 4194304 | tf_op jit(solution)/shard_map/prepare/pallas_call | solution.py:172
  19.1 0.0 collective-permute-done.2.refs_10_
  19.1 0.0 collective-permute-done.1.refs_9_
  19.1 0.0 collective-permute-done.refs_8_
  19.2 4.6 %attend.1 = (bf16[512,2048]{1,0:T(8,128)(2,1)S(1)}, bf16[512,2048]{1,0:T(8,128)(2,1)S(1)}, bf16[512,256]{1,0:T(8,128)(2,1)S(1)}, bf16[512,256]{1,0:T(8,128)(2,1)...) custom-call(bf16[1,256]{1,0:T(2,128)(2,1)S(1)} %get-tuple-element.26, ...), custom_call_target="tpu_custom_call" | custom-call | flops 1073741824 | bytes 4194304 | tf_op jit(solution)/shard_map/attend/pallas_call | solution.py:193
  23.8 1.3 %collective-permute-start.3 = (bf16[128,512]{1,0:T(8,128)(2,1)S(1)}, bf16[128,512]{1,0:T(8,128)(2,1)S(1)}, u32[]{:S(2)}, u32[]{:S(2)}) collective-permute-start(bf16[128,512]{1,0:T(8,128)(2,1)S(1)} %get-tuple-element.42), channel_id=1, source_target_pairs={{2,0},{4,2},{6,4},{3,1},{5,3},{7,5},{10,8},{12,10},{14,12},{11,9},... | collective-permute-start | bytes 393224 | tf_op jit(solution)/shard_map/ppermute | solution.py:215
  25.1 1.3 %collective-permute-start.4 = (bf16[128,512]{1,0:T(8,128)(2,1)S(1)}, bf16[128,512]{1,0:T(8,128)(2,1)S(1)}, u32[]{:S(2)}, u32[]{:S(2)}) collective-permute-start(bf16[128,512]{1,0:T(8,128)(2,1)S(1)} %get-tuple-element.43), channel_id=1, source_target_pairs={{4,0},{6,2},{5,1},{7,3},{12,8},{14,10},{13,9},{15,11},{20,16},{22,... | collective-permute-start | bytes 393224 | tf_op jit(solution)/shard_map/ppermute | solution.py:215
  26.4 1.3 %collective-permute-start.5 = (bf16[128,512]{1,0:T(8,128)(2,1)S(1)}, bf16[128,512]{1,0:T(8,128)(2,1)S(1)}, u32[]{:S(2)}, u32[]{:S(2)}) collective-permute-start(bf16[128,512]{1,0:T(8,128)(2,1)S(1)} %get-tuple-element.44), channel_id=1, source_target_pairs={{6,0},{7,1},{14,8},{15,9},{22,16},{23,17},{30,24},{31,25}} | collective-permute-start | bytes 393224 | tf_op jit(solution)/shard_map/ppermute | solution.py:215
  27.7 1.9 %finish.1 = (bf16[128,2048]{1,0:T(8,128)(2,1)}, bf16[128,2048]{1,0:T(8,128)(2,1)}, f32[16,18,128]{2,1,0:T(8,128)}) custom-call(bf16[512,2048]{1,0:T(8,128)(2,1)S(1)} %get-tuple-element.34.probs_ref, bf16[512,2048]{1,0:T(8,128)(2,1)S(1)} %get-tuple-element.35.dscore_ref, bf16[512,256]{1,0:T(8,128)(2,1)S(1)} %get-tuple-element.36.keys_ref, ...), custom_call_target="tpu_custom_call" | custom-call | flops 536870912 | bytes 4194304 | tf_op jit(solution)/shard_map/finish/pallas_call | solution.py:218
  29.6 9.2 %all-to-all-start = ((f32[16,18,128]{2,1,0:T(8,128)}), f32[16,18,128]{2,1,0:T(8,128)S(1)}, u32[]{:S(2)}, u32[]{:S(2)}) async-start(f32[16,18,128]{2,1,0:T(8,128)} %get-tuple-element.45), calls=%async_computation | async-start | bytes 393216 | tf_op jit(solution)/shard_map/all_to_all | solution.py:233
  38.8 0.0 collective-permute-done.3
  38.8 2.9 %collective-permute-done.4 = bf16[128,512]{1,0:T(8,128)(2,1)S(1)} collective-permute-done((bf16[128,512]{1,0:T(8,128)(2,1)S(1)}, bf16[128,512]{1,0:T(8,128)(2,1)S(1)}, u32[]{:S(2)}, u32[]{:S(2)}) %collective-permute-start.4) | collective-permute-done | bytes 131104 | tf_op jit(solution)/shard_map/ppermute | solution.py:215
  41.7 0.0 collective-permute-done.5
  41.7 0.1 add_convert_fusion
  41.8 0.7 %slice_bitcast_fusion = (bf16[1,128,256]{2,1,0:T(8,128)(2,1)}, bf16[1,128,256]{2,1,0:T(8,128)(2,1)}) fusion(bf16[128,512]{1,0:T(8,128)(2,1)S(1)} %add_convert_fusion), kind=kLoop, calls=%fused_computation.2 | loop fusion | bytes 262144 | tf_op jit(solution)/shard_map/broadcast_in_dim | solution.py:243
  42.5 5.4 %all-to-all-done = f32[16,18,128]{2,1,0:T(8,128)S(1)} async-done(((f32[16,18,128]{2,1,0:T(8,128)}), f32[16,18,128]{2,1,0:T(8,128)S(1)}, u32[]{:S(2)}, u32[]{:S(2)}) %all-to-all-start) | async-done | bytes 147488 | tf_op jit(solution)/shard_map/all_to_all | solution.py:233
  47.9 0.6 %slice_bitcast_fusion.3 = f32[256]{0:T(256)} fusion(f32[18,128]{1,0:T(8,128)S(1)} %broadcast_multiply_fusion), kind=kLoop, calls=%fused_computation.6 | loop fusion | bytes 2048 | tf_op jit(solution)/shard_map/reshape | solution.py:245
  48.5 0.6 %slice_bitcast_fusion.2 = f32[2048]{0:T(1024)} fusion(f32[18,128]{1,0:T(8,128)S(1)} %broadcast_multiply_fusion), kind=kLoop, calls=%fused_computation.4 | loop fusion | bytes 16384 | tf_op jit(solution)/shard_map/reshape | solution.py:244
  (2 shorter events, 0.0 us)
Async XLA Ops:
  1.5 17.6 %collective-permute-start.2 = (bf16[128,512]{1,0:T(8,128)(2,1)S(1)}, bf16[128,512]{1,0:T(8,128)(2,1)S(1)}, u32[]{:S(2)}, u32[]{:S(2)}) collective-permute-start(bf16[128,512]{1,0:T(8,128)(2,1)S(1)} %pad_maximum_fusion), channel_id=1, source_target_pairs={{0,6},{1,7},{8,14},{9,15},{16,22},{17,23},{24,30},{25,31}} | collective-permute-start | bytes 393224 | tf_op jit(solution)/shard_map/ppermute | solution.py:169
  8.5 10.7 %collective-permute-start.1 = (bf16[128,512]{1,0:T(8,128)(2,1)S(1)}, bf16[128,512]{1,0:T(8,128)(2,1)S(1)}, u32[]{:S(2)}, u32[]{:S(2)}) collective-permute-start(bf16[128,512]{1,0:T(8,128)(2,1)S(1)} %pad_maximum_fusion), channel_id=1, source_target_pairs={{0,4},{2,6},{1,5},{3,7},{8,12},{10,14},{9,13},{11,15},{16,20},{18,... | collective-permute-start | bytes 393224 | tf_op jit(solution)/shard_map/ppermute | solution.py:169
  9.8 9.4 %collective-permute-start = (bf16[128,512]{1,0:T(8,128)(2,1)S(1)}, bf16[128,512]{1,0:T(8,128)(2,1)S(1)}, u32[]{:S(2)}, u32[]{:S(2)}) collective-permute-start(bf16[128,512]{1,0:T(8,128)(2,1)S(1)} %pad_maximum_fusion), channel_id=1, source_target_pairs={{0,2},{2,4},{4,6},{1,3},{3,5},{5,7},{8,10},{10,12},{12,14},{9,11},... | collective-permute-start | bytes 393224 | tf_op jit(solution)/shard_map/ppermute | solution.py:169
  13.6 1.0 %copy-start = (bf16[1,128,2048]{2,1,0:T(8,128)(2,1)S(1)}, bf16[1,128,2048]{2,1,0:T(8,128)(2,1)}, u32[]{:S(2)}) copy-start(bf16[1,128,2048]{2,1,0:T(8,128)(2,1)} %param.7) | copy-start | bytes 1572868
  14.7 1.0 %copy-start.1 = (bf16[1,128,2048]{2,1,0:T(8,128)(2,1)S(1)}, bf16[1,128,2048]{2,1,0:T(8,128)(2,1)}, u32[]{:S(2)}) copy-start(bf16[1,128,2048]{2,1,0:T(8,128)(2,1)} %param.12) | copy-start | bytes 1572868
  15.7 0.8 %copy-start.2 = (bf16[1,128,256]{2,1,0:T(8,128)(2,1)S(1)}, bf16[1,128,256]{2,1,0:T(8,128)(2,1)}, u32[]{:S(2)}) copy-start(bf16[1,128,256]{2,1,0:T(8,128)(2,1)} %param.9) | copy-start | bytes 196612
  16.5 0.8 %copy-start.3 = (bf16[1,128,256]{2,1,0:T(8,128)(2,1)S(1)}, bf16[1,128,256]{2,1,0:T(8,128)(2,1)}, u32[]{:S(2)}) copy-start(bf16[1,128,256]{2,1,0:T(8,128)(2,1)} %param.10) | copy-start | bytes 196612
  17.4 0.7 %copy-start.4 = (s32[1,8]{1,0:T(1,128)S(1)}, s32[1,8]{1,0:T(1,128)}, u32[]{:S(2)}) copy-start(s32[1,8]{1,0:T(1,128)} %len_ref.1) | copy-start | bytes 100
  23.8 15.1 %collective-permute-start.3 = (bf16[128,512]{1,0:T(8,128)(2,1)S(1)}, bf16[128,512]{1,0:T(8,128)(2,1)S(1)}, u32[]{:S(2)}, u32[]{:S(2)}) collective-permute-start(bf16[128,512]{1,0:T(8,128)(2,1)S(1)} %get-tuple-element.42), channel_id=1, source_target_pairs={{2,0},{4,2},{6,4},{3,1},{5,3},{7,5},{10,8},{12,10},{14,12},{11,9},... | collective-permute-start | bytes 393224 | tf_op jit(solution)/shard_map/ppermute | solution.py:215
  25.1 16.6 %collective-permute-start.4 = (bf16[128,512]{1,0:T(8,128)(2,1)S(1)}, bf16[128,512]{1,0:T(8,128)(2,1)S(1)}, u32[]{:S(2)}, u32[]{:S(2)}) collective-permute-start(bf16[128,512]{1,0:T(8,128)(2,1)S(1)} %get-tuple-element.43), channel_id=1, source_target_pairs={{4,0},{6,2},{5,1},{7,3},{12,8},{14,10},{13,9},{15,11},{20,16},{22,... | collective-permute-start | bytes 393224 | tf_op jit(solution)/shard_map/ppermute | solution.py:215
  26.4 15.3 %collective-permute-start.5 = (bf16[128,512]{1,0:T(8,128)(2,1)S(1)}, bf16[128,512]{1,0:T(8,128)(2,1)S(1)}, u32[]{:S(2)}, u32[]{:S(2)}) collective-permute-start(bf16[128,512]{1,0:T(8,128)(2,1)S(1)} %get-tuple-element.44), channel_id=1, source_target_pairs={{6,0},{7,1},{14,8},{15,9},{22,16},{23,17},{30,24},{31,25}} | collective-permute-start | bytes 393224 | tf_op jit(solution)/shard_map/ppermute | solution.py:215
  29.6 18.3 %all-to-all-start = ((f32[16,18,128]{2,1,0:T(8,128)}), f32[16,18,128]{2,1,0:T(8,128)S(1)}, u32[]{:S(2)}, u32[]{:S(2)}) async-start(f32[16,18,128]{2,1,0:T(8,128)} %get-tuple-element.45), calls=%async_computation | async-start | bytes 393216 | tf_op jit(solution)/shard_map/all_to_all | solution.py:233

commit v3 on v2

v3 whole, which is shorter than its diff:
```python
import functools

import jax
import jax.numpy as jnp
from jax import lax
from jax.experimental import pallas as pl
from jax.experimental.pallas import tpu as pltpu
from jax.sharding import PartitionSpec as P

HEAD_DIM = 128
HEADS = 32
KV_HEADS = 4
GROUP = HEADS // KV_HEADS
PAIR = 2
SCALE = HEAD_DIM ** (-0.5)
LOG2E = 1.4426950408889634
NEGATIVE = -1e30
VMEM = pl.BlockSpec(memory_space=pltpu.VMEM)
SMEM = pl.BlockSpec(memory_space=pltpu.SMEM)


def dot(left, right, left_dim, right_dim):
    return lax.dot_general(
        left, right, (((left_dim,), (right_dim,)), ((), ())), preferred_element_type=jnp.float32
    )


def head_cols(head):
    return slice(head * HEAD_DIM, (head + 1) * HEAD_DIM)


def shape(dims, dtype):
    return jax.ShapeDtypeStruct(dims, dtype)


def params(mebibytes):
    return pltpu.CompilerParams(vmem_limit_bytes=mebibytes * 1024 * 1024)


def biased(values, bias):
    return (values.astype(jnp.float32) + bias.astype(jnp.float32)).astype(jnp.bfloat16)


def prepare_kernel(
    slots, len_ref, pair_ref, qb_ref, vb_ref, q_ref, g_ref, bias_ref, queries_ref, grads_ref,
    score_ref, dprob_ref, live_ref,
):
    tok = q_ref.shape[0]
    kv_heads = vb_ref.shape[0]
    rank = lax.axis_index("ctx")
    query_pos = rank * tok + lax.broadcasted_iota(jnp.int32, (1, tok), 1)
    start = jnp.zeros((1, tok), jnp.int32)
    end = jnp.int32(0)
    for doc in range(len_ref.shape[1]):
        length = len_ref[0, doc]
        end = end + length
        start = start + jnp.where(query_pos >= end, length, 0)
    offsets = lax.broadcasted_iota(jnp.int32, (tok, tok), 0)
    for slot in range(slots):
        key_pos = (rank - slot) * tok + offsets
        live = (key_pos >= start) & (key_pos <= query_pos)
        live_ref[slot * tok : (slot + 1) * tok, :] = jnp.where(live, 0.0, NEGATIVE)
    bias_ref[...] = vb_ref[...]
    column = lax.broadcasted_iota(jnp.int32, (tok, HEAD_DIM), 1)
    for kv_head in range(kv_heads):
        keys = pair_ref[:, head_cols(kv_head)]
        values = biased(pair_ref[:, head_cols(kv_heads + kv_head)], vb_ref[kv_head : kv_head + 1, :])
        for head in range(kv_head * GROUP, (kv_head + 1) * GROUP):
            at = slice(head * tok, (head + 1) * tok)
            queries_ref[at, :HEAD_DIM] = biased(q_ref[:, head_cols(head)], qb_ref[head : head + 1, :])
            queries_ref[at, HEAD_DIM:] = (column == head).astype(jnp.bfloat16)
            grads_ref[at, :] = g_ref[:, head_cols(head)]
        rows = slice(kv_head * GROUP * tok, (kv_head + 1) * GROUP * tok)
        score_ref[:, rows] = dot(keys, queries_ref[rows, :HEAD_DIM], 1, 1)
        dprob_ref[:, rows] = dot(values, grads_ref[rows, :], 1, 1)


def attend_kernel(slots, *refs):
    bias_ref, queries_ref, grads_ref, score_ref, dprob_ref, live_ref = refs[:6]
    pair_refs = refs[6 : 6 + slots][::-1]
    refs = refs[6 + slots :]
    probs_ref, dscore_ref, keys_ref, values_ref, sums_ref, own_ref = refs[:6]
    out_refs = refs[6:]
    tok = pair_refs[0].shape[0]
    kv_heads = bias_ref.shape[0]
    kv_width = kv_heads * HEAD_DIM
    heads = kv_heads * GROUP
    for slot in range(slots):
        rows = slice(slot * tok, (slot + 1) * tok)
        keys_ref[rows, :] = pair_refs[slot][:, :kv_width]
        for kv_head in range(kv_heads):
            values_ref[rows, head_cols(kv_head)] = biased(
                pair_refs[slot][:, head_cols(kv_heads + kv_head)], bias_ref[kv_head : kv_head + 1, :]
            )
    for kv_head in range(kv_heads):
        cols = head_cols(kv_head)
        keys = keys_ref[tok:, cols]
        values = values_ref[tok:, cols]
        key_term = jnp.zeros((slots * tok, 2 * HEAD_DIM), jnp.float32)
        value_term = jnp.zeros((slots * tok, HEAD_DIM), jnp.float32)
        for pair in range(GROUP // PAIR):
            first = kv_head * GROUP + pair * PAIR
            at = slice(first * tok, (first + PAIR) * tok)
            queries = queries_ref[at, :]
            grads = grads_ref[at, :]
            live = jnp.concatenate([live_ref[...]] * PAIR, axis=1)
            score = jnp.concatenate(
                [score_ref[:, at], dot(keys, queries[:, :HEAD_DIM], 1, 1)], axis=0
            )
            score = score * (SCALE * LOG2E) + live
            row_max = jnp.max(score, axis=0, keepdims=True)
            weights = jnp.exp2(score - row_max)
            probs = weights * (1.0 / jnp.sum(weights, axis=0, keepdims=True))
            dprob = jnp.concatenate([dprob_ref[:, at], dot(values, grads, 1, 1)], axis=0)
            delta = jnp.sum(probs * dprob, axis=0, keepdims=True)
            dscore = (probs * (dprob - delta)).astype(jnp.bfloat16)
            probs = probs.astype(jnp.bfloat16)
            probs_ref[:, at] = probs
            dscore_ref[:, at] = dscore
            value_term = value_term + dot(probs, grads, 1, 0)
            key_term = key_term + dot(dscore, queries, 1, 0)
        over_queries = key_term[:, HEAD_DIM:]
        key_term = key_term[:, :HEAD_DIM] * SCALE
        high = over_queries.astype(jnp.bfloat16)
        low = (over_queries - high.astype(jnp.float32)).astype(jnp.bfloat16)
        all_keys = keys_ref[:, cols]
        query_sums = (dot(high, all_keys, 0, 0) + dot(low, all_keys, 0, 0)) * SCALE
        of_group = slice(kv_head * GROUP, (kv_head + 1) * GROUP)
        sums_ref[of_group, :] = query_sums[of_group]
        sums_ref[heads + kv_head : heads + kv_head + 1, :] = jnp.sum(
            value_term, axis=0, keepdims=True
        )
        value_cols = head_cols(kv_heads + kv_head)
        own_ref[:, cols] = key_term[:tok]
        own_ref[:, value_cols] = value_term[:tok]
        for slot in range(1, slots):
            rows = slice(slot * tok, (slot + 1) * tok)
            out_refs[slot - 1][:, cols] = key_term[rows].astype(jnp.bfloat16)
            out_refs[slot - 1][:, value_cols] = value_term[rows].astype(jnp.bfloat16)


def finish_kernel(probs_ref, dscore_ref, keys_ref, values_ref, attn_ref, qg_ref):
    tok = attn_ref.shape[0]
    kv_heads = keys_ref.shape[1] // HEAD_DIM
    for kv_head in range(kv_heads):
        cols = head_cols(kv_head)
        keys_t = keys_ref[:, cols].T
        values_t = values_ref[:, cols].T
        for pair in range(GROUP // PAIR):
            first = kv_head * GROUP + pair * PAIR
            at = slice(first * tok, (first + PAIR) * tok)
            attn = dot(values_t, probs_ref[:, at], 1, 0).T
            query_grad = (dot(keys_t, dscore_ref[:, at], 1, 0) * SCALE).T
            for n in range(PAIR):
                head = first + n
                rows = slice(n * tok, (n + 1) * tok)
                attn_ref[:, head_cols(head)] = attn[rows].astype(jnp.bfloat16)
                qg_ref[:, head_cols(head)] = query_grad[rows].astype(jnp.bfloat16)


def collect_kernel(batches, parts, kv_parts, *refs):
    sum_refs, refs = refs[:parts], refs[parts:]
    own_ref, refs = refs[0], refs[1:]
    back_refs, refs = refs[:kv_parts], refs[kv_parts:]
    kg_ref, vg_ref, qb_ref, vb_ref = refs
    heads = qb_ref.shape[0]
    kv_width = kg_ref.shape[1]
    total = sum_refs[0][...]
    for ref in sum_refs[1:]:
        total = total + ref[...]
    total = total * (1.0 / batches)
    qb_ref[...] = total[:heads]
    vb_ref[...] = total[heads:]
    term = own_ref[...]
    for ref in back_refs:
        term = term + ref[...].astype(jnp.float32)
    term = term.astype(jnp.bfloat16)
    kg_ref[...] = term[:, :kv_width]
    vg_ref[...] = term[:, kv_width:]


def total_of(parts):
    return functools.reduce(lambda left, right: left + right, parts)


def exchange(axis, part):
    size = lax.axis_size(axis)
    if size & (size - 1):
        return [part] + [
            lax.ppermute(part, axis, [(i, (i + shift) % size) for i in range(size)])
            for shift in range(1, size)
        ]
    parts, step = [part], 1
    while step < size:
        part = total_of(parts)
        parts = [part, lax.ppermute(part, axis, [(i, i ^ step) for i in range(size)])]
        step *= 2
    return parts


def shards(q_proj, q_bias, k_proj, v_proj, v_bias, dout, lengths):
    _, tok, width = q_proj.shape
    kv_width = k_proj.shape[2]
    heads = width // HEAD_DIM
    kv_heads = kv_width // HEAD_DIM
    ctx = lax.axis_size("ctx")
    batches = lax.axis_size("dp")
    rows = ctx * tok
    columns = heads * tok
    pair = jnp.concatenate([k_proj[0], v_proj[0]], axis=1)
    pairs = [
        lax.ppermute(pair, "ctx", [(i, i + shift) for i in range(ctx - shift)])
        for shift in range(ctx - 1, 0, -1)
    ] + [pair]
    prepared = pl.pallas_call(
        functools.partial(prepare_kernel, ctx),
        out_shape=[
            shape((kv_heads, HEAD_DIM), jnp.bfloat16),
            shape((columns, 2 * HEAD_DIM), jnp.bfloat16),
            shape((columns, HEAD_DIM), jnp.bfloat16),
            shape((tok, columns), jnp.float32),
            shape((tok, columns), jnp.float32),
            shape((rows, tok), jnp.float32),
        ],
        in_specs=[SMEM] + [VMEM] * 5,
        out_specs=[VMEM] * 6,
        compiler_params=params(16),
        cost_estimate=pl.CostEstimate(
            flops=4 * tok * tok * width, bytes_accessed=16 * tok * width, transcendentals=0
        ),
        name="prepare",
    )(
        lengths,
        pair,
        q_bias.reshape(heads, HEAD_DIM),
        v_bias.reshape(kv_heads, HEAD_DIM),
        q_proj[0],
        dout[0],
    )
    term = shape((tok, 2 * kv_width), jnp.bfloat16)
    probs, dscore, all_keys, all_values, sums, own, *terms = pl.pallas_call(
        functools.partial(attend_kernel, ctx),
        out_shape=[
            shape((rows, columns), jnp.bfloat16),
            shape((rows, columns), jnp.bfloat16),
            shape((rows, kv_width), jnp.bfloat16),
            shape((rows, kv_width), jnp.bfloat16),
            shape((heads + kv_heads, HEAD_DIM), jnp.float32),
            shape((tok, 2 * kv_width), jnp.float32),
        ]
        + [term] * (ctx - 1),
        in_specs=[VMEM] * (6 + ctx),
        out_specs=[VMEM] * (6 + ctx - 1),
        compiler_params=params(40),
        cost_estimate=pl.CostEstimate(
            flops=8 * rows * tok * width,
            bytes_accessed=4 * rows * columns,
            transcendentals=rows * columns,
        ),
        name="attend",
    )(*prepared, *pairs)
    back = [
        lax.ppermute(term, "ctx", [(i, i - shift) for i in range(shift, ctx)])
        for shift, term in enumerate(terms, 1)
    ]
    attn, q_grad = pl.pallas_call(
        finish_kernel,
        out_shape=[
            shape((tok, width), jnp.bfloat16),
            shape((tok, width), jnp.bfloat16),
        ],
        in_specs=[VMEM] * 4,
        out_specs=[VMEM] * 2,
        compiler_params=params(24),
        cost_estimate=pl.CostEstimate(
            flops=4 * rows * tok * width, bytes_accessed=4 * rows * columns, transcendentals=0
        ),
        name="finish",
    )(probs, dscore, all_keys, all_values)
    sums = exchange("ctx", total_of(exchange("dp", sums)))
    k_grad, v_grad, q_sum, v_sum = pl.pallas_call(
        functools.partial(collect_kernel, batches, len(sums), len(back)),
        out_shape=[
            shape((tok, kv_width), jnp.bfloat16),
            shape((tok, kv_width), jnp.bfloat16),
            shape((heads, HEAD_DIM), jnp.float32),
            shape((kv_heads, HEAD_DIM), jnp.float32),
        ],
        in_specs=[VMEM] * (len(sums) + 1 + len(back)),
        out_specs=[VMEM] * 4,
        compiler_params=params(8),
        cost_estimate=pl.CostEstimate(
            flops=8 * tok * kv_width, bytes_accessed=16 * tok * kv_width, transcendentals=0
        ),
        name="collect",
    )(*sums, own, *back)
    return (
        attn[None],
        q_grad[None],
        k_grad[None],
        v_grad[None],
        q_sum.reshape(width),
        v_sum.reshape(kv_width),
    )


def solution(mesh):
    tokens = P("dp", "ctx", "tp")
    return jax.shard_map(
        shards,
        mesh=mesh,
        in_specs=(tokens, P("tp"), tokens, tokens, P("tp"), tokens, P("dp", None)),
        out_specs=(tokens, tokens, tokens, tokens, P("tp"), P("tp")),
        check_vma=False,
    )
```

time: 49.7 us -> 44.8 us (0.901)
  local copies, waits for them, and re-layouts: 7.59 us -> 4.07 us
  starting transfers between devices: 23.8 us -> 22.5 us
  Pallas kernels: 7.61 us -> 8.7 us
  waiting for transfers between devices: 8.33 us -> 7.42 us
    all_to_all x1 -> x0, starting transfers between devices: 9.23 us -> none  [shards(): lax.all_to_all(sums, ('dp', 'ctx'), split_axis=0, concat_axis=0, tiled=True)]
    ppermute x0 -> x4, starting transfers between devices: none -> 7.91 us  [exchange(): lax.ppermute(part, axis, [(i, i ^ step) for i in range(size)])]
    ppermute x0 -> x4, waiting for transfers between devices: none -> 7.41 us  [exchange(): lax.ppermute(part, axis, [(i, i ^ step) for i in range(size)])]
    all_to_all x1 -> x0, waiting for transfers between devices: 5.44 us -> none  [shards(): lax.all_to_all(sums, ('dp', 'ctx'), split_axis=0, concat_axis=0, tiled=True)]
    ppermute x3, waiting for transfers between devices: 2.89 us -> 0.01 us  [shards(): lax.ppermute(term, 'ctx', [(i, i - shift) for i in range(shift, ctx)])]
    broadcast_in_dim x3 -> x0, local copies, waits for them, and re-layouts: 2.01 us -> none  [the longest x1 0.69 us: shards(): q_bias[None]]
    reshape x2 -> x0, local copies, waits for them, and re-layouts: 1.16 us -> none  [the longest x1 0.6 us: shards(): sums[:heads].reshape(width)]
    pallas_call x0 -> x1, Pallas kernels: none -> 0.7 us  [shards(): pl.pallas_call(functools.partial(collect_kernel, batches, len(sums), len(...]
  transfers between devices with their start and end apart: 7 -> 10, of which waited for: 2 -> 3; matrix products, arithmetic and copies ran while one was open for 4% -> 0% of each run, Pallas kernels for 6% -> 7%
where the time goes in v3:
time: 44.8 us; the launch traced here: 44.4 us
  starting transfers between devices  22.5 us (50%)
  Pallas kernels  8.7 us (19%)
  waiting for transfers between devices  7.42 us (17%)
  local copies, waits for them, and re-layouts  4.07 us (9%)
  other arithmetic  0.89 us (2%)
  between operations  0.75 us (2%)
    ppermute x3, starting transfers between devices, shards(): lax.ppermute(pair, 'ctx', [(i, i + shift) for i in range(ctx - shift)])  10.7 us
    ppermute x4, starting transfers between devices, exchange(): lax.ppermute(part, axis, [(i, i ^ step) for i in range(size)])  7.91 us
    ppermute x4, waiting for transfers between devices, exchange(): lax.ppermute(part, axis, [(i, i ^ step) for i in range(size)])  7.41 us
    pallas_call x1, Pallas kernels, shards(): pl.pallas_call(functools.partial(attend_kernel, ctx), out_shape=[shape((r...  5.08 us
    unnamed x10, local copies, waits for them, and re-layouts  4.07 us
    ppermute x3, starting transfers between devices, shards(): lax.ppermute(term, 'ctx', [(i, i - shift) for i in range(shift, ctx)])  3.88 us
    pallas_call x1, Pallas kernels, shards(): pl.pallas_call(finish_kernel, out_shape=[shape((tok, width), jnp.bfloat16...  1.8 us
    pallas_call x1, Pallas kernels, shards(): pl.pallas_call(functools.partial(prepare_kernel, ctx), out_shape=[shape((...  1.11 us
  transfers between devices with their start and end apart: 10, of which 3 were waited for; matrix products, arithmetic and copies ran while one was open for 0% of the time, Pallas kernels for 7%

profile of v3, /device:TPU:0, one launch (start us, length us, event | category | flops | bytes accessed | tf_op | source)
XLA Modules:
  0.0 44.4 jit_solution(5361352486862977448)
XLA Ops:
  0.6 0.9 %pad_maximum_fusion.pair_ref.refs_9_ = bf16[128,512]{1,0:T(8,128)(2,1)S(1)} fusion(bf16[128,256]{1,0:T(8,128)(2,1)} %bitcast.16, bf16[128,256]{1,0:T(8,128)(2,1)} %bitcast.17), kind=kLoop, calls=%fused_computation | loop fusion | flops 262144 | bytes 262144 | tf_op jit(solution)/shard_map/concatenate | solution.py:210
  1.5 4.9 %collective-permute-start.2 = (bf16[128,512]{1,0:T(8,128)(2,1)S(1)}, bf16[128,512]{1,0:T(8,128)(2,1)S(1)}, u32[]{:S(2)}, u32[]{:S(2)}) collective-permute-start(bf16[128,512]{1,0:T(8,128)(2,1)S(1)} %pad_maximum_fusion.pair_ref.refs_9_), channel_id=1, source_target_pairs={{0,2},{2,4},{4,6},{1,3},{3,5},{5,7},{8,10},{10,12},{12,14},{9,11},... | collective-permute-start | bytes 393224 | tf_op jit(solution)/shard_map/ppermute | solution.py:212
  6.5 4.5 %collective-permute-start.1 = (bf16[128,512]{1,0:T(8,128)(2,1)S(1)}, bf16[128,512]{1,0:T(8,128)(2,1)S(1)}, u32[]{:S(2)}, u32[]{:S(2)}) collective-permute-start(bf16[128,512]{1,0:T(8,128)(2,1)S(1)} %pad_maximum_fusion.pair_ref.refs_9_), channel_id=1, source_target_pairs={{0,4},{2,6},{1,5},{3,7},{8,12},{10,14},{9,13},{11,15},{16,20},{18,... | collective-permute-start | bytes 393224 | tf_op jit(solution)/shard_map/ppermute | solution.py:212
  11.0 1.3 %collective-permute-start = (bf16[128,512]{1,0:T(8,128)(2,1)S(1)}, bf16[128,512]{1,0:T(8,128)(2,1)S(1)}, u32[]{:S(2)}, u32[]{:S(2)}) collective-permute-start(bf16[128,512]{1,0:T(8,128)(2,1)S(1)} %pad_maximum_fusion.pair_ref.refs_9_), channel_id=1, source_target_pairs={{0,6},{1,7},{8,14},{9,15},{16,22},{17,23},{24,30},{25,31}} | collective-permute-start | bytes 393224 | tf_op jit(solution)/shard_map/ppermute | solution.py:212
  12.3 0.0 copy-start
  12.3 1.0 %copy-done = bf16[1,128,2048]{2,1,0:T(8,128)(2,1)S(1)} copy-done((bf16[1,128,2048]{2,1,0:T(8,128)(2,1)S(1)}, bf16[1,128,2048]{2,1,0:T(8,128)(2,1)}, u32[]{:S(2)}) %copy-start) | copy-done | bytes 524312
  13.3 0.0 copy-start.1
  13.3 1.0 %copy-done.1 = bf16[1,128,2048]{2,1,0:T(8,128)(2,1)S(1)} copy-done((bf16[1,128,2048]{2,1,0:T(8,128)(2,1)S(1)}, bf16[1,128,2048]{2,1,0:T(8,128)(2,1)}, u32[]{:S(2)}) %copy-start.1) | copy-done | bytes 524312
  14.4 0.0 copy-start.2
  14.4 0.7 %copy-done.2 = bf16[2048]{0:T(1024)(128)(2,1)S(1)} copy-done((bf16[2048]{0:T(1024)(128)(2,1)S(1)}, bf16[2048]{0:T(1024)(128)(2,1)}, u32[]{:S(2)}) %copy-start.2) | copy-done | bytes 4120
  15.0 0.0 copy-start.3
  15.0 0.7 %copy-done.3 = s32[1,8]{1,0:T(1,128)S(1)} copy-done((s32[1,8]{1,0:T(1,128)S(1)}, s32[1,8]{1,0:T(1,128)}, u32[]{:S(2)}) %copy-start.3) | copy-done | bytes 56
  15.7 0.0 copy-start.4
  15.7 0.7 %copy-done.4 = bf16[256]{0:T(256)(128)(2,1)S(1)} copy-done((bf16[256]{0:T(256)(128)(2,1)S(1)}, bf16[256]{0:T(256)(128)(2,1)}, u32[]{:S(2)}) %copy-start.4) | copy-done | bytes 536
  16.4 1.1 %prepare.1 = (bf16[2,128]{1,0:T(2,128)(2,1)S(1)}, bf16[2048,256]{1,0:T(8,128)(2,1)S(1)}, bf16[2048,128]{1,0:T(8,128)(2,1)S(1)}, f32[128,2048]{1,0:T(8,128)S(1)},...) custom-call(s32[1,8]{1,0:T(1,128)S(1)} %copy-done.3, bf16[128,512]{1,0:T(8,128)(2,1)S(1)} %pad_maximum_fusion.pair_ref.refs_9_, ...), custom_call_target="tpu_custom_call" | custom-call | flops 134217728 | bytes 4194304 | tf_op jit(solution)/shard_map/prepare/pallas_call | solution.py:215
  17.5 0.0 collective-permute-done.2.refs_8_
  17.5 0.0 collective-permute-done.1.refs_7_
  17.5 0.0 collective-permute-done.refs_6_
  17.5 5.1 %attend.1 = (bf16[512,2048]{1,0:T(8,128)(2,1)S(1)}, bf16[512,2048]{1,0:T(8,128)(2,1)S(1)}, bf16[512,256]{1,0:T(8,128)(2,1)S(1)}, bf16[512,256]{1,0:T(8,128)(2,1)...) custom-call(bf16[2,128]{1,0:T(2,128)(2,1)S(1)} %get-tuple-element.27, ...), custom_call_target="tpu_custom_call" | custom-call | flops 1073741824 | bytes 4194304 | tf_op jit(solution)/shard_map/attend/pallas_call | solution.py:241
  22.6 1.3 %collective-permute-start.7 = (bf16[128,512]{1,0:T(8,128)(2,1)S(1)}, bf16[128,512]{1,0:T(8,128)(2,1)S(1)}, u32[]{:S(2)}, u32[]{:S(2)}) collective-permute-start(bf16[128,512]{1,0:T(8,128)(2,1)S(1)} %get-tuple-element.41), channel_id=1, source_target_pairs={{2,0},{4,2},{6,4},{3,1},{5,3},{7,5},{10,8},{12,10},{14,12},{11,9},... | collective-permute-start | bytes 393224 | tf_op jit(solution)/shard_map/ppermute | solution.py:263
  23.9 1.3 %collective-permute-start.8 = (bf16[128,512]{1,0:T(8,128)(2,1)S(1)}, bf16[128,512]{1,0:T(8,128)(2,1)S(1)}, u32[]{:S(2)}, u32[]{:S(2)}) collective-permute-start(bf16[128,512]{1,0:T(8,128)(2,1)S(1)} %get-tuple-element.42), channel_id=1, source_target_pairs={{4,0},{6,2},{5,1},{7,3},{12,8},{14,10},{13,9},{15,11},{20,16},{22,... | collective-permute-start | bytes 393224 | tf_op jit(solution)/shard_map/ppermute | solution.py:263
  25.2 1.3 %collective-permute-start.9 = (bf16[128,512]{1,0:T(8,128)(2,1)S(1)}, bf16[128,512]{1,0:T(8,128)(2,1)S(1)}, u32[]{:S(2)}, u32[]{:S(2)}) collective-permute-start(bf16[128,512]{1,0:T(8,128)(2,1)S(1)} %get-tuple-element.43), channel_id=1, source_target_pairs={{6,0},{7,1},{14,8},{15,9},{22,16},{23,17},{30,24},{31,25}} | collective-permute-start | bytes 393224 | tf_op jit(solution)/shard_map/ppermute | solution.py:263
  26.5 1.6 %collective-permute-start.3 = (f32[18,128]{1,0:T(8,128)S(1)}, f32[18,128]{1,0:T(8,128)S(1)}, u32[]{:S(2)}, u32[]{:S(2)}) collective-permute-start(f32[18,128]{1,0:T(8,128)S(1)} %get-tuple-element.39), channel_id=1, source_target_pairs={{0,8},{8,0},{16,24},{24,16},{1,9},{9,1},{17,25},{25,17},{2,10},{10... | collective-permute-start | bytes 27656 | tf_op jit(solution)/shard_map/ppermute | solution.py:196
  28.1 2.2 %collective-permute-done.3 = f32[18,128]{1,0:T(8,128)S(1)} collective-permute-done((f32[18,128]{1,0:T(8,128)S(1)}, f32[18,128]{1,0:T(8,128)S(1)}, u32[]{:S(2)}, u32[]{:S(2)}) %collective-permute-start.3) | collective-permute-done | bytes 9248 | tf_op jit(solution)/shard_map/ppermute | solution.py:196
  30.3 1.5 %collective-permute-start.4 = (f32[18,128]{1,0:T(8,128)S(1)}, f32[18,128]{1,0:T(8,128)S(1)}, u32[]{:S(2)}, u32[]{:S(2)}) collective-permute-start(f32[18,128]{1,0:T(8,128)S(1)} %add.9), channel_id=1, source_target_pairs={{0,16},{8,24},{16,0},{24,8},{1,17},{9,25},{17,1},{25,9},{2,18},{10... | collective-permute-start | bytes 27656 | tf_op jit(solution)/shard_map/ppermute | solution.py:196
  31.8 2.2 %collective-permute-done.4 = f32[18,128]{1,0:T(8,128)S(1)} collective-permute-done((f32[18,128]{1,0:T(8,128)S(1)}, f32[18,128]{1,0:T(8,128)S(1)}, u32[]{:S(2)}, u32[]{:S(2)}) %collective-permute-start.4) | collective-permute-done | bytes 9248 | tf_op jit(solution)/shard_map/ppermute | solution.py:196
  34.0 2.0 %collective-permute-start.5 = (f32[18,128]{1,0:T(8,128)S(1)}, f32[18,128]{1,0:T(8,128)S(1)}, u32[]{:S(2)}, u32[]{:S(2)}) collective-permute-start(f32[18,128]{1,0:T(8,128)S(1)} %add.10), channel_id=1, source_target_pairs={{0,2},{2,0},{4,6},{6,4},{1,3},{3,1},{5,7},{7,5},{8,10},{10,8},{12,... | collective-permute-start | bytes 27656 | tf_op jit(solution)/shard_map/ppermute | solution.py:196
  36.0 3.0 %collective-permute-done.5 = f32[18,128]{1,0:T(8,128)S(1)} collective-permute-done((f32[18,128]{1,0:T(8,128)S(1)}, f32[18,128]{1,0:T(8,128)S(1)}, u32[]{:S(2)}, u32[]{:S(2)}) %collective-permute-start.5) | collective-permute-done | bytes 9248 | tf_op jit(solution)/shard_map/ppermute | solution.py:196
  39.0 2.8 %collective-permute-start.6 = (f32[18,128]{1,0:T(8,128)S(1)}, f32[18,128]{1,0:T(8,128)S(1)}, u32[]{:S(2)}, u32[]{:S(2)}) collective-permute-start(f32[18,128]{1,0:T(8,128)S(1)} %add.11.refs_0_), channel_id=1, source_target_pairs={{0,4},{2,6},{4,0},{6,2},{1,5},{3,7},{5,1},{7,3},{8,12},{10,14},{12... | collective-permute-start | bytes 27656 | tf_op jit(solution)/shard_map/ppermute | solution.py:196
  41.8 1.8 %finish.1 = (bf16[128,2048]{1,0:T(8,128)(2,1)}, bf16[128,2048]{1,0:T(8,128)(2,1)}) custom-call(bf16[512,2048]{1,0:T(8,128)(2,1)S(1)} %get-tuple-element.33.probs_ref, bf16[512,2048]{1,0:T(8,128)(2,1)S(1)} %get-tuple-element.34.dscore_ref, bf16[512,256]{1,0:T(8,128)(2,1)S(1)} %get-tuple-element.35.keys_ref, bf16[512,256]{1,0:T(8,128)(2,1)S(1)} %get-tuple-element.36.values_ref), custom_call_target="tpu_custom_call" | custom-call | flops 536870912 | bytes 4194304 | tf_op jit(solution)/shard_map/finish/pallas_call | solution.py:266
  43.6 0.0 collective-permute-done.6.refs_1_
  43.6 0.0 collective-permute-done.7.refs_3_
  43.6 0.0 collective-permute-done.8.refs_4_
  43.7 0.0 collective-permute-done.9.refs_5_
  43.7 0.7 %collect.1 = (bf16[128,256]{1,0:T(8,128)(2,1)}, bf16[128,256]{1,0:T(8,128)(2,1)}, f32[16,128]{1,0:T(8,128)}, f32[2,128]{1,0:T(2,128)}) custom-call(f32[18,128]{1,0:T(8,128)S(1)} %add.11.refs_0_, f32[18,128]{1,0:T(8,128)S(1)} %collective-permute-done.6.refs_1_, f32[128,512]{1,0:T(8,128)S(1)} %get-tuple-element.40.refs_2_, ...), custom_call_target="tpu_custom_call" | custom-call | flops 262144 | bytes 524288 | tf_op jit(solution)/shard_map/collect/pallas_call | solution.py:281
  (3 shorter events, 0.0 us)
Async XLA Ops:
  1.5 16.0 %collective-permute-start.2 = (bf16[128,512]{1,0:T(8,128)(2,1)S(1)}, bf16[128,512]{1,0:T(8,128)(2,1)S(1)}, u32[]{:S(2)}, u32[]{:S(2)}) collective-permute-start(bf16[128,512]{1,0:T(8,128)(2,1)S(1)} %pad_maximum_fusion.pair_ref.refs_9_), channel_id=1, source_target_pairs={{0,2},{2,4},{4,6},{1,3},{3,5},{5,7},{8,10},{10,12},{12,14},{9,11},... | collective-permute-start | bytes 393224 | tf_op jit(solution)/shard_map/ppermute | solution.py:212
  6.5 11.0 %collective-permute-start.1 = (bf16[128,512]{1,0:T(8,128)(2,1)S(1)}, bf16[128,512]{1,0:T(8,128)(2,1)S(1)}, u32[]{:S(2)}, u32[]{:S(2)}) collective-permute-start(bf16[128,512]{1,0:T(8,128)(2,1)S(1)} %pad_maximum_fusion.pair_ref.refs_9_), channel_id=1, source_target_pairs={{0,4},{2,6},{1,5},{3,7},{8,12},{10,14},{9,13},{11,15},{16,20},{18,... | collective-permute-start | bytes 393224 | tf_op jit(solution)/shard_map/ppermute | solution.py:212
  11.0 6.5 %collective-permute-start = (bf16[128,512]{1,0:T(8,128)(2,1)S(1)}, bf16[128,512]{1,0:T(8,128)(2,1)S(1)}, u32[]{:S(2)}, u32[]{:S(2)}) collective-permute-start(bf16[128,512]{1,0:T(8,128)(2,1)S(1)} %pad_maximum_fusion.pair_ref.refs_9_), channel_id=1, source_target_pairs={{0,6},{1,7},{8,14},{9,15},{16,22},{17,23},{24,30},{25,31}} | collective-permute-start | bytes 393224 | tf_op jit(solution)/shard_map/ppermute | solution.py:212
  12.3 1.0 %copy-start = (bf16[1,128,2048]{2,1,0:T(8,128)(2,1)S(1)}, bf16[1,128,2048]{2,1,0:T(8,128)(2,1)}, u32[]{:S(2)}) copy-start(bf16[1,128,2048]{2,1,0:T(8,128)(2,1)} %param.7) | copy-start | bytes 1572868
  13.3 1.0 %copy-start.1 = (bf16[1,128,2048]{2,1,0:T(8,128)(2,1)S(1)}, bf16[1,128,2048]{2,1,0:T(8,128)(2,1)}, u32[]{:S(2)}) copy-start(bf16[1,128,2048]{2,1,0:T(8,128)(2,1)} %param.12) | copy-start | bytes 1572868
  14.4 0.7 %copy-start.2 = (bf16[2048]{0:T(1024)(128)(2,1)S(1)}, bf16[2048]{0:T(1024)(128)(2,1)}, u32[]{:S(2)}) copy-start(bf16[2048]{0:T(1024)(128)(2,1)} %param.8) | copy-start | bytes 12292
  15.0 0.7 %copy-start.3 = (s32[1,8]{1,0:T(1,128)S(1)}, s32[1,8]{1,0:T(1,128)}, u32[]{:S(2)}) copy-start(s32[1,8]{1,0:T(1,128)} %len_ref.1) | copy-start | bytes 100
  15.7 0.7 %copy-start.4 = (bf16[256]{0:T(256)(128)(2,1)S(1)}, bf16[256]{0:T(256)(128)(2,1)}, u32[]{:S(2)}) copy-start(bf16[256]{0:T(256)(128)(2,1)} %param.11) | copy-start | bytes 1540
  22.6 21.0 %collective-permute-start.7 = (bf16[128,512]{1,0:T(8,128)(2,1)S(1)}, bf16[128,512]{1,0:T(8,128)(2,1)S(1)}, u32[]{:S(2)}, u32[]{:S(2)}) collective-permute-start(bf16[128,512]{1,0:T(8,128)(2,1)S(1)} %get-tuple-element.41), channel_id=1, source_target_pairs={{2,0},{4,2},{6,4},{3,1},{5,3},{7,5},{10,8},{12,10},{14,12},{11,9},... | collective-permute-start | bytes 393224 | tf_op jit(solution)/shard_map/ppermute | solution.py:263
  23.9 19.7 %collective-permute-start.8 = (bf16[128,512]{1,0:T(8,128)(2,1)S(1)}, bf16[128,512]{1,0:T(8,128)(2,1)S(1)}, u32[]{:S(2)}, u32[]{:S(2)}) collective-permute-start(bf16[128,512]{1,0:T(8,128)(2,1)S(1)} %get-tuple-element.42), channel_id=1, source_target_pairs={{4,0},{6,2},{5,1},{7,3},{12,8},{14,10},{13,9},{15,11},{20,16},{22,... | collective-permute-start | bytes 393224 | tf_op jit(solution)/shard_map/ppermute | solution.py:263
  25.2 18.5 %collective-permute-start.9 = (bf16[128,512]{1,0:T(8,128)(2,1)S(1)}, bf16[128,512]{1,0:T(8,128)(2,1)S(1)}, u32[]{:S(2)}, u32[]{:S(2)}) collective-permute-start(bf16[128,512]{1,0:T(8,128)(2,1)S(1)} %get-tuple-element.43), channel_id=1, source_target_pairs={{6,0},{7,1},{14,8},{15,9},{22,16},{23,17},{30,24},{31,25}} | collective-permute-start | bytes 393224 | tf_op jit(solution)/shard_map/ppermute | solution.py:263
  26.5 3.8 %collective-permute-start.3 = (f32[18,128]{1,0:T(8,128)S(1)}, f32[18,128]{1,0:T(8,128)S(1)}, u32[]{:S(2)}, u32[]{:S(2)}) collective-permute-start(f32[18,128]{1,0:T(8,128)S(1)} %get-tuple-element.39), channel_id=1, source_target_pairs={{0,8},{8,0},{16,24},{24,16},{1,9},{9,1},{17,25},{25,17},{2,10},{10... | collective-permute-start | bytes 27656 | tf_op jit(solution)/shard_map/ppermute | solution.py:196
  30.3 3.7 %collective-permute-start.4 = (f32[18,128]{1,0:T(8,128)S(1)}, f32[18,128]{1,0:T(8,128)S(1)}, u32[]{:S(2)}, u32[]{:S(2)}) collective-permute-start(f32[18,128]{1,0:T(8,128)S(1)} %add.9), channel_id=1, source_target_pairs={{0,16},{8,24},{16,0},{24,8},{1,17},{9,25},{17,1},{25,9},{2,18},{10... | collective-permute-start | bytes 27656 | tf_op jit(solution)/shard_map/ppermute | solution.py:196
  34.0 5.1 %collective-permute-start.5 = (f32[18,128]{1,0:T(8,128)S(1)}, f32[18,128]{1,0:T(8,128)S(1)}, u32[]{:S(2)}, u32[]{:S(2)}) collective-permute-start(f32[18,128]{1,0:T(8,128)S(1)} %add.10), channel_id=1, source_target_pairs={{0,2},{2,0},{4,6},{6,4},{1,3},{3,1},{5,7},{7,5},{8,10},{10,8},{12,... | collective-permute-start | bytes 27656 | tf_op jit(solution)/shard_map/ppermute | solution.py:196
  39.0 4.6 %collective-permute-start.6 = (f32[18,128]{1,0:T(8,128)S(1)}, f32[18,128]{1,0:T(8,128)S(1)}, u32[]{:S(2)}, u32[]{:S(2)}) collective-permute-start(f32[18,128]{1,0:T(8,128)S(1)} %add.11.refs_0_), channel_id=1, source_target_pairs={{0,4},{2,6},{4,0},{6,2},{1,5},{3,7},{5,1},{7,3},{8,12},{10,14},{12... | collective-permute-start | bytes 27656 | tf_op jit(solution)/shard_map/ppermute | solution.py:196

commit v4 on v3

--- a/solution.py
+++ b/solution.py
@@ -158,17 +158,12 @@
                 qg_ref[:, head_cols(head)] = query_grad[rows].astype(jnp.bfloat16)
 
 
-def collect_kernel(batches, parts, kv_parts, *refs):
-    sum_refs, refs = refs[:parts], refs[parts:]
-    own_ref, refs = refs[0], refs[1:]
+def collect_kernel(batches, kv_parts, sums_ref, own_ref, *refs):
     back_refs, refs = refs[:kv_parts], refs[kv_parts:]
     kg_ref, vg_ref, qb_ref, vb_ref = refs
     heads = qb_ref.shape[0]
     kv_width = kg_ref.shape[1]
-    total = sum_refs[0][...]
-    for ref in sum_refs[1:]:
-        total = total + ref[...]
-    total = total * (1.0 / batches)
+    total = jnp.sum(sums_ref[...], axis=0) * (1.0 / batches)
     qb_ref[...] = total[:heads]
     vb_ref[...] = total[heads:]
     term = own_ref[...]
@@ -179,23 +174,9 @@
     vg_ref[...] = term[:, kv_width:]
 
 
-def total_of(parts):
-    return functools.reduce(lambda left, right: left + right, parts)
-
-
-def exchange(axis, part):
-    size = lax.axis_size(axis)
-    if size & (size - 1):
-        return [part] + [
-            lax.ppermute(part, axis, [(i, (i + shift) % size) for i in range(size)])
-            for shift in range(1, size)
-        ]
-    parts, step = [part], 1
-    while step < size:
-        part = total_of(parts)
-        parts = [part, lax.ppermute(part, axis, [(i, i ^ step) for i in range(size)])]
-        step *= 2
-    return parts
+def gathered(axis, part):
+    copies = jnp.broadcast_to(part, (lax.axis_size(axis),) + part.shape)
+    return lax.all_to_all(copies, axis, split_axis=0, concat_axis=0, tiled=True)
 
 
 def shards(q_proj, q_bias, k_proj, v_proj, v_bias, dout, lengths):
@@ -277,23 +258,23 @@
         ),
         name="finish",
     )(probs, dscore, all_keys, all_values)
-    sums = exchange("ctx", total_of(exchange("dp", sums)))
+    sums = gathered("ctx", jnp.sum(gathered("dp", sums), axis=0))
     k_grad, v_grad, q_sum, v_sum = pl.pallas_call(
-        functools.partial(collect_kernel, batches, len(sums), len(back)),
+        functools.partial(collect_kernel, batches, len(back)),
         out_shape=[
             shape((tok, kv_width), jnp.bfloat16),
             shape((tok, kv_width), jnp.bfloat16),
             shape((heads, HEAD_DIM), jnp.float32),
             shape((kv_heads, HEAD_DIM), jnp.float32),
         ],
-        in_specs=[VMEM] * (len(sums) + 1 + len(back)),
+        in_specs=[VMEM] * (2 + len(back)),
         out_specs=[VMEM] * 4,
         compiler_params=params(8),
         cost_estimate=pl.CostEstimate(
             flops=8 * tok * kv_width, bytes_accessed=16 * tok * kv_width, transcendentals=0
         ),
         name="collect",
-    )(*sums, own, *back)
+    )(sums, own, *back)
     return (
         attn[None],
         q_grad[None],

time: 44.8 us -> 51.2 us (1.14)
  blocking collectives: 0 us -> 8.32 us
  waiting for transfers between devices: 7.42 us -> 2.33 us
  local copies, waits for them, and re-layouts: 4.07 us -> 7.63 us
  starting transfers between devices: 22.5 us -> 21.5 us
    all_to_all x0 -> x1, blocking collectives: none -> 8.32 us  [gathered(): return lax.all_to_all(copies, axis, split_axis=0, concat_axis=0, tiled=True)]
    ppermute x4 -> x0, starting transfers between devices: 7.91 us -> none  [exchange(): lax.ppermute(part, axis, [(i, i ^ step) for i in range(size)])]
    ppermute x4 -> x0, waiting for transfers between devices: 7.41 us -> none  [exchange(): lax.ppermute(part, axis, [(i, i ^ step) for i in range(size)])]
    all_to_all x0 -> x1, starting transfers between devices: none -> 6.9 us  [gathered(): return lax.all_to_all(copies, axis, split_axis=0, concat_axis=0, tiled=True)]
    unnamed x10 -> x14, local copies, waits for them, and re-layouts: 4.07 us -> 6.99 us
    all_to_all x0 -> x1, waiting for transfers between devices: none -> 2.32 us  [gathered(): return lax.all_to_all(copies, axis, split_axis=0, concat_axis=0, tiled=True)]
    broadcast_in_dim x0 -> x2, local copies, waits for them, and re-layouts: none -> 0.63 us  [gathered(): copies = jnp.broadcast_to(part, (lax.axis_size(axis),) + part.shape)]
  transfers between devices with their start and end apart: 10 -> 7, of which waited for: 3 -> 1; matrix products, arithmetic and copies ran while one was open for 0% -> 1% of each run, Pallas kernels for 7% -> 6%
where the time goes in v4:
time: 51.2 us; the launch traced here: 50.6 us
  starting transfers between devices  21.5 us (42%)
  Pallas kernels  9.17 us (18%)
  blocking collectives  8.32 us (16%)
  local copies, waits for them, and re-layouts  7.63 us (15%)
  waiting for transfers between devices  2.33 us (5%)
  other arithmetic  0.89 us (2%)
  between operations  0.74 us (1%)
    ppermute x3, starting transfers between devices, shards(): lax.ppermute(pair, 'ctx', [(i, i + shift) for i in range(ctx - shift)])  10.7 us
    all_to_all x1, blocking collectives, gathered(): return lax.all_to_all(copies, axis, split_axis=0, concat_axis=0, tiled=True)  8.32 us
    unnamed x14, local copies, waits for them, and re-layouts  6.99 us
    all_to_all x1, starting transfers between devices, gathered(): return lax.all_to_all(copies, axis, split_axis=0, concat_axis=0, tiled=True)  6.9 us
    pallas_call x1, Pallas kernels, shards(): pl.pallas_call(functools.partial(attend_kernel, ctx), out_shape=[shape((r...  5.58 us
    ppermute x3, starting transfers between devices, shards(): lax.ppermute(term, 'ctx', [(i, i - shift) for i in range(shift, ctx)])  3.86 us
    all_to_all x1, waiting for transfers between devices, gathered(): return lax.all_to_all(copies, axis, split_axis=0, concat_axis=0, tiled=True)  2.32 us
    pallas_call x1, Pallas kernels, shards(): pl.pallas_call(finish_kernel, out_shape=[shape((tok, width), jnp.bfloat16...  1.79 us
  transfers between devices with their start and end apart: 7, of which 1 were waited for; matrix products, arithmetic and copies ran while one was open for 1% of the time, Pallas kernels for 6%

profile of v4, /device:TPU:0, one launch (start us, length us, event | category | flops | bytes accessed | tf_op | source)
XLA Modules:
  0.0 50.6 jit_solution(13748938579300771318)
XLA Ops:
  0.6 0.9 %pad_maximum_fusion.pair_ref.refs_9_ = bf16[128,512]{1,0:T(8,128)(2,1)S(1)} fusion(bf16[128,256]{1,0:T(8,128)(2,1)} %bitcast.16, bf16[128,256]{1,0:T(8,128)(2,1)} %bitcast.17), kind=kLoop, calls=%fused_computation | loop fusion | flops 262144 | bytes 262144 | tf_op jit(solution)/shard_map/concatenate | solution.py:191
  1.5 4.9 %collective-permute-start.2 = (bf16[128,512]{1,0:T(8,128)(2,1)S(1)}, bf16[128,512]{1,0:T(8,128)(2,1)S(1)}, u32[]{:S(2)}, u32[]{:S(2)}) collective-permute-start(bf16[128,512]{1,0:T(8,128)(2,1)S(1)} %pad_maximum_fusion.pair_ref.refs_9_), channel_id=1, source_target_pairs={{0,2},{2,4},{4,6},{1,3},{3,5},{5,7},{8,10},{10,12},{12,14},{9,11},... | collective-permute-start | bytes 393224 | tf_op jit(solution)/shard_map/ppermute | solution.py:193
  6.5 4.5 %collective-permute-start.1 = (bf16[128,512]{1,0:T(8,128)(2,1)S(1)}, bf16[128,512]{1,0:T(8,128)(2,1)S(1)}, u32[]{:S(2)}, u32[]{:S(2)}) collective-permute-start(bf16[128,512]{1,0:T(8,128)(2,1)S(1)} %pad_maximum_fusion.pair_ref.refs_9_), channel_id=1, source_target_pairs={{0,4},{2,6},{1,5},{3,7},{8,12},{10,14},{9,13},{11,15},{16,20},{18,... | collective-permute-start | bytes 393224 | tf_op jit(solution)/shard_map/ppermute | solution.py:193
  11.0 1.3 %collective-permute-start = (bf16[128,512]{1,0:T(8,128)(2,1)S(1)}, bf16[128,512]{1,0:T(8,128)(2,1)S(1)}, u32[]{:S(2)}, u32[]{:S(2)}) collective-permute-start(bf16[128,512]{1,0:T(8,128)(2,1)S(1)} %pad_maximum_fusion.pair_ref.refs_9_), channel_id=1, source_target_pairs={{0,6},{1,7},{8,14},{9,15},{16,22},{17,23},{24,30},{25,31}} | collective-permute-start | bytes 393224 | tf_op jit(solution)/shard_map/ppermute | solution.py:193
  12.3 0.0 copy-start.2
  12.3 1.0 %copy-done.2 = bf16[1,128,2048]{2,1,0:T(8,128)(2,1)S(1)} copy-done((bf16[1,128,2048]{2,1,0:T(8,128)(2,1)S(1)}, bf16[1,128,2048]{2,1,0:T(8,128)(2,1)}, u32[]{:S(2)}) %copy-start.2) | copy-done | bytes 524312
  13.3 0.0 copy-start.3
  13.3 1.0 %copy-done.3 = bf16[1,128,2048]{2,1,0:T(8,128)(2,1)S(1)} copy-done((bf16[1,128,2048]{2,1,0:T(8,128)(2,1)S(1)}, bf16[1,128,2048]{2,1,0:T(8,128)(2,1)}, u32[]{:S(2)}) %copy-start.3) | copy-done | bytes 524312
  14.4 0.0 copy-start.4
  14.4 0.7 %copy-done.4 = bf16[2048]{0:T(1024)(128)(2,1)S(1)} copy-done((bf16[2048]{0:T(1024)(128)(2,1)S(1)}, bf16[2048]{0:T(1024)(128)(2,1)}, u32[]{:S(2)}) %copy-start.4) | copy-done | bytes 4120
  15.0 0.0 copy-start.5
  15.0 0.7 %copy-done.5 = s32[1,8]{1,0:T(1,128)S(1)} copy-done((s32[1,8]{1,0:T(1,128)S(1)}, s32[1,8]{1,0:T(1,128)}, u32[]{:S(2)}) %copy-start.5) | copy-done | bytes 56
  15.7 0.0 copy-start.6
  15.7 0.7 %copy-done.6 = bf16[256]{0:T(256)(128)(2,1)S(1)} copy-done((bf16[256]{0:T(256)(128)(2,1)S(1)}, bf16[256]{0:T(256)(128)(2,1)}, u32[]{:S(2)}) %copy-start.6) | copy-done | bytes 536
  16.4 1.1 %prepare.1 = (bf16[2,128]{1,0:T(2,128)(2,1)S(1)}, bf16[2048,256]{1,0:T(8,128)(2,1)S(1)}, bf16[2048,128]{1,0:T(8,128)(2,1)S(1)}, f32[128,2048]{1,0:T(8,128)S(1)},...) custom-call(s32[1,8]{1,0:T(1,128)S(1)} %copy-done.5, bf16[128,512]{1,0:T(8,128)(2,1)S(1)} %pad_maximum_fusion.pair_ref.refs_9_, ...), custom_call_target="tpu_custom_call" | custom-call | flops 134217728 | bytes 4194304 | tf_op jit(solution)/shard_map/prepare/pallas_call | solution.py:196
  17.5 0.0 collective-permute-done.2.refs_8_
  17.5 0.0 collective-permute-done.1.refs_7_
  17.5 0.0 collective-permute-done.refs_6_
  17.5 5.6 %attend.1 = (bf16[512,2048]{1,0:T(8,128)(2,1)S(1)}, bf16[512,2048]{1,0:T(8,128)(2,1)S(1)}, bf16[512,256]{1,0:T(8,128)(2,1)S(1)}, bf16[512,256]{1,0:T(8,128)(2,1)...) custom-call(bf16[2,128]{1,0:T(2,128)(2,1)S(1)} %get-tuple-element.27, ...), custom_call_target="tpu_custom_call" | custom-call | flops 1073741824 | bytes 4194304 | tf_op jit(solution)/shard_map/attend/pallas_call | solution.py:222
  23.1 0.0 copy-start
  23.1 1.3 %copy-done = bf16[512,2048]{1,0:T(8,128)(2,1)} copy-done((bf16[512,2048]{1,0:T(8,128)(2,1)}, bf16[512,2048]{1,0:T(8,128)(2,1)S(1)}, u32[]{:S(2)}) %copy-start) | copy-done | bytes 2097176
  24.4 1.3 %collective-permute-start.3 = (bf16[128,512]{1,0:T(8,128)(2,1)}, bf16[128,512]{1,0:T(8,128)(2,1)S(1)}, u32[]{:S(2)}, u32[]{:S(2)}) collective-permute-start(bf16[128,512]{1,0:T(8,128)(2,1)} %get-tuple-element.41), channel_id=1, source_target_pairs={{2,0},{4,2},{6,4},{3,1},{5,3},{7,5},{10,8},{12,10},{14,12},{11,9},... | collective-permute-start | bytes 393224 | tf_op jit(solution)/shard_map/ppermute | solution.py:244
  25.7 1.3 %collective-permute-start.4 = (bf16[128,512]{1,0:T(8,128)(2,1)}, bf16[128,512]{1,0:T(8,128)(2,1)S(1)}, u32[]{:S(2)}, u32[]{:S(2)}) collective-permute-start(bf16[128,512]{1,0:T(8,128)(2,1)} %get-tuple-element.42), channel_id=1, source_target_pairs={{4,0},{6,2},{5,1},{7,3},{12,8},{14,10},{13,9},{15,11},{20,16},{22,... | collective-permute-start | bytes 393224 | tf_op jit(solution)/shard_map/ppermute | solution.py:244
  27.0 1.3 %collective-permute-start.5 = (bf16[128,512]{1,0:T(8,128)(2,1)S(1)}, bf16[128,512]{1,0:T(8,128)(2,1)S(1)}, u32[]{:S(2)}, u32[]{:S(2)}) collective-permute-start(bf16[128,512]{1,0:T(8,128)(2,1)S(1)} %get-tuple-element.43), channel_id=1, source_target_pairs={{6,0},{7,1},{14,8},{15,9},{22,16},{23,17},{30,24},{31,25}} | collective-permute-start | bytes 393224 | tf_op jit(solution)/shard_map/ppermute | solution.py:244
  28.3 8.3 %all_to_all.10 = f32[4,18,128]{2,1,0:T(8,128)S(1)} all-to-all(f32[4,18,128]{2,1,0:T(8,128)S(1)} %broadcast_in_dim.20), channel_id=1, replica_groups=mesh['dp'=4,'ctx'=4,'tp'=2] {'dp'}, dimensions={0} | all-to-all | bytes 73728 | tf_op jit(solution)/shard_map/all_to_all | solution.py:179
  36.6 0.6 %broadcast_in_dim.21 = f32[4,18,128]{2,1,0:T(8,128)} broadcast(f32[18,128]{1,0:T(8,128)S(1)} %reduce_sum.9), dimensions={1,2} | broadcast | bytes 46080 | tf_op jit(solution)/shard_map/broadcast_in_dim | solution.py:178
  37.3 6.9 %all-to-all-start.1 = ((f32[4,18,128]{2,1,0:T(8,128)}), f32[4,18,128]{2,1,0:T(8,128)S(1)}, u32[]{:S(2)}, u32[]{:S(2)}) async-start(f32[4,18,128]{2,1,0:T(8,128)} %broadcast_in_dim.21), calls=%async_computation.1 | async-start | bytes 98304 | tf_op jit(solution)/shard_map/all_to_all | solution.py:179
  44.2 0.0 copy-start.1
  44.2 1.6 %copy-done.1 = bf16[512,2048]{1,0:T(8,128)(2,1)S(1)} copy-done((bf16[512,2048]{1,0:T(8,128)(2,1)S(1)}, bf16[512,2048]{1,0:T(8,128)(2,1)}, u32[]{:S(2)}) %copy-start.1) | copy-done | bytes 2097176
  45.8 1.8 %finish.1 = (bf16[128,2048]{1,0:T(8,128)(2,1)}, bf16[128,2048]{1,0:T(8,128)(2,1)}) custom-call(bf16[512,2048]{1,0:T(8,128)(2,1)S(1)} %get-tuple-element.33.probs_ref, bf16[512,2048]{1,0:T(8,128)(2,1)S(1)} %copy-done.1, bf16[512,256]{1,0:T(8,128)(2,1)S(1)} %get-tuple-element.35.keys_ref, bf16[512,256]{1,0:T(8,128)(2,1)S(1)} %get-tuple-element.36.values_ref), custom_call_target="tpu_custom_call" | custom-call | flops 536870912 | bytes 4194304 | tf_op jit(solution)/shard_map/finish/pallas_call | solution.py:247
  47.6 2.3 %all-to-all-done.1.sums_ref = f32[4,18,128]{2,1,0:T(8,128)S(1)} async-done(((f32[4,18,128]{2,1,0:T(8,128)}), f32[4,18,128]{2,1,0:T(8,128)S(1)}, u32[]{:S(2)}, u32[]{:S(2)}) %all-to-all-start.1) | async-done | bytes 36896 | tf_op jit(solution)/shard_map/all_to_all | solution.py:179
  49.9 0.0 collective-permute-done.3.refs_0_
  49.9 0.0 collective-permute-done.4.refs_1_
  49.9 0.0 collective-permute-done.5.refs_2_
  49.9 0.7 %collect.1 = (bf16[128,256]{1,0:T(8,128)(2,1)}, bf16[128,256]{1,0:T(8,128)(2,1)}, f32[16,128]{1,0:T(8,128)}, f32[2,128]{1,0:T(2,128)}) custom-call(f32[4,18,128]{2,1,0:T(8,128)S(1)} %all-to-all-done.1.sums_ref, f32[128,512]{1,0:T(8,128)S(1)} %get-tuple-element.40.own_ref, bf16[128,512]{1,0:T(8,128)(2,1)S(1)} %collective-permute-done.3.refs_0_, ...), custom_call_target="tpu_custom_call" | custom-call | flops 262144 | bytes 524288 | tf_op jit(solution)/shard_map/collect/pallas_call | solution.py:262
  (2 shorter events, 0.0 us)
Async XLA Ops:
  1.5 16.0 %collective-permute-start.2 = (bf16[128,512]{1,0:T(8,128)(2,1)S(1)}, bf16[128,512]{1,0:T(8,128)(2,1)S(1)}, u32[]{:S(2)}, u32[]{:S(2)}) collective-permute-start(bf16[128,512]{1,0:T(8,128)(2,1)S(1)} %pad_maximum_fusion.pair_ref.refs_9_), channel_id=1, source_target_pairs={{0,2},{2,4},{4,6},{1,3},{3,5},{5,7},{8,10},{10,12},{12,14},{9,11},... | collective-permute-start | bytes 393224 | tf_op jit(solution)/shard_map/ppermute | solution.py:193
  6.5 11.0 %collective-permute-start.1 = (bf16[128,512]{1,0:T(8,128)(2,1)S(1)}, bf16[128,512]{1,0:T(8,128)(2,1)S(1)}, u32[]{:S(2)}, u32[]{:S(2)}) collective-permute-start(bf16[128,512]{1,0:T(8,128)(2,1)S(1)} %pad_maximum_fusion.pair_ref.refs_9_), channel_id=1, source_target_pairs={{0,4},{2,6},{1,5},{3,7},{8,12},{10,14},{9,13},{11,15},{16,20},{18,... | collective-permute-start | bytes 393224 | tf_op jit(solution)/shard_map/ppermute | solution.py:193
  11.0 6.5 %collective-permute-start = (bf16[128,512]{1,0:T(8,128)(2,1)S(1)}, bf16[128,512]{1,0:T(8,128)(2,1)S(1)}, u32[]{:S(2)}, u32[]{:S(2)}) collective-permute-start(bf16[128,512]{1,0:T(8,128)(2,1)S(1)} %pad_maximum_fusion.pair_ref.refs_9_), channel_id=1, source_target_pairs={{0,6},{1,7},{8,14},{9,15},{16,22},{17,23},{24,30},{25,31}} | collective-permute-start | bytes 393224 | tf_op jit(solution)/shard_map/ppermute | solution.py:193
  12.3 1.0 %copy-start.2 = (bf16[1,128,2048]{2,1,0:T(8,128)(2,1)S(1)}, bf16[1,128,2048]{2,1,0:T(8,128)(2,1)}, u32[]{:S(2)}) copy-start(bf16[1,128,2048]{2,1,0:T(8,128)(2,1)} %param.7) | copy-start | bytes 1572868
  13.3 1.0 %copy-start.3 = (bf16[1,128,2048]{2,1,0:T(8,128)(2,1)S(1)}, bf16[1,128,2048]{2,1,0:T(8,128)(2,1)}, u32[]{:S(2)}) copy-start(bf16[1,128,2048]{2,1,0:T(8,128)(2,1)} %param.12) | copy-start | bytes 1572868
  14.4 0.7 %copy-start.4 = (bf16[2048]{0:T(1024)(128)(2,1)S(1)}, bf16[2048]{0:T(1024)(128)(2,1)}, u32[]{:S(2)}) copy-start(bf16[2048]{0:T(1024)(128)(2,1)} %param.8) | copy-start | bytes 12292
  15.0 0.7 %copy-start.5 = (s32[1,8]{1,0:T(1,128)S(1)}, s32[1,8]{1,0:T(1,128)}, u32[]{:S(2)}) copy-start(s32[1,8]{1,0:T(1,128)} %len_ref.1) | copy-start | bytes 100
  15.7 0.7 %copy-start.6 = (bf16[256]{0:T(256)(128)(2,1)S(1)}, bf16[256]{0:T(256)(128)(2,1)}, u32[]{:S(2)}) copy-start(bf16[256]{0:T(256)(128)(2,1)} %param.11) | copy-start | bytes 1540
  23.1 1.3 %copy-start = (bf16[512,2048]{1,0:T(8,128)(2,1)}, bf16[512,2048]{1,0:T(8,128)(2,1)S(1)}, u32[]{:S(2)}) copy-start(bf16[512,2048]{1,0:T(8,128)(2,1)S(1)} %get-tuple-element.34.dscore_ref) | copy-start | bytes 6291460
  24.4 25.5 %collective-permute-start.3 = (bf16[128,512]{1,0:T(8,128)(2,1)}, bf16[128,512]{1,0:T(8,128)(2,1)S(1)}, u32[]{:S(2)}, u32[]{:S(2)}) collective-permute-start(bf16[128,512]{1,0:T(8,128)(2,1)} %get-tuple-element.41), channel_id=1, source_target_pairs={{2,0},{4,2},{6,4},{3,1},{5,3},{7,5},{10,8},{12,10},{14,12},{11,9},... | collective-permute-start | bytes 393224 | tf_op jit(solution)/shard_map/ppermute | solution.py:244
  25.7 24.2 %collective-permute-start.4 = (bf16[128,512]{1,0:T(8,128)(2,1)}, bf16[128,512]{1,0:T(8,128)(2,1)S(1)}, u32[]{:S(2)}, u32[]{:S(2)}) collective-permute-start(bf16[128,512]{1,0:T(8,128)(2,1)} %get-tuple-element.42), channel_id=1, source_target_pairs={{4,0},{6,2},{5,1},{7,3},{12,8},{14,10},{13,9},{15,11},{20,16},{22,... | collective-permute-start | bytes 393224 | tf_op jit(solution)/shard_map/ppermute | solution.py:244
  27.0 22.9 %collective-permute-start.5 = (bf16[128,512]{1,0:T(8,128)(2,1)S(1)}, bf16[128,512]{1,0:T(8,128)(2,1)S(1)}, u32[]{:S(2)}, u32[]{:S(2)}) collective-permute-start(bf16[128,512]{1,0:T(8,128)(2,1)S(1)} %get-tuple-element.43), channel_id=1, source_target_pairs={{6,0},{7,1},{14,8},{15,9},{22,16},{23,17},{30,24},{31,25}} | collective-permute-start | bytes 393224 | tf_op jit(solution)/shard_map/ppermute | solution.py:244
  37.3 12.6 %all-to-all-start.1 = ((f32[4,18,128]{2,1,0:T(8,128)}), f32[4,18,128]{2,1,0:T(8,128)S(1)}, u32[]{:S(2)}, u32[]{:S(2)}) async-start(f32[4,18,128]{2,1,0:T(8,128)} %broadcast_in_dim.21), calls=%async_computation.1 | async-start | bytes 98304 | tf_op jit(solution)/shard_map/all_to_all | solution.py:179
  44.2 1.6 %copy-start.1 = (bf16[512,2048]{1,0:T(8,128)(2,1)S(1)}, bf16[512,2048]{1,0:T(8,128)(2,1)}, u32[]{:S(2)}) copy-start(bf16[512,2048]{1,0:T(8,128)(2,1)} %copy-done) | copy-start | bytes 6291460

commit v5 on v3

--- a/solution.py
+++ b/solution.py
@@ -185,17 +185,10 @@
 
 def exchange(axis, part):
     size = lax.axis_size(axis)
-    if size & (size - 1):
-        return [part] + [
-            lax.ppermute(part, axis, [(i, (i + shift) % size) for i in range(size)])
-            for shift in range(1, size)
-        ]
-    parts, step = [part], 1
-    while step < size:
-        part = total_of(parts)
-        parts = [part, lax.ppermute(part, axis, [(i, i ^ step) for i in range(size)])]
-        step *= 2
-    return parts
+    return [part] + [
+        lax.ppermute(part, axis, [(i, (i + shift) % size) for i in range(size)])
+        for shift in range(1, size)
+    ]
 
 
 def shards(q_proj, q_bias, k_proj, v_proj, v_bias, dout, lengths):

time: 44.8 us -> 45.9 us (1.025)
  starting transfers between devices: 22.5 us -> 29.5 us
  waiting for transfers between devices: 7.42 us -> 1.52 us
    ppermute x4 -> x6, starting transfers between devices: 7.91 us -> 14.9 us  [exchange(): lax.ppermute(part, axis, [(i, (i + shift) % size) for i in range(size)])]
    ppermute x4 -> x6, waiting for transfers between devices: 7.41 us -> 1.51 us  [exchange(): lax.ppermute(part, axis, [(i, (i + shift) % size) for i in range(size)])]
  transfers between devices with their start and end apart: 10 -> 12, of which waited for: 3 -> 2; matrix products, arithmetic and copies ran while one was open for 0% -> 0% of each run, Pallas kernels for 7% -> 6%
where the time goes in v5:
time: 45.9 us; the launch traced here: 45.4 us
  starting transfers between devices  29.5 us (64%)
  Pallas kernels  8.7 us (19%)
  local copies, waits for them, and re-layouts  4.07 us (9%)
  waiting for transfers between devices  1.52 us (3%)
  other arithmetic  0.89 us (2%)
  between operations  0.77 us (2%)
    ppermute x6, starting transfers between devices, exchange(): lax.ppermute(part, axis, [(i, (i + shift) % size) for i in range(size)])  14.9 us
    ppermute x3, starting transfers between devices, shards(): lax.ppermute(pair, 'ctx', [(i, i + shift) for i in range(ctx - shift)])  10.7 us
    pallas_call x1, Pallas kernels, shards(): pl.pallas_call(functools.partial(attend_kernel, ctx), out_shape=[shape((r...  5.08 us
    unnamed x10, local copies, waits for them, and re-layouts  4.07 us
    ppermute x3, starting transfers between devices, shards(): lax.ppermute(term, 'ctx', [(i, i - shift) for i in range(shift, ctx)])  3.86 us
    pallas_call x1, Pallas kernels, shards(): pl.pallas_call(finish_kernel, out_shape=[shape((tok, width), jnp.bfloat16...  1.8 us
    ppermute x6, waiting for transfers between devices, exchange(): lax.ppermute(part, axis, [(i, (i + shift) % size) for i in range(size)])  1.51 us
    pallas_call x1, Pallas kernels, shards(): pl.pallas_call(functools.partial(prepare_kernel, ctx), out_shape=[shape((...  1.11 us
  transfers between devices with their start and end apart: 12, of which 2 were waited for; matrix products, arithmetic and copies ran while one was open for 0% of the time, Pallas kernels for 6%

profile of v5, /device:TPU:0, one launch (start us, length us, event | category | flops | bytes accessed | tf_op | source)
XLA Modules:
  0.0 45.4 jit_solution(16119434224497434684)
XLA Ops:
  0.6 0.9 %pad_maximum_fusion.pair_ref.refs_9_ = bf16[128,512]{1,0:T(8,128)(2,1)S(1)} fusion(bf16[128,256]{1,0:T(8,128)(2,1)} %bitcast.16, bf16[128,256]{1,0:T(8,128)(2,1)} %bitcast.17), kind=kLoop, calls=%fused_computation | loop fusion | flops 262144 | bytes 262144 | tf_op jit(solution)/shard_map/concatenate | solution.py:203
  1.5 4.9 %collective-permute-start.2 = (bf16[128,512]{1,0:T(8,128)(2,1)S(1)}, bf16[128,512]{1,0:T(8,128)(2,1)S(1)}, u32[]{:S(2)}, u32[]{:S(2)}) collective-permute-start(bf16[128,512]{1,0:T(8,128)(2,1)S(1)} %pad_maximum_fusion.pair_ref.refs_9_), channel_id=1, source_target_pairs={{0,2},{2,4},{4,6},{1,3},{3,5},{5,7},{8,10},{10,12},{12,14},{9,11},... | collective-permute-start | bytes 393224 | tf_op jit(solution)/shard_map/ppermute | solution.py:205
  6.5 4.5 %collective-permute-start.1 = (bf16[128,512]{1,0:T(8,128)(2,1)S(1)}, bf16[128,512]{1,0:T(8,128)(2,1)S(1)}, u32[]{:S(2)}, u32[]{:S(2)}) collective-permute-start(bf16[128,512]{1,0:T(8,128)(2,1)S(1)} %pad_maximum_fusion.pair_ref.refs_9_), channel_id=1, source_target_pairs={{0,4},{2,6},{1,5},{3,7},{8,12},{10,14},{9,13},{11,15},{16,20},{18,... | collective-permute-start | bytes 393224 | tf_op jit(solution)/shard_map/ppermute | solution.py:205
  11.0 1.3 %collective-permute-start = (bf16[128,512]{1,0:T(8,128)(2,1)S(1)}, bf16[128,512]{1,0:T(8,128)(2,1)S(1)}, u32[]{:S(2)}, u32[]{:S(2)}) collective-permute-start(bf16[128,512]{1,0:T(8,128)(2,1)S(1)} %pad_maximum_fusion.pair_ref.refs_9_), channel_id=1, source_target_pairs={{0,6},{1,7},{8,14},{9,15},{16,22},{17,23},{24,30},{25,31}} | collective-permute-start | bytes 393224 | tf_op jit(solution)/shard_map/ppermute | solution.py:205
  12.3 0.0 copy-start
  12.3 1.0 %copy-done = bf16[1,128,2048]{2,1,0:T(8,128)(2,1)S(1)} copy-done((bf16[1,128,2048]{2,1,0:T(8,128)(2,1)S(1)}, bf16[1,128,2048]{2,1,0:T(8,128)(2,1)}, u32[]{:S(2)}) %copy-start) | copy-done | bytes 524312
  13.3 0.0 copy-start.1
  13.3 1.0 %copy-done.1 = bf16[1,128,2048]{2,1,0:T(8,128)(2,1)S(1)} copy-done((bf16[1,128,2048]{2,1,0:T(8,128)(2,1)S(1)}, bf16[1,128,2048]{2,1,0:T(8,128)(2,1)}, u32[]{:S(2)}) %copy-start.1) | copy-done | bytes 524312
  14.4 0.0 copy-start.2
  14.4 0.7 %copy-done.2 = bf16[2048]{0:T(1024)(128)(2,1)S(1)} copy-done((bf16[2048]{0:T(1024)(128)(2,1)S(1)}, bf16[2048]{0:T(1024)(128)(2,1)}, u32[]{:S(2)}) %copy-start.2) | copy-done | bytes 4120
  15.0 0.0 copy-start.3
  15.0 0.7 %copy-done.3 = s32[1,8]{1,0:T(1,128)S(1)} copy-done((s32[1,8]{1,0:T(1,128)S(1)}, s32[1,8]{1,0:T(1,128)}, u32[]{:S(2)}) %copy-start.3) | copy-done | bytes 56
  15.7 0.0 copy-start.4
  15.7 0.7 %copy-done.4 = bf16[256]{0:T(256)(128)(2,1)S(1)} copy-done((bf16[256]{0:T(256)(128)(2,1)S(1)}, bf16[256]{0:T(256)(128)(2,1)}, u32[]{:S(2)}) %copy-start.4) | copy-done | bytes 536
  16.4 1.1 %prepare.1 = (bf16[2,128]{1,0:T(2,128)(2,1)S(1)}, bf16[2048,256]{1,0:T(8,128)(2,1)S(1)}, bf16[2048,128]{1,0:T(8,128)(2,1)S(1)}, f32[128,2048]{1,0:T(8,128)S(1)},...) custom-call(s32[1,8]{1,0:T(1,128)S(1)} %copy-done.3, bf16[128,512]{1,0:T(8,128)(2,1)S(1)} %pad_maximum_fusion.pair_ref.refs_9_, ...), custom_call_target="tpu_custom_call" | custom-call | flops 134217728 | bytes 4194304 | tf_op jit(solution)/shard_map/prepare/pallas_call | solution.py:208
  17.5 0.0 collective-permute-done.2.refs_8_
  17.5 0.0 collective-permute-done.1.refs_7_
  17.5 0.0 collective-permute-done.refs_6_
  17.5 5.1 %attend.1 = (bf16[512,2048]{1,0:T(8,128)(2,1)S(1)}, bf16[512,2048]{1,0:T(8,128)(2,1)S(1)}, bf16[512,256]{1,0:T(8,128)(2,1)S(1)}, bf16[512,256]{1,0:T(8,128)(2,1)...) custom-call(bf16[2,128]{1,0:T(2,128)(2,1)S(1)} %get-tuple-element.27, ...), custom_call_target="tpu_custom_call" | custom-call | flops 1073741824 | bytes 4194304 | tf_op jit(solution)/shard_map/attend/pallas_call | solution.py:234
  22.6 2.5 %collective-permute-start.5 = (f32[18,128]{1,0:T(8,128)S(1)}, f32[18,128]{1,0:T(8,128)S(1)}, u32[]{:S(2)}, u32[]{:S(2)}) collective-permute-start(f32[18,128]{1,0:T(8,128)S(1)} %get-tuple-element.39), channel_id=1, source_target_pairs={{0,24},{8,0},{16,8},{24,16},{1,25},{9,1},{17,9},{25,17},{2,26},{10... | collective-permute-start | bytes 27656 | tf_op jit(solution)/shard_map/ppermute | solution.py:189
  25.1 0.5 %collective-permute-start.4 = (f32[18,128]{1,0:T(8,128)S(1)}, f32[18,128]{1,0:T(8,128)S(1)}, u32[]{:S(2)}, u32[]{:S(2)}) collective-permute-start(f32[18,128]{1,0:T(8,128)S(1)} %get-tuple-element.39), channel_id=1, source_target_pairs={{0,16},{8,24},{16,0},{24,8},{1,17},{9,25},{17,1},{25,9},{2,18},{10... | collective-permute-start | bytes 27656 | tf_op jit(solution)/shard_map/ppermute | solution.py:189
  25.6 0.6 %collective-permute-start.3 = (f32[18,128]{1,0:T(8,128)S(1)}, f32[18,128]{1,0:T(8,128)S(1)}, u32[]{:S(2)}, u32[]{:S(2)}) collective-permute-start(f32[18,128]{1,0:T(8,128)S(1)} %get-tuple-element.39), channel_id=1, source_target_pairs={{0,8},{8,16},{16,24},{24,0},{1,9},{9,17},{17,25},{25,1},{2,10},{10... | collective-permute-start | bytes 27656 | tf_op jit(solution)/shard_map/ppermute | solution.py:189
  26.2 1.3 %collective-permute-start.9 = (bf16[128,512]{1,0:T(8,128)(2,1)S(1)}, bf16[128,512]{1,0:T(8,128)(2,1)S(1)}, u32[]{:S(2)}, u32[]{:S(2)}) collective-permute-start(bf16[128,512]{1,0:T(8,128)(2,1)S(1)} %get-tuple-element.41), channel_id=1, source_target_pairs={{2,0},{4,2},{6,4},{3,1},{5,3},{7,5},{10,8},{12,10},{14,12},{11,9},... | collective-permute-start | bytes 393224 | tf_op jit(solution)/shard_map/ppermute | solution.py:256
  27.5 1.3 %collective-permute-start.10 = (bf16[128,512]{1,0:T(8,128)(2,1)S(1)}, bf16[128,512]{1,0:T(8,128)(2,1)S(1)}, u32[]{:S(2)}, u32[]{:S(2)}) collective-permute-start(bf16[128,512]{1,0:T(8,128)(2,1)S(1)} %get-tuple-element.42), channel_id=1, source_target_pairs={{4,0},{6,2},{5,1},{7,3},{12,8},{14,10},{13,9},{15,11},{20,16},{22,... | collective-permute-start | bytes 393224 | tf_op jit(solution)/shard_map/ppermute | solution.py:256
  28.8 0.0 collective-permute-done.5
  28.8 1.3 %collective-permute-start.11 = (bf16[128,512]{1,0:T(8,128)(2,1)S(1)}, bf16[128,512]{1,0:T(8,128)(2,1)S(1)}, u32[]{:S(2)}, u32[]{:S(2)}) collective-permute-start(bf16[128,512]{1,0:T(8,128)(2,1)S(1)} %get-tuple-element.43), channel_id=1, source_target_pairs={{6,0},{7,1},{14,8},{15,9},{22,16},{23,17},{30,24},{31,25}} | collective-permute-start | bytes 393224 | tf_op jit(solution)/shard_map/ppermute | solution.py:256
  30.1 0.0 collective-permute-done.4
  30.1 0.1 collective-permute-done.3
  30.2 5.6 %collective-permute-start.8 = (f32[18,128]{1,0:T(8,128)S(1)}, f32[18,128]{1,0:T(8,128)S(1)}, u32[]{:S(2)}, u32[]{:S(2)}) collective-permute-start(f32[18,128]{1,0:T(8,128)S(1)} %add_add_fusion.refs_0_), channel_id=1, source_target_pairs={{0,6},{2,0},{4,2},{6,4},{1,7},{3,1},{5,3},{7,5},{8,14},{10,8},{12,... | collective-permute-start | bytes 27656 | tf_op jit(solution)/shard_map/ppermute | solution.py:189
  35.8 0.0 collective-permute-start.7
  35.8 1.4 %collective-permute-done.8.refs_3_ = f32[18,128]{1,0:T(8,128)S(1)} collective-permute-done((f32[18,128]{1,0:T(8,128)S(1)}, f32[18,128]{1,0:T(8,128)S(1)}, u32[]{:S(2)}, u32[]{:S(2)}) %collective-permute-start.8) | collective-permute-done | bytes 9248 | tf_op jit(solution)/shard_map/ppermute | solution.py:189
  37.2 5.7 %collective-permute-start.6 = (f32[18,128]{1,0:T(8,128)S(1)}, f32[18,128]{1,0:T(8,128)S(1)}, u32[]{:S(2)}, u32[]{:S(2)}) collective-permute-start(f32[18,128]{1,0:T(8,128)S(1)} %add_add_fusion.refs_0_), channel_id=1, source_target_pairs={{0,2},{2,4},{4,6},{6,0},{1,3},{3,5},{5,7},{7,1},{8,10},{10,12},{12... | collective-permute-start | bytes 27656 | tf_op jit(solution)/shard_map/ppermute | solution.py:189
  42.9 1.8 %finish.1 = (bf16[128,2048]{1,0:T(8,128)(2,1)}, bf16[128,2048]{1,0:T(8,128)(2,1)}) custom-call(bf16[512,2048]{1,0:T(8,128)(2,1)S(1)} %get-tuple-element.33.probs_ref, bf16[512,2048]{1,0:T(8,128)(2,1)S(1)} %get-tuple-element.34.dscore_ref, bf16[512,256]{1,0:T(8,128)(2,1)S(1)} %get-tuple-element.35.keys_ref, bf16[512,256]{1,0:T(8,128)(2,1)S(1)} %get-tuple-element.36.values_ref), custom_call_target="tpu_custom_call" | custom-call | flops 536870912 | bytes 4194304 | tf_op jit(solution)/shard_map/finish/pallas_call | solution.py:259
  44.7 0.0 collective-permute-done.7.refs_2_
  44.7 0.0 collective-permute-done.6.refs_1_
  44.7 0.0 collective-permute-done.9.refs_5_
  44.7 0.0 collective-permute-done.10.refs_6_
  44.7 0.0 collective-permute-done.11.refs_7_
  44.7 0.7 %collect.1 = (bf16[128,256]{1,0:T(8,128)(2,1)}, bf16[128,256]{1,0:T(8,128)(2,1)}, f32[16,128]{1,0:T(8,128)}, f32[2,128]{1,0:T(2,128)}) custom-call(f32[18,128]{1,0:T(8,128)S(1)} %add_add_fusion.refs_0_, f32[18,128]{1,0:T(8,128)S(1)} %collective-permute-done.6.refs_1_, f32[18,128]{1,0:T(8,128)S(1)} %collective-permute-done.7.refs_2_, ...), custom_call_target="tpu_custom_call" | custom-call | flops 262144 | bytes 524288 | tf_op jit(solution)/shard_map/collect/pallas_call | solution.py:274
  (1 shorter events, 0.0 us)
Async XLA Ops:
  1.5 16.0 %collective-permute-start.2 = (bf16[128,512]{1,0:T(8,128)(2,1)S(1)}, bf16[128,512]{1,0:T(8,128)(2,1)S(1)}, u32[]{:S(2)}, u32[]{:S(2)}) collective-permute-start(bf16[128,512]{1,0:T(8,128)(2,1)S(1)} %pad_maximum_fusion.pair_ref.refs_9_), channel_id=1, source_target_pairs={{0,2},{2,4},{4,6},{1,3},{3,5},{5,7},{8,10},{10,12},{12,14},{9,11},... | collective-permute-start | bytes 393224 | tf_op jit(solution)/shard_map/ppermute | solution.py:205
  6.5 11.0 %collective-permute-start.1 = (bf16[128,512]{1,0:T(8,128)(2,1)S(1)}, bf16[128,512]{1,0:T(8,128)(2,1)S(1)}, u32[]{:S(2)}, u32[]{:S(2)}) collective-permute-start(bf16[128,512]{1,0:T(8,128)(2,1)S(1)} %pad_maximum_fusion.pair_ref.refs_9_), channel_id=1, source_target_pairs={{0,4},{2,6},{1,5},{3,7},{8,12},{10,14},{9,13},{11,15},{16,20},{18,... | collective-permute-start | bytes 393224 | tf_op jit(solution)/shard_map/ppermute | solution.py:205
  11.0 6.5 %collective-permute-start = (bf16[128,512]{1,0:T(8,128)(2,1)S(1)}, bf16[128,512]{1,0:T(8,128)(2,1)S(1)}, u32[]{:S(2)}, u32[]{:S(2)}) collective-permute-start(bf16[128,512]{1,0:T(8,128)(2,1)S(1)} %pad_maximum_fusion.pair_ref.refs_9_), channel_id=1, source_target_pairs={{0,6},{1,7},{8,14},{9,15},{16,22},{17,23},{24,30},{25,31}} | collective-permute-start | bytes 393224 | tf_op jit(solution)/shard_map/ppermute | solution.py:205
  12.3 1.0 %copy-start = (bf16[1,128,2048]{2,1,0:T(8,128)(2,1)S(1)}, bf16[1,128,2048]{2,1,0:T(8,128)(2,1)}, u32[]{:S(2)}) copy-start(bf16[1,128,2048]{2,1,0:T(8,128)(2,1)} %param.7) | copy-start | bytes 1572868
  13.3 1.0 %copy-start.1 = (bf16[1,128,2048]{2,1,0:T(8,128)(2,1)S(1)}, bf16[1,128,2048]{2,1,0:T(8,128)(2,1)}, u32[]{:S(2)}) copy-start(bf16[1,128,2048]{2,1,0:T(8,128)(2,1)} %param.12) | copy-start | bytes 1572868
  14.4 0.7 %copy-start.2 = (bf16[2048]{0:T(1024)(128)(2,1)S(1)}, bf16[2048]{0:T(1024)(128)(2,1)}, u32[]{:S(2)}) copy-start(bf16[2048]{0:T(1024)(128)(2,1)} %param.8) | copy-start | bytes 12292
  15.0 0.7 %copy-start.3 = (s32[1,8]{1,0:T(1,128)S(1)}, s32[1,8]{1,0:T(1,128)}, u32[]{:S(2)}) copy-start(s32[1,8]{1,0:T(1,128)} %len_ref.1) | copy-start | bytes 100
  15.7 0.7 %copy-start.4 = (bf16[256]{0:T(256)(128)(2,1)S(1)}, bf16[256]{0:T(256)(128)(2,1)}, u32[]{:S(2)}) copy-start(bf16[256]{0:T(256)(128)(2,1)} %param.11) | copy-start | bytes 1540
  22.6 6.2 %collective-permute-start.5 = (f32[18,128]{1,0:T(8,128)S(1)}, f32[18,128]{1,0:T(8,128)S(1)}, u32[]{:S(2)}, u32[]{:S(2)}) collective-permute-start(f32[18,128]{1,0:T(8,128)S(1)} %get-tuple-element.39), channel_id=1, source_target_pairs={{0,24},{8,0},{16,8},{24,16},{1,25},{9,1},{17,9},{25,17},{2,26},{10... | collective-permute-start | bytes 27656 | tf_op jit(solution)/shard_map/ppermute | solution.py:189
  25.1 5.0 %collective-permute-start.4 = (f32[18,128]{1,0:T(8,128)S(1)}, f32[18,128]{1,0:T(8,128)S(1)}, u32[]{:S(2)}, u32[]{:S(2)}) collective-permute-start(f32[18,128]{1,0:T(8,128)S(1)} %get-tuple-element.39), channel_id=1, source_target_pairs={{0,16},{8,24},{16,0},{24,8},{1,17},{9,25},{17,1},{25,9},{2,18},{10... | collective-permute-start | bytes 27656 | tf_op jit(solution)/shard_map/ppermute | solution.py:189
  25.6 4.6 %collective-permute-start.3 = (f32[18,128]{1,0:T(8,128)S(1)}, f32[18,128]{1,0:T(8,128)S(1)}, u32[]{:S(2)}, u32[]{:S(2)}) collective-permute-start(f32[18,128]{1,0:T(8,128)S(1)} %get-tuple-element.39), channel_id=1, source_target_pairs={{0,8},{8,16},{16,24},{24,0},{1,9},{9,17},{17,25},{25,1},{2,10},{10... | collective-permute-start | bytes 27656 | tf_op jit(solution)/shard_map/ppermute | solution.py:189
  26.2 18.5 %collective-permute-start.9 = (bf16[128,512]{1,0:T(8,128)(2,1)S(1)}, bf16[128,512]{1,0:T(8,128)(2,1)S(1)}, u32[]{:S(2)}, u32[]{:S(2)}) collective-permute-start(bf16[128,512]{1,0:T(8,128)(2,1)S(1)} %get-tuple-element.41), channel_id=1, source_target_pairs={{2,0},{4,2},{6,4},{3,1},{5,3},{7,5},{10,8},{12,10},{14,12},{11,9},... | collective-permute-start | bytes 393224 | tf_op jit(solution)/shard_map/ppermute | solution.py:256
  27.5 17.2 %collective-permute-start.10 = (bf16[128,512]{1,0:T(8,128)(2,1)S(1)}, bf16[128,512]{1,0:T(8,128)(2,1)S(1)}, u32[]{:S(2)}, u32[]{:S(2)}) collective-permute-start(bf16[128,512]{1,0:T(8,128)(2,1)S(1)} %get-tuple-element.42), channel_id=1, source_target_pairs={{4,0},{6,2},{5,1},{7,3},{12,8},{14,10},{13,9},{15,11},{20,16},{22,... | collective-permute-start | bytes 393224 | tf_op jit(solution)/shard_map/ppermute | solution.py:256
  28.8 15.9 %collective-permute-start.11 = (bf16[128,512]{1,0:T(8,128)(2,1)S(1)}, bf16[128,512]{1,0:T(8,128)(2,1)S(1)}, u32[]{:S(2)}, u32[]{:S(2)}) collective-permute-start(bf16[128,512]{1,0:T(8,128)(2,1)S(1)} %get-tuple-element.43), channel_id=1, source_target_pairs={{6,0},{7,1},{14,8},{15,9},{22,16},{23,17},{30,24},{31,25}} | collective-permute-start | bytes 393224 | tf_op jit(solution)/shard_map/ppermute | solution.py:256
  30.2 7.0 %collective-permute-start.8 = (f32[18,128]{1,0:T(8,128)S(1)}, f32[18,128]{1,0:T(8,128)S(1)}, u32[]{:S(2)}, u32[]{:S(2)}) collective-permute-start(f32[18,128]{1,0:T(8,128)S(1)} %add_add_fusion.refs_0_), channel_id=1, source_target_pairs={{0,6},{2,0},{4,2},{6,4},{1,7},{3,1},{5,3},{7,5},{8,14},{10,8},{12,... | collective-permute-start | bytes 27656 | tf_op jit(solution)/shard_map/ppermute | solution.py:189
  35.8 8.9 %collective-permute-start.7 = (f32[18,128]{1,0:T(8,128)S(1)}, f32[18,128]{1,0:T(8,128)S(1)}, u32[]{:S(2)}, u32[]{:S(2)}) collective-permute-start(f32[18,128]{1,0:T(8,128)S(1)} %add_add_fusion.refs_0_), channel_id=1, source_target_pairs={{0,4},{2,6},{4,0},{6,2},{1,5},{3,7},{5,1},{7,3},{8,12},{10,14},{12... | collective-permute-start | bytes 27656 | tf_op jit(solution)/shard_map/ppermute | solution.py:189
  37.2 7.5 %collective-permute-start.6 = (f32[18,128]{1,0:T(8,128)S(1)}, f32[18,128]{1,0:T(8,128)S(1)}, u32[]{:S(2)}, u32[]{:S(2)}) collective-permute-start(f32[18,128]{1,0:T(8,128)S(1)} %add_add_fusion.refs_0_), channel_id=1, source_target_pairs={{0,2},{2,4},{4,6},{6,0},{1,3},{3,5},{5,7},{7,1},{8,10},{10,12},{12... | collective-permute-start | bytes 27656 | tf_op jit(solution)/shard_map/ppermute | solution.py:189

commit v6 on v5

--- a/solution.py
+++ b/solution.py
@@ -12,6 +12,7 @@
 KV_HEADS = 4
 GROUP = HEADS // KV_HEADS
 PAIR = 2
+BLOCK = 64
 SCALE = HEAD_DIM ** (-0.5)
 LOG2E = 1.4426950408889634
 NEGATIVE = -1e30
@@ -80,7 +81,8 @@
     pair_refs = refs[6 : 6 + slots][::-1]
     refs = refs[6 + slots :]
     probs_ref, dscore_ref, keys_ref, values_ref, sums_ref, own_ref = refs[:6]
-    out_refs = refs[6:]
+    out_refs = refs[6 : 6 + slots - 1]
+    weights_ref, all_dprob_ref = refs[6 + slots - 1 :]
     tok = pair_refs[0].shape[0]
     kv_heads = bias_ref.shape[0]
     kv_width = kv_heads * HEAD_DIM
@@ -92,33 +94,40 @@
             values_ref[rows, head_cols(kv_head)] = biased(
                 pair_refs[slot][:, head_cols(kv_heads + kv_head)], bias_ref[kv_head : kv_head + 1, :]
             )
+    blocks = [slice(row, row + BLOCK) for row in range(0, slots * tok, BLOCK)]
     for kv_head in range(kv_heads):
         cols = head_cols(kv_head)
-        keys = keys_ref[tok:, cols]
-        values = values_ref[tok:, cols]
-        key_term = jnp.zeros((slots * tok, 2 * HEAD_DIM), jnp.float32)
-        value_term = jnp.zeros((slots * tok, HEAD_DIM), jnp.float32)
+        group = slice(kv_head * GROUP * tok, (kv_head + 1) * GROUP * tok)
+        weights_ref[tok:, group] = dot(keys_ref[tok:, cols], queries_ref[group, :HEAD_DIM], 1, 1)
+        all_dprob_ref[tok:, group] = dot(values_ref[tok:, cols], grads_ref[group, :], 1, 1)
         for pair in range(GROUP // PAIR):
             first = kv_head * GROUP + pair * PAIR
             at = slice(first * tok, (first + PAIR) * tok)
-            queries = queries_ref[at, :]
-            grads = grads_ref[at, :]
-            live = jnp.concatenate([live_ref[...]] * PAIR, axis=1)
-            score = jnp.concatenate(
-                [score_ref[:, at], dot(keys, queries[:, :HEAD_DIM], 1, 1)], axis=0
-            )
-            score = score * (SCALE * LOG2E) + live
-            row_max = jnp.max(score, axis=0, keepdims=True)
-            weights = jnp.exp2(score - row_max)
-            probs = weights * (1.0 / jnp.sum(weights, axis=0, keepdims=True))
-            dprob = jnp.concatenate([dprob_ref[:, at], dot(values, grads, 1, 1)], axis=0)
-            delta = jnp.sum(probs * dprob, axis=0, keepdims=True)
-            dscore = (probs * (dprob - delta)).astype(jnp.bfloat16)
-            probs = probs.astype(jnp.bfloat16)
-            probs_ref[:, at] = probs
-            dscore_ref[:, at] = dscore
-            value_term = value_term + dot(probs, grads, 1, 0)
-            key_term = key_term + dot(dscore, queries, 1, 0)
+            row_max = None
+            for block in blocks:
+                score = (score_ref if block.start < tok else weights_ref)[block, at]
+                score = score + jnp.concatenate([live_ref[block, :]] * PAIR, axis=1)
+                weights_ref[block, at] = score
+                part = jnp.max(score.reshape(-1, 8, PAIR * tok), axis=0)
+                row_max = part if row_max is None else jnp.maximum(row_max, part)
+            row_max = jnp.max(row_max, axis=0, keepdims=True)
+            total = jnp.zeros((8, PAIR * tok), jnp.float32)
+            delta = jnp.zeros((8, PAIR * tok), jnp.float32)
+            for block in blocks:
+                dprob = (dprob_ref if block.start < tok else all_dprob_ref)[block, at]
+                weights = jnp.exp2((weights_ref[block, at] - row_max) * (SCALE * LOG2E))
+                weights_ref[block, at] = weights
+                total = total + jnp.sum(weights.reshape(-1, 8, PAIR * tok), axis=0)
+                delta = delta + jnp.sum((weights * dprob).reshape(-1, 8, PAIR * tok), axis=0)
+            inverse = 1.0 / jnp.sum(total, axis=0, keepdims=True)
+            delta = jnp.sum(delta, axis=0, keepdims=True) * inverse
+            for block in blocks:
+                dprob = (dprob_ref if block.start < tok else all_dprob_ref)[block, at]
+                probs = weights_ref[block, at] * inverse
+                probs_ref[block, at] = probs.astype(jnp.bfloat16)
+                dscore_ref[block, at] = (probs * (dprob - delta)).astype(jnp.bfloat16)
+        value_term = dot(probs_ref[:, group], grads_ref[group, :], 1, 0)
+        key_term = dot(dscore_ref[:, group], queries_ref[group, :], 1, 0)
         over_queries = key_term[:, HEAD_DIM:]
         key_term = key_term[:, :HEAD_DIM] * SCALE
         high = over_queries.astype(jnp.bfloat16)
@@ -185,6 +194,12 @@
 
 def exchange(axis, part):
     size = lax.axis_size(axis)
+    if axis == "ctx" and not size & (size - 1):
+        step = 1
+        while 2 * step < size:
+            part = part + lax.ppermute(part, axis, [(i, i ^ step) for i in range(size)])
+            step *= 2
+        return [part, lax.ppermute(part, axis, [(i, i ^ step) for i in range(size)])]
     return [part] + [
         lax.ppermute(part, axis, [(i, (i + shift) % size) for i in range(size)])
         for shift in range(1, size)
@@ -244,7 +259,11 @@
         + [term] * (ctx - 1),
         in_specs=[VMEM] * (6 + ctx),
         out_specs=[VMEM] * (6 + ctx - 1),
-        compiler_params=params(40),
+        scratch_shapes=[
+            pltpu.VMEM((rows, columns), jnp.float32),
+            pltpu.VMEM((rows, columns), jnp.float32),
+        ],
+        compiler_params=params(24 if ctx < 8 else 48),
         cost_estimate=pl.CostEstimate(
             flops=8 * rows * tok * width,
             bytes_accessed=4 * rows * columns,

time: 45.9 us -> 43.2 us (0.941)
  starting transfers between devices: 29.5 us -> 26.7 us
  waiting for transfers between devices: 1.52 us -> 2.48 us
  Pallas kernels: 8.7 us -> 7.83 us
    ppermute x6 -> x3, starting transfers between devices: 14.9 us -> 3.61 us  [exchange(): lax.ppermute(part, axis, [(i, (i + shift) % size) for i in range(size)])]
    ppermute x0 -> x2, starting transfers between devices: none -> 8.51 us  [the longest x1 6.5 us: exchange(): lax.ppermute(part, axis, [(i, i ^ step) for i in range(size)])]
    ppermute x0 -> x2, waiting for transfers between devices: none -> 2.37 us  [the longest x1 2.37 us: exchange(): part = part + lax.ppermute(part, axis, [(i, i ^ step) for i in range(size)])]
    ppermute x6 -> x3, waiting for transfers between devices: 1.51 us -> 0.1 us  [exchange(): lax.ppermute(part, axis, [(i, (i + shift) % size) for i in range(size)])]
    pallas_call x1, Pallas kernels: 5.08 us -> 4.24 us  [shards(): pl.pallas_call(functools.partial(attend_kernel, ctx), out_shape=[shape((r...]
  transfers between devices with their start and end apart: 12 -> 11, of which waited for: 2 -> 2; matrix products, arithmetic and copies ran while one was open for 0% -> 0% of each run, Pallas kernels for 6% -> 7%
where the time goes in v6:
time: 43.2 us; the launch traced here: 42.8 us
  starting transfers between devices  26.7 us (62%)
  Pallas kernels  7.83 us (18%)
  local copies, waits for them, and re-layouts  4.07 us (9%)
  waiting for transfers between devices  2.48 us (6%)
  other arithmetic  0.89 us (2%)
  between operations  0.77 us (2%)
    ppermute x3, starting transfers between devices, shards(): lax.ppermute(pair, 'ctx', [(i, i + shift) for i in range(ctx - shift)])  10.7 us
    ppermute x1, starting transfers between devices, exchange(): lax.ppermute(part, axis, [(i, i ^ step) for i in range(size)])  6.5 us
    pallas_call x1, Pallas kernels, shards(): pl.pallas_call(functools.partial(attend_kernel, ctx), out_shape=[shape((r...  4.24 us
    unnamed x10, local copies, waits for them, and re-layouts  4.07 us
    ppermute x3, starting transfers between devices, shards(): lax.ppermute(term, 'ctx', [(i, i - shift) for i in range(shift, ctx)])  3.86 us
    ppermute x3, starting transfers between devices, exchange(): lax.ppermute(part, axis, [(i, (i + shift) % size) for i in range(size)])  3.61 us
    ppermute x1, waiting for transfers between devices, exchange(): part = part + lax.ppermute(part, axis, [(i, i ^ step) for i in range(size)])  2.37 us
    ppermute x1, starting transfers between devices, exchange(): part = part + lax.ppermute(part, axis, [(i, i ^ step) for i in range(size)])  2.01 us
  transfers between devices with their start and end apart: 11, of which 2 were waited for; matrix products, arithmetic and copies ran while one was open for 0% of the time, Pallas kernels for 7%

profile of v6, /device:TPU:0, one launch (start us, length us, event | category | flops | bytes accessed | tf_op | source)
XLA Modules:
  0.0 42.8 jit_solution(4466704895261730459)
XLA Ops:
  0.6 0.9 %pad_maximum_fusion.pair_ref.refs_9_ = bf16[128,512]{1,0:T(8,128)(2,1)S(1)} fusion(bf16[128,256]{1,0:T(8,128)(2,1)} %bitcast.16, bf16[128,256]{1,0:T(8,128)(2,1)} %bitcast.17), kind=kLoop, calls=%fused_computation | loop fusion | flops 262144 | bytes 262144 | tf_op jit(solution)/shard_map/concatenate | solution.py:218
  1.5 4.9 %collective-permute-start.2 = (bf16[128,512]{1,0:T(8,128)(2,1)S(1)}, bf16[128,512]{1,0:T(8,128)(2,1)S(1)}, u32[]{:S(2)}, u32[]{:S(2)}) collective-permute-start(bf16[128,512]{1,0:T(8,128)(2,1)S(1)} %pad_maximum_fusion.pair_ref.refs_9_), channel_id=1, source_target_pairs={{0,2},{2,4},{4,6},{1,3},{3,5},{5,7},{8,10},{10,12},{12,14},{9,11},... | collective-permute-start | bytes 393224 | tf_op jit(solution)/shard_map/ppermute | solution.py:220
  6.5 4.5 %collective-permute-start.1 = (bf16[128,512]{1,0:T(8,128)(2,1)S(1)}, bf16[128,512]{1,0:T(8,128)(2,1)S(1)}, u32[]{:S(2)}, u32[]{:S(2)}) collective-permute-start(bf16[128,512]{1,0:T(8,128)(2,1)S(1)} %pad_maximum_fusion.pair_ref.refs_9_), channel_id=1, source_target_pairs={{0,4},{2,6},{1,5},{3,7},{8,12},{10,14},{9,13},{11,15},{16,20},{18,... | collective-permute-start | bytes 393224 | tf_op jit(solution)/shard_map/ppermute | solution.py:220
  11.0 1.3 %collective-permute-start = (bf16[128,512]{1,0:T(8,128)(2,1)S(1)}, bf16[128,512]{1,0:T(8,128)(2,1)S(1)}, u32[]{:S(2)}, u32[]{:S(2)}) collective-permute-start(bf16[128,512]{1,0:T(8,128)(2,1)S(1)} %pad_maximum_fusion.pair_ref.refs_9_), channel_id=1, source_target_pairs={{0,6},{1,7},{8,14},{9,15},{16,22},{17,23},{24,30},{25,31}} | collective-permute-start | bytes 393224 | tf_op jit(solution)/shard_map/ppermute | solution.py:220
  12.3 0.0 copy-start
  12.3 1.0 %copy-done = bf16[1,128,2048]{2,1,0:T(8,128)(2,1)S(1)} copy-done((bf16[1,128,2048]{2,1,0:T(8,128)(2,1)S(1)}, bf16[1,128,2048]{2,1,0:T(8,128)(2,1)}, u32[]{:S(2)}) %copy-start) | copy-done | bytes 524312
  13.3 0.0 copy-start.1
  13.3 1.0 %copy-done.1 = bf16[1,128,2048]{2,1,0:T(8,128)(2,1)S(1)} copy-done((bf16[1,128,2048]{2,1,0:T(8,128)(2,1)S(1)}, bf16[1,128,2048]{2,1,0:T(8,128)(2,1)}, u32[]{:S(2)}) %copy-start.1) | copy-done | bytes 524312
  14.4 0.0 copy-start.2
  14.4 0.7 %copy-done.2 = bf16[2048]{0:T(1024)(128)(2,1)S(1)} copy-done((bf16[2048]{0:T(1024)(128)(2,1)S(1)}, bf16[2048]{0:T(1024)(128)(2,1)}, u32[]{:S(2)}) %copy-start.2) | copy-done | bytes 4120
  15.0 0.0 copy-start.3
  15.0 0.7 %copy-done.3 = s32[1,8]{1,0:T(1,128)S(1)} copy-done((s32[1,8]{1,0:T(1,128)S(1)}, s32[1,8]{1,0:T(1,128)}, u32[]{:S(2)}) %copy-start.3) | copy-done | bytes 56
  15.7 0.0 copy-start.4
  15.7 0.7 %copy-done.4 = bf16[256]{0:T(256)(128)(2,1)S(1)} copy-done((bf16[256]{0:T(256)(128)(2,1)S(1)}, bf16[256]{0:T(256)(128)(2,1)}, u32[]{:S(2)}) %copy-start.4) | copy-done | bytes 536
  16.4 1.1 %prepare.1 = (bf16[2,128]{1,0:T(2,128)(2,1)S(1)}, bf16[2048,256]{1,0:T(8,128)(2,1)S(1)}, bf16[2048,128]{1,0:T(8,128)(2,1)S(1)}, f32[128,2048]{1,0:T(8,128)S(1)},...) custom-call(s32[1,8]{1,0:T(1,128)S(1)} %copy-done.3, bf16[128,512]{1,0:T(8,128)(2,1)S(1)} %pad_maximum_fusion.pair_ref.refs_9_, ...), custom_call_target="tpu_custom_call" | custom-call | flops 134217728 | bytes 4194304 | tf_op jit(solution)/shard_map/prepare/pallas_call | solution.py:223
  17.5 0.0 collective-permute-done.2.refs_8_
  17.5 0.0 collective-permute-done.1.refs_7_
  17.5 0.0 collective-permute-done.refs_6_
  17.5 4.2 %attend.1 = (bf16[512,2048]{1,0:T(8,128)(2,1)S(1)}, bf16[512,2048]{1,0:T(8,128)(2,1)S(1)}, bf16[512,256]{1,0:T(8,128)(2,1)S(1)}, bf16[512,256]{1,0:T(8,128)(2,1)...) custom-call(bf16[2,128]{1,0:T(2,128)(2,1)S(1)} %get-tuple-element.27, ...), custom_call_target="tpu_custom_call" | custom-call | flops 1073741824 | bytes 4194304 | tf_op jit(solution)/shard_map/attend/pallas_call | solution.py:249
  21.8 2.5 %collective-permute-start.5 = (f32[18,128]{1,0:T(8,128)S(1)}, f32[18,128]{1,0:T(8,128)S(1)}, u32[]{:S(2)}, u32[]{:S(2)}) collective-permute-start(f32[18,128]{1,0:T(8,128)S(1)} %get-tuple-element.39), channel_id=1, source_target_pairs={{0,24},{8,0},{16,8},{24,16},{1,25},{9,1},{17,9},{25,17},{2,26},{10... | collective-permute-start | bytes 27656 | tf_op jit(solution)/shard_map/ppermute | solution.py:204
  24.3 0.5 %collective-permute-start.4 = (f32[18,128]{1,0:T(8,128)S(1)}, f32[18,128]{1,0:T(8,128)S(1)}, u32[]{:S(2)}, u32[]{:S(2)}) collective-permute-start(f32[18,128]{1,0:T(8,128)S(1)} %get-tuple-element.39), channel_id=1, source_target_pairs={{0,16},{8,24},{16,0},{24,8},{1,17},{9,25},{17,1},{25,9},{2,18},{10... | collective-permute-start | bytes 27656 | tf_op jit(solution)/shard_map/ppermute | solution.py:204
  24.8 0.6 %collective-permute-start.3 = (f32[18,128]{1,0:T(8,128)S(1)}, f32[18,128]{1,0:T(8,128)S(1)}, u32[]{:S(2)}, u32[]{:S(2)}) collective-permute-start(f32[18,128]{1,0:T(8,128)S(1)} %get-tuple-element.39), channel_id=1, source_target_pairs={{0,8},{8,16},{16,24},{24,0},{1,9},{9,17},{17,25},{25,1},{2,10},{10... | collective-permute-start | bytes 27656 | tf_op jit(solution)/shard_map/ppermute | solution.py:204
  25.4 1.3 %collective-permute-start.8 = (bf16[128,512]{1,0:T(8,128)(2,1)S(1)}, bf16[128,512]{1,0:T(8,128)(2,1)S(1)}, u32[]{:S(2)}, u32[]{:S(2)}) collective-permute-start(bf16[128,512]{1,0:T(8,128)(2,1)S(1)} %get-tuple-element.41), channel_id=1, source_target_pairs={{2,0},{4,2},{6,4},{3,1},{5,3},{7,5},{10,8},{12,10},{14,12},{11,9},... | collective-permute-start | bytes 393224 | tf_op jit(solution)/shard_map/ppermute | solution.py:275
  26.7 1.3 %collective-permute-start.9 = (bf16[128,512]{1,0:T(8,128)(2,1)S(1)}, bf16[128,512]{1,0:T(8,128)(2,1)S(1)}, u32[]{:S(2)}, u32[]{:S(2)}) collective-permute-start(bf16[128,512]{1,0:T(8,128)(2,1)S(1)} %get-tuple-element.42), channel_id=1, source_target_pairs={{4,0},{6,2},{5,1},{7,3},{12,8},{14,10},{13,9},{15,11},{20,16},{22,... | collective-permute-start | bytes 393224 | tf_op jit(solution)/shard_map/ppermute | solution.py:275
  28.0 0.0 collective-permute-done.5
  28.0 1.3 %collective-permute-start.10 = (bf16[128,512]{1,0:T(8,128)(2,1)S(1)}, bf16[128,512]{1,0:T(8,128)(2,1)S(1)}, u32[]{:S(2)}, u32[]{:S(2)}) collective-permute-start(bf16[128,512]{1,0:T(8,128)(2,1)S(1)} %get-tuple-element.43), channel_id=1, source_target_pairs={{6,0},{7,1},{14,8},{15,9},{22,16},{23,17},{30,24},{31,25}} | collective-permute-start | bytes 393224 | tf_op jit(solution)/shard_map/ppermute | solution.py:275
  29.3 0.0 collective-permute-done.4
  29.3 0.1 collective-permute-done.3
  29.4 2.0 %collective-permute-start.6 = (f32[18,128]{1,0:T(8,128)S(1)}, f32[18,128]{1,0:T(8,128)S(1)}, u32[]{:S(2)}, u32[]{:S(2)}) collective-permute-start(f32[18,128]{1,0:T(8,128)S(1)} %add_add_fusion), channel_id=1, source_target_pairs={{0,2},{2,0},{4,6},{6,4},{1,3},{3,1},{5,7},{7,5},{8,10},{10,8},{12,... | collective-permute-start | bytes 27656 | tf_op jit(solution)/shard_map/ppermute | solution.py:200
  31.4 2.4 %collective-permute-done.6 = f32[18,128]{1,0:T(8,128)S(1)} collective-permute-done((f32[18,128]{1,0:T(8,128)S(1)}, f32[18,128]{1,0:T(8,128)S(1)}, u32[]{:S(2)}, u32[]{:S(2)}) %collective-permute-start.6) | collective-permute-done | bytes 9248 | tf_op jit(solution)/shard_map/ppermute | solution.py:200
  33.8 6.5 %collective-permute-start.7 = (f32[18,128]{1,0:T(8,128)S(1)}, f32[18,128]{1,0:T(8,128)S(1)}, u32[]{:S(2)}, u32[]{:S(2)}) collective-permute-start(f32[18,128]{1,0:T(8,128)S(1)} %add.15.refs_0_), channel_id=1, source_target_pairs={{0,4},{2,6},{4,0},{6,2},{1,5},{3,7},{5,1},{7,3},{8,12},{10,14},{12... | collective-permute-start | bytes 27656 | tf_op jit(solution)/shard_map/ppermute | solution.py:202
  40.3 1.8 %finish.1 = (bf16[128,2048]{1,0:T(8,128)(2,1)}, bf16[128,2048]{1,0:T(8,128)(2,1)}) custom-call(bf16[512,2048]{1,0:T(8,128)(2,1)S(1)} %get-tuple-element.33.probs_ref, bf16[512,2048]{1,0:T(8,128)(2,1)S(1)} %get-tuple-element.34.dscore_ref, bf16[512,256]{1,0:T(8,128)(2,1)S(1)} %get-tuple-element.35.keys_ref, bf16[512,256]{1,0:T(8,128)(2,1)S(1)} %get-tuple-element.36.values_ref), custom_call_target="tpu_custom_call" | custom-call | flops 536870912 | bytes 4194304 | tf_op jit(solution)/shard_map/finish/pallas_call | solution.py:278
  42.0 0.0 collective-permute-done.7.refs_1_
  42.0 0.0 collective-permute-done.8.refs_3_
  42.0 0.0 collective-permute-done.9.refs_4_
  42.1 0.0 collective-permute-done.10.refs_5_
  42.1 0.7 %collect.1 = (bf16[128,256]{1,0:T(8,128)(2,1)}, bf16[128,256]{1,0:T(8,128)(2,1)}, f32[16,128]{1,0:T(8,128)}, f32[2,128]{1,0:T(2,128)}) custom-call(f32[18,128]{1,0:T(8,128)S(1)} %add.15.refs_0_, f32[18,128]{1,0:T(8,128)S(1)} %collective-permute-done.7.refs_1_, f32[128,512]{1,0:T(8,128)S(1)} %get-tuple-element.40.refs_2_, ...), custom_call_target="tpu_custom_call" | custom-call | flops 262144 | bytes 524288 | tf_op jit(solution)/shard_map/collect/pallas_call | solution.py:293
  (2 shorter events, 0.0 us)
Async XLA Ops:
  1.5 16.0 %collective-permute-start.2 = (bf16[128,512]{1,0:T(8,128)(2,1)S(1)}, bf16[128,512]{1,0:T(8,128)(2,1)S(1)}, u32[]{:S(2)}, u32[]{:S(2)}) collective-permute-start(bf16[128,512]{1,0:T(8,128)(2,1)S(1)} %pad_maximum_fusion.pair_ref.refs_9_), channel_id=1, source_target_pairs={{0,2},{2,4},{4,6},{1,3},{3,5},{5,7},{8,10},{10,12},{12,14},{9,11},... | collective-permute-start | bytes 393224 | tf_op jit(solution)/shard_map/ppermute | solution.py:220
  6.5 11.0 %collective-permute-start.1 = (bf16[128,512]{1,0:T(8,128)(2,1)S(1)}, bf16[128,512]{1,0:T(8,128)(2,1)S(1)}, u32[]{:S(2)}, u32[]{:S(2)}) collective-permute-start(bf16[128,512]{1,0:T(8,128)(2,1)S(1)} %pad_maximum_fusion.pair_ref.refs_9_), channel_id=1, source_target_pairs={{0,4},{2,6},{1,5},{3,7},{8,12},{10,14},{9,13},{11,15},{16,20},{18,... | collective-permute-start | bytes 393224 | tf_op jit(solution)/shard_map/ppermute | solution.py:220
  11.0 6.5 %collective-permute-start = (bf16[128,512]{1,0:T(8,128)(2,1)S(1)}, bf16[128,512]{1,0:T(8,128)(2,1)S(1)}, u32[]{:S(2)}, u32[]{:S(2)}) collective-permute-start(bf16[128,512]{1,0:T(8,128)(2,1)S(1)} %pad_maximum_fusion.pair_ref.refs_9_), channel_id=1, source_target_pairs={{0,6},{1,7},{8,14},{9,15},{16,22},{17,23},{24,30},{25,31}} | collective-permute-start | bytes 393224 | tf_op jit(solution)/shard_map/ppermute | solution.py:220
  12.3 1.0 %copy-start = (bf16[1,128,2048]{2,1,0:T(8,128)(2,1)S(1)}, bf16[1,128,2048]{2,1,0:T(8,128)(2,1)}, u32[]{:S(2)}) copy-start(bf16[1,128,2048]{2,1,0:T(8,128)(2,1)} %param.7) | copy-start | bytes 1572868
  13.3 1.0 %copy-start.1 = (bf16[1,128,2048]{2,1,0:T(8,128)(2,1)S(1)}, bf16[1,128,2048]{2,1,0:T(8,128)(2,1)}, u32[]{:S(2)}) copy-start(bf16[1,128,2048]{2,1,0:T(8,128)(2,1)} %param.12) | copy-start | bytes 1572868
  14.4 0.7 %copy-start.2 = (bf16[2048]{0:T(1024)(128)(2,1)S(1)}, bf16[2048]{0:T(1024)(128)(2,1)}, u32[]{:S(2)}) copy-start(bf16[2048]{0:T(1024)(128)(2,1)} %param.8) | copy-start | bytes 12292
  15.0 0.7 %copy-start.3 = (s32[1,8]{1,0:T(1,128)S(1)}, s32[1,8]{1,0:T(1,128)}, u32[]{:S(2)}) copy-start(s32[1,8]{1,0:T(1,128)} %len_ref.1) | copy-start | bytes 100
  15.7 0.7 %copy-start.4 = (bf16[256]{0:T(256)(128)(2,1)S(1)}, bf16[256]{0:T(256)(128)(2,1)}, u32[]{:S(2)}) copy-start(bf16[256]{0:T(256)(128)(2,1)} %param.11) | copy-start | bytes 1540
  21.8 6.2 %collective-permute-start.5 = (f32[18,128]{1,0:T(8,128)S(1)}, f32[18,128]{1,0:T(8,128)S(1)}, u32[]{:S(2)}, u32[]{:S(2)}) collective-permute-start(f32[18,128]{1,0:T(8,128)S(1)} %get-tuple-element.39), channel_id=1, source_target_pairs={{0,24},{8,0},{16,8},{24,16},{1,25},{9,1},{17,9},{25,17},{2,26},{10... | collective-permute-start | bytes 27656 | tf_op jit(solution)/shard_map/ppermute | solution.py:204
  24.3 5.0 %collective-permute-start.4 = (f32[18,128]{1,0:T(8,128)S(1)}, f32[18,128]{1,0:T(8,128)S(1)}, u32[]{:S(2)}, u32[]{:S(2)}) collective-permute-start(f32[18,128]{1,0:T(8,128)S(1)} %get-tuple-element.39), channel_id=1, source_target_pairs={{0,16},{8,24},{16,0},{24,8},{1,17},{9,25},{17,1},{25,9},{2,18},{10... | collective-permute-start | bytes 27656 | tf_op jit(solution)/shard_map/ppermute | solution.py:204
  24.8 4.6 %collective-permute-start.3 = (f32[18,128]{1,0:T(8,128)S(1)}, f32[18,128]{1,0:T(8,128)S(1)}, u32[]{:S(2)}, u32[]{:S(2)}) collective-permute-start(f32[18,128]{1,0:T(8,128)S(1)} %get-tuple-element.39), channel_id=1, source_target_pairs={{0,8},{8,16},{16,24},{24,0},{1,9},{9,17},{17,25},{25,1},{2,10},{10... | collective-permute-start | bytes 27656 | tf_op jit(solution)/shard_map/ppermute | solution.py:204
  25.4 16.7 %collective-permute-start.8 = (bf16[128,512]{1,0:T(8,128)(2,1)S(1)}, bf16[128,512]{1,0:T(8,128)(2,1)S(1)}, u32[]{:S(2)}, u32[]{:S(2)}) collective-permute-start(bf16[128,512]{1,0:T(8,128)(2,1)S(1)} %get-tuple-element.41), channel_id=1, source_target_pairs={{2,0},{4,2},{6,4},{3,1},{5,3},{7,5},{10,8},{12,10},{14,12},{11,9},... | collective-permute-start | bytes 393224 | tf_op jit(solution)/shard_map/ppermute | solution.py:275
  26.7 15.4 %collective-permute-start.9 = (bf16[128,512]{1,0:T(8,128)(2,1)S(1)}, bf16[128,512]{1,0:T(8,128)(2,1)S(1)}, u32[]{:S(2)}, u32[]{:S(2)}) collective-permute-start(bf16[128,512]{1,0:T(8,128)(2,1)S(1)} %get-tuple-element.42), channel_id=1, source_target_pairs={{4,0},{6,2},{5,1},{7,3},{12,8},{14,10},{13,9},{15,11},{20,16},{22,... | collective-permute-start | bytes 393224 | tf_op jit(solution)/shard_map/ppermute | solution.py:275
  28.0 14.1 %collective-permute-start.10 = (bf16[128,512]{1,0:T(8,128)(2,1)S(1)}, bf16[128,512]{1,0:T(8,128)(2,1)S(1)}, u32[]{:S(2)}, u32[]{:S(2)}) collective-permute-start(bf16[128,512]{1,0:T(8,128)(2,1)S(1)} %get-tuple-element.43), channel_id=1, source_target_pairs={{6,0},{7,1},{14,8},{15,9},{22,16},{23,17},{30,24},{31,25}} | collective-permute-start | bytes 393224 | tf_op jit(solution)/shard_map/ppermute | solution.py:275
  29.4 4.4 %collective-permute-start.6 = (f32[18,128]{1,0:T(8,128)S(1)}, f32[18,128]{1,0:T(8,128)S(1)}, u32[]{:S(2)}, u32[]{:S(2)}) collective-permute-start(f32[18,128]{1,0:T(8,128)S(1)} %add_add_fusion), channel_id=1, source_target_pairs={{0,2},{2,0},{4,6},{6,4},{1,3},{3,1},{5,7},{7,5},{8,10},{10,8},{12,... | collective-permute-start | bytes 27656 | tf_op jit(solution)/shard_map/ppermute | solution.py:200
  33.8 8.3 %collective-permute-start.7 = (f32[18,128]{1,0:T(8,128)S(1)}, f32[18,128]{1,0:T(8,128)S(1)}, u32[]{:S(2)}, u32[]{:S(2)}) collective-permute-start(f32[18,128]{1,0:T(8,128)S(1)} %add.15.refs_0_), channel_id=1, source_target_pairs={{0,4},{2,6},{4,0},{6,2},{1,5},{3,7},{5,1},{7,3},{8,12},{10,14},{12... | collective-permute-start | bytes 27656 | tf_op jit(solution)/shard_map/ppermute | solution.py:202

commit v7 on v6

--- a/solution.py
+++ b/solution.py
@@ -17,6 +17,7 @@
 LOG2E = 1.4426950408889634
 NEGATIVE = -1e30
 VMEM = pl.BlockSpec(memory_space=pltpu.VMEM)
+ANY = pl.BlockSpec(memory_space=pl.ANY)
 SMEM = pl.BlockSpec(memory_space=pltpu.SMEM)
 
 
@@ -188,18 +189,32 @@
     vg_ref[...] = term[:, kv_width:]
 
 
-def total_of(parts):
-    return functools.reduce(lambda left, right: left + right, parts)
+def total_kernel(*refs):
+    out_ref = refs[-2]
+    total = refs[0][...]
+    for ref in refs[1:-3]:
+        total = total + ref[...]
+    out_ref[...] = total
+
+
+def total_after(parts, received):
+    return pl.pallas_call(
+        total_kernel,
+        out_shape=[
+            shape(parts[0].shape, parts[0].dtype),
+            shape(received.shape, received.dtype),
+        ],
+        in_specs=[VMEM] * len(parts) + [ANY],
+        out_specs=[VMEM, ANY],
+        input_output_aliases={len(parts): 1},
+        compiler_params=params(4),
+        cost_estimate=pl.CostEstimate(flops=parts[0].size, bytes_accessed=0, transcendentals=0),
+        name="total",
+    )(*parts, received)
 
 
 def exchange(axis, part):
     size = lax.axis_size(axis)
-    if axis == "ctx" and not size & (size - 1):
-        step = 1
-        while 2 * step < size:
-            part = part + lax.ppermute(part, axis, [(i, i ^ step) for i in range(size)])
-            step *= 2
-        return [part, lax.ppermute(part, axis, [(i, i ^ step) for i in range(size)])]
     return [part] + [
         lax.ppermute(part, axis, [(i, (i + shift) % size) for i in range(size)])
         for shift in range(1, size)
@@ -289,7 +304,8 @@
         ),
         name="finish",
     )(probs, dscore, all_keys, all_values)
-    sums = exchange("ctx", total_of(exchange("dp", sums)))
+    sums, back[0] = total_after(exchange("dp", sums), back[0])
+    sums = exchange("ctx", sums)
     k_grad, v_grad, q_sum, v_sum = pl.pallas_call(
         functools.partial(collect_kernel, batches, len(sums), len(back)),
         out_shape=[

time: 43.2 us -> 46.7 us (1.081)
  waiting for transfers between devices: 2.48 us -> 6.59 us
  starting transfers between devices: 26.7 us -> 26.2 us
    ppermute x2 -> x0, starting transfers between devices: 8.51 us -> none  [the longest x1 6.5 us: exchange(): lax.ppermute(part, axis, [(i, i ^ step) for i in range(size)])]
    ppermute x3 -> x6, starting transfers between devices: 3.61 us -> 11.6 us  [exchange(): lax.ppermute(part, axis, [(i, (i + shift) % size) for i in range(size)])]
    ppermute x3 -> x6, waiting for transfers between devices: 0.1 us -> 6.58 us  [exchange(): lax.ppermute(part, axis, [(i, (i + shift) % size) for i in range(size)])]
    ppermute x2 -> x0, waiting for transfers between devices: 2.37 us -> none  [the longest x1 2.37 us: exchange(): part = part + lax.ppermute(part, axis, [(i, i ^ step) for i in range(size)])]
  transfers between devices with their start and end apart: 11 -> 12, of which waited for: 2 -> 5; matrix products, arithmetic and copies ran while one was open for 0% -> 0% of each run, Pallas kernels for 7% -> 6%
where the time goes in v7:
time: 46.7 us; the launch traced here: 46.3 us
  starting transfers between devices  26.2 us (56%)
  Pallas kernels  7.84 us (17%)
  waiting for transfers between devices  6.59 us (14%)
  local copies, waits for them, and re-layouts  4.07 us (9%)
  other arithmetic  0.88 us (2%)
  between operations  0.75 us (2%)
    ppermute x6, starting transfers between devices, exchange(): lax.ppermute(part, axis, [(i, (i + shift) % size) for i in range(size)])  11.6 us
    ppermute x3, starting transfers between devices, shards(): lax.ppermute(pair, 'ctx', [(i, i + shift) for i in range(ctx - shift)])  10.7 us
    ppermute x6, waiting for transfers between devices, exchange(): lax.ppermute(part, axis, [(i, (i + shift) % size) for i in range(size)])  6.58 us
    pallas_call x1, Pallas kernels, shards(): pl.pallas_call(functools.partial(attend_kernel, ctx), out_shape=[shape((r...  4.24 us
    unnamed x10, local copies, waits for them, and re-layouts  4.07 us
    ppermute x3, starting transfers between devices, shards(): lax.ppermute(term, 'ctx', [(i, i - shift) for i in range(shift, ctx)])  3.88 us
    pallas_call x1, Pallas kernels, shards(): pl.pallas_call(finish_kernel, out_shape=[shape((tok, width), jnp.bfloat16...  1.79 us
    pallas_call x1, Pallas kernels, shards(): pl.pallas_call(functools.partial(prepare_kernel, ctx), out_shape=[shape((...  1.11 us
  transfers between devices with their start and end apart: 12, of which 5 were waited for; matrix products, arithmetic and copies ran while one was open for 0% of the time, Pallas kernels for 6%

profile of v7, /device:TPU:0, one launch (start us, length us, event | category | flops | bytes accessed | tf_op | source)
XLA Modules:
  0.0 46.3 jit_solution(12712159516815611949)
XLA Ops:
  0.6 0.9 %pad_maximum_fusion.pair_ref.refs_9_ = bf16[128,512]{1,0:T(8,128)(2,1)S(1)} fusion(bf16[128,256]{1,0:T(8,128)(2,1)} %bitcast.16, bf16[128,256]{1,0:T(8,128)(2,1)} %bitcast.17), kind=kLoop, calls=%fused_computation | loop fusion | flops 262144 | bytes 262144 | tf_op jit(solution)/shard_map/concatenate | solution.py:233
  1.5 4.9 %collective-permute-start.2 = (bf16[128,512]{1,0:T(8,128)(2,1)S(1)}, bf16[128,512]{1,0:T(8,128)(2,1)S(1)}, u32[]{:S(2)}, u32[]{:S(2)}) collective-permute-start(bf16[128,512]{1,0:T(8,128)(2,1)S(1)} %pad_maximum_fusion.pair_ref.refs_9_), channel_id=1, source_target_pairs={{0,2},{2,4},{4,6},{1,3},{3,5},{5,7},{8,10},{10,12},{12,14},{9,11},... | collective-permute-start | bytes 393224 | tf_op jit(solution)/shard_map/ppermute | solution.py:235
  6.5 4.5 %collective-permute-start.1 = (bf16[128,512]{1,0:T(8,128)(2,1)S(1)}, bf16[128,512]{1,0:T(8,128)(2,1)S(1)}, u32[]{:S(2)}, u32[]{:S(2)}) collective-permute-start(bf16[128,512]{1,0:T(8,128)(2,1)S(1)} %pad_maximum_fusion.pair_ref.refs_9_), channel_id=1, source_target_pairs={{0,4},{2,6},{1,5},{3,7},{8,12},{10,14},{9,13},{11,15},{16,20},{18,... | collective-permute-start | bytes 393224 | tf_op jit(solution)/shard_map/ppermute | solution.py:235
  11.0 1.3 %collective-permute-start = (bf16[128,512]{1,0:T(8,128)(2,1)S(1)}, bf16[128,512]{1,0:T(8,128)(2,1)S(1)}, u32[]{:S(2)}, u32[]{:S(2)}) collective-permute-start(bf16[128,512]{1,0:T(8,128)(2,1)S(1)} %pad_maximum_fusion.pair_ref.refs_9_), channel_id=1, source_target_pairs={{0,6},{1,7},{8,14},{9,15},{16,22},{17,23},{24,30},{25,31}} | collective-permute-start | bytes 393224 | tf_op jit(solution)/shard_map/ppermute | solution.py:235
  12.3 0.0 copy-start
  12.3 1.0 %copy-done = bf16[1,128,2048]{2,1,0:T(8,128)(2,1)S(1)} copy-done((bf16[1,128,2048]{2,1,0:T(8,128)(2,1)S(1)}, bf16[1,128,2048]{2,1,0:T(8,128)(2,1)}, u32[]{:S(2)}) %copy-start) | copy-done | bytes 524312
  13.3 0.0 copy-start.1
  13.3 1.0 %copy-done.1 = bf16[1,128,2048]{2,1,0:T(8,128)(2,1)S(1)} copy-done((bf16[1,128,2048]{2,1,0:T(8,128)(2,1)S(1)}, bf16[1,128,2048]{2,1,0:T(8,128)(2,1)}, u32[]{:S(2)}) %copy-start.1) | copy-done | bytes 524312
  14.4 0.0 copy-start.2
  14.4 0.7 %copy-done.2 = bf16[2048]{0:T(1024)(128)(2,1)S(1)} copy-done((bf16[2048]{0:T(1024)(128)(2,1)S(1)}, bf16[2048]{0:T(1024)(128)(2,1)}, u32[]{:S(2)}) %copy-start.2) | copy-done | bytes 4120
  15.0 0.0 copy-start.3
  15.0 0.7 %copy-done.3 = s32[1,8]{1,0:T(1,128)S(1)} copy-done((s32[1,8]{1,0:T(1,128)S(1)}, s32[1,8]{1,0:T(1,128)}, u32[]{:S(2)}) %copy-start.3) | copy-done | bytes 56
  15.7 0.0 copy-start.4
  15.7 0.7 %copy-done.4 = bf16[256]{0:T(256)(128)(2,1)S(1)} copy-done((bf16[256]{0:T(256)(128)(2,1)S(1)}, bf16[256]{0:T(256)(128)(2,1)}, u32[]{:S(2)}) %copy-start.4) | copy-done | bytes 536
  16.4 1.1 %prepare.1 = (bf16[2,128]{1,0:T(2,128)(2,1)S(1)}, bf16[2048,256]{1,0:T(8,128)(2,1)S(1)}, bf16[2048,128]{1,0:T(8,128)(2,1)S(1)}, f32[128,2048]{1,0:T(8,128)S(1)},...) custom-call(s32[1,8]{1,0:T(1,128)S(1)} %copy-done.3, bf16[128,512]{1,0:T(8,128)(2,1)S(1)} %pad_maximum_fusion.pair_ref.refs_9_, ...), custom_call_target="tpu_custom_call" | custom-call | flops 134217728 | bytes 4194304 | tf_op jit(solution)/shard_map/prepare/pallas_call | solution.py:238
  17.5 0.0 collective-permute-done.2.refs_8_
  17.5 0.0 collective-permute-done.1.refs_7_
  17.5 0.0 collective-permute-done.refs_6_
  17.5 4.2 %attend.1 = (bf16[512,2048]{1,0:T(8,128)(2,1)S(1)}, bf16[512,2048]{1,0:T(8,128)(2,1)S(1)}, bf16[512,256]{1,0:T(8,128)(2,1)S(1)}, bf16[512,256]{1,0:T(8,128)(2,1)...) custom-call(bf16[2,128]{1,0:T(2,128)(2,1)S(1)} %get-tuple-element.29, ...), custom_call_target="tpu_custom_call" | custom-call | flops 1073741824 | bytes 4194304 | tf_op jit(solution)/shard_map/attend/pallas_call | solution.py:264
  21.8 1.3 %collective-permute-start.6 = (bf16[128,512]{1,0:T(8,128)(2,1)S(1)}, bf16[128,512]{1,0:T(8,128)(2,1)S(1)}, u32[]{:S(2)}, u32[]{:S(2)}) collective-permute-start(bf16[128,512]{1,0:T(8,128)(2,1)S(1)} %get-tuple-element.42), channel_id=1, source_target_pairs={{2,0},{4,2},{6,4},{3,1},{5,3},{7,5},{10,8},{12,10},{14,12},{11,9},... | collective-permute-start | bytes 393224 | tf_op jit(solution)/shard_map/ppermute | solution.py:290
  23.1 1.3 %collective-permute-start.10 = (bf16[128,512]{1,0:T(8,128)(2,1)S(1)}, bf16[128,512]{1,0:T(8,128)(2,1)S(1)}, u32[]{:S(2)}, u32[]{:S(2)}) collective-permute-start(bf16[128,512]{1,0:T(8,128)(2,1)S(1)} %get-tuple-element.46), channel_id=1, source_target_pairs={{4,0},{6,2},{5,1},{7,3},{12,8},{14,10},{13,9},{15,11},{20,16},{22,... | collective-permute-start | bytes 393224 | tf_op jit(solution)/shard_map/ppermute | solution.py:290
  24.4 1.3 %collective-permute-start.11 = (bf16[128,512]{1,0:T(8,128)(2,1)S(1)}, bf16[128,512]{1,0:T(8,128)(2,1)S(1)}, u32[]{:S(2)}, u32[]{:S(2)}) collective-permute-start(bf16[128,512]{1,0:T(8,128)(2,1)S(1)} %get-tuple-element.47), channel_id=1, source_target_pairs={{6,0},{7,1},{14,8},{15,9},{22,16},{23,17},{30,24},{31,25}} | collective-permute-start | bytes 393224 | tf_op jit(solution)/shard_map/ppermute | solution.py:290
  25.7 2.5 %collective-permute-start.5 = (f32[18,128]{1,0:T(8,128)S(1)}, f32[18,128]{1,0:T(8,128)S(1)}, u32[]{:S(2)}, u32[]{:S(2)}) collective-permute-start(f32[18,128]{1,0:T(8,128)S(1)} %get-tuple-element.41.refs_0_), channel_id=1, source_target_pairs={{0,24},{8,0},{16,8},{24,16},{1,25},{9,1},{17,9},{25,17},{2,26},{10... | collective-permute-start | bytes 27656 | tf_op jit(solution)/shard_map/ppermute | solution.py:219
  28.2 0.5 %collective-permute-start.4 = (f32[18,128]{1,0:T(8,128)S(1)}, f32[18,128]{1,0:T(8,128)S(1)}, u32[]{:S(2)}, u32[]{:S(2)}) collective-permute-start(f32[18,128]{1,0:T(8,128)S(1)} %get-tuple-element.41.refs_0_), channel_id=1, source_target_pairs={{0,16},{8,24},{16,0},{24,8},{1,17},{9,25},{17,1},{25,9},{2,18},{10... | collective-permute-start | bytes 27656 | tf_op jit(solution)/shard_map/ppermute | solution.py:219
  28.7 0.9 %collective-permute-done.5.refs_3_ = f32[18,128]{1,0:T(8,128)S(1)} collective-permute-done((f32[18,128]{1,0:T(8,128)S(1)}, f32[18,128]{1,0:T(8,128)S(1)}, u32[]{:S(2)}, u32[]{:S(2)}) %collective-permute-start.5) | collective-permute-done | bytes 9248 | tf_op jit(solution)/shard_map/ppermute | solution.py:219
  29.6 2.2 %collective-permute-start.3 = (f32[18,128]{1,0:T(8,128)S(1)}, f32[18,128]{1,0:T(8,128)S(1)}, u32[]{:S(2)}, u32[]{:S(2)}) collective-permute-start(f32[18,128]{1,0:T(8,128)S(1)} %get-tuple-element.41.refs_0_), channel_id=1, source_target_pairs={{0,8},{8,16},{16,24},{24,0},{1,9},{9,17},{17,25},{25,1},{2,10},{10... | collective-permute-start | bytes 27656 | tf_op jit(solution)/shard_map/ppermute | solution.py:219
  31.8 0.2 collective-permute-done.4.refs_2_
  32.0 2.4 %collective-permute-done.3.refs_1_ = f32[18,128]{1,0:T(8,128)S(1)} collective-permute-done((f32[18,128]{1,0:T(8,128)S(1)}, f32[18,128]{1,0:T(8,128)S(1)}, u32[]{:S(2)}, u32[]{:S(2)}) %collective-permute-start.3) | collective-permute-done | bytes 9248 | tf_op jit(solution)/shard_map/ppermute | solution.py:219
  34.4 0.0 collective-permute-done.6.refs_4_
  34.4 5.7 %collective-permute-start.9 = (f32[18,128]{1,0:T(8,128)S(1)}, f32[18,128]{1,0:T(8,128)S(1)}, u32[]{:S(2)}, u32[]{:S(2)}) collective-permute-start(f32[18,128]{1,0:T(8,128)S(1)} %get-tuple-element.43.refs_0_), channel_id=1, source_target_pairs={{0,6},{2,0},{4,2},{6,4},{1,7},{3,1},{5,3},{7,5},{8,14},{10,8},{12,... | collective-permute-start | bytes 27656 | tf_op jit(solution)/shard_map/ppermute | solution.py:219
  40.1 0.0 collective-permute-start.8
  40.1 0.6 %collective-permute-start.7 = (f32[18,128]{1,0:T(8,128)S(1)}, f32[18,128]{1,0:T(8,128)S(1)}, u32[]{:S(2)}, u32[]{:S(2)}) collective-permute-start(f32[18,128]{1,0:T(8,128)S(1)} %get-tuple-element.43.refs_0_), channel_id=1, source_target_pairs={{0,2},{2,4},{4,6},{6,0},{1,3},{3,5},{5,7},{7,1},{8,10},{10,12},{12... | collective-permute-start | bytes 27656 | tf_op jit(solution)/shard_map/ppermute | solution.py:219
  40.8 1.8 %finish.1 = (bf16[128,2048]{1,0:T(8,128)(2,1)}, bf16[128,2048]{1,0:T(8,128)(2,1)}) custom-call(bf16[512,2048]{1,0:T(8,128)(2,1)S(1)} %get-tuple-element.35.probs_ref, bf16[512,2048]{1,0:T(8,128)(2,1)S(1)} %get-tuple-element.36.dscore_ref, bf16[512,256]{1,0:T(8,128)(2,1)S(1)} %get-tuple-element.37.keys_ref, bf16[512,256]{1,0:T(8,128)(2,1)S(1)} %get-tuple-element.38.values_ref), custom_call_target="tpu_custom_call" | custom-call | flops 536870912 | bytes 4194304 | tf_op jit(solution)/shard_map/finish/pallas_call | solution.py:293
  42.6 0.0 collective-permute-done.10.refs_6_
  42.6 0.0 collective-permute-done.11.refs_7_
  42.6 0.0 collective-permute-done.9.refs_3_
  42.6 2.1 %collective-permute-done.8.refs_2_ = f32[18,128]{1,0:T(8,128)S(1)} collective-permute-done((f32[18,128]{1,0:T(8,128)S(1)}, f32[18,128]{1,0:T(8,128)S(1)}, u32[]{:S(2)}, u32[]{:S(2)}) %collective-permute-start.8) | collective-permute-done | bytes 9248 | tf_op jit(solution)/shard_map/ppermute | solution.py:219
  44.7 0.9 %collective-permute-done.7.refs_1_ = f32[18,128]{1,0:T(8,128)S(1)} collective-permute-done((f32[18,128]{1,0:T(8,128)S(1)}, f32[18,128]{1,0:T(8,128)S(1)}, u32[]{:S(2)}, u32[]{:S(2)}) %collective-permute-start.7) | collective-permute-done | bytes 9248 | tf_op jit(solution)/shard_map/ppermute | solution.py:219
  45.6 0.7 %collect.1 = (bf16[128,256]{1,0:T(8,128)(2,1)}, bf16[128,256]{1,0:T(8,128)(2,1)}, f32[16,128]{1,0:T(8,128)}, f32[2,128]{1,0:T(2,128)}) custom-call(f32[18,128]{1,0:T(8,128)S(1)} %get-tuple-element.43.refs_0_, f32[18,128]{1,0:T(8,128)S(1)} %collective-permute-done.7.refs_1_, f32[18,128]{1,0:T(8,128)S(1)} %collective-permute-done.8.refs_2_, ...), custom_call_target="tpu_custom_call" | custom-call | flops 262144 | bytes 524288 | tf_op jit(solution)/shard_map/collect/pallas_call | solution.py:309
  (1 shorter events, 0.0 us)
Async XLA Ops:
  1.5 16.0 %collective-permute-start.2 = (bf16[128,512]{1,0:T(8,128)(2,1)S(1)}, bf16[128,512]{1,0:T(8,128)(2,1)S(1)}, u32[]{:S(2)}, u32[]{:S(2)}) collective-permute-start(bf16[128,512]{1,0:T(8,128)(2,1)S(1)} %pad_maximum_fusion.pair_ref.refs_9_), channel_id=1, source_target_pairs={{0,2},{2,4},{4,6},{1,3},{3,5},{5,7},{8,10},{10,12},{12,14},{9,11},... | collective-permute-start | bytes 393224 | tf_op jit(solution)/shard_map/ppermute | solution.py:235
  6.5 11.0 %collective-permute-start.1 = (bf16[128,512]{1,0:T(8,128)(2,1)S(1)}, bf16[128,512]{1,0:T(8,128)(2,1)S(1)}, u32[]{:S(2)}, u32[]{:S(2)}) collective-permute-start(bf16[128,512]{1,0:T(8,128)(2,1)S(1)} %pad_maximum_fusion.pair_ref.refs_9_), channel_id=1, source_target_pairs={{0,4},{2,6},{1,5},{3,7},{8,12},{10,14},{9,13},{11,15},{16,20},{18,... | collective-permute-start | bytes 393224 | tf_op jit(solution)/shard_map/ppermute | solution.py:235
  11.0 6.5 %collective-permute-start = (bf16[128,512]{1,0:T(8,128)(2,1)S(1)}, bf16[128,512]{1,0:T(8,128)(2,1)S(1)}, u32[]{:S(2)}, u32[]{:S(2)}) collective-permute-start(bf16[128,512]{1,0:T(8,128)(2,1)S(1)} %pad_maximum_fusion.pair_ref.refs_9_), channel_id=1, source_target_pairs={{0,6},{1,7},{8,14},{9,15},{16,22},{17,23},{24,30},{25,31}} | collective-permute-start | bytes 393224 | tf_op jit(solution)/shard_map/ppermute | solution.py:235
  12.3 1.0 %copy-start = (bf16[1,128,2048]{2,1,0:T(8,128)(2,1)S(1)}, bf16[1,128,2048]{2,1,0:T(8,128)(2,1)}, u32[]{:S(2)}) copy-start(bf16[1,128,2048]{2,1,0:T(8,128)(2,1)} %param.7) | copy-start | bytes 1572868
  13.3 1.0 %copy-start.1 = (bf16[1,128,2048]{2,1,0:T(8,128)(2,1)S(1)}, bf16[1,128,2048]{2,1,0:T(8,128)(2,1)}, u32[]{:S(2)}) copy-start(bf16[1,128,2048]{2,1,0:T(8,128)(2,1)} %param.12) | copy-start | bytes 1572868
  14.4 0.7 %copy-start.2 = (bf16[2048]{0:T(1024)(128)(2,1)S(1)}, bf16[2048]{0:T(1024)(128)(2,1)}, u32[]{:S(2)}) copy-start(bf16[2048]{0:T(1024)(128)(2,1)} %param.8) | copy-start | bytes 12292
  15.0 0.7 %copy-start.3 = (s32[1,8]{1,0:T(1,128)S(1)}, s32[1,8]{1,0:T(1,128)}, u32[]{:S(2)}) copy-start(s32[1,8]{1,0:T(1,128)} %len_ref.1) | copy-start | bytes 100
  15.7 0.7 %copy-start.4 = (bf16[256]{0:T(256)(128)(2,1)S(1)}, bf16[256]{0:T(256)(128)(2,1)}, u32[]{:S(2)}) copy-start(bf16[256]{0:T(256)(128)(2,1)} %param.11) | copy-start | bytes 1540
  21.8 12.7 %collective-permute-start.6 = (bf16[128,512]{1,0:T(8,128)(2,1)S(1)}, bf16[128,512]{1,0:T(8,128)(2,1)S(1)}, u32[]{:S(2)}, u32[]{:S(2)}) collective-permute-start(bf16[128,512]{1,0:T(8,128)(2,1)S(1)} %get-tuple-element.42), channel_id=1, source_target_pairs={{2,0},{4,2},{6,4},{3,1},{5,3},{7,5},{10,8},{12,10},{14,12},{11,9},... | collective-permute-start | bytes 393224 | tf_op jit(solution)/shard_map/ppermute | solution.py:290
  23.1 19.5 %collective-permute-start.10 = (bf16[128,512]{1,0:T(8,128)(2,1)S(1)}, bf16[128,512]{1,0:T(8,128)(2,1)S(1)}, u32[]{:S(2)}, u32[]{:S(2)}) collective-permute-start(bf16[128,512]{1,0:T(8,128)(2,1)S(1)} %get-tuple-element.46), channel_id=1, source_target_pairs={{4,0},{6,2},{5,1},{7,3},{12,8},{14,10},{13,9},{15,11},{20,16},{22,... | collective-permute-start | bytes 393224 | tf_op jit(solution)/shard_map/ppermute | solution.py:290
  24.4 18.2 %collective-permute-start.11 = (bf16[128,512]{1,0:T(8,128)(2,1)S(1)}, bf16[128,512]{1,0:T(8,128)(2,1)S(1)}, u32[]{:S(2)}, u32[]{:S(2)}) collective-permute-start(bf16[128,512]{1,0:T(8,128)(2,1)S(1)} %get-tuple-element.47), channel_id=1, source_target_pairs={{6,0},{7,1},{14,8},{15,9},{22,16},{23,17},{30,24},{31,25}} | collective-permute-start | bytes 393224 | tf_op jit(solution)/shard_map/ppermute | solution.py:290
  25.7 3.9 %collective-permute-start.5 = (f32[18,128]{1,0:T(8,128)S(1)}, f32[18,128]{1,0:T(8,128)S(1)}, u32[]{:S(2)}, u32[]{:S(2)}) collective-permute-start(f32[18,128]{1,0:T(8,128)S(1)} %get-tuple-element.41.refs_0_), channel_id=1, source_target_pairs={{0,24},{8,0},{16,8},{24,16},{1,25},{9,1},{17,9},{25,17},{2,26},{10... | collective-permute-start | bytes 27656 | tf_op jit(solution)/shard_map/ppermute | solution.py:219
  28.2 3.8 %collective-permute-start.4 = (f32[18,128]{1,0:T(8,128)S(1)}, f32[18,128]{1,0:T(8,128)S(1)}, u32[]{:S(2)}, u32[]{:S(2)}) collective-permute-start(f32[18,128]{1,0:T(8,128)S(1)} %get-tuple-element.41.refs_0_), channel_id=1, source_target_pairs={{0,16},{8,24},{16,0},{24,8},{1,17},{9,25},{17,1},{25,9},{2,18},{10... | collective-permute-start | bytes 27656 | tf_op jit(solution)/shard_map/ppermute | solution.py:219
  29.6 4.9 %collective-permute-start.3 = (f32[18,128]{1,0:T(8,128)S(1)}, f32[18,128]{1,0:T(8,128)S(1)}, u32[]{:S(2)}, u32[]{:S(2)}) collective-permute-start(f32[18,128]{1,0:T(8,128)S(1)} %get-tuple-element.41.refs_0_), channel_id=1, source_target_pairs={{0,8},{8,16},{16,24},{24,0},{1,9},{9,17},{17,25},{25,1},{2,10},{10... | collective-permute-start | bytes 27656 | tf_op jit(solution)/shard_map/ppermute | solution.py:219
  34.4 8.1 %collective-permute-start.9 = (f32[18,128]{1,0:T(8,128)S(1)}, f32[18,128]{1,0:T(8,128)S(1)}, u32[]{:S(2)}, u32[]{:S(2)}) collective-permute-start(f32[18,128]{1,0:T(8,128)S(1)} %get-tuple-element.43.refs_0_), channel_id=1, source_target_pairs={{0,6},{2,0},{4,2},{6,4},{1,7},{3,1},{5,3},{7,5},{8,14},{10,8},{12,... | collective-permute-start | bytes 27656 | tf_op jit(solution)/shard_map/ppermute | solution.py:219
  40.1 4.6 %collective-permute-start.8 = (f32[18,128]{1,0:T(8,128)S(1)}, f32[18,128]{1,0:T(8,128)S(1)}, u32[]{:S(2)}, u32[]{:S(2)}) collective-permute-start(f32[18,128]{1,0:T(8,128)S(1)} %get-tuple-element.43.refs_0_), channel_id=1, source_target_pairs={{0,4},{2,6},{4,0},{6,2},{1,5},{3,7},{5,1},{7,3},{8,12},{10,14},{12... | collective-permute-start | bytes 27656 | tf_op jit(solution)/shard_map/ppermute | solution.py:219
  40.1 5.5 %collective-permute-start.7 = (f32[18,128]{1,0:T(8,128)S(1)}, f32[18,128]{1,0:T(8,128)S(1)}, u32[]{:S(2)}, u32[]{:S(2)}) collective-permute-start(f32[18,128]{1,0:T(8,128)S(1)} %get-tuple-element.43.refs_0_), channel_id=1, source_target_pairs={{0,2},{2,4},{4,6},{6,0},{1,3},{3,5},{5,7},{7,1},{8,10},{10,12},{12... | collective-permute-start | bytes 27656 | tf_op jit(solution)/shard_map/ppermute | solution.py:219

commit v8 on v5

v8 whole, which is shorter than its diff:
```python
import functools

import jax
import jax.numpy as jnp
from jax import lax
from jax.experimental import pallas as pl
from jax.experimental.pallas import tpu as pltpu
from jax.sharding import PartitionSpec as P

HEAD_DIM = 128
HEADS = 32
KV_HEADS = 4
GROUP = HEADS // KV_HEADS
PAIR = 2
BLOCK = 64
SCALE = HEAD_DIM ** (-0.5)
LOG2E = 1.4426950408889634
NEGATIVE = -1e30
VMEM = pl.BlockSpec(memory_space=pltpu.VMEM)
HBM = pl.BlockSpec(memory_space=pltpu.HBM)


def dot(left, right, left_dim, right_dim):
    return lax.dot_general(
        left, right, (((left_dim,), (right_dim,)), ((), ())), preferred_element_type=jnp.float32
    )


def head_cols(head):
    return slice(head * HEAD_DIM, (head + 1) * HEAD_DIM)


def shape(dims, dtype):
    return jax.ShapeDtypeStruct(dims, dtype)


def params(mebibytes):
    return pltpu.CompilerParams(vmem_limit_bytes=mebibytes * 1024 * 1024)


def biased(values, bias):
    return (values.astype(jnp.float32) + bias.astype(jnp.float32)).astype(jnp.bfloat16)


def pack_kernel(
    q_ref, g_ref, k_ref, v_ref, qb_ref, vb_ref, len_ref, q_own, g_own, qb_own, vb_own, start_ref,
    *refs,
):
    pair_refs, len_own, sems = refs[:-2], refs[-2], refs[-1]
    moves = [(len_ref, len_own)]
    for kv_head, pair_ref in enumerate(pair_refs):
        at = pl.ds(kv_head * HEAD_DIM, HEAD_DIM)
        moves.append((k_ref.at[:, at], pair_ref.at[:, pl.ds(0, HEAD_DIM)]))
        moves.append((v_ref.at[:, at], pair_ref.at[:, pl.ds(HEAD_DIM, HEAD_DIM)]))
    moves += [(vb_ref, vb_own), (qb_ref, qb_own), (q_ref, q_own), (g_ref, g_own)]
    copies = [
        pltpu.make_async_copy(source, target, sems.at[n])
        for n, (source, target) in enumerate(moves)
    ]
    for copy in copies:
        copy.start()
    tok = start_ref.shape[1]
    rank = lax.axis_index("ctx")
    query_pos = rank * tok + lax.broadcasted_iota(jnp.int32, (1, tok), 1)
    start = jnp.zeros((1, tok), jnp.int32)
    end = jnp.int32(0)
    copies[0].wait()
    for doc in range(len_own.shape[1]):
        length = len_own[0, doc]
        end = end + length
        start = start + jnp.where(query_pos >= end, length, 0)
    start_ref[...] = start
    for copy in copies[1:]:
        copy.wait()


def prepare_kernel(
    slots, q_ref, g_ref, qb_ref, vb_ref, start_ref, *refs
):
    tok = q_ref.shape[0]
    kv_heads = vb_ref.shape[0]
    pair_refs = refs[:kv_heads]
    queries_ref, grads_ref, score_ref, dprob_ref, live_ref = refs[kv_heads:]
    rank = lax.axis_index("ctx")
    query_pos = rank * tok + lax.broadcasted_iota(jnp.int32, (1, tok), 1)
    start = start_ref[...]
    offsets = lax.broadcasted_iota(jnp.int32, (tok, tok), 0)
    for slot in range(slots):
        key_pos = (rank - slot) * tok + offsets
        live = (key_pos >= start) & (key_pos <= query_pos)
        live_ref[slot * tok : (slot + 1) * tok, :] = jnp.where(live, 0.0, NEGATIVE)
    column = lax.broadcasted_iota(jnp.int32, (tok, HEAD_DIM), 1)
    for kv_head in range(kv_heads):
        keys = pair_refs[kv_head][:, :HEAD_DIM]
        values = biased(pair_refs[kv_head][:, HEAD_DIM:], vb_ref[kv_head : kv_head + 1, :])
        for head in range(kv_head * GROUP, (kv_head + 1) * GROUP):
            at = slice(head * tok, (head + 1) * tok)
            queries_ref[at, :HEAD_DIM] = biased(q_ref[:, head_cols(head)], qb_ref[head : head + 1, :])
            queries_ref[at, HEAD_DIM:] = (column == head).astype(jnp.bfloat16)
            grads_ref[at, :] = g_ref[:, head_cols(head)]
        rows = slice(kv_head * GROUP * tok, (kv_head + 1) * GROUP * tok)
        score_ref[:, rows] = dot(keys, queries_ref[rows, :HEAD_DIM], 1, 1)
        dprob_ref[:, rows] = dot(values, grads_ref[rows, :], 1, 1)


def outputs_of_head(probs_ref, dscore_ref, keys_ref, values_ref, attn_ref, qg_ref, base):
    tok = attn_ref.shape[0]
    keys_t = keys_ref[...].T
    values_t = values_ref[...].T
    for pair in range(GROUP // PAIR):
        at = slice(pair * PAIR * tok, (pair + 1) * PAIR * tok)
        attn = dot(values_t, probs_ref[:, at], 1, 0).T
        query_grad = (dot(keys_t, dscore_ref[:, at], 1, 0) * SCALE).T
        for n in range(PAIR):
            cols = slice(base + (pair * PAIR + n) * HEAD_DIM, base + (pair * PAIR + n + 1) * HEAD_DIM)
            rows = slice(n * tok, (n + 1) * tok)
            attn_ref[:, cols] = attn[rows].astype(jnp.bfloat16)
            qg_ref[:, cols] = query_grad[rows].astype(jnp.bfloat16)


def attend_kernel(slots, kv_head, last, *refs):
    bias_ref, queries_ref, grads_ref, score_ref, dprob_ref, live_ref = refs[:6]
    pair_refs = refs[6 : 6 + slots][::-1]
    refs = refs[6 + slots :]
    if kv_head:
        filled_refs, refs = refs[: slots + 1], refs[slots + 1 :]
    sums_ref, own_ref = refs[:2]
    out_refs = refs[2 : 2 + slots - 1]
    refs = refs[2 + slots - 1 :]
    keys_ref, values_ref, probs_ref, dscore_ref = refs[:4] if last else refs[2:6]
    weights_ref, all_dprob_ref = refs[-2:]
    tok = pair_refs[0].shape[0]
    kv_heads = bias_ref.shape[0]
    heads = kv_heads * GROUP
    for slot in range(slots):
        rows = slice(slot * tok, (slot + 1) * tok)
        keys_ref[rows, :] = pair_refs[slot][:, :HEAD_DIM]
        values_ref[rows, :] = biased(
            pair_refs[slot][:, HEAD_DIM:], bias_ref[kv_head : kv_head + 1, :]
        )
    blocks = [slice(row, row + BLOCK) for row in range(0, slots * tok, BLOCK)]
    base = kv_head * GROUP * tok
    group = slice(base, base + GROUP * tok)
    weights_ref[tok:, :] = dot(keys_ref[tok:, :], queries_ref[group, :HEAD_DIM], 1, 1)
    all_dprob_ref[tok:, :] = dot(values_ref[tok:, :], grads_ref[group, :], 1, 1)
    for pair in range(GROUP // PAIR):
        at = slice(pair * PAIR * tok, (pair + 1) * PAIR * tok)
        of_all = slice(base + at.start, base + at.stop)
        row_max = None
        for block in blocks:
            own = block.start < tok
            score = score_ref[block, of_all] if own else weights_ref[block, at]
            score = score + jnp.concatenate([live_ref[block, :]] * PAIR, axis=1)
            weights_ref[block, at] = score
            part = jnp.max(score.reshape(-1, 8, PAIR * tok), axis=0)
            row_max = part if row_max is None else jnp.maximum(row_max, part)
        row_max = jnp.max(row_max, axis=0, keepdims=True)
        total = jnp.zeros((8, PAIR * tok), jnp.float32)
        delta = jnp.zeros((8, PAIR * tok), jnp.float32)
        for block in blocks:
            dprob = dprob_ref[block, of_all] if block.start < tok else all_dprob_ref[block, at]
            weights = jnp.exp2((weights_ref[block, at] - row_max) * (SCALE * LOG2E))
            weights_ref[block, at] = weights
            total = total + jnp.sum(weights.reshape(-1, 8, PAIR * tok), axis=0)
            delta = delta + jnp.sum((weights * dprob).reshape(-1, 8, PAIR * tok), axis=0)
        inverse = 1.0 / jnp.sum(total, axis=0, keepdims=True)
        delta = jnp.sum(delta, axis=0, keepdims=True) * inverse
        for block in blocks:
            dprob = dprob_ref[block, of_all] if block.start < tok else all_dprob_ref[block, at]
            probs = weights_ref[block, at] * inverse
            probs_ref[block, at] = probs.astype(jnp.bfloat16)
            dscore_ref[block, at] = (probs * (dprob - delta)).astype(jnp.bfloat16)
    value_term = dot(probs_ref[...], grads_ref[group, :], 1, 0)
    key_term = dot(dscore_ref[...], queries_ref[group, :], 1, 0)
    over_queries = key_term[:, HEAD_DIM:]
    key_term = key_term[:, :HEAD_DIM] * SCALE
    high = over_queries.astype(jnp.bfloat16)
    low = (over_queries - high.astype(jnp.float32)).astype(jnp.bfloat16)
    query_sums = (dot(high, keys_ref[...], 0, 0) + dot(low, keys_ref[...], 0, 0)) * SCALE
    of_group = slice(kv_head * GROUP, (kv_head + 1) * GROUP)
    sums_ref[of_group, :] = query_sums[of_group]
    sums_ref[heads + kv_head : heads + kv_head + 1, :] = jnp.sum(value_term, axis=0, keepdims=True)
    key_cols, value_cols = head_cols(kv_head), head_cols(kv_heads + kv_head)
    own_ref[:, key_cols] = key_term[:tok]
    own_ref[:, value_cols] = value_term[:tok]
    for slot in range(1, slots):
        rows = slice(slot * tok, (slot + 1) * tok)
        out_refs[slot - 1][:, key_cols] = key_term[rows].astype(jnp.bfloat16)
        out_refs[slot - 1][:, value_cols] = value_term[rows].astype(jnp.bfloat16)
    if kv_head:
        filled_sums_ref, *filled_refs = filled_refs
        sums_ref[: of_group.start, :] = filled_sums_ref[: of_group.start, :]
        sums_ref[heads : heads + kv_head, :] = filled_sums_ref[heads : heads + kv_head, :]
        for filled_ref, out_ref in zip(filled_refs, (own_ref, *out_refs)):
            for first in (0, kv_heads):
                cols = slice(first * HEAD_DIM, (first + kv_head) * HEAD_DIM)
                out_ref[:, cols] = filled_ref[:, cols]
    if not last:
        outputs_of_head(probs_ref, dscore_ref, keys_ref, values_ref, refs[0], refs[1], 0)


def attend(slots, kv_head, bias, prepared, pairs, filled):
    queries, _, _, _, live = prepared
    rows, tok = live.shape
    kv_heads = bias.shape[0]
    last = kv_head == kv_heads - 1
    width = GROUP * HEAD_DIM
    scores = (rows, GROUP * tok)
    outs = [
        shape((kv_heads * GROUP + kv_heads, HEAD_DIM), jnp.float32),
        shape((tok, 2 * kv_heads * HEAD_DIM), jnp.float32),
    ] + [shape((tok, 2 * kv_heads * HEAD_DIM), jnp.bfloat16)] * (slots - 1)
    held = [
        (shape((rows, HEAD_DIM), jnp.bfloat16), pltpu.VMEM((rows, HEAD_DIM), jnp.bfloat16)),
        (shape((rows, HEAD_DIM), jnp.bfloat16), pltpu.VMEM((rows, HEAD_DIM), jnp.bfloat16)),
        (shape(scores, jnp.bfloat16), pltpu.VMEM(scores, jnp.bfloat16)),
        (shape(scores, jnp.bfloat16), pltpu.VMEM(scores, jnp.bfloat16)),
    ]
    if last:
        more, scratch = [out for out, _ in held], []
    else:
        more, scratch = [shape((tok, width), jnp.bfloat16)] * 2, [kept for _, kept in held]
    results = pl.pallas_call(
        functools.partial(attend_kernel, slots, kv_head, last),
        out_shape=outs + more,
        in_specs=[VMEM] * (6 + slots + len(filled)),
        out_specs=[VMEM] * (len(outs) + len(more)),
        scratch_shapes=scratch + [pltpu.VMEM(scores, jnp.float32)] * 2,
        compiler_params=params(20 if slots < 8 else 36),
        cost_estimate=pl.CostEstimate(
            flops=8 * rows * tok * width,
            bytes_accessed=4 * rows * GROUP * tok,
            transcendentals=rows * GROUP * tok,
        ),
        name="attend",
    )(bias, *prepared, *pairs, *filled)
    return results[: len(outs)], results[len(outs) :]


def finish_kernel(done, *refs):
    held, before, (attn_ref, qg_ref) = refs[:4], refs[4 : 4 + 2 * done], refs[4 + 2 * done :]
    width = GROUP * HEAD_DIM
    for n in range(done):
        attn_ref[:, n * width : (n + 1) * width] = before[2 * n][...]
        qg_ref[:, n * width : (n + 1) * width] = before[2 * n + 1][...]
    outputs_of_head(*held, attn_ref, qg_ref, done * width)


def collect_kernel(batches, parts, kv_parts, *refs):
    sum_refs, refs = refs[:parts], refs[parts:]
    own_ref, refs = refs[0], refs[1:]
    back_refs, refs = refs[:kv_parts], refs[kv_parts:]
    kg_ref, vg_ref, qb_ref, vb_ref = refs
    heads = qb_ref.shape[0]
    kv_width = kg_ref.shape[1]
    total = sum_refs[0][...]
    for ref in sum_refs[1:]:
        total = total + ref[...]
    total = total * (1.0 / batches)
    qb_ref[...] = total[:heads]
    vb_ref[...] = total[heads:]
    term = own_ref[...]
    for ref in back_refs:
        term = term + ref[...].astype(jnp.float32)
    term = term.astype(jnp.bfloat16)
    kg_ref[...] = term[:, :kv_width]
    vg_ref[...] = term[:, kv_width:]


def total_of(parts):
    return functools.reduce(lambda left, right: left + right, parts)


def exchange(axis, part):
    size = lax.axis_size(axis)
    if axis == "ctx" and not size & (size - 1):
        step = 1
        while 2 * step < size:
            part = part + lax.ppermute(part, axis, [(i, i ^ step) for i in range(size)])
            step *= 2
        return [part, lax.ppermute(part, axis, [(i, i ^ step) for i in range(size)])]
    return [part] + [
        lax.ppermute(part, axis, [(i, (i + shift) % size) for i in range(size)])
        for shift in range(1, size)
    ]


def shards(q_proj, q_bias, k_proj, v_proj, v_bias, dout, lengths):
    _, tok, width = q_proj.shape
    kv_width = k_proj.shape[2]
    heads = width // HEAD_DIM
    kv_heads = kv_width // HEAD_DIM
    ctx = lax.axis_size("ctx")
    batches = lax.axis_size("dp")
    rows = ctx * tok
    columns = heads * tok
    q_own, g_own, qb_own, vb_own, start, *own_pairs = pl.pallas_call(
        pack_kernel,
        out_shape=[
            shape((tok, width), jnp.bfloat16),
            shape((tok, width), jnp.bfloat16),
            shape((heads, HEAD_DIM), jnp.bfloat16),
            shape((kv_heads, HEAD_DIM), jnp.bfloat16),
            shape((1, tok), jnp.int32),
        ]
        + [shape((tok, 2 * HEAD_DIM), jnp.bfloat16)] * kv_heads,
        in_specs=[HBM] * 7,
        out_specs=[VMEM] * (5 + kv_heads),
        scratch_shapes=[
            pltpu.SMEM(lengths.shape, jnp.int32),
            pltpu.SemaphoreType.DMA((5 + 2 * kv_heads,)),
        ],
        compiler_params=params(4),
        cost_estimate=pl.CostEstimate(flops=0, bytes_accessed=8 * tok * width, transcendentals=0),
        name="pack",
    )(
        *[
            pltpu.with_memory_space_constraint(array, pltpu.HBM)
            for array in (
                q_proj[0],
                dout[0],
                k_proj[0],
                v_proj[0],
                q_bias.reshape(heads, HEAD_DIM),
                v_bias.reshape(kv_heads, HEAD_DIM),
                lengths,
            )
        ]
    )
    pairs = [
        [
            lax.ppermute(pair, "ctx", [(i, i + shift) for i in range(ctx - shift)])
            for shift in range(ctx - 1, 0, -1)
        ]
        + [pair]
        for pair in own_pairs
    ]
    prepared = pl.pallas_call(
        functools.partial(prepare_kernel, ctx),
        out_shape=[
            shape((columns, 2 * HEAD_DIM), jnp.bfloat16),
            shape((columns, HEAD_DIM), jnp.bfloat16),
            shape((tok, columns), jnp.float32),
            shape((tok, columns), jnp.float32),
            shape((rows, tok), jnp.float32),
        ],
        in_specs=[VMEM] * (5 + kv_heads),
        out_specs=[VMEM] * 5,
        compiler_params=params(16),
        cost_estimate=pl.CostEstimate(
            flops=4 * tok * tok * width, bytes_accessed=16 * tok * width, transcendentals=0
        ),
        name="prepare",
    )(q_own, g_own, qb_own, vb_own, start, *own_pairs)
    filled, done = [], []
    for kv_head in range(kv_heads):
        filled, made = attend(ctx, kv_head, vb_own, prepared, pairs[kv_head], filled)
        done.append(made)
    sums, own, *terms = filled
    *before, last_made = done
    keys, values, probs, dscore = last_made
    before = [array for made in before for array in made]
    back = [
        lax.ppermute(term, "ctx", [(i, i - shift) for i in range(shift, ctx)])
        for shift, term in enumerate(terms, 1)
    ]
    attn, q_grad = pl.pallas_call(
        functools.partial(finish_kernel, kv_heads - 1),
        out_shape=[shape((tok, width), jnp.bfloat16)] * 2,
        in_specs=[VMEM] * (4 + len(before)),
        out_specs=[VMEM] * 2,
        compiler_params=params(16),
        cost_estimate=pl.CostEstimate(
            flops=4 * rows * tok * GROUP * HEAD_DIM,
            bytes_accessed=4 * tok * width,
            transcendentals=0,
        ),
        name="finish",
    )(probs, dscore, keys, values, *before)
    sums = exchange("ctx", total_of(exchange("dp", sums)))
    k_grad, v_grad, q_sum, v_sum = pl.pallas_call(
        functools.partial(collect_kernel, batches, len(sums), len(back)),
        out_shape=[
            shape((tok, kv_width), jnp.bfloat16),
            shape((tok, kv_width), jnp.bfloat16),
            shape((heads, HEAD_DIM), jnp.float32),
            shape((kv_heads, HEAD_DIM), jnp.float32),
        ],
        in_specs=[VMEM] * (len(sums) + 1 + len(back)),
        out_specs=[VMEM] * 4,
        compiler_params=params(8),
        cost_estimate=pl.CostEstimate(
            flops=8 * tok * kv_width, bytes_accessed=16 * tok * kv_width, transcendentals=0
        ),
        name="collect",
    )(*sums, own, *back)
    return (
        attn[None],
        q_grad[None],
        k_grad[None],
        v_grad[None],
        q_sum.reshape(width),
        v_sum.reshape(kv_width),
    )


def solution(mesh):
    tokens = P("dp", "ctx", "tp")
    return jax.shard_map(
        shards,
        mesh=mesh,
        in_specs=(tokens, P("tp"), tokens, tokens, P("tp"), tokens, P("dp", None)),
        out_specs=(tokens, tokens, tokens, tokens, P("tp"), P("tp")),
        check_vma=False,
    )
```

time: 45.9 us -> 43.6 us (0.950)
  local copies, waits for them, and re-layouts: 4.07 us -> 0 us
  starting transfers between devices: 29.5 us -> 31 us
  waiting for transfers between devices: 1.52 us -> 2.62 us
  other arithmetic: 0.89 us -> 0.01 us
    ppermute x6 -> x3, starting transfers between devices: 14.9 us -> 3.6 us  [exchange(): lax.ppermute(part, axis, [(i, (i + shift) % size) for i in range(size)])]
    ppermute x0 -> x2, starting transfers between devices: none -> 8.89 us  [the longest x1 6.87 us: exchange(): lax.ppermute(part, axis, [(i, i ^ step) for i in range(size)])]
    unnamed x10 -> x0, local copies, waits for them, and re-layouts: 4.07 us -> none
    ppermute x3 -> x6, starting transfers between devices: 10.7 us -> 14.6 us  [shards(): lax.ppermute(pair, 'ctx', [(i, i + shift) for i in range(ctx - shift)])]
    ppermute x0 -> x2, waiting for transfers between devices: none -> 2.51 us  [the longest x1 2.34 us: exchange(): part = part + lax.ppermute(part, axis, [(i, i ^ step) for i in range(size)])]
    ppermute x6 -> x3, waiting for transfers between devices: 1.51 us -> 0.09 us  [exchange(): lax.ppermute(part, axis, [(i, (i + shift) % size) for i in range(size)])]
    concatenate x1 -> x0, other arithmetic: 0.88 us -> none  [shards(): pair = jnp.concatenate([k_proj[0], v_proj[0]], axis=1)]
    pallas_call x2 -> x4, Pallas kernels: 6.89 us -> 7.61 us  [the longest x2 4.71 us: attend(): pl.pallas_call(functools.partial(attend_kernel, slots, kv_head, last), ou...]
  transfers between devices with their start and end apart: 12 -> 14, of which waited for: 2 -> 3; matrix products, arithmetic and copies ran while one was open for 0% -> 0% of each run, Pallas kernels for 6% -> 11%
where the time goes in v8:
time: 43.6 us; the launch traced here: 43.3 us
  starting transfers between devices  31 us (71%)
  Pallas kernels  8.89 us (20%)
  waiting for transfers between devices  2.62 us (6%)
  between operations  0.8 us (2%)
    ppermute x6, starting transfers between devices, shards(): lax.ppermute(pair, 'ctx', [(i, i + shift) for i in range(ctx - shift)])  14.6 us
    ppermute x1, starting transfers between devices, exchange(): lax.ppermute(part, axis, [(i, i ^ step) for i in range(size)])  6.87 us
    pallas_call x2, Pallas kernels, attend(): pl.pallas_call(functools.partial(attend_kernel, slots, kv_head, last), ou...  4.71 us
    ppermute x3, starting transfers between devices, shards(): lax.ppermute(term, 'ctx', [(i, i - shift) for i in range(shift, ctx)])  3.86 us
    ppermute x3, starting transfers between devices, exchange(): lax.ppermute(part, axis, [(i, (i + shift) % size) for i in range(size)])  3.6 us
    ppermute x1, waiting for transfers between devices, exchange(): part = part + lax.ppermute(part, axis, [(i, i ^ step) for i in range(size)])  2.34 us
    ppermute x1, starting transfers between devices, exchange(): part = part + lax.ppermute(part, axis, [(i, i ^ step) for i in range(size)])  2.02 us
    pallas_call x1, Pallas kernels, shards(): pl.pallas_call(functools.partial(finish_kernel, kv_heads - 1), out_shape=...  1.51 us
  transfers between devices with their start and end apart: 14, of which 3 were waited for; matrix products, arithmetic and copies ran while one was open for 0% of the time, Pallas kernels for 11%

profile of v8, /device:TPU:0, one launch (start us, length us, event | category | flops | bytes accessed | tf_op | source)
XLA Modules:
  0.0 43.3 jit_solution(810121552642694933)
XLA Ops:
  0.6 1.4 %pack.1 = (bf16[128,2048]{1,0:T(8,128)(2,1)S(1)}, bf16[128,2048]{1,0:T(8,128)(2,1)S(1)}, bf16[16,128]{1,0:T(8,128)(2,1)S(1)}, bf16[2,128]{1,0:T(2,128)(2,1)S(1)}...) custom-call(bf16[128,2048]{1,0:T(8,128)(2,1)} %bitcast.12, ...), custom_call_target="tpu_custom_call" | custom-call | bytes 2097152 | tf_op jit(solution)/shard_map/pack/pallas_call | solution.py:297
  2.0 4.9 %collective-permute-start.5 = (bf16[128,256]{1,0:T(8,128)(2,1)S(1)}, bf16[128,256]{1,0:T(8,128)(2,1)S(1)}, u32[]{:S(2)}, u32[]{:S(2)}) collective-permute-start(bf16[128,256]{1,0:T(8,128)(2,1)S(1)} %get-tuple-element.45.refs_0_.refs_9_), channel_id=1, source_target_pairs={{0,2},{2,4},{4,6},{1,3},{3,5},{5,7},{8,10},{10,12},{12,14},{9,11},... | collective-permute-start | bytes 196616 | tf_op jit(solution)/shard_map/ppermute | solution.py:332
  7.0 4.5 %collective-permute-start.4 = (bf16[128,256]{1,0:T(8,128)(2,1)S(1)}, bf16[128,256]{1,0:T(8,128)(2,1)S(1)}, u32[]{:S(2)}, u32[]{:S(2)}) collective-permute-start(bf16[128,256]{1,0:T(8,128)(2,1)S(1)} %get-tuple-element.45.refs_0_.refs_9_), channel_id=1, source_target_pairs={{0,4},{2,6},{1,5},{3,7},{8,12},{10,14},{9,13},{11,15},{16,20},{18,... | collective-permute-start | bytes 196616 | tf_op jit(solution)/shard_map/ppermute | solution.py:332
  11.5 1.3 %collective-permute-start.3 = (bf16[128,256]{1,0:T(8,128)(2,1)S(1)}, bf16[128,256]{1,0:T(8,128)(2,1)S(1)}, u32[]{:S(2)}, u32[]{:S(2)}) collective-permute-start(bf16[128,256]{1,0:T(8,128)(2,1)S(1)} %get-tuple-element.45.refs_0_.refs_9_), channel_id=1, source_target_pairs={{0,6},{1,7},{8,14},{9,15},{16,22},{17,23},{24,30},{25,31}} | collective-permute-start | bytes 196616 | tf_op jit(solution)/shard_map/ppermute | solution.py:332
  12.8 1.3 %collective-permute-start.2 = (bf16[128,256]{1,0:T(8,128)(2,1)S(1)}, bf16[128,256]{1,0:T(8,128)(2,1)S(1)}, u32[]{:S(2)}, u32[]{:S(2)}) collective-permute-start(bf16[128,256]{1,0:T(8,128)(2,1)S(1)} %get-tuple-element.46.refs_1_.refs_9_), channel_id=1, source_target_pairs={{0,2},{2,4},{4,6},{1,3},{3,5},{5,7},{8,10},{10,12},{12,14},{9,11},... | collective-permute-start | bytes 196616 | tf_op jit(solution)/shard_map/ppermute | solution.py:332
  14.1 1.3 %collective-permute-start.1 = (bf16[128,256]{1,0:T(8,128)(2,1)S(1)}, bf16[128,256]{1,0:T(8,128)(2,1)S(1)}, u32[]{:S(2)}, u32[]{:S(2)}) collective-permute-start(bf16[128,256]{1,0:T(8,128)(2,1)S(1)} %get-tuple-element.46.refs_1_.refs_9_), channel_id=1, source_target_pairs={{0,4},{2,6},{1,5},{3,7},{8,12},{10,14},{9,13},{11,15},{16,20},{18,... | collective-permute-start | bytes 196616 | tf_op jit(solution)/shard_map/ppermute | solution.py:332
  15.4 0.0 collective-permute-done.5.refs_8_
  15.4 1.3 %collective-permute-start = (bf16[128,256]{1,0:T(8,128)(2,1)S(1)}, bf16[128,256]{1,0:T(8,128)(2,1)S(1)}, u32[]{:S(2)}, u32[]{:S(2)}) collective-permute-start(bf16[128,256]{1,0:T(8,128)(2,1)S(1)} %get-tuple-element.46.refs_1_.refs_9_), channel_id=1, source_target_pairs={{0,6},{1,7},{8,14},{9,15},{16,22},{17,23},{24,30},{25,31}} | collective-permute-start | bytes 196616 | tf_op jit(solution)/shard_map/ppermute | solution.py:332
  16.7 0.6 %prepare.1 = (bf16[2048,256]{1,0:T(8,128)(2,1)S(1)}, bf16[2048,128]{1,0:T(8,128)(2,1)S(1)}, f32[128,2048]{1,0:T(8,128)S(1)}, f32[128,2048]{1,0:T(8,128)S(1)}, f32[512,128]{1,0:T(8,128)S(1)}) custom-call(bf16[128,2048]{1,0:T(8,128)(2,1)S(1)} %get-tuple-element.41.q_ref, bf16[128,2048]{1,0:T(8,128)(2,1)S(1)} %get-tuple-element.42.g_ref, ...), custom_call_target="tpu_custom_call" | custom-call | flops 134217728 | bytes 4194304 | tf_op jit(solution)/shard_map/prepare/pallas_call | solution.py:338
  17.3 0.0 collective-permute-done.4.refs_7_
  17.3 0.0 collective-permute-done.3.refs_6_
  17.3 2.5 %attend.2 = (f32[18,128]{1,0:T(8,128)S(1)}, f32[128,512]{1,0:T(8,128)S(1)}, bf16[128,512]{1,0:T(8,128)(2,1)S(1)}, bf16[128,512]{1,0:T(8,128)(2,1)S(1)}, bf16[128...) custom-call(bf16[2,128]{1,0:T(2,128)(2,1)S(1)} %get-tuple-element.40.vb_ref.refs_0_, ...), custom_call_target="tpu_custom_call" | custom-call | flops 536870912 | bytes 2097152 | tf_op jit(solution)/shard_map/attend/pallas_call | solution.py:223
  19.8 0.0 collective-permute-done.2.refs_8_
  19.8 0.0 collective-permute-done.1.refs_7_
  19.8 0.0 collective-permute-done.refs_6_
  19.8 2.2 %attend.3 = (f32[18,128]{1,0:T(8,128)S(1)}, f32[128,512]{1,0:T(8,128)S(1)}, bf16[128,512]{1,0:T(8,128)(2,1)S(1)}, bf16[128,512]{1,0:T(8,128)(2,1)S(1)}, bf16[128...) custom-call(bf16[2,128]{1,0:T(2,128)(2,1)S(1)} %get-tuple-element.40, ...), custom_call_target="tpu_custom_call" | custom-call | flops 536870912 | bytes 2097152 | tf_op jit(solution)/shard_map/attend/pallas_call | solution.py:223
  22.1 2.5 %collective-permute-start.8 = (f32[18,128]{1,0:T(8,128)S(1)}, f32[18,128]{1,0:T(8,128)S(1)}, u32[]{:S(2)}, u32[]{:S(2)}) collective-permute-start(f32[18,128]{1,0:T(8,128)S(1)} %get-tuple-element.65), channel_id=1, source_target_pairs={{0,24},{8,0},{16,8},{24,16},{1,25},{9,1},{17,9},{25,17},{2,26},{10... | collective-permute-start | bytes 27656 | tf_op jit(solution)/shard_map/ppermute | solution.py:283
  24.6 0.5 %collective-permute-start.7 = (f32[18,128]{1,0:T(8,128)S(1)}, f32[18,128]{1,0:T(8,128)S(1)}, u32[]{:S(2)}, u32[]{:S(2)}) collective-permute-start(f32[18,128]{1,0:T(8,128)S(1)} %get-tuple-element.65), channel_id=1, source_target_pairs={{0,16},{8,24},{16,0},{24,8},{1,17},{9,25},{17,1},{25,9},{2,18},{10... | collective-permute-start | bytes 27656 | tf_op jit(solution)/shard_map/ppermute | solution.py:283
  25.1 0.6 %collective-permute-start.6 = (f32[18,128]{1,0:T(8,128)S(1)}, f32[18,128]{1,0:T(8,128)S(1)}, u32[]{:S(2)}, u32[]{:S(2)}) collective-permute-start(f32[18,128]{1,0:T(8,128)S(1)} %get-tuple-element.65), channel_id=1, source_target_pairs={{0,8},{8,16},{16,24},{24,0},{1,9},{9,17},{17,25},{25,1},{2,10},{10... | collective-permute-start | bytes 27656 | tf_op jit(solution)/shard_map/ppermute | solution.py:283
  25.7 1.3 %collective-permute-start.11 = (bf16[128,512]{1,0:T(8,128)(2,1)S(1)}, bf16[128,512]{1,0:T(8,128)(2,1)S(1)}, u32[]{:S(2)}, u32[]{:S(2)}) collective-permute-start(bf16[128,512]{1,0:T(8,128)(2,1)S(1)} %get-tuple-element.67), channel_id=1, source_target_pairs={{2,0},{4,2},{6,4},{3,1},{5,3},{7,5},{10,8},{12,10},{14,12},{11,9},... | collective-permute-start | bytes 393224 | tf_op jit(solution)/shard_map/ppermute | solution.py:364
  26.9 1.3 %collective-permute-start.12 = (bf16[128,512]{1,0:T(8,128)(2,1)S(1)}, bf16[128,512]{1,0:T(8,128)(2,1)S(1)}, u32[]{:S(2)}, u32[]{:S(2)}) collective-permute-start(bf16[128,512]{1,0:T(8,128)(2,1)S(1)} %get-tuple-element.68), channel_id=1, source_target_pairs={{4,0},{6,2},{5,1},{7,3},{12,8},{14,10},{13,9},{15,11},{20,16},{22,... | collective-permute-start | bytes 393224 | tf_op jit(solution)/shard_map/ppermute | solution.py:364
  28.2 0.0 collective-permute-done.8
  28.3 1.3 %collective-permute-start.13 = (bf16[128,512]{1,0:T(8,128)(2,1)S(1)}, bf16[128,512]{1,0:T(8,128)(2,1)S(1)}, u32[]{:S(2)}, u32[]{:S(2)}) collective-permute-start(bf16[128,512]{1,0:T(8,128)(2,1)S(1)} %get-tuple-element.69), channel_id=1, source_target_pairs={{6,0},{7,1},{14,8},{15,9},{22,16},{23,17},{30,24},{31,25}} | collective-permute-start | bytes 393224 | tf_op jit(solution)/shard_map/ppermute | solution.py:364
  29.6 0.0 collective-permute-done.7
  29.6 0.1 collective-permute-done.6
  29.7 2.0 %collective-permute-start.9 = (f32[18,128]{1,0:T(8,128)S(1)}, f32[18,128]{1,0:T(8,128)S(1)}, u32[]{:S(2)}, u32[]{:S(2)}) collective-permute-start(f32[18,128]{1,0:T(8,128)S(1)} %add_add_fusion), channel_id=1, source_target_pairs={{0,2},{2,0},{4,6},{6,4},{1,3},{3,1},{5,7},{7,5},{8,10},{10,8},{12,... | collective-permute-start | bytes 27656 | tf_op jit(solution)/shard_map/ppermute | solution.py:279
  31.7 2.3 %collective-permute-done.9 = f32[18,128]{1,0:T(8,128)S(1)} collective-permute-done((f32[18,128]{1,0:T(8,128)S(1)}, f32[18,128]{1,0:T(8,128)S(1)}, u32[]{:S(2)}, u32[]{:S(2)}) %collective-permute-start.9) | collective-permute-done | bytes 9248 | tf_op jit(solution)/shard_map/ppermute | solution.py:279
  34.0 6.9 %collective-permute-start.10 = (f32[18,128]{1,0:T(8,128)S(1)}, f32[18,128]{1,0:T(8,128)S(1)}, u32[]{:S(2)}, u32[]{:S(2)}) collective-permute-start(f32[18,128]{1,0:T(8,128)S(1)} %add.15.refs_0_), channel_id=1, source_target_pairs={{0,4},{2,6},{4,0},{6,2},{1,5},{3,7},{5,1},{7,3},{8,12},{10,14},{12... | collective-permute-start | bytes 27656 | tf_op jit(solution)/shard_map/ppermute | solution.py:281
  40.9 1.5 %finish.1 = (bf16[128,2048]{1,0:T(8,128)(2,1)}, bf16[128,2048]{1,0:T(8,128)(2,1)}) custom-call(bf16[512,1024]{1,0:T(8,128)(2,1)S(1)} %get-tuple-element.57.refs_0_, bf16[512,1024]{1,0:T(8,128)(2,1)S(1)} %get-tuple-element.58.refs_1_, bf16[512,128]{1,0:T(8,128)(2,1)S(1)} %get-tuple-element.59.refs_2_, bf16[512,128]{1,0:T(8,128)(2,1)S(1)} %get-tuple-element.60.refs_3_, ...), custom_call_target="tpu_custom_call" | custom-call | flops 268435456 | bytes 1048576 | tf_op jit(solution)/shard_map/finish/pallas_call | solution.py:367
  42.4 0.2 collective-permute-done.10.refs_1_
  42.6 0.0 collective-permute-done.11.refs_3_
  42.6 0.0 collective-permute-done.12.refs_4_
  42.6 0.0 collective-permute-done.13.refs_5_
  42.6 0.7 %collect.1 = (bf16[128,256]{1,0:T(8,128)(2,1)}, bf16[128,256]{1,0:T(8,128)(2,1)}, f32[16,128]{1,0:T(8,128)}, f32[2,128]{1,0:T(2,128)}) custom-call(f32[18,128]{1,0:T(8,128)S(1)} %add.15.refs_0_, f32[18,128]{1,0:T(8,128)S(1)} %collective-permute-done.10.refs_1_, f32[128,512]{1,0:T(8,128)S(1)} %get-tuple-element.66.refs_2_, ...), custom_call_target="tpu_custom_call" | custom-call | flops 262144 | bytes 524288 | tf_op jit(solution)/shard_map/collect/pallas_call | solution.py:381
  (2 shorter events, 0.0 us)
Async XLA Ops:
  2.0 13.3 %collective-permute-start.5 = (bf16[128,256]{1,0:T(8,128)(2,1)S(1)}, bf16[128,256]{1,0:T(8,128)(2,1)S(1)}, u32[]{:S(2)}, u32[]{:S(2)}) collective-permute-start(bf16[128,256]{1,0:T(8,128)(2,1)S(1)} %get-tuple-element.45.refs_0_.refs_9_), channel_id=1, source_target_pairs={{0,2},{2,4},{4,6},{1,3},{3,5},{5,7},{8,10},{10,12},{12,14},{9,11},... | collective-permute-start | bytes 196616 | tf_op jit(solution)/shard_map/ppermute | solution.py:332
  7.0 10.3 %collective-permute-start.4 = (bf16[128,256]{1,0:T(8,128)(2,1)S(1)}, bf16[128,256]{1,0:T(8,128)(2,1)S(1)}, u32[]{:S(2)}, u32[]{:S(2)}) collective-permute-start(bf16[128,256]{1,0:T(8,128)(2,1)S(1)} %get-tuple-element.45.refs_0_.refs_9_), channel_id=1, source_target_pairs={{0,4},{2,6},{1,5},{3,7},{8,12},{10,14},{9,13},{11,15},{16,20},{18,... | collective-permute-start | bytes 196616 | tf_op jit(solution)/shard_map/ppermute | solution.py:332
  11.5 5.8 %collective-permute-start.3 = (bf16[128,256]{1,0:T(8,128)(2,1)S(1)}, bf16[128,256]{1,0:T(8,128)(2,1)S(1)}, u32[]{:S(2)}, u32[]{:S(2)}) collective-permute-start(bf16[128,256]{1,0:T(8,128)(2,1)S(1)} %get-tuple-element.45.refs_0_.refs_9_), channel_id=1, source_target_pairs={{0,6},{1,7},{8,14},{9,15},{16,22},{17,23},{24,30},{25,31}} | collective-permute-start | bytes 196616 | tf_op jit(solution)/shard_map/ppermute | solution.py:332
  12.8 7.0 %collective-permute-start.2 = (bf16[128,256]{1,0:T(8,128)(2,1)S(1)}, bf16[128,256]{1,0:T(8,128)(2,1)S(1)}, u32[]{:S(2)}, u32[]{:S(2)}) collective-permute-start(bf16[128,256]{1,0:T(8,128)(2,1)S(1)} %get-tuple-element.46.refs_1_.refs_9_), channel_id=1, source_target_pairs={{0,2},{2,4},{4,6},{1,3},{3,5},{5,7},{8,10},{10,12},{12,14},{9,11},... | collective-permute-start | bytes 196616 | tf_op jit(solution)/shard_map/ppermute | solution.py:332
  14.1 5.7 %collective-permute-start.1 = (bf16[128,256]{1,0:T(8,128)(2,1)S(1)}, bf16[128,256]{1,0:T(8,128)(2,1)S(1)}, u32[]{:S(2)}, u32[]{:S(2)}) collective-permute-start(bf16[128,256]{1,0:T(8,128)(2,1)S(1)} %get-tuple-element.46.refs_1_.refs_9_), channel_id=1, source_target_pairs={{0,4},{2,6},{1,5},{3,7},{8,12},{10,14},{9,13},{11,15},{16,20},{18,... | collective-permute-start | bytes 196616 | tf_op jit(solution)/shard_map/ppermute | solution.py:332
  15.4 4.4 %collective-permute-start = (bf16[128,256]{1,0:T(8,128)(2,1)S(1)}, bf16[128,256]{1,0:T(8,128)(2,1)S(1)}, u32[]{:S(2)}, u32[]{:S(2)}) collective-permute-start(bf16[128,256]{1,0:T(8,128)(2,1)S(1)} %get-tuple-element.46.refs_1_.refs_9_), channel_id=1, source_target_pairs={{0,6},{1,7},{8,14},{9,15},{16,22},{17,23},{24,30},{25,31}} | collective-permute-start | bytes 196616 | tf_op jit(solution)/shard_map/ppermute | solution.py:332
  22.1 6.2 %collective-permute-start.8 = (f32[18,128]{1,0:T(8,128)S(1)}, f32[18,128]{1,0:T(8,128)S(1)}, u32[]{:S(2)}, u32[]{:S(2)}) collective-permute-start(f32[18,128]{1,0:T(8,128)S(1)} %get-tuple-element.65), channel_id=1, source_target_pairs={{0,24},{8,0},{16,8},{24,16},{1,25},{9,1},{17,9},{25,17},{2,26},{10... | collective-permute-start | bytes 27656 | tf_op jit(solution)/shard_map/ppermute | solution.py:283
  24.6 5.0 %collective-permute-start.7 = (f32[18,128]{1,0:T(8,128)S(1)}, f32[18,128]{1,0:T(8,128)S(1)}, u32[]{:S(2)}, u32[]{:S(2)}) collective-permute-start(f32[18,128]{1,0:T(8,128)S(1)} %get-tuple-element.65), channel_id=1, source_target_pairs={{0,16},{8,24},{16,0},{24,8},{1,17},{9,25},{17,1},{25,9},{2,18},{10... | collective-permute-start | bytes 27656 | tf_op jit(solution)/shard_map/ppermute | solution.py:283
  25.1 4.6 %collective-permute-start.6 = (f32[18,128]{1,0:T(8,128)S(1)}, f32[18,128]{1,0:T(8,128)S(1)}, u32[]{:S(2)}, u32[]{:S(2)}) collective-permute-start(f32[18,128]{1,0:T(8,128)S(1)} %get-tuple-element.65), channel_id=1, source_target_pairs={{0,8},{8,16},{16,24},{24,0},{1,9},{9,17},{17,25},{25,1},{2,10},{10... | collective-permute-start | bytes 27656 | tf_op jit(solution)/shard_map/ppermute | solution.py:283
  25.7 16.9 %collective-permute-start.11 = (bf16[128,512]{1,0:T(8,128)(2,1)S(1)}, bf16[128,512]{1,0:T(8,128)(2,1)S(1)}, u32[]{:S(2)}, u32[]{:S(2)}) collective-permute-start(bf16[128,512]{1,0:T(8,128)(2,1)S(1)} %get-tuple-element.67), channel_id=1, source_target_pairs={{2,0},{4,2},{6,4},{3,1},{5,3},{7,5},{10,8},{12,10},{14,12},{11,9},... | collective-permute-start | bytes 393224 | tf_op jit(solution)/shard_map/ppermute | solution.py:364
  26.9 15.6 %collective-permute-start.12 = (bf16[128,512]{1,0:T(8,128)(2,1)S(1)}, bf16[128,512]{1,0:T(8,128)(2,1)S(1)}, u32[]{:S(2)}, u32[]{:S(2)}) collective-permute-start(bf16[128,512]{1,0:T(8,128)(2,1)S(1)} %get-tuple-element.68), channel_id=1, source_target_pairs={{4,0},{6,2},{5,1},{7,3},{12,8},{14,10},{13,9},{15,11},{20,16},{22,... | collective-permute-start | bytes 393224 | tf_op jit(solution)/shard_map/ppermute | solution.py:364
  28.3 14.3 %collective-permute-start.13 = (bf16[128,512]{1,0:T(8,128)(2,1)S(1)}, bf16[128,512]{1,0:T(8,128)(2,1)S(1)}, u32[]{:S(2)}, u32[]{:S(2)}) collective-permute-start(bf16[128,512]{1,0:T(8,128)(2,1)S(1)} %get-tuple-element.69), channel_id=1, source_target_pairs={{6,0},{7,1},{14,8},{15,9},{22,16},{23,17},{30,24},{31,25}} | collective-permute-start | bytes 393224 | tf_op jit(solution)/shard_map/ppermute | solution.py:364
  29.7 4.4 %collective-permute-start.9 = (f32[18,128]{1,0:T(8,128)S(1)}, f32[18,128]{1,0:T(8,128)S(1)}, u32[]{:S(2)}, u32[]{:S(2)}) collective-permute-start(f32[18,128]{1,0:T(8,128)S(1)} %add_add_fusion), channel_id=1, source_target_pairs={{0,2},{2,0},{4,6},{6,4},{1,3},{3,1},{5,7},{7,5},{8,10},{10,8},{12,... | collective-permute-start | bytes 27656 | tf_op jit(solution)/shard_map/ppermute | solution.py:279
  34.0 8.5 %collective-permute-start.10 = (f32[18,128]{1,0:T(8,128)S(1)}, f32[18,128]{1,0:T(8,128)S(1)}, u32[]{:S(2)}, u32[]{:S(2)}) collective-permute-start(f32[18,128]{1,0:T(8,128)S(1)} %add.15.refs_0_), channel_id=1, source_target_pairs={{0,4},{2,6},{4,0},{6,2},{1,5},{3,7},{5,1},{7,3},{8,12},{10,14},{12... | collective-permute-start | bytes 27656 | tf_op jit(solution)/shard_map/ppermute | solution.py:281

commit v9 on v7

--- a/solution.py
+++ b/solution.py
@@ -232,7 +232,7 @@
     columns = heads * tok
     pair = jnp.concatenate([k_proj[0], v_proj[0]], axis=1)
     pairs = [
-        lax.ppermute(pair, "ctx", [(i, i + shift) for i in range(ctx - shift)])
+        lax.ppermute(pair, "ctx", [(i, (i + shift) % ctx) for i in range(ctx)])
         for shift in range(ctx - 1, 0, -1)
     ] + [pair]
     prepared = pl.pallas_call(
@@ -287,7 +287,7 @@
         name="attend",
     )(*prepared, *pairs)
     back = [
-        lax.ppermute(term, "ctx", [(i, i - shift) for i in range(shift, ctx)])
+        lax.ppermute(term, "ctx", [(i, (i - shift) % ctx) for i in range(ctx)])
         for shift, term in enumerate(terms, 1)
     ]
     attn, q_grad = pl.pallas_call(

time: 46.7 us -> 44.8 us (0.959)
  starting transfers between devices: 26.2 us -> 21.7 us
  waiting for transfers between devices: 6.59 us -> 9.26 us
    ppermute x6, starting transfers between devices: 14.6 us -> 12 us  [the longest x3 7.01 us: shards(): lax.ppermute(pair, 'ctx', [(i, (i + shift) % ctx) for i in range(ctx)])]
    ppermute x6, waiting for transfers between devices: 0.02 us -> 2.09 us  [the longest x3 2.08 us: shards(): lax.ppermute(pair, 'ctx', [(i, (i + shift) % ctx) for i in range(ctx)])]
    ppermute x6, starting transfers between devices: 11.6 us -> 9.67 us  [exchange(): lax.ppermute(part, axis, [(i, (i + shift) % size) for i in range(size)])]
    ppermute x6, waiting for transfers between devices: 6.58 us -> 7.17 us  [exchange(): lax.ppermute(part, axis, [(i, (i + shift) % size) for i in range(size)])]
  transfers between devices with their start and end apart: 12 -> 12, of which waited for: 5 -> 6; matrix products, arithmetic and copies ran while one was open for 0% -> 0% of each run, Pallas kernels for 6% -> 7%
where the time goes in v9:
time: 44.8 us; the launch traced here: 44.5 us
  starting transfers between devices  21.7 us (48%)
  waiting for transfers between devices  9.26 us (21%)
  Pallas kernels  7.85 us (18%)
  local copies, waits for them, and re-layouts  4.08 us (9%)
  other arithmetic  0.88 us (2%)
  between operations  0.68 us (2%)
    ppermute x6, starting transfers between devices, exchange(): lax.ppermute(part, axis, [(i, (i + shift) % size) for i in range(size)])  9.67 us
    ppermute x6, waiting for transfers between devices, exchange(): lax.ppermute(part, axis, [(i, (i + shift) % size) for i in range(size)])  7.17 us
    ppermute x3, starting transfers between devices, shards(): lax.ppermute(pair, 'ctx', [(i, (i + shift) % ctx) for i in range(ctx)])  7.01 us
    ppermute x3, starting transfers between devices, shards(): lax.ppermute(term, 'ctx', [(i, (i - shift) % ctx) for i in range(ctx)])  5.03 us
    pallas_call x1, Pallas kernels, shards(): pl.pallas_call(functools.partial(attend_kernel, ctx), out_shape=[shape((r...  4.25 us
    unnamed x10, local copies, waits for them, and re-layouts  4.08 us
    ppermute x3, waiting for transfers between devices, shards(): lax.ppermute(pair, 'ctx', [(i, (i + shift) % ctx) for i in range(ctx)])  2.08 us
    pallas_call x1, Pallas kernels, shards(): pl.pallas_call(finish_kernel, out_shape=[shape((tok, width), jnp.bfloat16...  1.79 us
  transfers between devices with their start and end apart: 12, of which 6 were waited for; matrix products, arithmetic and copies ran while one was open for 0% of the time, Pallas kernels for 7%

profile of v9, /device:TPU:0, one launch (start us, length us, event | category | flops | bytes accessed | tf_op | source)
XLA Modules:
  0.0 44.5 jit_solution(11630832333712300348)
XLA Ops:
  0.6 0.9 %pad_maximum_fusion.pair_ref.refs_9_ = bf16[128,512]{1,0:T(8,128)(2,1)S(1)} fusion(bf16[128,256]{1,0:T(8,128)(2,1)} %bitcast.16, bf16[128,256]{1,0:T(8,128)(2,1)} %bitcast.17), kind=kLoop, calls=%fused_computation | loop fusion | flops 262144 | bytes 262144 | tf_op jit(solution)/shard_map/concatenate | solution.py:233
  1.5 3.1 %collective-permute-start.2 = (bf16[128,512]{1,0:T(8,128)(2,1)S(1)}, bf16[128,512]{1,0:T(8,128)(2,1)S(1)}, u32[]{:S(2)}, u32[]{:S(2)}) collective-permute-start(bf16[128,512]{1,0:T(8,128)(2,1)S(1)} %pad_maximum_fusion.pair_ref.refs_9_), channel_id=1, source_target_pairs={{0,2},{2,4},{4,6},{6,0},{1,3},{3,5},{5,7},{7,1},{8,10},{10,12},{12... | collective-permute-start | bytes 393224 | tf_op jit(solution)/shard_map/ppermute | solution.py:235
  4.6 2.6 %collective-permute-start.1 = (bf16[128,512]{1,0:T(8,128)(2,1)S(1)}, bf16[128,512]{1,0:T(8,128)(2,1)S(1)}, u32[]{:S(2)}, u32[]{:S(2)}) collective-permute-start(bf16[128,512]{1,0:T(8,128)(2,1)S(1)} %pad_maximum_fusion.pair_ref.refs_9_), channel_id=1, source_target_pairs={{0,4},{2,6},{4,0},{6,2},{1,5},{3,7},{5,1},{7,3},{8,12},{10,14},{12... | collective-permute-start | bytes 393224 | tf_op jit(solution)/shard_map/ppermute | solution.py:235
  7.2 1.3 %collective-permute-start = (bf16[128,512]{1,0:T(8,128)(2,1)S(1)}, bf16[128,512]{1,0:T(8,128)(2,1)S(1)}, u32[]{:S(2)}, u32[]{:S(2)}) collective-permute-start(bf16[128,512]{1,0:T(8,128)(2,1)S(1)} %pad_maximum_fusion.pair_ref.refs_9_), channel_id=1, source_target_pairs={{0,6},{2,0},{4,2},{6,4},{1,7},{3,1},{5,3},{7,5},{8,14},{10,8},{12,... | collective-permute-start | bytes 393224 | tf_op jit(solution)/shard_map/ppermute | solution.py:235
  8.5 0.0 copy-start
  8.5 1.0 %copy-done = bf16[1,128,2048]{2,1,0:T(8,128)(2,1)S(1)} copy-done((bf16[1,128,2048]{2,1,0:T(8,128)(2,1)S(1)}, bf16[1,128,2048]{2,1,0:T(8,128)(2,1)}, u32[]{:S(2)}) %copy-start) | copy-done | bytes 524312
  9.6 0.0 copy-start.1
  9.6 1.0 %copy-done.1 = bf16[1,128,2048]{2,1,0:T(8,128)(2,1)S(1)} copy-done((bf16[1,128,2048]{2,1,0:T(8,128)(2,1)S(1)}, bf16[1,128,2048]{2,1,0:T(8,128)(2,1)}, u32[]{:S(2)}) %copy-start.1) | copy-done | bytes 524312
  10.6 0.0 copy-start.2
  10.6 0.7 %copy-done.2 = bf16[2048]{0:T(1024)(128)(2,1)S(1)} copy-done((bf16[2048]{0:T(1024)(128)(2,1)S(1)}, bf16[2048]{0:T(1024)(128)(2,1)}, u32[]{:S(2)}) %copy-start.2) | copy-done | bytes 4120
  11.3 0.0 copy-start.3
  11.3 0.7 %copy-done.3 = s32[1,8]{1,0:T(1,128)S(1)} copy-done((s32[1,8]{1,0:T(1,128)S(1)}, s32[1,8]{1,0:T(1,128)}, u32[]{:S(2)}) %copy-start.3) | copy-done | bytes 56
  12.0 0.0 copy-start.4
  12.0 0.7 %copy-done.4 = bf16[256]{0:T(256)(128)(2,1)S(1)} copy-done((bf16[256]{0:T(256)(128)(2,1)S(1)}, bf16[256]{0:T(256)(128)(2,1)}, u32[]{:S(2)}) %copy-start.4) | copy-done | bytes 536
  12.6 1.1 %prepare.1 = (bf16[2,128]{1,0:T(2,128)(2,1)S(1)}, bf16[2048,256]{1,0:T(8,128)(2,1)S(1)}, bf16[2048,128]{1,0:T(8,128)(2,1)S(1)}, f32[128,2048]{1,0:T(8,128)S(1)},...) custom-call(s32[1,8]{1,0:T(1,128)S(1)} %copy-done.3, bf16[128,512]{1,0:T(8,128)(2,1)S(1)} %pad_maximum_fusion.pair_ref.refs_9_, ...), custom_call_target="tpu_custom_call" | custom-call | flops 134217728 | bytes 4194304 | tf_op jit(solution)/shard_map/prepare/pallas_call | solution.py:238
  13.7 0.0 collective-permute-done.2.refs_8_
  13.7 2.1 %collective-permute-done.1.refs_7_ = bf16[128,512]{1,0:T(8,128)(2,1)S(1)} collective-permute-done((bf16[128,512]{1,0:T(8,128)(2,1)S(1)}, bf16[128,512]{1,0:T(8,128)(2,1)S(1)}, u32[]{:S(2)}, u32[]{:S(2)}) %collective-permute-start.1) | collective-permute-done | bytes 131104 | tf_op jit(solution)/shard_map/ppermute | solution.py:235
  15.8 0.0 collective-permute-done.refs_6_
  15.8 4.2 %attend.1 = (bf16[512,2048]{1,0:T(8,128)(2,1)S(1)}, bf16[512,2048]{1,0:T(8,128)(2,1)S(1)}, bf16[512,256]{1,0:T(8,128)(2,1)S(1)}, bf16[512,256]{1,0:T(8,128)(2,1)...) custom-call(bf16[2,128]{1,0:T(2,128)(2,1)S(1)} %get-tuple-element.29, ...), custom_call_target="tpu_custom_call" | custom-call | flops 1073741824 | bytes 4194304 | tf_op jit(solution)/shard_map/attend/pallas_call | solution.py:264
  20.1 4.4 %collective-permute-start.6 = (bf16[128,512]{1,0:T(8,128)(2,1)S(1)}, bf16[128,512]{1,0:T(8,128)(2,1)S(1)}, u32[]{:S(2)}, u32[]{:S(2)}) collective-permute-start(bf16[128,512]{1,0:T(8,128)(2,1)S(1)} %get-tuple-element.42), channel_id=1, source_target_pairs={{0,6},{2,0},{4,2},{6,4},{1,7},{3,1},{5,3},{7,5},{8,14},{10,8},{12,... | collective-permute-start | bytes 393224 | tf_op jit(solution)/shard_map/ppermute | solution.py:290
  24.5 0.4 collective-permute-start.10
  24.9 0.2 collective-permute-start.11
  25.1 2.4 %collective-permute-start.5 = (f32[18,128]{1,0:T(8,128)S(1)}, f32[18,128]{1,0:T(8,128)S(1)}, u32[]{:S(2)}, u32[]{:S(2)}) collective-permute-start(f32[18,128]{1,0:T(8,128)S(1)} %get-tuple-element.41.refs_0_), channel_id=1, source_target_pairs={{0,24},{8,0},{16,8},{24,16},{1,25},{9,1},{17,9},{25,17},{2,26},{10... | collective-permute-start | bytes 27656 | tf_op jit(solution)/shard_map/ppermute | solution.py:219
  27.6 0.5 %collective-permute-start.4 = (f32[18,128]{1,0:T(8,128)S(1)}, f32[18,128]{1,0:T(8,128)S(1)}, u32[]{:S(2)}, u32[]{:S(2)}) collective-permute-start(f32[18,128]{1,0:T(8,128)S(1)} %get-tuple-element.41.refs_0_), channel_id=1, source_target_pairs={{0,16},{8,24},{16,0},{24,8},{1,17},{9,25},{17,1},{25,9},{2,18},{10... | collective-permute-start | bytes 27656 | tf_op jit(solution)/shard_map/ppermute | solution.py:219
  28.1 0.9 %collective-permute-done.5.refs_3_ = f32[18,128]{1,0:T(8,128)S(1)} collective-permute-done((f32[18,128]{1,0:T(8,128)S(1)}, f32[18,128]{1,0:T(8,128)S(1)}, u32[]{:S(2)}, u32[]{:S(2)}) %collective-permute-start.5) | collective-permute-done | bytes 9248 | tf_op jit(solution)/shard_map/ppermute | solution.py:219
  29.0 2.2 %collective-permute-start.3 = (f32[18,128]{1,0:T(8,128)S(1)}, f32[18,128]{1,0:T(8,128)S(1)}, u32[]{:S(2)}, u32[]{:S(2)}) collective-permute-start(f32[18,128]{1,0:T(8,128)S(1)} %get-tuple-element.41.refs_0_), channel_id=1, source_target_pairs={{0,8},{8,16},{16,24},{24,0},{1,9},{9,17},{17,25},{25,1},{2,10},{10... | collective-permute-start | bytes 27656 | tf_op jit(solution)/shard_map/ppermute | solution.py:219
  31.2 0.1 collective-permute-done.4.refs_2_
  31.3 2.5 %collective-permute-done.3.refs_1_ = f32[18,128]{1,0:T(8,128)S(1)} collective-permute-done((f32[18,128]{1,0:T(8,128)S(1)}, f32[18,128]{1,0:T(8,128)S(1)}, u32[]{:S(2)}, u32[]{:S(2)}) %collective-permute-start.3) | collective-permute-done | bytes 9248 | tf_op jit(solution)/shard_map/ppermute | solution.py:219
  33.8 0.0 collective-permute-done.6.refs_4_
  33.8 3.6 %collective-permute-start.9 = (f32[18,128]{1,0:T(8,128)S(1)}, f32[18,128]{1,0:T(8,128)S(1)}, u32[]{:S(2)}, u32[]{:S(2)}) collective-permute-start(f32[18,128]{1,0:T(8,128)S(1)} %get-tuple-element.43.refs_0_), channel_id=1, source_target_pairs={{0,6},{2,0},{4,2},{6,4},{1,7},{3,1},{5,3},{7,5},{8,14},{10,8},{12,... | collective-permute-start | bytes 27656 | tf_op jit(solution)/shard_map/ppermute | solution.py:219
  37.5 0.8 %collective-permute-start.8 = (f32[18,128]{1,0:T(8,128)S(1)}, f32[18,128]{1,0:T(8,128)S(1)}, u32[]{:S(2)}, u32[]{:S(2)}) collective-permute-start(f32[18,128]{1,0:T(8,128)S(1)} %get-tuple-element.43.refs_0_), channel_id=1, source_target_pairs={{0,4},{2,6},{4,0},{6,2},{1,5},{3,7},{5,1},{7,3},{8,12},{10,14},{12... | collective-permute-start | bytes 27656 | tf_op jit(solution)/shard_map/ppermute | solution.py:219
  38.3 0.0 collective-permute-start.7
  38.3 1.8 %finish.1 = (bf16[128,2048]{1,0:T(8,128)(2,1)}, bf16[128,2048]{1,0:T(8,128)(2,1)}) custom-call(bf16[512,2048]{1,0:T(8,128)(2,1)S(1)} %get-tuple-element.35.probs_ref, bf16[512,2048]{1,0:T(8,128)(2,1)S(1)} %get-tuple-element.36.dscore_ref, bf16[512,256]{1,0:T(8,128)(2,1)S(1)} %get-tuple-element.37.keys_ref, bf16[512,256]{1,0:T(8,128)(2,1)S(1)} %get-tuple-element.38.values_ref), custom_call_target="tpu_custom_call" | custom-call | flops 536870912 | bytes 4194304 | tf_op jit(solution)/shard_map/finish/pallas_call | solution.py:293
  40.1 0.0 collective-permute-done.10.refs_6_
  40.1 0.0 collective-permute-done.11.refs_7_
  40.1 0.0 collective-permute-done.9.refs_3_
  40.1 1.9 %collective-permute-done.8.refs_2_ = f32[18,128]{1,0:T(8,128)S(1)} collective-permute-done((f32[18,128]{1,0:T(8,128)S(1)}, f32[18,128]{1,0:T(8,128)S(1)}, u32[]{:S(2)}, u32[]{:S(2)}) %collective-permute-start.8) | collective-permute-done | bytes 9248 | tf_op jit(solution)/shard_map/ppermute | solution.py:219
  42.1 1.7 %collective-permute-done.7.refs_1_ = f32[18,128]{1,0:T(8,128)S(1)} collective-permute-done((f32[18,128]{1,0:T(8,128)S(1)}, f32[18,128]{1,0:T(8,128)S(1)}, u32[]{:S(2)}, u32[]{:S(2)}) %collective-permute-start.7) | collective-permute-done | bytes 9248 | tf_op jit(solution)/shard_map/ppermute | solution.py:219
  43.8 0.7 %collect.1 = (bf16[128,256]{1,0:T(8,128)(2,1)}, bf16[128,256]{1,0:T(8,128)(2,1)}, f32[16,128]{1,0:T(8,128)}, f32[2,128]{1,0:T(2,128)}) custom-call(f32[18,128]{1,0:T(8,128)S(1)} %get-tuple-element.43.refs_0_, f32[18,128]{1,0:T(8,128)S(1)} %collective-permute-done.7.refs_1_, f32[18,128]{1,0:T(8,128)S(1)} %collective-permute-done.8.refs_2_, ...), custom_call_target="tpu_custom_call" | custom-call | flops 262144 | bytes 524288 | tf_op jit(solution)/shard_map/collect/pallas_call | solution.py:309
  (1 shorter events, 0.0 us)
Async XLA Ops:
  1.5 12.2 %collective-permute-start.2 = (bf16[128,512]{1,0:T(8,128)(2,1)S(1)}, bf16[128,512]{1,0:T(8,128)(2,1)S(1)}, u32[]{:S(2)}, u32[]{:S(2)}) collective-permute-start(bf16[128,512]{1,0:T(8,128)(2,1)S(1)} %pad_maximum_fusion.pair_ref.refs_9_), channel_id=1, source_target_pairs={{0,2},{2,4},{4,6},{6,0},{1,3},{3,5},{5,7},{7,1},{8,10},{10,12},{12... | collective-permute-start | bytes 393224 | tf_op jit(solution)/shard_map/ppermute | solution.py:235
  4.6 11.2 %collective-permute-start.1 = (bf16[128,512]{1,0:T(8,128)(2,1)S(1)}, bf16[128,512]{1,0:T(8,128)(2,1)S(1)}, u32[]{:S(2)}, u32[]{:S(2)}) collective-permute-start(bf16[128,512]{1,0:T(8,128)(2,1)S(1)} %pad_maximum_fusion.pair_ref.refs_9_), channel_id=1, source_target_pairs={{0,4},{2,6},{4,0},{6,2},{1,5},{3,7},{5,1},{7,3},{8,12},{10,14},{12... | collective-permute-start | bytes 393224 | tf_op jit(solution)/shard_map/ppermute | solution.py:235
  7.2 8.6 %collective-permute-start = (bf16[128,512]{1,0:T(8,128)(2,1)S(1)}, bf16[128,512]{1,0:T(8,128)(2,1)S(1)}, u32[]{:S(2)}, u32[]{:S(2)}) collective-permute-start(bf16[128,512]{1,0:T(8,128)(2,1)S(1)} %pad_maximum_fusion.pair_ref.refs_9_), channel_id=1, source_target_pairs={{0,6},{2,0},{4,2},{6,4},{1,7},{3,1},{5,3},{7,5},{8,14},{10,8},{12,... | collective-permute-start | bytes 393224 | tf_op jit(solution)/shard_map/ppermute | solution.py:235
  8.5 1.0 %copy-start = (bf16[1,128,2048]{2,1,0:T(8,128)(2,1)S(1)}, bf16[1,128,2048]{2,1,0:T(8,128)(2,1)}, u32[]{:S(2)}) copy-start(bf16[1,128,2048]{2,1,0:T(8,128)(2,1)} %param.7) | copy-start | bytes 1572868
  9.6 1.0 %copy-start.1 = (bf16[1,128,2048]{2,1,0:T(8,128)(2,1)S(1)}, bf16[1,128,2048]{2,1,0:T(8,128)(2,1)}, u32[]{:S(2)}) copy-start(bf16[1,128,2048]{2,1,0:T(8,128)(2,1)} %param.12) | copy-start | bytes 1572868
  10.6 0.7 %copy-start.2 = (bf16[2048]{0:T(1024)(128)(2,1)S(1)}, bf16[2048]{0:T(1024)(128)(2,1)}, u32[]{:S(2)}) copy-start(bf16[2048]{0:T(1024)(128)(2,1)} %param.8) | copy-start | bytes 12292
  11.3 0.7 %copy-start.3 = (s32[1,8]{1,0:T(1,128)S(1)}, s32[1,8]{1,0:T(1,128)}, u32[]{:S(2)}) copy-start(s32[1,8]{1,0:T(1,128)} %len_ref.1) | copy-start | bytes 100
  12.0 0.7 %copy-start.4 = (bf16[256]{0:T(256)(128)(2,1)S(1)}, bf16[256]{0:T(256)(128)(2,1)}, u32[]{:S(2)}) copy-start(bf16[256]{0:T(256)(128)(2,1)} %param.11) | copy-start | bytes 1540
  20.1 13.8 %collective-permute-start.6 = (bf16[128,512]{1,0:T(8,128)(2,1)S(1)}, bf16[128,512]{1,0:T(8,128)(2,1)S(1)}, u32[]{:S(2)}, u32[]{:S(2)}) collective-permute-start(bf16[128,512]{1,0:T(8,128)(2,1)S(1)} %get-tuple-element.42), channel_id=1, source_target_pairs={{0,6},{2,0},{4,2},{6,4},{1,7},{3,1},{5,3},{7,5},{8,14},{10,8},{12,... | collective-permute-start | bytes 393224 | tf_op jit(solution)/shard_map/ppermute | solution.py:290
  24.5 15.6 %collective-permute-start.10 = (bf16[128,512]{1,0:T(8,128)(2,1)S(1)}, bf16[128,512]{1,0:T(8,128)(2,1)S(1)}, u32[]{:S(2)}, u32[]{:S(2)}) collective-permute-start(bf16[128,512]{1,0:T(8,128)(2,1)S(1)} %get-tuple-element.46), channel_id=1, source_target_pairs={{0,4},{2,6},{4,0},{6,2},{1,5},{3,7},{5,1},{7,3},{8,12},{10,14},{12... | collective-permute-start | bytes 393224 | tf_op jit(solution)/shard_map/ppermute | solution.py:290
  24.9 15.3 %collective-permute-start.11 = (bf16[128,512]{1,0:T(8,128)(2,1)S(1)}, bf16[128,512]{1,0:T(8,128)(2,1)S(1)}, u32[]{:S(2)}, u32[]{:S(2)}) collective-permute-start(bf16[128,512]{1,0:T(8,128)(2,1)S(1)} %get-tuple-element.47), channel_id=1, source_target_pairs={{0,2},{2,4},{4,6},{6,0},{1,3},{3,5},{5,7},{7,1},{8,10},{10,12},{12... | collective-permute-start | bytes 393224 | tf_op jit(solution)/shard_map/ppermute | solution.py:290
  25.1 3.8 %collective-permute-start.5 = (f32[18,128]{1,0:T(8,128)S(1)}, f32[18,128]{1,0:T(8,128)S(1)}, u32[]{:S(2)}, u32[]{:S(2)}) collective-permute-start(f32[18,128]{1,0:T(8,128)S(1)} %get-tuple-element.41.refs_0_), channel_id=1, source_target_pairs={{0,24},{8,0},{16,8},{24,16},{1,25},{9,1},{17,9},{25,17},{2,26},{10... | collective-permute-start | bytes 27656 | tf_op jit(solution)/shard_map/ppermute | solution.py:219
  27.6 3.8 %collective-permute-start.4 = (f32[18,128]{1,0:T(8,128)S(1)}, f32[18,128]{1,0:T(8,128)S(1)}, u32[]{:S(2)}, u32[]{:S(2)}) collective-permute-start(f32[18,128]{1,0:T(8,128)S(1)} %get-tuple-element.41.refs_0_), channel_id=1, source_target_pairs={{0,16},{8,24},{16,0},{24,8},{1,17},{9,25},{17,1},{25,9},{2,18},{10... | collective-permute-start | bytes 27656 | tf_op jit(solution)/shard_map/ppermute | solution.py:219
  29.0 4.9 %collective-permute-start.3 = (f32[18,128]{1,0:T(8,128)S(1)}, f32[18,128]{1,0:T(8,128)S(1)}, u32[]{:S(2)}, u32[]{:S(2)}) collective-permute-start(f32[18,128]{1,0:T(8,128)S(1)} %get-tuple-element.41.refs_0_), channel_id=1, source_target_pairs={{0,8},{8,16},{16,24},{24,0},{1,9},{9,17},{17,25},{25,1},{2,10},{10... | collective-permute-start | bytes 27656 | tf_op jit(solution)/shard_map/ppermute | solution.py:219
  33.8 6.3 %collective-permute-start.9 = (f32[18,128]{1,0:T(8,128)S(1)}, f32[18,128]{1,0:T(8,128)S(1)}, u32[]{:S(2)}, u32[]{:S(2)}) collective-permute-start(f32[18,128]{1,0:T(8,128)S(1)} %get-tuple-element.43.refs_0_), channel_id=1, source_target_pairs={{0,6},{2,0},{4,2},{6,4},{1,7},{3,1},{5,3},{7,5},{8,14},{10,8},{12,... | collective-permute-start | bytes 27656 | tf_op jit(solution)/shard_map/ppermute | solution.py:219
  37.5 4.6 %collective-permute-start.8 = (f32[18,128]{1,0:T(8,128)S(1)}, f32[18,128]{1,0:T(8,128)S(1)}, u32[]{:S(2)}, u32[]{:S(2)}) collective-permute-start(f32[18,128]{1,0:T(8,128)S(1)} %get-tuple-element.43.refs_0_), channel_id=1, source_target_pairs={{0,4},{2,6},{4,0},{6,2},{1,5},{3,7},{5,1},{7,3},{8,12},{10,14},{12... | collective-permute-start | bytes 27656 | tf_op jit(solution)/shard_map/ppermute | solution.py:219
  38.3 5.5 %collective-permute-start.7 = (f32[18,128]{1,0:T(8,128)S(1)}, f32[18,128]{1,0:T(8,128)S(1)}, u32[]{:S(2)}, u32[]{:S(2)}) collective-permute-start(f32[18,128]{1,0:T(8,128)S(1)} %get-tuple-element.43.refs_0_), channel_id=1, source_target_pairs={{0,2},{2,4},{4,6},{6,0},{1,3},{3,5},{5,7},{7,1},{8,10},{10,12},{12... | collective-permute-start | bytes 27656 | tf_op jit(solution)/shard_map/ppermute | solution.py:219

commit v10 on v9

--- a/solution.py
+++ b/solution.py
@@ -189,28 +189,31 @@
     vg_ref[...] = term[:, kv_width:]
 
 
-def total_kernel(*refs):
-    out_ref = refs[-2]
+def total_kernel(count, *refs):
     total = refs[0][...]
-    for ref in refs[1:-3]:
+    for ref in refs[1:count]:
         total = total + ref[...]
-    out_ref[...] = total
-
-
-def total_after(parts, received):
-    return pl.pallas_call(
-        total_kernel,
-        out_shape=[
-            shape(parts[0].shape, parts[0].dtype),
-            shape(received.shape, received.dtype),
-        ],
-        in_specs=[VMEM] * len(parts) + [ANY],
-        out_specs=[VMEM, ANY],
-        input_output_aliases={len(parts): 1},
+    refs[count + (len(refs) - count - 1) // 2][...] = total
+
+
+def total_between(parts, passed):
+    count = len(parts)
+    total, *passed = pl.pallas_call(
+        functools.partial(total_kernel, count),
+        out_shape=[shape(array.shape, array.dtype) for array in (parts[0], *passed)],
+        in_specs=[VMEM] * count + [ANY] * len(passed),
+        out_specs=[VMEM] + [ANY] * len(passed),
+        input_output_aliases={count + n: 1 + n for n in range(len(passed))},
         compiler_params=params(4),
         cost_estimate=pl.CostEstimate(flops=parts[0].size, bytes_accessed=0, transcendentals=0),
         name="total",
-    )(*parts, received)
+    )(*parts, *passed)
+    return total, passed
+
+
+def send_back(term, shift):
+    size = lax.axis_size("ctx")
+    return lax.ppermute(term, "ctx", [(i, (i - shift) % size) for i in range(size)])
 
 
 def exchange(axis, part):
@@ -286,10 +289,6 @@
         ),
         name="attend",
     )(*prepared, *pairs)
-    back = [
-        lax.ppermute(term, "ctx", [(i, (i - shift) % ctx) for i in range(ctx)])
-        for shift, term in enumerate(terms, 1)
-    ]
     attn, q_grad = pl.pallas_call(
         finish_kernel,
         out_shape=[
@@ -304,7 +303,10 @@
         ),
         name="finish",
     )(probs, dscore, all_keys, all_values)
-    sums, back[0] = total_after(exchange("dp", sums), back[0])
+    early = -(-len(terms) // 2)
+    back = [send_back(term, shift) for shift, term in enumerate(terms[:early], 1)]
+    sums, (back[0], *terms) = total_between(exchange("dp", sums), [back[0], *terms[early:]])
+    back += [send_back(term, shift) for shift, term in enumerate(terms, early + 1)]
     sums = exchange("ctx", sums)
     k_grad, v_grad, q_sum, v_sum = pl.pallas_call(
         functools.partial(collect_kernel, batches, len(sums), len(back)),

time: 44.8 us -> 42.4 us (0.946)
  starting transfers between devices: 21.7 us -> 19.8 us
    ppermute x6, starting transfers between devices: 9.67 us -> 7.92 us  [exchange(): lax.ppermute(part, axis, [(i, (i + shift) % size) for i in range(size)])]
  transfers between devices with their start and end apart: 12 -> 12, of which waited for: 6 -> 5; matrix products, arithmetic and copies ran while one was open for 0% -> 0% of each run, Pallas kernels for 7% -> 7%
where the time goes in v10:
time: 42.4 us; the launch traced here: 42.1 us
  starting transfers between devices  19.8 us (47%)
  waiting for transfers between devices  8.83 us (21%)
  Pallas kernels  7.85 us (19%)
  local copies, waits for them, and re-layouts  4.08 us (10%)
  other arithmetic  0.88 us (2%)
  between operations  0.68 us (2%)
    ppermute x6, starting transfers between devices, exchange(): lax.ppermute(part, axis, [(i, (i + shift) % size) for i in range(size)])  7.92 us
    ppermute x3, starting transfers between devices, shards(): lax.ppermute(pair, 'ctx', [(i, (i + shift) % ctx) for i in range(ctx)])  7.01 us
    ppermute x6, waiting for transfers between devices, exchange(): lax.ppermute(part, axis, [(i, (i + shift) % size) for i in range(size)])  6.74 us
    ppermute x3, starting transfers between devices, send_back(): lax.ppermute(term, 'ctx', [(i, (i - shift) % size) for i in range(size)])  4.85 us
    pallas_call x1, Pallas kernels, shards(): pl.pallas_call(functools.partial(attend_kernel, ctx), out_shape=[shape((r...  4.25 us
    unnamed x10, local copies, waits for them, and re-layouts  4.08 us
    ppermute x3, waiting for transfers between devices, shards(): lax.ppermute(pair, 'ctx', [(i, (i + shift) % ctx) for i in range(ctx)])  2.08 us
    pallas_call x1, Pallas kernels, shards(): pl.pallas_call(finish_kernel, out_shape=[shape((tok, width), jnp.bfloat16...  1.79 us
  transfers between devices with their start and end apart: 12, of which 5 were waited for; matrix products, arithmetic and copies ran while one was open for 0% of the time, Pallas kernels for 7%

profile of v10, /device:TPU:0, one launch (start us, length us, event | category | flops | bytes accessed | tf_op | source)
XLA Modules:
  0.0 42.1 jit_solution(14182539668115451899)
XLA Ops:
  0.6 0.9 %pad_maximum_fusion.pair_ref.refs_9_ = bf16[128,512]{1,0:T(8,128)(2,1)S(1)} fusion(bf16[128,256]{1,0:T(8,128)(2,1)} %bitcast.16, bf16[128,256]{1,0:T(8,128)(2,1)} %bitcast.17), kind=kLoop, calls=%fused_computation | loop fusion | flops 262144 | bytes 262144 | tf_op jit(solution)/shard_map/concatenate | solution.py:236
  1.5 3.1 %collective-permute-start.2 = (bf16[128,512]{1,0:T(8,128)(2,1)S(1)}, bf16[128,512]{1,0:T(8,128)(2,1)S(1)}, u32[]{:S(2)}, u32[]{:S(2)}) collective-permute-start(bf16[128,512]{1,0:T(8,128)(2,1)S(1)} %pad_maximum_fusion.pair_ref.refs_9_), channel_id=1, source_target_pairs={{0,2},{2,4},{4,6},{6,0},{1,3},{3,5},{5,7},{7,1},{8,10},{10,12},{12... | collective-permute-start | bytes 393224 | tf_op jit(solution)/shard_map/ppermute | solution.py:238
  4.6 2.6 %collective-permute-start.1 = (bf16[128,512]{1,0:T(8,128)(2,1)S(1)}, bf16[128,512]{1,0:T(8,128)(2,1)S(1)}, u32[]{:S(2)}, u32[]{:S(2)}) collective-permute-start(bf16[128,512]{1,0:T(8,128)(2,1)S(1)} %pad_maximum_fusion.pair_ref.refs_9_), channel_id=1, source_target_pairs={{0,4},{2,6},{4,0},{6,2},{1,5},{3,7},{5,1},{7,3},{8,12},{10,14},{12... | collective-permute-start | bytes 393224 | tf_op jit(solution)/shard_map/ppermute | solution.py:238
  7.2 1.3 %collective-permute-start = (bf16[128,512]{1,0:T(8,128)(2,1)S(1)}, bf16[128,512]{1,0:T(8,128)(2,1)S(1)}, u32[]{:S(2)}, u32[]{:S(2)}) collective-permute-start(bf16[128,512]{1,0:T(8,128)(2,1)S(1)} %pad_maximum_fusion.pair_ref.refs_9_), channel_id=1, source_target_pairs={{0,6},{2,0},{4,2},{6,4},{1,7},{3,1},{5,3},{7,5},{8,14},{10,8},{12,... | collective-permute-start | bytes 393224 | tf_op jit(solution)/shard_map/ppermute | solution.py:238
  8.5 0.0 copy-start
  8.5 1.0 %copy-done = bf16[1,128,2048]{2,1,0:T(8,128)(2,1)S(1)} copy-done((bf16[1,128,2048]{2,1,0:T(8,128)(2,1)S(1)}, bf16[1,128,2048]{2,1,0:T(8,128)(2,1)}, u32[]{:S(2)}) %copy-start) | copy-done | bytes 524312
  9.6 0.0 copy-start.1
  9.6 1.0 %copy-done.1 = bf16[1,128,2048]{2,1,0:T(8,128)(2,1)S(1)} copy-done((bf16[1,128,2048]{2,1,0:T(8,128)(2,1)S(1)}, bf16[1,128,2048]{2,1,0:T(8,128)(2,1)}, u32[]{:S(2)}) %copy-start.1) | copy-done | bytes 524312
  10.6 0.0 copy-start.2
  10.6 0.7 %copy-done.2 = bf16[2048]{0:T(1024)(128)(2,1)S(1)} copy-done((bf16[2048]{0:T(1024)(128)(2,1)S(1)}, bf16[2048]{0:T(1024)(128)(2,1)}, u32[]{:S(2)}) %copy-start.2) | copy-done | bytes 4120
  11.3 0.0 copy-start.3
  11.3 0.7 %copy-done.3 = s32[1,8]{1,0:T(1,128)S(1)} copy-done((s32[1,8]{1,0:T(1,128)S(1)}, s32[1,8]{1,0:T(1,128)}, u32[]{:S(2)}) %copy-start.3) | copy-done | bytes 56
  12.0 0.0 copy-start.4
  12.0 0.7 %copy-done.4 = bf16[256]{0:T(256)(128)(2,1)S(1)} copy-done((bf16[256]{0:T(256)(128)(2,1)S(1)}, bf16[256]{0:T(256)(128)(2,1)}, u32[]{:S(2)}) %copy-start.4) | copy-done | bytes 536
  12.6 1.1 %prepare.1 = (bf16[2,128]{1,0:T(2,128)(2,1)S(1)}, bf16[2048,256]{1,0:T(8,128)(2,1)S(1)}, bf16[2048,128]{1,0:T(8,128)(2,1)S(1)}, f32[128,2048]{1,0:T(8,128)S(1)},...) custom-call(s32[1,8]{1,0:T(1,128)S(1)} %copy-done.3, bf16[128,512]{1,0:T(8,128)(2,1)S(1)} %pad_maximum_fusion.pair_ref.refs_9_, ...), custom_call_target="tpu_custom_call" | custom-call | flops 134217728 | bytes 4194304 | tf_op jit(solution)/shard_map/prepare/pallas_call | solution.py:241
  13.7 0.0 collective-permute-done.2.refs_8_
  13.7 2.1 %collective-permute-done.1.refs_7_ = bf16[128,512]{1,0:T(8,128)(2,1)S(1)} collective-permute-done((bf16[128,512]{1,0:T(8,128)(2,1)S(1)}, bf16[128,512]{1,0:T(8,128)(2,1)S(1)}, u32[]{:S(2)}, u32[]{:S(2)}) %collective-permute-start.1) | collective-permute-done | bytes 131104 | tf_op jit(solution)/shard_map/ppermute | solution.py:238
  15.8 0.0 collective-permute-done.refs_6_
  15.8 4.2 %attend.1 = (bf16[512,2048]{1,0:T(8,128)(2,1)S(1)}, bf16[512,2048]{1,0:T(8,128)(2,1)S(1)}, bf16[512,256]{1,0:T(8,128)(2,1)S(1)}, bf16[512,256]{1,0:T(8,128)(2,1)...) custom-call(bf16[2,128]{1,0:T(2,128)(2,1)S(1)} %get-tuple-element.30, ...), custom_call_target="tpu_custom_call" | custom-call | flops 1073741824 | bytes 4194304 | tf_op jit(solution)/shard_map/attend/pallas_call | solution.py:267
  20.1 4.4 %collective-permute-start.6 = (bf16[128,512]{1,0:T(8,128)(2,1)S(1)}, bf16[128,512]{1,0:T(8,128)(2,1)S(1)}, u32[]{:S(2)}, u32[]{:S(2)}) collective-permute-start(bf16[128,512]{1,0:T(8,128)(2,1)S(1)} %get-tuple-element.43), channel_id=1, source_target_pairs={{0,6},{2,0},{4,2},{6,4},{1,7},{3,1},{5,3},{7,5},{8,14},{10,8},{12,... | collective-permute-start | bytes 393224 | tf_op jit(solution)/shard_map/ppermute | solution.py:216
  24.5 2.4 %collective-permute-start.5 = (f32[18,128]{1,0:T(8,128)S(1)}, f32[18,128]{1,0:T(8,128)S(1)}, u32[]{:S(2)}, u32[]{:S(2)}) collective-permute-start(f32[18,128]{1,0:T(8,128)S(1)} %get-tuple-element.42.refs_0_), channel_id=1, source_target_pairs={{0,24},{8,0},{16,8},{24,16},{1,25},{9,1},{17,9},{25,17},{2,26},{10... | collective-permute-start | bytes 27656 | tf_op jit(solution)/shard_map/ppermute | solution.py:222
  26.9 0.5 %collective-permute-start.4 = (f32[18,128]{1,0:T(8,128)S(1)}, f32[18,128]{1,0:T(8,128)S(1)}, u32[]{:S(2)}, u32[]{:S(2)}) collective-permute-start(f32[18,128]{1,0:T(8,128)S(1)} %get-tuple-element.42.refs_0_), channel_id=1, source_target_pairs={{0,16},{8,24},{16,0},{24,8},{1,17},{9,25},{17,1},{25,9},{2,18},{10... | collective-permute-start | bytes 27656 | tf_op jit(solution)/shard_map/ppermute | solution.py:222
  27.4 0.6 %collective-permute-start.3 = (f32[18,128]{1,0:T(8,128)S(1)}, f32[18,128]{1,0:T(8,128)S(1)}, u32[]{:S(2)}, u32[]{:S(2)}) collective-permute-start(f32[18,128]{1,0:T(8,128)S(1)} %get-tuple-element.42.refs_0_), channel_id=1, source_target_pairs={{0,8},{8,16},{16,24},{24,0},{1,9},{9,17},{17,25},{25,1},{2,10},{10... | collective-permute-start | bytes 27656 | tf_op jit(solution)/shard_map/ppermute | solution.py:222
  28.0 0.4 collective-permute-start.10
  28.4 0.0 collective-permute-done.5.refs_3_
  28.4 2.2 %collective-permute-done.4.refs_2_ = f32[18,128]{1,0:T(8,128)S(1)} collective-permute-done((f32[18,128]{1,0:T(8,128)S(1)}, f32[18,128]{1,0:T(8,128)S(1)}, u32[]{:S(2)}, u32[]{:S(2)}) %collective-permute-start.4) | collective-permute-done | bytes 9248 | tf_op jit(solution)/shard_map/ppermute | solution.py:222
  30.6 1.4 %collective-permute-done.3.refs_1_ = f32[18,128]{1,0:T(8,128)S(1)} collective-permute-done((f32[18,128]{1,0:T(8,128)S(1)}, f32[18,128]{1,0:T(8,128)S(1)}, u32[]{:S(2)}, u32[]{:S(2)}) %collective-permute-start.3) | collective-permute-done | bytes 9248 | tf_op jit(solution)/shard_map/ppermute | solution.py:222
  32.0 0.0 collective-permute-done.6.refs_4_
  32.0 0.1 collective-permute-start.11
  32.1 3.8 %collective-permute-start.9 = (f32[18,128]{1,0:T(8,128)S(1)}, f32[18,128]{1,0:T(8,128)S(1)}, u32[]{:S(2)}, u32[]{:S(2)}) collective-permute-start(f32[18,128]{1,0:T(8,128)S(1)} %get-tuple-element.45.refs_0_), channel_id=1, source_target_pairs={{0,6},{2,0},{4,2},{6,4},{1,7},{3,1},{5,3},{7,5},{8,14},{10,8},{12,... | collective-permute-start | bytes 27656 | tf_op jit(solution)/shard_map/ppermute | solution.py:222
  35.9 0.0 collective-permute-start.8
  35.9 0.6 %collective-permute-start.7 = (f32[18,128]{1,0:T(8,128)S(1)}, f32[18,128]{1,0:T(8,128)S(1)}, u32[]{:S(2)}, u32[]{:S(2)}) collective-permute-start(f32[18,128]{1,0:T(8,128)S(1)} %get-tuple-element.45.refs_0_), channel_id=1, source_target_pairs={{0,2},{2,4},{4,6},{6,0},{1,3},{3,5},{5,7},{7,1},{8,10},{10,12},{12... | collective-permute-start | bytes 27656 | tf_op jit(solution)/shard_map/ppermute | solution.py:222
  36.5 1.8 %finish.1 = (bf16[128,2048]{1,0:T(8,128)(2,1)}, bf16[128,2048]{1,0:T(8,128)(2,1)}) custom-call(bf16[512,2048]{1,0:T(8,128)(2,1)S(1)} %get-tuple-element.36.probs_ref, bf16[512,2048]{1,0:T(8,128)(2,1)S(1)} %get-tuple-element.37.dscore_ref, bf16[512,256]{1,0:T(8,128)(2,1)S(1)} %get-tuple-element.38.keys_ref, bf16[512,256]{1,0:T(8,128)(2,1)S(1)} %get-tuple-element.39.values_ref), custom_call_target="tpu_custom_call" | custom-call | flops 536870912 | bytes 4194304 | tf_op jit(solution)/shard_map/finish/pallas_call | solution.py:292
  38.3 0.0 collective-permute-done.10.refs_6_
  38.3 0.0 collective-permute-done.9.refs_3_
  38.3 2.2 %collective-permute-done.8.refs_2_ = f32[18,128]{1,0:T(8,128)S(1)} collective-permute-done((f32[18,128]{1,0:T(8,128)S(1)}, f32[18,128]{1,0:T(8,128)S(1)}, u32[]{:S(2)}, u32[]{:S(2)}) %collective-permute-start.8) | collective-permute-done | bytes 9248 | tf_op jit(solution)/shard_map/ppermute | solution.py:222
  40.5 0.9 %collective-permute-done.7.refs_1_ = f32[18,128]{1,0:T(8,128)S(1)} collective-permute-done((f32[18,128]{1,0:T(8,128)S(1)}, f32[18,128]{1,0:T(8,128)S(1)}, u32[]{:S(2)}, u32[]{:S(2)}) %collective-permute-start.7) | collective-permute-done | bytes 9248 | tf_op jit(solution)/shard_map/ppermute | solution.py:222
  41.4 0.0 collective-permute-done.11.refs_7_
  41.4 0.7 %collect.1 = (bf16[128,256]{1,0:T(8,128)(2,1)}, bf16[128,256]{1,0:T(8,128)(2,1)}, f32[16,128]{1,0:T(8,128)}, f32[2,128]{1,0:T(2,128)}) custom-call(f32[18,128]{1,0:T(8,128)S(1)} %get-tuple-element.45.refs_0_, f32[18,128]{1,0:T(8,128)S(1)} %collective-permute-done.7.refs_1_, f32[18,128]{1,0:T(8,128)S(1)} %collective-permute-done.8.refs_2_, ...), custom_call_target="tpu_custom_call" | custom-call | flops 262144 | bytes 524288 | tf_op jit(solution)/shard_map/collect/pallas_call | solution.py:311
  (1 shorter events, 0.0 us)
Async XLA Ops:
  1.5 12.2 %collective-permute-start.2 = (bf16[128,512]{1,0:T(8,128)(2,1)S(1)}, bf16[128,512]{1,0:T(8,128)(2,1)S(1)}, u32[]{:S(2)}, u32[]{:S(2)}) collective-permute-start(bf16[128,512]{1,0:T(8,128)(2,1)S(1)} %pad_maximum_fusion.pair_ref.refs_9_), channel_id=1, source_target_pairs={{0,2},{2,4},{4,6},{6,0},{1,3},{3,5},{5,7},{7,1},{8,10},{10,12},{12... | collective-permute-start | bytes 393224 | tf_op jit(solution)/shard_map/ppermute | solution.py:238
  4.6 11.2 %collective-permute-start.1 = (bf16[128,512]{1,0:T(8,128)(2,1)S(1)}, bf16[128,512]{1,0:T(8,128)(2,1)S(1)}, u32[]{:S(2)}, u32[]{:S(2)}) collective-permute-start(bf16[128,512]{1,0:T(8,128)(2,1)S(1)} %pad_maximum_fusion.pair_ref.refs_9_), channel_id=1, source_target_pairs={{0,4},{2,6},{4,0},{6,2},{1,5},{3,7},{5,1},{7,3},{8,12},{10,14},{12... | collective-permute-start | bytes 393224 | tf_op jit(solution)/shard_map/ppermute | solution.py:238
  7.2 8.6 %collective-permute-start = (bf16[128,512]{1,0:T(8,128)(2,1)S(1)}, bf16[128,512]{1,0:T(8,128)(2,1)S(1)}, u32[]{:S(2)}, u32[]{:S(2)}) collective-permute-start(bf16[128,512]{1,0:T(8,128)(2,1)S(1)} %pad_maximum_fusion.pair_ref.refs_9_), channel_id=1, source_target_pairs={{0,6},{2,0},{4,2},{6,4},{1,7},{3,1},{5,3},{7,5},{8,14},{10,8},{12,... | collective-permute-start | bytes 393224 | tf_op jit(solution)/shard_map/ppermute | solution.py:238
  8.5 1.0 %copy-start = (bf16[1,128,2048]{2,1,0:T(8,128)(2,1)S(1)}, bf16[1,128,2048]{2,1,0:T(8,128)(2,1)}, u32[]{:S(2)}) copy-start(bf16[1,128,2048]{2,1,0:T(8,128)(2,1)} %param.7) | copy-start | bytes 1572868
  9.6 1.0 %copy-start.1 = (bf16[1,128,2048]{2,1,0:T(8,128)(2,1)S(1)}, bf16[1,128,2048]{2,1,0:T(8,128)(2,1)}, u32[]{:S(2)}) copy-start(bf16[1,128,2048]{2,1,0:T(8,128)(2,1)} %param.12) | copy-start | bytes 1572868
  10.6 0.7 %copy-start.2 = (bf16[2048]{0:T(1024)(128)(2,1)S(1)}, bf16[2048]{0:T(1024)(128)(2,1)}, u32[]{:S(2)}) copy-start(bf16[2048]{0:T(1024)(128)(2,1)} %param.8) | copy-start | bytes 12292
  11.3 0.7 %copy-start.3 = (s32[1,8]{1,0:T(1,128)S(1)}, s32[1,8]{1,0:T(1,128)}, u32[]{:S(2)}) copy-start(s32[1,8]{1,0:T(1,128)} %len_ref.1) | copy-start | bytes 100
  12.0 0.7 %copy-start.4 = (bf16[256]{0:T(256)(128)(2,1)S(1)}, bf16[256]{0:T(256)(128)(2,1)}, u32[]{:S(2)}) copy-start(bf16[256]{0:T(256)(128)(2,1)} %param.11) | copy-start | bytes 1540
  20.1 11.9 %collective-permute-start.6 = (bf16[128,512]{1,0:T(8,128)(2,1)S(1)}, bf16[128,512]{1,0:T(8,128)(2,1)S(1)}, u32[]{:S(2)}, u32[]{:S(2)}) collective-permute-start(bf16[128,512]{1,0:T(8,128)(2,1)S(1)} %get-tuple-element.43), channel_id=1, source_target_pairs={{0,6},{2,0},{4,2},{6,4},{1,7},{3,1},{5,3},{7,5},{8,14},{10,8},{12,... | collective-permute-start | bytes 393224 | tf_op jit(solution)/shard_map/ppermute | solution.py:216
  24.5 3.9 %collective-permute-start.5 = (f32[18,128]{1,0:T(8,128)S(1)}, f32[18,128]{1,0:T(8,128)S(1)}, u32[]{:S(2)}, u32[]{:S(2)}) collective-permute-start(f32[18,128]{1,0:T(8,128)S(1)} %get-tuple-element.42.refs_0_), channel_id=1, source_target_pairs={{0,24},{8,0},{16,8},{24,16},{1,25},{9,1},{17,9},{25,17},{2,26},{10... | collective-permute-start | bytes 27656 | tf_op jit(solution)/shard_map/ppermute | solution.py:222
  26.9 3.7 %collective-permute-start.4 = (f32[18,128]{1,0:T(8,128)S(1)}, f32[18,128]{1,0:T(8,128)S(1)}, u32[]{:S(2)}, u32[]{:S(2)}) collective-permute-start(f32[18,128]{1,0:T(8,128)S(1)} %get-tuple-element.42.refs_0_), channel_id=1, source_target_pairs={{0,16},{8,24},{16,0},{24,8},{1,17},{9,25},{17,1},{25,9},{2,18},{10... | collective-permute-start | bytes 27656 | tf_op jit(solution)/shard_map/ppermute | solution.py:222
  27.4 4.6 %collective-permute-start.3 = (f32[18,128]{1,0:T(8,128)S(1)}, f32[18,128]{1,0:T(8,128)S(1)}, u32[]{:S(2)}, u32[]{:S(2)}) collective-permute-start(f32[18,128]{1,0:T(8,128)S(1)} %get-tuple-element.42.refs_0_), channel_id=1, source_target_pairs={{0,8},{8,16},{16,24},{24,0},{1,9},{9,17},{17,25},{25,1},{2,10},{10... | collective-permute-start | bytes 27656 | tf_op jit(solution)/shard_map/ppermute | solution.py:222
  28.0 10.2 %collective-permute-start.10 = (bf16[128,512]{1,0:T(8,128)(2,1)S(1)}, bf16[128,512]{1,0:T(8,128)(2,1)S(1)}, u32[]{:S(2)}, u32[]{:S(2)}) collective-permute-start(bf16[128,512]{1,0:T(8,128)(2,1)S(1)} %get-tuple-element.48), channel_id=1, source_target_pairs={{0,4},{2,6},{4,0},{6,2},{1,5},{3,7},{5,1},{7,3},{8,12},{10,14},{12... | collective-permute-start | bytes 393224 | tf_op jit(solution)/shard_map/ppermute | solution.py:216
  32.0 9.4 %collective-permute-start.11 = (bf16[128,512]{1,0:T(8,128)(2,1)S(1)}, bf16[128,512]{1,0:T(8,128)(2,1)S(1)}, u32[]{:S(2)}, u32[]{:S(2)}) collective-permute-start(bf16[128,512]{1,0:T(8,128)(2,1)S(1)} %get-tuple-element.49), channel_id=1, source_target_pairs={{0,2},{2,4},{4,6},{6,0},{1,3},{3,5},{5,7},{7,1},{8,10},{10,12},{12... | collective-permute-start | bytes 393224 | tf_op jit(solution)/shard_map/ppermute | solution.py:216
  32.1 6.2 %collective-permute-start.9 = (f32[18,128]{1,0:T(8,128)S(1)}, f32[18,128]{1,0:T(8,128)S(1)}, u32[]{:S(2)}, u32[]{:S(2)}) collective-permute-start(f32[18,128]{1,0:T(8,128)S(1)} %get-tuple-element.45.refs_0_), channel_id=1, source_target_pairs={{0,6},{2,0},{4,2},{6,4},{1,7},{3,1},{5,3},{7,5},{8,14},{10,8},{12,... | collective-permute-start | bytes 27656 | tf_op jit(solution)/shard_map/ppermute | solution.py:222
  35.9 4.6 %collective-permute-start.8 = (f32[18,128]{1,0:T(8,128)S(1)}, f32[18,128]{1,0:T(8,128)S(1)}, u32[]{:S(2)}, u32[]{:S(2)}) collective-permute-start(f32[18,128]{1,0:T(8,128)S(1)} %get-tuple-element.45.refs_0_), channel_id=1, source_target_pairs={{0,4},{2,6},{4,0},{6,2},{1,5},{3,7},{5,1},{7,3},{8,12},{10,14},{12... | collective-permute-start | bytes 27656 | tf_op jit(solution)/shard_map/ppermute | solution.py:222
  35.9 5.5 %collective-permute-start.7 = (f32[18,128]{1,0:T(8,128)S(1)}, f32[18,128]{1,0:T(8,128)S(1)}, u32[]{:S(2)}, u32[]{:S(2)}) collective-permute-start(f32[18,128]{1,0:T(8,128)S(1)} %get-tuple-element.45.refs_0_), channel_id=1, source_target_pairs={{0,2},{2,4},{4,6},{6,0},{1,3},{3,5},{5,7},{7,1},{8,10},{10,12},{12... | collective-permute-start | bytes 27656 | tf_op jit(solution)/shard_map/ppermute | solution.py:222

commit v11 on v10

--- a/solution.py
+++ b/solution.py
@@ -149,7 +149,7 @@
             out_refs[slot - 1][:, value_cols] = value_term[rows].astype(jnp.bfloat16)
 
 
-def finish_kernel(probs_ref, dscore_ref, keys_ref, values_ref, attn_ref, qg_ref):
+def finish_kernel(probs_ref, dscore_ref, keys_ref, values_ref, _, attn_ref, qg_ref, __):
     tok = attn_ref.shape[0]
     kv_heads = keys_ref.shape[1] // HEAD_DIM
     for kv_head in range(kv_heads):
@@ -168,47 +168,59 @@
                 qg_ref[:, head_cols(head)] = query_grad[rows].astype(jnp.bfloat16)
 
 
-def collect_kernel(batches, parts, kv_parts, *refs):
-    sum_refs, refs = refs[:parts], refs[parts:]
-    own_ref, refs = refs[0], refs[1:]
-    back_refs, refs = refs[:kv_parts], refs[kv_parts:]
-    kg_ref, vg_ref, qb_ref, vb_ref = refs
-    heads = qb_ref.shape[0]
-    kv_width = kg_ref.shape[1]
-    total = sum_refs[0][...]
-    for ref in sum_refs[1:]:
-        total = total + ref[...]
+def collect_kernel(batches, messages, *refs):
+    sum_refs, refs = refs[:2], refs[2:]
+    own_ref, early_ref, refs = refs[0], refs[1], refs[2:]
+    message_refs, (kg_ref, vg_ref, qb_ref, vb_ref) = refs[:messages], refs[messages:]
+    heads, kv_heads = qb_ref.shape[0], vb_ref.shape[0]
+    tok, kv_width = kg_ref.shape
+    total = sum_refs[0][...] + sum_refs[1][...]
+    term = own_ref[...] + early_ref[...].astype(jnp.float32)
+    for ref in message_refs:
+        sums = ref[tok:, :].astype(jnp.float32)
+        sums = sums[:, :HEAD_DIM] + sums[:, HEAD_DIM : 2 * HEAD_DIM]
+        total = total + sums[: heads + kv_heads]
+        term = term + ref[:tok, :].astype(jnp.float32)
     total = total * (1.0 / batches)
     qb_ref[...] = total[:heads]
     vb_ref[...] = total[heads:]
-    term = own_ref[...]
-    for ref in back_refs:
-        term = term + ref[...].astype(jnp.float32)
     term = term.astype(jnp.bfloat16)
     kg_ref[...] = term[:, :kv_width]
     vg_ref[...] = term[:, kv_width:]
 
 
 def total_kernel(count, *refs):
-    total = refs[0][...]
-    for ref in refs[1:count]:
+    parts, refs = refs[:count], refs[count:]
+    sent = (len(refs) - 1) // 2
+    term_refs, total_ref, message_refs = refs[:sent], refs[sent], refs[sent + 1 :]
+    total = parts[0][...]
+    for ref in parts[1:]:
         total = total + ref[...]
-    refs[count + (len(refs) - count - 1) // 2][...] = total
-
-
-def total_between(parts, passed):
-    count = len(parts)
-    total, *passed = pl.pallas_call(
-        functools.partial(total_kernel, count),
-        out_shape=[shape(array.shape, array.dtype) for array in (parts[0], *passed)],
-        in_specs=[VMEM] * count + [ANY] * len(passed),
-        out_specs=[VMEM] + [ANY] * len(passed),
-        input_output_aliases={count + n: 1 + n for n in range(len(passed))},
-        compiler_params=params(4),
+    total_ref[...] = total
+    for term_ref, message_ref in zip(term_refs, message_refs):
+        tok = term_ref.shape[0]
+        rows = message_ref.shape[0] - tok
+        high = jnp.concatenate([total, jnp.zeros((rows - total.shape[0], HEAD_DIM), jnp.float32)])
+        message_ref[:tok, :] = term_ref[...]
+        message_ref[tok:, :] = jnp.zeros((rows, term_ref.shape[1]), jnp.bfloat16)
+        message_ref[tok:, :HEAD_DIM] = high.astype(jnp.bfloat16)
+        low = high - high.astype(jnp.bfloat16).astype(jnp.float32)
+        message_ref[tok:, HEAD_DIM : 2 * HEAD_DIM] = low.astype(jnp.bfloat16)
+
+
+def total_with(parts, terms):
+    rows = -(-parts[0].shape[0] // 16) * 16
+    total, *messages = pl.pallas_call(
+        functools.partial(total_kernel, len(parts)),
+        out_shape=[shape(parts[0].shape, parts[0].dtype)]
+        + [shape((term.shape[0] + rows, term.shape[1]), term.dtype) for term in terms],
+        in_specs=[VMEM] * (len(parts) + len(terms)),
+        out_specs=[VMEM] * (1 + len(terms)),
+        compiler_params=params(8),
         cost_estimate=pl.CostEstimate(flops=parts[0].size, bytes_accessed=0, transcendentals=0),
         name="total",
-    )(*parts, *passed)
-    return total, passed
+    )(*parts, *terms)
+    return total, messages
 
 
 def send_back(term, shift):
@@ -289,41 +301,44 @@
         ),
         name="attend",
     )(*prepared, *pairs)
-    attn, q_grad = pl.pallas_call(
+    half = ctx // 2
+    early = send_back(terms.pop(half - 1), half)
+    attn, q_grad, early = pl.pallas_call(
         finish_kernel,
         out_shape=[
             shape((tok, width), jnp.bfloat16),
             shape((tok, width), jnp.bfloat16),
+            shape(early.shape, early.dtype),
         ],
-        in_specs=[VMEM] * 4,
-        out_specs=[VMEM] * 2,
+        in_specs=[VMEM] * 4 + [ANY],
+        out_specs=[VMEM] * 2 + [ANY],
+        input_output_aliases={4: 2},
         compiler_params=params(24),
         cost_estimate=pl.CostEstimate(
             flops=4 * rows * tok * width, bytes_accessed=4 * rows * columns, transcendentals=0
         ),
         name="finish",
-    )(probs, dscore, all_keys, all_values)
-    early = -(-len(terms) // 2)
-    back = [send_back(term, shift) for shift, term in enumerate(terms[:early], 1)]
-    sums, (back[0], *terms) = total_between(exchange("dp", sums), [back[0], *terms[early:]])
-    back += [send_back(term, shift) for shift, term in enumerate(terms, early + 1)]
-    sums = exchange("ctx", sums)
+    )(probs, dscore, all_keys, all_values, early)
+    sums, messages = total_with(exchange("dp", sums), terms)
+    shifts = [shift for shift in range(1, ctx) if shift != half]
+    back = [send_back(message, shift) for shift, message in zip(shifts, messages)]
+    sums = [sums, send_back(sums, half)]
     k_grad, v_grad, q_sum, v_sum = pl.pallas_call(
-        functools.partial(collect_kernel, batches, len(sums), len(back)),
+        functools.partial(collect_kernel, batches, len(back)),
         out_shape=[
             shape((tok, kv_width), jnp.bfloat16),
             shape((tok, kv_width), jnp.bfloat16),
             shape((heads, HEAD_DIM), jnp.float32),
             shape((kv_heads, HEAD_DIM), jnp.float32),
         ],
-        in_specs=[VMEM] * (len(sums) + 1 + len(back)),
+        in_specs=[VMEM] * (4 + len(back)),
         out_specs=[VMEM] * 4,
         compiler_params=params(8),
         cost_estimate=pl.CostEstimate(
             flops=8 * tok * kv_width, bytes_accessed=16 * tok * kv_width, transcendentals=0
         ),
         name="collect",
-    )(*sums, own, *back)
+    )(*sums, own, early, *back)
     return (
         attn[None],
         q_grad[None],

time: 42.4 us -> 42.4 us (level)
  starting transfers between devices: 19.8 us -> 17 us
  waiting for transfers between devices: 8.83 us -> 11.5 us
    ppermute x3 -> x4, waiting for transfers between devices: 0.01 us -> 5.4 us  [send_back(): lax.ppermute(term, 'ctx', [(i, (i - shift) % size) for i in range(size)])]
    ppermute x6 -> x3, starting transfers between devices: 7.92 us -> 3.55 us  [exchange(): lax.ppermute(part, axis, [(i, (i + shift) % size) for i in range(size)])]
    ppermute x6 -> x3, waiting for transfers between devices: 6.74 us -> 4 us  [exchange(): lax.ppermute(part, axis, [(i, (i + shift) % size) for i in range(size)])]
    ppermute x3 -> x4, starting transfers between devices: 4.85 us -> 6.48 us  [send_back(): lax.ppermute(term, 'ctx', [(i, (i - shift) % size) for i in range(size)])]
  transfers between devices with their start and end apart: 12 -> 10, of which waited for: 5 -> 5; matrix products, arithmetic and copies ran while one was open for 0% -> 0% of each run, Pallas kernels for 7% -> 7%
where the time goes in v11:
time: 42.4 us; the launch traced here: 42.1 us
  starting transfers between devices  17 us (40%)
  waiting for transfers between devices  11.5 us (27%)
  Pallas kernels  7.89 us (19%)
  local copies, waits for them, and re-layouts  4.08 us (10%)
  other arithmetic  0.88 us (2%)
  between operations  0.68 us (2%)
    ppermute x3, starting transfers between devices, shards(): lax.ppermute(pair, 'ctx', [(i, (i + shift) % ctx) for i in range(ctx)])  7.01 us
    ppermute x4, starting transfers between devices, send_back(): lax.ppermute(term, 'ctx', [(i, (i - shift) % size) for i in range(size)])  6.48 us
    ppermute x4, waiting for transfers between devices, send_back(): lax.ppermute(term, 'ctx', [(i, (i - shift) % size) for i in range(size)])  5.4 us
    pallas_call x1, Pallas kernels, shards(): pl.pallas_call(functools.partial(attend_kernel, ctx), out_shape=[shape((r...  4.25 us
    unnamed x10, local copies, waits for them, and re-layouts  4.08 us
    ppermute x3, waiting for transfers between devices, exchange(): lax.ppermute(part, axis, [(i, (i + shift) % size) for i in range(size)])  4 us
    ppermute x3, starting transfers between devices, exchange(): lax.ppermute(part, axis, [(i, (i + shift) % size) for i in range(size)])  3.55 us
    ppermute x3, waiting for transfers between devices, shards(): lax.ppermute(pair, 'ctx', [(i, (i + shift) % ctx) for i in range(ctx)])  2.08 us
  transfers between devices with their start and end apart: 10, of which 5 were waited for; matrix products, arithmetic and copies ran while one was open for 0% of the time, Pallas kernels for 7%

profile of v11, /device:TPU:0, one launch (start us, length us, event | category | flops | bytes accessed | tf_op | source)
XLA Modules:
  0.0 42.1 jit_solution(8704516664147257660)
XLA Ops:
  0.6 0.9 %pad_maximum_fusion.pair_ref.refs_9_ = bf16[128,512]{1,0:T(8,128)(2,1)S(1)} fusion(bf16[128,256]{1,0:T(8,128)(2,1)} %bitcast.16, bf16[128,256]{1,0:T(8,128)(2,1)} %bitcast.17), kind=kLoop, calls=%fused_computation | loop fusion | flops 262144 | bytes 262144 | tf_op jit(solution)/shard_map/concatenate | solution.py:248
  1.5 3.1 %collective-permute-start.2 = (bf16[128,512]{1,0:T(8,128)(2,1)S(1)}, bf16[128,512]{1,0:T(8,128)(2,1)S(1)}, u32[]{:S(2)}, u32[]{:S(2)}) collective-permute-start(bf16[128,512]{1,0:T(8,128)(2,1)S(1)} %pad_maximum_fusion.pair_ref.refs_9_), channel_id=1, source_target_pairs={{0,2},{2,4},{4,6},{6,0},{1,3},{3,5},{5,7},{7,1},{8,10},{10,12},{12... | collective-permute-start | bytes 393224 | tf_op jit(solution)/shard_map/ppermute | solution.py:250
  4.6 2.6 %collective-permute-start.1 = (bf16[128,512]{1,0:T(8,128)(2,1)S(1)}, bf16[128,512]{1,0:T(8,128)(2,1)S(1)}, u32[]{:S(2)}, u32[]{:S(2)}) collective-permute-start(bf16[128,512]{1,0:T(8,128)(2,1)S(1)} %pad_maximum_fusion.pair_ref.refs_9_), channel_id=1, source_target_pairs={{0,4},{2,6},{4,0},{6,2},{1,5},{3,7},{5,1},{7,3},{8,12},{10,14},{12... | collective-permute-start | bytes 393224 | tf_op jit(solution)/shard_map/ppermute | solution.py:250
  7.2 1.3 %collective-permute-start = (bf16[128,512]{1,0:T(8,128)(2,1)S(1)}, bf16[128,512]{1,0:T(8,128)(2,1)S(1)}, u32[]{:S(2)}, u32[]{:S(2)}) collective-permute-start(bf16[128,512]{1,0:T(8,128)(2,1)S(1)} %pad_maximum_fusion.pair_ref.refs_9_), channel_id=1, source_target_pairs={{0,6},{2,0},{4,2},{6,4},{1,7},{3,1},{5,3},{7,5},{8,14},{10,8},{12,... | collective-permute-start | bytes 393224 | tf_op jit(solution)/shard_map/ppermute | solution.py:250
  8.5 0.0 copy-start
  8.5 1.0 %copy-done = bf16[1,128,2048]{2,1,0:T(8,128)(2,1)S(1)} copy-done((bf16[1,128,2048]{2,1,0:T(8,128)(2,1)S(1)}, bf16[1,128,2048]{2,1,0:T(8,128)(2,1)}, u32[]{:S(2)}) %copy-start) | copy-done | bytes 524312
  9.6 0.0 copy-start.1
  9.6 1.0 %copy-done.1 = bf16[1,128,2048]{2,1,0:T(8,128)(2,1)S(1)} copy-done((bf16[1,128,2048]{2,1,0:T(8,128)(2,1)S(1)}, bf16[1,128,2048]{2,1,0:T(8,128)(2,1)}, u32[]{:S(2)}) %copy-start.1) | copy-done | bytes 524312
  10.6 0.0 copy-start.2
  10.6 0.7 %copy-done.2 = bf16[2048]{0:T(1024)(128)(2,1)S(1)} copy-done((bf16[2048]{0:T(1024)(128)(2,1)S(1)}, bf16[2048]{0:T(1024)(128)(2,1)}, u32[]{:S(2)}) %copy-start.2) | copy-done | bytes 4120
  11.3 0.0 copy-start.3
  11.3 0.7 %copy-done.3 = s32[1,8]{1,0:T(1,128)S(1)} copy-done((s32[1,8]{1,0:T(1,128)S(1)}, s32[1,8]{1,0:T(1,128)}, u32[]{:S(2)}) %copy-start.3) | copy-done | bytes 56
  12.0 0.0 copy-start.4
  12.0 0.7 %copy-done.4 = bf16[256]{0:T(256)(128)(2,1)S(1)} copy-done((bf16[256]{0:T(256)(128)(2,1)S(1)}, bf16[256]{0:T(256)(128)(2,1)}, u32[]{:S(2)}) %copy-start.4) | copy-done | bytes 536
  12.6 1.1 %prepare.1 = (bf16[2,128]{1,0:T(2,128)(2,1)S(1)}, bf16[2048,256]{1,0:T(8,128)(2,1)S(1)}, bf16[2048,128]{1,0:T(8,128)(2,1)S(1)}, f32[128,2048]{1,0:T(8,128)S(1)},...) custom-call(s32[1,8]{1,0:T(1,128)S(1)} %copy-done.3, bf16[128,512]{1,0:T(8,128)(2,1)S(1)} %pad_maximum_fusion.pair_ref.refs_9_, ...), custom_call_target="tpu_custom_call" | custom-call | flops 134217728 | bytes 4194304 | tf_op jit(solution)/shard_map/prepare/pallas_call | solution.py:253
  13.7 0.0 collective-permute-done.2.refs_8_
  13.7 2.1 %collective-permute-done.1.refs_7_ = bf16[128,512]{1,0:T(8,128)(2,1)S(1)} collective-permute-done((bf16[128,512]{1,0:T(8,128)(2,1)S(1)}, bf16[128,512]{1,0:T(8,128)(2,1)S(1)}, u32[]{:S(2)}, u32[]{:S(2)}) %collective-permute-start.1) | collective-permute-done | bytes 131104 | tf_op jit(solution)/shard_map/ppermute | solution.py:250
  15.8 0.0 collective-permute-done.refs_6_
  15.8 4.2 %attend.1 = (bf16[512,2048]{1,0:T(8,128)(2,1)S(1)}, bf16[512,2048]{1,0:T(8,128)(2,1)S(1)}, bf16[512,256]{1,0:T(8,128)(2,1)S(1)}, bf16[512,256]{1,0:T(8,128)(2,1)...) custom-call(bf16[2,128]{1,0:T(2,128)(2,1)S(1)} %get-tuple-element.31, ...), custom_call_target="tpu_custom_call" | custom-call | flops 1073741824 | bytes 4194304 | tf_op jit(solution)/shard_map/attend/pallas_call | solution.py:279
  20.1 2.3 %collective-permute-start.3 = (bf16[128,512]{1,0:T(8,128)(2,1)S(1)}, bf16[128,512]{1,0:T(8,128)(2,1)S(1)}, u32[]{:S(2)}, u32[]{:S(2)}) collective-permute-start(bf16[128,512]{1,0:T(8,128)(2,1)S(1)} %get-tuple-element.41), channel_id=1, source_target_pairs={{0,4},{2,6},{4,0},{6,2},{1,5},{3,7},{5,1},{7,3},{8,12},{10,14},{12... | collective-permute-start | bytes 393224 | tf_op jit(solution)/shard_map/ppermute | solution.py:228
  22.4 2.5 %collective-permute-start.6 = (f32[18,128]{1,0:T(8,128)S(1)}, f32[18,128]{1,0:T(8,128)S(1)}, u32[]{:S(2)}, u32[]{:S(2)}) collective-permute-start(f32[18,128]{1,0:T(8,128)S(1)} %get-tuple-element.44.refs_0_), channel_id=1, source_target_pairs={{0,24},{8,0},{16,8},{24,16},{1,25},{9,1},{17,9},{25,17},{2,26},{10... | collective-permute-start | bytes 27656 | tf_op jit(solution)/shard_map/ppermute | solution.py:234
  24.9 0.5 %collective-permute-start.5 = (f32[18,128]{1,0:T(8,128)S(1)}, f32[18,128]{1,0:T(8,128)S(1)}, u32[]{:S(2)}, u32[]{:S(2)}) collective-permute-start(f32[18,128]{1,0:T(8,128)S(1)} %get-tuple-element.44.refs_0_), channel_id=1, source_target_pairs={{0,16},{8,24},{16,0},{24,8},{1,17},{9,25},{17,1},{25,9},{2,18},{10... | collective-permute-start | bytes 27656 | tf_op jit(solution)/shard_map/ppermute | solution.py:234
  25.4 0.6 %collective-permute-start.4 = (f32[18,128]{1,0:T(8,128)S(1)}, f32[18,128]{1,0:T(8,128)S(1)}, u32[]{:S(2)}, u32[]{:S(2)}) collective-permute-start(f32[18,128]{1,0:T(8,128)S(1)} %get-tuple-element.44.refs_0_), channel_id=1, source_target_pairs={{0,8},{8,16},{16,24},{24,0},{1,9},{9,17},{17,25},{25,1},{2,10},{10... | collective-permute-start | bytes 27656 | tf_op jit(solution)/shard_map/ppermute | solution.py:234
  26.0 0.3 collective-permute-done.6.refs_3_
  26.3 2.3 %collective-permute-done.5.refs_2_ = f32[18,128]{1,0:T(8,128)S(1)} collective-permute-done((f32[18,128]{1,0:T(8,128)S(1)}, f32[18,128]{1,0:T(8,128)S(1)}, u32[]{:S(2)}, u32[]{:S(2)}) %collective-permute-start.5) | collective-permute-done | bytes 9248 | tf_op jit(solution)/shard_map/ppermute | solution.py:234
  28.6 1.4 %collective-permute-done.4.refs_1_ = f32[18,128]{1,0:T(8,128)S(1)} collective-permute-done((f32[18,128]{1,0:T(8,128)S(1)}, f32[18,128]{1,0:T(8,128)S(1)}, u32[]{:S(2)}, u32[]{:S(2)}) %collective-permute-start.4) | collective-permute-done | bytes 9248 | tf_op jit(solution)/shard_map/ppermute | solution.py:234
  30.0 3.4 %collective-permute-start.8 = (bf16[160,512]{1,0:T(8,128)(2,1)S(1)}, bf16[160,512]{1,0:T(8,128)(2,1)S(1)}, u32[]{:S(2)}, u32[]{:S(2)}) collective-permute-start(bf16[160,512]{1,0:T(8,128)(2,1)S(1)} %get-tuple-element.50), channel_id=1, source_target_pairs={{0,6},{2,0},{4,2},{6,4},{1,7},{3,1},{5,3},{7,5},{8,14},{10,8},{12,... | collective-permute-start | bytes 491528 | tf_op jit(solution)/shard_map/ppermute | solution.py:228
  33.4 0.0 collective-permute-start.9
  33.4 0.7 %collective-permute-start.7 = (f32[18,128]{1,0:T(8,128)S(1)}, f32[18,128]{1,0:T(8,128)S(1)}, u32[]{:S(2)}, u32[]{:S(2)}) collective-permute-start(f32[18,128]{1,0:T(8,128)S(1)} %get-tuple-element.47.refs_0_), channel_id=1, source_target_pairs={{0,4},{2,6},{4,0},{6,2},{1,5},{3,7},{5,1},{7,3},{8,12},{10,14},{12... | collective-permute-start | bytes 27656 | tf_op jit(solution)/shard_map/ppermute | solution.py:228
  34.2 0.0 collective-permute-done.3._
  34.2 1.8 %finish.1 = (bf16[128,2048]{1,0:T(8,128)(2,1)}, bf16[128,2048]{1,0:T(8,128)(2,1)}, bf16[128,512]{1,0:T(8,128)(2,1)S(1)}) custom-call(bf16[512,2048]{1,0:T(8,128)(2,1)S(1)} %get-tuple-element.37.probs_ref, bf16[512,2048]{1,0:T(8,128)(2,1)S(1)} %get-tuple-element.38.dscore_ref, ...), custom_call_target="tpu_custom_call", output_to_operand_aliasing={{2}: (4, {})} | custom-call | flops 536870912 | bytes 4194304 | tf_op jit(solution)/shard_map/finish/pallas_call | solution.py:306
  36.0 5.4 %collective-permute-done.7.refs_1_ = f32[18,128]{1,0:T(8,128)S(1)} collective-permute-done((f32[18,128]{1,0:T(8,128)S(1)}, f32[18,128]{1,0:T(8,128)S(1)}, u32[]{:S(2)}, u32[]{:S(2)}) %collective-permute-start.7) | collective-permute-done | bytes 9248 | tf_op jit(solution)/shard_map/ppermute | solution.py:228
  41.4 0.0 collective-permute-done.8.refs_4_
  41.4 0.0 collective-permute-done.9.refs_5_
  41.4 0.7 %collect.1 = (bf16[128,256]{1,0:T(8,128)(2,1)}, bf16[128,256]{1,0:T(8,128)(2,1)}, f32[16,128]{1,0:T(8,128)}, f32[2,128]{1,0:T(2,128)}) custom-call(f32[18,128]{1,0:T(8,128)S(1)} %get-tuple-element.47.refs_0_, f32[18,128]{1,0:T(8,128)S(1)} %collective-permute-done.7.refs_1_, f32[128,512]{1,0:T(8,128)S(1)} %get-tuple-element.48.refs_2_, ...), custom_call_target="tpu_custom_call" | custom-call | flops 262144 | bytes 524288 | tf_op jit(solution)/shard_map/collect/pallas_call | solution.py:326
  (1 shorter events, 0.0 us)
Async XLA Ops:
  1.5 12.2 %collective-permute-start.2 = (bf16[128,512]{1,0:T(8,128)(2,1)S(1)}, bf16[128,512]{1,0:T(8,128)(2,1)S(1)}, u32[]{:S(2)}, u32[]{:S(2)}) collective-permute-start(bf16[128,512]{1,0:T(8,128)(2,1)S(1)} %pad_maximum_fusion.pair_ref.refs_9_), channel_id=1, source_target_pairs={{0,2},{2,4},{4,6},{6,0},{1,3},{3,5},{5,7},{7,1},{8,10},{10,12},{12... | collective-permute-start | bytes 393224 | tf_op jit(solution)/shard_map/ppermute | solution.py:250
  4.6 11.2 %collective-permute-start.1 = (bf16[128,512]{1,0:T(8,128)(2,1)S(1)}, bf16[128,512]{1,0:T(8,128)(2,1)S(1)}, u32[]{:S(2)}, u32[]{:S(2)}) collective-permute-start(bf16[128,512]{1,0:T(8,128)(2,1)S(1)} %pad_maximum_fusion.pair_ref.refs_9_), channel_id=1, source_target_pairs={{0,4},{2,6},{4,0},{6,2},{1,5},{3,7},{5,1},{7,3},{8,12},{10,14},{12... | collective-permute-start | bytes 393224 | tf_op jit(solution)/shard_map/ppermute | solution.py:250
  7.2 8.6 %collective-permute-start = (bf16[128,512]{1,0:T(8,128)(2,1)S(1)}, bf16[128,512]{1,0:T(8,128)(2,1)S(1)}, u32[]{:S(2)}, u32[]{:S(2)}) collective-permute-start(bf16[128,512]{1,0:T(8,128)(2,1)S(1)} %pad_maximum_fusion.pair_ref.refs_9_), channel_id=1, source_target_pairs={{0,6},{2,0},{4,2},{6,4},{1,7},{3,1},{5,3},{7,5},{8,14},{10,8},{12,... | collective-permute-start | bytes 393224 | tf_op jit(solution)/shard_map/ppermute | solution.py:250
  8.5 1.0 %copy-start = (bf16[1,128,2048]{2,1,0:T(8,128)(2,1)S(1)}, bf16[1,128,2048]{2,1,0:T(8,128)(2,1)}, u32[]{:S(2)}) copy-start(bf16[1,128,2048]{2,1,0:T(8,128)(2,1)} %param.7) | copy-start | bytes 1572868
  9.6 1.0 %copy-start.1 = (bf16[1,128,2048]{2,1,0:T(8,128)(2,1)S(1)}, bf16[1,128,2048]{2,1,0:T(8,128)(2,1)}, u32[]{:S(2)}) copy-start(bf16[1,128,2048]{2,1,0:T(8,128)(2,1)} %param.12) | copy-start | bytes 1572868
  10.6 0.7 %copy-start.2 = (bf16[2048]{0:T(1024)(128)(2,1)S(1)}, bf16[2048]{0:T(1024)(128)(2,1)}, u32[]{:S(2)}) copy-start(bf16[2048]{0:T(1024)(128)(2,1)} %param.8) | copy-start | bytes 12292
  11.3 0.7 %copy-start.3 = (s32[1,8]{1,0:T(1,128)S(1)}, s32[1,8]{1,0:T(1,128)}, u32[]{:S(2)}) copy-start(s32[1,8]{1,0:T(1,128)} %len_ref.1) | copy-start | bytes 100
  12.0 0.7 %copy-start.4 = (bf16[256]{0:T(256)(128)(2,1)S(1)}, bf16[256]{0:T(256)(128)(2,1)}, u32[]{:S(2)}) copy-start(bf16[256]{0:T(256)(128)(2,1)} %param.11) | copy-start | bytes 1540
  20.1 14.1 %collective-permute-start.3 = (bf16[128,512]{1,0:T(8,128)(2,1)S(1)}, bf16[128,512]{1,0:T(8,128)(2,1)S(1)}, u32[]{:S(2)}, u32[]{:S(2)}) collective-permute-start(bf16[128,512]{1,0:T(8,128)(2,1)S(1)} %get-tuple-element.41), channel_id=1, source_target_pairs={{0,4},{2,6},{4,0},{6,2},{1,5},{3,7},{5,1},{7,3},{8,12},{10,14},{12... | collective-permute-start | bytes 393224 | tf_op jit(solution)/shard_map/ppermute | solution.py:228
  22.4 3.9 %collective-permute-start.6 = (f32[18,128]{1,0:T(8,128)S(1)}, f32[18,128]{1,0:T(8,128)S(1)}, u32[]{:S(2)}, u32[]{:S(2)}) collective-permute-start(f32[18,128]{1,0:T(8,128)S(1)} %get-tuple-element.44.refs_0_), channel_id=1, source_target_pairs={{0,24},{8,0},{16,8},{24,16},{1,25},{9,1},{17,9},{25,17},{2,26},{10... | collective-permute-start | bytes 27656 | tf_op jit(solution)/shard_map/ppermute | solution.py:234
  24.9 3.7 %collective-permute-start.5 = (f32[18,128]{1,0:T(8,128)S(1)}, f32[18,128]{1,0:T(8,128)S(1)}, u32[]{:S(2)}, u32[]{:S(2)}) collective-permute-start(f32[18,128]{1,0:T(8,128)S(1)} %get-tuple-element.44.refs_0_), channel_id=1, source_target_pairs={{0,16},{8,24},{16,0},{24,8},{1,17},{9,25},{17,1},{25,9},{2,18},{10... | collective-permute-start | bytes 27656 | tf_op jit(solution)/shard_map/ppermute | solution.py:234
  25.4 4.6 %collective-permute-start.4 = (f32[18,128]{1,0:T(8,128)S(1)}, f32[18,128]{1,0:T(8,128)S(1)}, u32[]{:S(2)}, u32[]{:S(2)}) collective-permute-start(f32[18,128]{1,0:T(8,128)S(1)} %get-tuple-element.44.refs_0_), channel_id=1, source_target_pairs={{0,8},{8,16},{16,24},{24,0},{1,9},{9,17},{17,25},{25,1},{2,10},{10... | collective-permute-start | bytes 27656 | tf_op jit(solution)/shard_map/ppermute | solution.py:234
  30.0 11.4 %collective-permute-start.8 = (bf16[160,512]{1,0:T(8,128)(2,1)S(1)}, bf16[160,512]{1,0:T(8,128)(2,1)S(1)}, u32[]{:S(2)}, u32[]{:S(2)}) collective-permute-start(bf16[160,512]{1,0:T(8,128)(2,1)S(1)} %get-tuple-element.50), channel_id=1, source_target_pairs={{0,6},{2,0},{4,2},{6,4},{1,7},{3,1},{5,3},{7,5},{8,14},{10,8},{12,... | collective-permute-start | bytes 491528 | tf_op jit(solution)/shard_map/ppermute | solution.py:228
  33.4 7.9 %collective-permute-start.9 = (bf16[160,512]{1,0:T(8,128)(2,1)S(1)}, bf16[160,512]{1,0:T(8,128)(2,1)S(1)}, u32[]{:S(2)}, u32[]{:S(2)}) collective-permute-start(bf16[160,512]{1,0:T(8,128)(2,1)S(1)} %get-tuple-element.51), channel_id=1, source_target_pairs={{0,2},{2,4},{4,6},{6,0},{1,3},{3,5},{5,7},{7,1},{8,10},{10,12},{12... | collective-permute-start | bytes 491528 | tf_op jit(solution)/shard_map/ppermute | solution.py:228
  33.4 7.9 %collective-permute-start.7 = (f32[18,128]{1,0:T(8,128)S(1)}, f32[18,128]{1,0:T(8,128)S(1)}, u32[]{:S(2)}, u32[]{:S(2)}) collective-permute-start(f32[18,128]{1,0:T(8,128)S(1)} %get-tuple-element.47.refs_0_), channel_id=1, source_target_pairs={{0,4},{2,6},{4,0},{6,2},{1,5},{3,7},{5,1},{7,3},{8,12},{10,14},{12... | collective-permute-start | bytes 27656 | tf_op jit(solution)/shard_map/ppermute | solution.py:228

commit v12 on v11

--- a/solution.py
+++ b/solution.py
@@ -41,6 +41,22 @@
 
 def biased(values, bias):
     return (values.astype(jnp.float32) + bias.astype(jnp.float32)).astype(jnp.bfloat16)
+
+
+def source_of(rank, slot, size):
+    if size & (size - 1):
+        return (rank + size - slot) % size
+    return rank ^ slot
+
+
+def fetch(array, axis, slot):
+    size = lax.axis_size(axis)
+    return lax.ppermute(array, axis, [(source_of(i, slot, size), i) for i in range(size)])
+
+
+def send_back(array, slot):
+    size = lax.axis_size("ctx")
+    return lax.ppermute(array, "ctx", [(i, source_of(i, slot, size)) for i in range(size)])
 
 
 def prepare_kernel(
@@ -59,7 +75,7 @@
         start = start + jnp.where(query_pos >= end, length, 0)
     offsets = lax.broadcasted_iota(jnp.int32, (tok, tok), 0)
     for slot in range(slots):
-        key_pos = (rank - slot) * tok + offsets
+        key_pos = source_of(rank, slot, slots) * tok + offsets
         live = (key_pos >= start) & (key_pos <= query_pos)
         live_ref[slot * tok : (slot + 1) * tok, :] = jnp.where(live, 0.0, NEGATIVE)
     bias_ref[...] = vb_ref[...]
@@ -79,7 +95,7 @@
 
 def attend_kernel(slots, *refs):
     bias_ref, queries_ref, grads_ref, score_ref, dprob_ref, live_ref = refs[:6]
-    pair_refs = refs[6 : 6 + slots][::-1]
+    pair_refs = refs[6 : 6 + slots]
     refs = refs[6 + slots :]
     probs_ref, dscore_ref, keys_ref, values_ref, sums_ref, own_ref = refs[:6]
     out_refs = refs[6 : 6 + slots - 1]
@@ -223,17 +239,8 @@
     return total, messages
 
 
-def send_back(term, shift):
-    size = lax.axis_size("ctx")
-    return lax.ppermute(term, "ctx", [(i, (i - shift) % size) for i in range(size)])
-
-
 def exchange(axis, part):
-    size = lax.axis_size(axis)
-    return [part] + [
-        lax.ppermute(part, axis, [(i, (i + shift) % size) for i in range(size)])
-        for shift in range(1, size)
-    ]
+    return [part] + [fetch(part, axis, slot) for slot in range(1, lax.axis_size(axis))]
 
 
 def shards(q_proj, q_bias, k_proj, v_proj, v_bias, dout, lengths):
@@ -246,10 +253,7 @@
     rows = ctx * tok
     columns = heads * tok
     pair = jnp.concatenate([k_proj[0], v_proj[0]], axis=1)
-    pairs = [
-        lax.ppermute(pair, "ctx", [(i, (i + shift) % ctx) for i in range(ctx)])
-        for shift in range(ctx - 1, 0, -1)
-    ] + [pair]
+    pairs = [pair] + [fetch(pair, "ctx", slot) for slot in range(1, ctx)]
     prepared = pl.pallas_call(
         functools.partial(prepare_kernel, ctx),
         out_shape=[
@@ -320,8 +324,8 @@
         name="finish",
     )(probs, dscore, all_keys, all_values, early)
     sums, messages = total_with(exchange("dp", sums), terms)
-    shifts = [shift for shift in range(1, ctx) if shift != half]
-    back = [send_back(message, shift) for shift, message in zip(shifts, messages)]
+    slots = [slot for slot in range(1, ctx) if slot != half]
+    back = [send_back(message, slot) for slot, message in zip(slots, messages)][::-1]
     sums = [sums, send_back(sums, half)]
     k_grad, v_grad, q_sum, v_sum = pl.pallas_call(
         functools.partial(collect_kernel, batches, len(back)),

time: 42.4 us -> 39.5 us (0.932)
  starting transfers between devices: 17 us -> 13.9 us
    ppermute x10, starting transfers between devices: 17 us -> 13.9 us  [the longest x6 9.31 us: fetch(): lax.ppermute(array, axis, [(source_of(i, slot, size), i) for i in range(s...]
  transfers between devices with their start and end apart: 10 -> 10, of which waited for: 5 -> 5; matrix products, arithmetic and copies ran while one was open for 0% -> 0% of each run, Pallas kernels for 7% -> 8%
where the time goes in v12:
time: 39.5 us; the launch traced here: 39.1 us
  starting transfers between devices  13.9 us (35%)
  waiting for transfers between devices  11.8 us (30%)
  Pallas kernels  7.87 us (20%)
  local copies, waits for them, and re-layouts  4.08 us (10%)
  other arithmetic  0.88 us (2%)
  between operations  0.68 us (2%)
    ppermute x6, starting transfers between devices, fetch(): lax.ppermute(array, axis, [(source_of(i, slot, size), i) for i in range(s...  9.31 us
    ppermute x6, waiting for transfers between devices, fetch(): lax.ppermute(array, axis, [(source_of(i, slot, size), i) for i in range(s...  8.39 us
    ppermute x4, starting transfers between devices, send_back(): lax.ppermute(array, 'ctx', [(i, source_of(i, slot, size)) for i in range(...  4.56 us
    pallas_call x1, Pallas kernels, shards(): pl.pallas_call(functools.partial(attend_kernel, ctx), out_shape=[shape((r...  4.24 us
    unnamed x10, local copies, waits for them, and re-layouts  4.08 us
    ppermute x4, waiting for transfers between devices, send_back(): lax.ppermute(array, 'ctx', [(i, source_of(i, slot, size)) for i in range(...  3.37 us
    pallas_call x1, Pallas kernels, shards(): pl.pallas_call(finish_kernel, out_shape=[shape((tok, width), jnp.bfloat16...  1.79 us
    pallas_call x1, Pallas kernels, shards(): pl.pallas_call(functools.partial(prepare_kernel, ctx), out_shape=[shape((...  1.11 us
  transfers between devices with their start and end apart: 10, of which 5 were waited for; matrix products, arithmetic and copies ran while one was open for 0% of the time, Pallas kernels for 8%

profile of v12, /device:TPU:0, one launch (start us, length us, event | category | flops | bytes accessed | tf_op | source)
XLA Modules:
  0.0 39.1 jit_solution(11641762482613908257)
XLA Ops:
  0.6 0.9 %pad_maximum_fusion.pair_ref.refs_6_ = bf16[128,512]{1,0:T(8,128)(2,1)S(1)} fusion(bf16[128,256]{1,0:T(8,128)(2,1)} %bitcast.16, bf16[128,256]{1,0:T(8,128)(2,1)} %bitcast.17), kind=kLoop, calls=%fused_computation | loop fusion | flops 262144 | bytes 262144 | tf_op jit(solution)/shard_map/concatenate | solution.py:255
  1.5 5.1 %collective-permute-start.2 = (bf16[128,512]{1,0:T(8,128)(2,1)S(1)}, bf16[128,512]{1,0:T(8,128)(2,1)S(1)}, u32[]{:S(2)}, u32[]{:S(2)}) collective-permute-start(bf16[128,512]{1,0:T(8,128)(2,1)S(1)} %pad_maximum_fusion.pair_ref.refs_6_), channel_id=1, source_target_pairs={{6,0},{4,2},{2,4},{0,6},{7,1},{5,3},{3,5},{1,7},{14,8},{12,10},{10... | collective-permute-start | bytes 393224 | tf_op jit(solution)/shard_map/ppermute | solution.py:54
  6.6 0.0 collective-permute-start.1
  6.6 0.6 %collective-permute-start = (bf16[128,512]{1,0:T(8,128)(2,1)S(1)}, bf16[128,512]{1,0:T(8,128)(2,1)S(1)}, u32[]{:S(2)}, u32[]{:S(2)}) collective-permute-start(bf16[128,512]{1,0:T(8,128)(2,1)S(1)} %pad_maximum_fusion.pair_ref.refs_6_), channel_id=1, source_target_pairs={{2,0},{0,2},{6,4},{4,6},{3,1},{1,3},{7,5},{5,7},{10,8},{8,10},{14,... | collective-permute-start | bytes 393224 | tf_op jit(solution)/shard_map/ppermute | solution.py:54
  7.3 0.0 copy-start
  7.3 1.0 %copy-done = bf16[1,128,2048]{2,1,0:T(8,128)(2,1)S(1)} copy-done((bf16[1,128,2048]{2,1,0:T(8,128)(2,1)S(1)}, bf16[1,128,2048]{2,1,0:T(8,128)(2,1)}, u32[]{:S(2)}) %copy-start) | copy-done | bytes 524312
  8.3 0.0 copy-start.1
  8.3 1.0 %copy-done.1 = bf16[1,128,2048]{2,1,0:T(8,128)(2,1)S(1)} copy-done((bf16[1,128,2048]{2,1,0:T(8,128)(2,1)S(1)}, bf16[1,128,2048]{2,1,0:T(8,128)(2,1)}, u32[]{:S(2)}) %copy-start.1) | copy-done | bytes 524312
  9.4 0.0 copy-start.2
  9.4 0.7 %copy-done.2 = bf16[2048]{0:T(1024)(128)(2,1)S(1)} copy-done((bf16[2048]{0:T(1024)(128)(2,1)S(1)}, bf16[2048]{0:T(1024)(128)(2,1)}, u32[]{:S(2)}) %copy-start.2) | copy-done | bytes 4120
  10.0 0.0 copy-start.3
  10.0 0.7 %copy-done.3 = s32[1,8]{1,0:T(1,128)S(1)} copy-done((s32[1,8]{1,0:T(1,128)S(1)}, s32[1,8]{1,0:T(1,128)}, u32[]{:S(2)}) %copy-start.3) | copy-done | bytes 56
  10.7 0.0 copy-start.4
  10.7 0.7 %copy-done.4 = bf16[256]{0:T(256)(128)(2,1)S(1)} copy-done((bf16[256]{0:T(256)(128)(2,1)S(1)}, bf16[256]{0:T(256)(128)(2,1)}, u32[]{:S(2)}) %copy-start.4) | copy-done | bytes 536
  11.4 1.1 %prepare.1 = (bf16[2,128]{1,0:T(2,128)(2,1)S(1)}, bf16[2048,256]{1,0:T(8,128)(2,1)S(1)}, bf16[2048,128]{1,0:T(8,128)(2,1)S(1)}, f32[128,2048]{1,0:T(8,128)S(1)},...) custom-call(s32[1,8]{1,0:T(1,128)S(1)} %copy-done.3, bf16[128,512]{1,0:T(8,128)(2,1)S(1)} %pad_maximum_fusion.pair_ref.refs_6_, ...), custom_call_target="tpu_custom_call" | custom-call | flops 134217728 | bytes 4194304 | tf_op jit(solution)/shard_map/prepare/pallas_call | solution.py:257
  12.5 0.0 collective-permute-done.2.refs_9_
  12.5 5.2 %collective-permute-done.1.refs_8_ = bf16[128,512]{1,0:T(8,128)(2,1)S(1)} collective-permute-done((bf16[128,512]{1,0:T(8,128)(2,1)S(1)}, bf16[128,512]{1,0:T(8,128)(2,1)S(1)}, u32[]{:S(2)}, u32[]{:S(2)}) %collective-permute-start.1) | collective-permute-done | bytes 131104 | tf_op jit(solution)/shard_map/ppermute | solution.py:54
  17.7 0.0 collective-permute-done.refs_7_
  17.7 4.2 %attend.1 = (bf16[512,2048]{1,0:T(8,128)(2,1)S(1)}, bf16[512,2048]{1,0:T(8,128)(2,1)S(1)}, bf16[512,256]{1,0:T(8,128)(2,1)S(1)}, bf16[512,256]{1,0:T(8,128)(2,1)...) custom-call(bf16[2,128]{1,0:T(2,128)(2,1)S(1)} %get-tuple-element.31, ...), custom_call_target="tpu_custom_call" | custom-call | flops 1073741824 | bytes 4194304 | tf_op jit(solution)/shard_map/attend/pallas_call | solution.py:283
  22.0 0.1 collective-permute-start.3
  22.0 2.5 %collective-permute-start.6 = (f32[18,128]{1,0:T(8,128)S(1)}, f32[18,128]{1,0:T(8,128)S(1)}, u32[]{:S(2)}, u32[]{:S(2)}) collective-permute-start(f32[18,128]{1,0:T(8,128)S(1)} %get-tuple-element.44.refs_0_), channel_id=1, source_target_pairs={{24,0},{16,8},{8,16},{0,24},{25,1},{17,9},{9,17},{1,25},{26,2},{18... | collective-permute-start | bytes 27656 | tf_op jit(solution)/shard_map/ppermute | solution.py:54
  24.6 0.5 %collective-permute-start.5 = (f32[18,128]{1,0:T(8,128)S(1)}, f32[18,128]{1,0:T(8,128)S(1)}, u32[]{:S(2)}, u32[]{:S(2)}) collective-permute-start(f32[18,128]{1,0:T(8,128)S(1)} %get-tuple-element.44.refs_0_), channel_id=1, source_target_pairs={{16,0},{24,8},{0,16},{8,24},{17,1},{25,9},{1,17},{9,25},{18,2},{26... | collective-permute-start | bytes 27656 | tf_op jit(solution)/shard_map/ppermute | solution.py:54
  25.1 0.5 %collective-permute-start.4 = (f32[18,128]{1,0:T(8,128)S(1)}, f32[18,128]{1,0:T(8,128)S(1)}, u32[]{:S(2)}, u32[]{:S(2)}) collective-permute-start(f32[18,128]{1,0:T(8,128)S(1)} %get-tuple-element.44.refs_0_), channel_id=1, source_target_pairs={{8,0},{0,8},{24,16},{16,24},{9,1},{1,9},{25,17},{17,25},{10,2},{2,... | collective-permute-start | bytes 27656 | tf_op jit(solution)/shard_map/ppermute | solution.py:54
  25.6 1.1 %collective-permute-done.6.refs_3_ = f32[18,128]{1,0:T(8,128)S(1)} collective-permute-done((f32[18,128]{1,0:T(8,128)S(1)}, f32[18,128]{1,0:T(8,128)S(1)}, u32[]{:S(2)}, u32[]{:S(2)}) %collective-permute-start.6) | collective-permute-done | bytes 9248 | tf_op jit(solution)/shard_map/ppermute | solution.py:54
  26.7 1.6 %collective-permute-done.5.refs_2_ = f32[18,128]{1,0:T(8,128)S(1)} collective-permute-done((f32[18,128]{1,0:T(8,128)S(1)}, f32[18,128]{1,0:T(8,128)S(1)}, u32[]{:S(2)}, u32[]{:S(2)}) %collective-permute-start.5) | collective-permute-done | bytes 9248 | tf_op jit(solution)/shard_map/ppermute | solution.py:54
  28.3 0.5 %collective-permute-done.4.refs_1_ = f32[18,128]{1,0:T(8,128)S(1)} collective-permute-done((f32[18,128]{1,0:T(8,128)S(1)}, f32[18,128]{1,0:T(8,128)S(1)}, u32[]{:S(2)}, u32[]{:S(2)}) %collective-permute-start.4) | collective-permute-done | bytes 9248 | tf_op jit(solution)/shard_map/ppermute | solution.py:54
  28.8 2.5 %collective-permute-start.8 = (bf16[160,512]{1,0:T(8,128)(2,1)S(1)}, bf16[160,512]{1,0:T(8,128)(2,1)S(1)}, u32[]{:S(2)}, u32[]{:S(2)}) collective-permute-start(bf16[160,512]{1,0:T(8,128)(2,1)S(1)} %get-tuple-element.50), channel_id=1, source_target_pairs={{0,6},{2,4},{4,2},{6,0},{1,7},{3,5},{5,3},{7,1},{8,14},{10,12},{12... | collective-permute-start | bytes 491528 | tf_op jit(solution)/shard_map/ppermute | solution.py:59
  31.3 0.9 %collective-permute-start.9 = (bf16[160,512]{1,0:T(8,128)(2,1)S(1)}, bf16[160,512]{1,0:T(8,128)(2,1)S(1)}, u32[]{:S(2)}, u32[]{:S(2)}) collective-permute-start(bf16[160,512]{1,0:T(8,128)(2,1)S(1)} %get-tuple-element.51), channel_id=1, source_target_pairs={{0,2},{2,0},{4,6},{6,4},{1,3},{3,1},{5,7},{7,5},{8,10},{10,8},{12,... | collective-permute-start | bytes 491528 | tf_op jit(solution)/shard_map/ppermute | solution.py:59
  32.3 1.0 %collective-permute-start.7 = (f32[18,128]{1,0:T(8,128)S(1)}, f32[18,128]{1,0:T(8,128)S(1)}, u32[]{:S(2)}, u32[]{:S(2)}) collective-permute-start(f32[18,128]{1,0:T(8,128)S(1)} %get-tuple-element.47.refs_0_), channel_id=1, source_target_pairs={{0,4},{2,6},{4,0},{6,2},{1,5},{3,7},{5,1},{7,3},{8,12},{10,14},{12... | collective-permute-start | bytes 27656 | tf_op jit(solution)/shard_map/ppermute | solution.py:59
  33.3 0.0 collective-permute-done.3._
  33.3 1.8 %finish.1 = (bf16[128,2048]{1,0:T(8,128)(2,1)}, bf16[128,2048]{1,0:T(8,128)(2,1)}, bf16[128,512]{1,0:T(8,128)(2,1)S(1)}) custom-call(bf16[512,2048]{1,0:T(8,128)(2,1)S(1)} %get-tuple-element.37.probs_ref, bf16[512,2048]{1,0:T(8,128)(2,1)S(1)} %get-tuple-element.38.dscore_ref, ...), custom_call_target="tpu_custom_call", output_to_operand_aliasing={{2}: (4, {})} | custom-call | flops 536870912 | bytes 4194304 | tf_op jit(solution)/shard_map/finish/pallas_call | solution.py:310
  35.1 3.4 %collective-permute-done.7.refs_1_ = f32[18,128]{1,0:T(8,128)S(1)} collective-permute-done((f32[18,128]{1,0:T(8,128)S(1)}, f32[18,128]{1,0:T(8,128)S(1)}, u32[]{:S(2)}, u32[]{:S(2)}) %collective-permute-start.7) | collective-permute-done | bytes 9248 | tf_op jit(solution)/shard_map/ppermute | solution.py:59
  38.4 0.0 collective-permute-done.8.refs_4_
  38.4 0.0 collective-permute-done.9.refs_5_
  38.4 0.7 %collect.1 = (bf16[128,256]{1,0:T(8,128)(2,1)}, bf16[128,256]{1,0:T(8,128)(2,1)}, f32[16,128]{1,0:T(8,128)}, f32[2,128]{1,0:T(2,128)}) custom-call(f32[18,128]{1,0:T(8,128)S(1)} %get-tuple-element.47.refs_0_, f32[18,128]{1,0:T(8,128)S(1)} %collective-permute-done.7.refs_1_, f32[128,512]{1,0:T(8,128)S(1)} %get-tuple-element.48.refs_2_, ...), custom_call_target="tpu_custom_call" | custom-call | flops 262144 | bytes 524288 | tf_op jit(solution)/shard_map/collect/pallas_call | solution.py:330
  (1 shorter events, 0.0 us)
Async XLA Ops:
  1.5 11.0 %collective-permute-start.2 = (bf16[128,512]{1,0:T(8,128)(2,1)S(1)}, bf16[128,512]{1,0:T(8,128)(2,1)S(1)}, u32[]{:S(2)}, u32[]{:S(2)}) collective-permute-start(bf16[128,512]{1,0:T(8,128)(2,1)S(1)} %pad_maximum_fusion.pair_ref.refs_6_), channel_id=1, source_target_pairs={{6,0},{4,2},{2,4},{0,6},{7,1},{5,3},{3,5},{1,7},{14,8},{12,10},{10... | collective-permute-start | bytes 393224 | tf_op jit(solution)/shard_map/ppermute | solution.py:54
  6.6 11.1 %collective-permute-start.1 = (bf16[128,512]{1,0:T(8,128)(2,1)S(1)}, bf16[128,512]{1,0:T(8,128)(2,1)S(1)}, u32[]{:S(2)}, u32[]{:S(2)}) collective-permute-start(bf16[128,512]{1,0:T(8,128)(2,1)S(1)} %pad_maximum_fusion.pair_ref.refs_6_), channel_id=1, source_target_pairs={{4,0},{6,2},{0,4},{2,6},{5,1},{7,3},{1,5},{3,7},{12,8},{14,10},{8,... | collective-permute-start | bytes 393224 | tf_op jit(solution)/shard_map/ppermute | solution.py:54
  6.6 11.1 %collective-permute-start = (bf16[128,512]{1,0:T(8,128)(2,1)S(1)}, bf16[128,512]{1,0:T(8,128)(2,1)S(1)}, u32[]{:S(2)}, u32[]{:S(2)}) collective-permute-start(bf16[128,512]{1,0:T(8,128)(2,1)S(1)} %pad_maximum_fusion.pair_ref.refs_6_), channel_id=1, source_target_pairs={{2,0},{0,2},{6,4},{4,6},{3,1},{1,3},{7,5},{5,7},{10,8},{8,10},{14,... | collective-permute-start | bytes 393224 | tf_op jit(solution)/shard_map/ppermute | solution.py:54
  7.3 1.0 %copy-start = (bf16[1,128,2048]{2,1,0:T(8,128)(2,1)S(1)}, bf16[1,128,2048]{2,1,0:T(8,128)(2,1)}, u32[]{:S(2)}) copy-start(bf16[1,128,2048]{2,1,0:T(8,128)(2,1)} %param.7) | copy-start | bytes 1572868
  8.3 1.0 %copy-start.1 = (bf16[1,128,2048]{2,1,0:T(8,128)(2,1)S(1)}, bf16[1,128,2048]{2,1,0:T(8,128)(2,1)}, u32[]{:S(2)}) copy-start(bf16[1,128,2048]{2,1,0:T(8,128)(2,1)} %param.12) | copy-start | bytes 1572868
  9.4 0.7 %copy-start.2 = (bf16[2048]{0:T(1024)(128)(2,1)S(1)}, bf16[2048]{0:T(1024)(128)(2,1)}, u32[]{:S(2)}) copy-start(bf16[2048]{0:T(1024)(128)(2,1)} %param.8) | copy-start | bytes 12292
  10.0 0.7 %copy-start.3 = (s32[1,8]{1,0:T(1,128)S(1)}, s32[1,8]{1,0:T(1,128)}, u32[]{:S(2)}) copy-start(s32[1,8]{1,0:T(1,128)} %len_ref.1) | copy-start | bytes 100
  10.7 0.7 %copy-start.4 = (bf16[256]{0:T(256)(128)(2,1)S(1)}, bf16[256]{0:T(256)(128)(2,1)}, u32[]{:S(2)}) copy-start(bf16[256]{0:T(256)(128)(2,1)} %param.11) | copy-start | bytes 1540
  22.0 11.3 %collective-permute-start.3 = (bf16[128,512]{1,0:T(8,128)(2,1)S(1)}, bf16[128,512]{1,0:T(8,128)(2,1)S(1)}, u32[]{:S(2)}, u32[]{:S(2)}) collective-permute-start(bf16[128,512]{1,0:T(8,128)(2,1)S(1)} %get-tuple-element.41), channel_id=1, source_target_pairs={{0,4},{2,6},{4,0},{6,2},{1,5},{3,7},{5,1},{7,3},{8,12},{10,14},{12... | collective-permute-start | bytes 393224 | tf_op jit(solution)/shard_map/ppermute | solution.py:59
  22.0 4.7 %collective-permute-start.6 = (f32[18,128]{1,0:T(8,128)S(1)}, f32[18,128]{1,0:T(8,128)S(1)}, u32[]{:S(2)}, u32[]{:S(2)}) collective-permute-start(f32[18,128]{1,0:T(8,128)S(1)} %get-tuple-element.44.refs_0_), channel_id=1, source_target_pairs={{24,0},{16,8},{8,16},{0,24},{25,1},{17,9},{9,17},{1,25},{26,2},{18... | collective-permute-start | bytes 27656 | tf_op jit(solution)/shard_map/ppermute | solution.py:54
  24.6 3.7 %collective-permute-start.5 = (f32[18,128]{1,0:T(8,128)S(1)}, f32[18,128]{1,0:T(8,128)S(1)}, u32[]{:S(2)}, u32[]{:S(2)}) collective-permute-start(f32[18,128]{1,0:T(8,128)S(1)} %get-tuple-element.44.refs_0_), channel_id=1, source_target_pairs={{16,0},{24,8},{0,16},{8,24},{17,1},{25,9},{1,17},{9,25},{18,2},{26... | collective-permute-start | bytes 27656 | tf_op jit(solution)/shard_map/ppermute | solution.py:54
  25.1 3.7 %collective-permute-start.4 = (f32[18,128]{1,0:T(8,128)S(1)}, f32[18,128]{1,0:T(8,128)S(1)}, u32[]{:S(2)}, u32[]{:S(2)}) collective-permute-start(f32[18,128]{1,0:T(8,128)S(1)} %get-tuple-element.44.refs_0_), channel_id=1, source_target_pairs={{8,0},{0,8},{24,16},{16,24},{9,1},{1,9},{25,17},{17,25},{10,2},{2,... | collective-permute-start | bytes 27656 | tf_op jit(solution)/shard_map/ppermute | solution.py:54
  28.8 9.7 %collective-permute-start.8 = (bf16[160,512]{1,0:T(8,128)(2,1)S(1)}, bf16[160,512]{1,0:T(8,128)(2,1)S(1)}, u32[]{:S(2)}, u32[]{:S(2)}) collective-permute-start(bf16[160,512]{1,0:T(8,128)(2,1)S(1)} %get-tuple-element.50), channel_id=1, source_target_pairs={{0,6},{2,4},{4,2},{6,0},{1,7},{3,5},{5,3},{7,1},{8,14},{10,12},{12... | collective-permute-start | bytes 491528 | tf_op jit(solution)/shard_map/ppermute | solution.py:59
  31.3 7.1 %collective-permute-start.9 = (bf16[160,512]{1,0:T(8,128)(2,1)S(1)}, bf16[160,512]{1,0:T(8,128)(2,1)S(1)}, u32[]{:S(2)}, u32[]{:S(2)}) collective-permute-start(bf16[160,512]{1,0:T(8,128)(2,1)S(1)} %get-tuple-element.51), channel_id=1, source_target_pairs={{0,2},{2,0},{4,6},{6,4},{1,3},{3,1},{5,7},{7,5},{8,10},{10,8},{12,... | collective-permute-start | bytes 491528 | tf_op jit(solution)/shard_map/ppermute | solution.py:59
  32.3 6.2 %collective-permute-start.7 = (f32[18,128]{1,0:T(8,128)S(1)}, f32[18,128]{1,0:T(8,128)S(1)}, u32[]{:S(2)}, u32[]{:S(2)}) collective-permute-start(f32[18,128]{1,0:T(8,128)S(1)} %get-tuple-element.47.refs_0_), channel_id=1, source_target_pairs={{0,4},{2,6},{4,0},{6,2},{1,5},{3,7},{5,1},{7,3},{8,12},{10,14},{12... | collective-permute-start | bytes 27656 | tf_op jit(solution)/shard_map/ppermute | solution.py:59

commit v13 on v10

--- a/solution.py
+++ b/solution.py
@@ -41,6 +41,22 @@
 
 def biased(values, bias):
     return (values.astype(jnp.float32) + bias.astype(jnp.float32)).astype(jnp.bfloat16)
+
+
+def source_of(rank, slot, size):
+    if size & (size - 1):
+        return (rank + size - slot) % size
+    return rank ^ slot
+
+
+def fetch(array, axis, slot):
+    size = lax.axis_size(axis)
+    return lax.ppermute(array, axis, [(source_of(i, slot, size), i) for i in range(size)])
+
+
+def send_back(array, slot):
+    size = lax.axis_size("ctx")
+    return lax.ppermute(array, "ctx", [(i, source_of(i, slot, size)) for i in range(size)])
 
 
 def prepare_kernel(
@@ -59,7 +75,7 @@
         start = start + jnp.where(query_pos >= end, length, 0)
     offsets = lax.broadcasted_iota(jnp.int32, (tok, tok), 0)
     for slot in range(slots):
-        key_pos = (rank - slot) * tok + offsets
+        key_pos = source_of(rank, slot, slots) * tok + offsets
         live = (key_pos >= start) & (key_pos <= query_pos)
         live_ref[slot * tok : (slot + 1) * tok, :] = jnp.where(live, 0.0, NEGATIVE)
     bias_ref[...] = vb_ref[...]
@@ -79,7 +95,7 @@
 
 def attend_kernel(slots, *refs):
     bias_ref, queries_ref, grads_ref, score_ref, dprob_ref, live_ref = refs[:6]
-    pair_refs = refs[6 : 6 + slots][::-1]
+    pair_refs = refs[6 : 6 + slots]
     refs = refs[6 + slots :]
     probs_ref, dscore_ref, keys_ref, values_ref, sums_ref, own_ref = refs[:6]
     out_refs = refs[6 : 6 + slots - 1]
@@ -211,17 +227,8 @@
     return total, passed
 
 
-def send_back(term, shift):
-    size = lax.axis_size("ctx")
-    return lax.ppermute(term, "ctx", [(i, (i - shift) % size) for i in range(size)])
-
-
 def exchange(axis, part):
-    size = lax.axis_size(axis)
-    return [part] + [
-        lax.ppermute(part, axis, [(i, (i + shift) % size) for i in range(size)])
-        for shift in range(1, size)
-    ]
+    return [part] + [fetch(part, axis, slot) for slot in range(1, lax.axis_size(axis))]
 
 
 def shards(q_proj, q_bias, k_proj, v_proj, v_bias, dout, lengths):
@@ -234,10 +241,7 @@
     rows = ctx * tok
     columns = heads * tok
     pair = jnp.concatenate([k_proj[0], v_proj[0]], axis=1)
-    pairs = [
-        lax.ppermute(pair, "ctx", [(i, (i + shift) % ctx) for i in range(ctx)])
-        for shift in range(ctx - 1, 0, -1)
-    ] + [pair]
+    pairs = [pair] + [fetch(pair, "ctx", slot) for slot in range(1, ctx)]
     prepared = pl.pallas_call(
         functools.partial(prepare_kernel, ctx),
         out_shape=[
@@ -303,10 +307,13 @@
         ),
         name="finish",
     )(probs, dscore, all_keys, all_values)
-    early = -(-len(terms) // 2)
-    back = [send_back(term, shift) for shift, term in enumerate(terms[:early], 1)]
-    sums, (back[0], *terms) = total_between(exchange("dp", sums), [back[0], *terms[early:]])
-    back += [send_back(term, shift) for shift, term in enumerate(terms, early + 1)]
+    half = ctx // 2
+    back = {slot: send_back(terms[slot - 1], slot) for slot in range(half, ctx)}
+    sums, (back[half], *terms) = total_between(
+        exchange("dp", sums), [back[half], *terms[: half - 1]]
+    )
+    back.update({slot: send_back(term, slot) for slot, term in enumerate(terms, 1)})
+    back = [back[slot] for slot in sorted(back)]
     sums = exchange("ctx", sums)
     k_grad, v_grad, q_sum, v_sum = pl.pallas_call(
         functools.partial(collect_kernel, batches, len(sums), len(back)),

time: 42.4 us -> 41.3 us (0.974)
  starting transfers between devices: 19.8 us -> 16.3 us
  waiting for transfers between devices: 8.83 us -> 11.1 us
    ppermute x12, starting transfers between devices: 19.8 us -> 16.3 us  [the longest x9 13.8 us: fetch(): lax.ppermute(array, axis, [(source_of(i, slot, size), i) for i in range(s...]
    ppermute x12, waiting for transfers between devices: 8.83 us -> 11.1 us  [the longest x9 6.83 us: fetch(): lax.ppermute(array, axis, [(source_of(i, slot, size), i) for i in range(s...]
where the time goes in v13:
time: 41.3 us; the launch traced here: 41 us
  starting transfers between devices  16.3 us (39%)
  waiting for transfers between devices  11.1 us (27%)
  Pallas kernels  7.85 us (19%)
  local copies, waits for them, and re-layouts  4.08 us (10%)
  other arithmetic  0.88 us (2%)
  between operations  0.69 us (2%)
    ppermute x9, starting transfers between devices, fetch(): lax.ppermute(array, axis, [(source_of(i, slot, size), i) for i in range(s...  13.8 us
    ppermute x9, waiting for transfers between devices, fetch(): lax.ppermute(array, axis, [(source_of(i, slot, size), i) for i in range(s...  6.83 us
    ppermute x3, waiting for transfers between devices, send_back(): lax.ppermute(array, 'ctx', [(i, source_of(i, slot, size)) for i in range(...  4.32 us
    pallas_call x1, Pallas kernels, shards(): pl.pallas_call(functools.partial(attend_kernel, ctx), out_shape=[shape((r...  4.24 us
    unnamed x10, local copies, waits for them, and re-layouts  4.08 us
    ppermute x3, starting transfers between devices, send_back(): lax.ppermute(array, 'ctx', [(i, source_of(i, slot, size)) for i in range(...  2.56 us
    pallas_call x1, Pallas kernels, shards(): pl.pallas_call(finish_kernel, out_shape=[shape((tok, width), jnp.bfloat16...  1.79 us
    pallas_call x1, Pallas kernels, shards(): pl.pallas_call(functools.partial(prepare_kernel, ctx), out_shape=[shape((...  1.11 us
  transfers between devices with their start and end apart: 12, of which 5 were waited for; matrix products, arithmetic and copies ran while one was open for 0% of the time, Pallas kernels for 7%

profile of v13, /device:TPU:0, one launch (start us, length us, event | category | flops | bytes accessed | tf_op | source)
XLA Modules:
  0.0 41.0 jit_solution(6512093210011531043)
XLA Ops:
  0.6 0.9 %pad_maximum_fusion.pair_ref.refs_6_ = bf16[128,512]{1,0:T(8,128)(2,1)S(1)} fusion(bf16[128,256]{1,0:T(8,128)(2,1)} %bitcast.16, bf16[128,256]{1,0:T(8,128)(2,1)} %bitcast.17), kind=kLoop, calls=%fused_computation | loop fusion | flops 262144 | bytes 262144 | tf_op jit(solution)/shard_map/concatenate | solution.py:243
  1.5 5.1 %collective-permute-start.2 = (bf16[128,512]{1,0:T(8,128)(2,1)S(1)}, bf16[128,512]{1,0:T(8,128)(2,1)S(1)}, u32[]{:S(2)}, u32[]{:S(2)}) collective-permute-start(bf16[128,512]{1,0:T(8,128)(2,1)S(1)} %pad_maximum_fusion.pair_ref.refs_6_), channel_id=1, source_target_pairs={{6,0},{4,2},{2,4},{0,6},{7,1},{5,3},{3,5},{1,7},{14,8},{12,10},{10... | collective-permute-start | bytes 393224 | tf_op jit(solution)/shard_map/ppermute | solution.py:54
  6.6 0.0 collective-permute-start.1
  6.6 0.6 %collective-permute-start = (bf16[128,512]{1,0:T(8,128)(2,1)S(1)}, bf16[128,512]{1,0:T(8,128)(2,1)S(1)}, u32[]{:S(2)}, u32[]{:S(2)}) collective-permute-start(bf16[128,512]{1,0:T(8,128)(2,1)S(1)} %pad_maximum_fusion.pair_ref.refs_6_), channel_id=1, source_target_pairs={{2,0},{0,2},{6,4},{4,6},{3,1},{1,3},{7,5},{5,7},{10,8},{8,10},{14,... | collective-permute-start | bytes 393224 | tf_op jit(solution)/shard_map/ppermute | solution.py:54
  7.3 0.0 copy-start
  7.3 1.0 %copy-done = bf16[1,128,2048]{2,1,0:T(8,128)(2,1)S(1)} copy-done((bf16[1,128,2048]{2,1,0:T(8,128)(2,1)S(1)}, bf16[1,128,2048]{2,1,0:T(8,128)(2,1)}, u32[]{:S(2)}) %copy-start) | copy-done | bytes 524312
  8.3 0.0 copy-start.1
  8.3 1.0 %copy-done.1 = bf16[1,128,2048]{2,1,0:T(8,128)(2,1)S(1)} copy-done((bf16[1,128,2048]{2,1,0:T(8,128)(2,1)S(1)}, bf16[1,128,2048]{2,1,0:T(8,128)(2,1)}, u32[]{:S(2)}) %copy-start.1) | copy-done | bytes 524312
  9.4 0.0 copy-start.2
  9.4 0.7 %copy-done.2 = bf16[2048]{0:T(1024)(128)(2,1)S(1)} copy-done((bf16[2048]{0:T(1024)(128)(2,1)S(1)}, bf16[2048]{0:T(1024)(128)(2,1)}, u32[]{:S(2)}) %copy-start.2) | copy-done | bytes 4120
  10.0 0.0 copy-start.3
  10.0 0.7 %copy-done.3 = s32[1,8]{1,0:T(1,128)S(1)} copy-done((s32[1,8]{1,0:T(1,128)S(1)}, s32[1,8]{1,0:T(1,128)}, u32[]{:S(2)}) %copy-start.3) | copy-done | bytes 56
  10.7 0.0 copy-start.4
  10.7 0.7 %copy-done.4 = bf16[256]{0:T(256)(128)(2,1)S(1)} copy-done((bf16[256]{0:T(256)(128)(2,1)S(1)}, bf16[256]{0:T(256)(128)(2,1)}, u32[]{:S(2)}) %copy-start.4) | copy-done | bytes 536
  11.4 1.1 %prepare.1 = (bf16[2,128]{1,0:T(2,128)(2,1)S(1)}, bf16[2048,256]{1,0:T(8,128)(2,1)S(1)}, bf16[2048,128]{1,0:T(8,128)(2,1)S(1)}, f32[128,2048]{1,0:T(8,128)S(1)},...) custom-call(s32[1,8]{1,0:T(1,128)S(1)} %copy-done.3, bf16[128,512]{1,0:T(8,128)(2,1)S(1)} %pad_maximum_fusion.pair_ref.refs_6_, ...), custom_call_target="tpu_custom_call" | custom-call | flops 134217728 | bytes 4194304 | tf_op jit(solution)/shard_map/prepare/pallas_call | solution.py:245
  12.5 0.0 collective-permute-done.2.refs_9_
  12.5 5.2 %collective-permute-done.1.refs_8_ = bf16[128,512]{1,0:T(8,128)(2,1)S(1)} collective-permute-done((bf16[128,512]{1,0:T(8,128)(2,1)S(1)}, bf16[128,512]{1,0:T(8,128)(2,1)S(1)}, u32[]{:S(2)}, u32[]{:S(2)}) %collective-permute-start.1) | collective-permute-done | bytes 131104 | tf_op jit(solution)/shard_map/ppermute | solution.py:54
  17.7 0.0 collective-permute-done.refs_7_
  17.7 4.2 %attend.1 = (bf16[512,2048]{1,0:T(8,128)(2,1)S(1)}, bf16[512,2048]{1,0:T(8,128)(2,1)S(1)}, bf16[512,256]{1,0:T(8,128)(2,1)S(1)}, bf16[512,256]{1,0:T(8,128)(2,1)...) custom-call(bf16[2,128]{1,0:T(2,128)(2,1)S(1)} %get-tuple-element.30, ...), custom_call_target="tpu_custom_call" | custom-call | flops 1073741824 | bytes 4194304 | tf_op jit(solution)/shard_map/attend/pallas_call | solution.py:271
  22.0 0.1 collective-permute-start.6
  22.0 2.5 %collective-permute-start.5 = (f32[18,128]{1,0:T(8,128)S(1)}, f32[18,128]{1,0:T(8,128)S(1)}, u32[]{:S(2)}, u32[]{:S(2)}) collective-permute-start(f32[18,128]{1,0:T(8,128)S(1)} %get-tuple-element.42.refs_0_), channel_id=1, source_target_pairs={{24,0},{16,8},{8,16},{0,24},{25,1},{17,9},{9,17},{1,25},{26,2},{18... | collective-permute-start | bytes 27656 | tf_op jit(solution)/shard_map/ppermute | solution.py:54
  24.6 0.5 %collective-permute-start.4 = (f32[18,128]{1,0:T(8,128)S(1)}, f32[18,128]{1,0:T(8,128)S(1)}, u32[]{:S(2)}, u32[]{:S(2)}) collective-permute-start(f32[18,128]{1,0:T(8,128)S(1)} %get-tuple-element.42.refs_0_), channel_id=1, source_target_pairs={{16,0},{24,8},{0,16},{8,24},{17,1},{25,9},{1,17},{9,25},{18,2},{26... | collective-permute-start | bytes 27656 | tf_op jit(solution)/shard_map/ppermute | solution.py:54
  25.1 0.5 %collective-permute-start.3 = (f32[18,128]{1,0:T(8,128)S(1)}, f32[18,128]{1,0:T(8,128)S(1)}, u32[]{:S(2)}, u32[]{:S(2)}) collective-permute-start(f32[18,128]{1,0:T(8,128)S(1)} %get-tuple-element.42.refs_0_), channel_id=1, source_target_pairs={{8,0},{0,8},{24,16},{16,24},{9,1},{1,9},{25,17},{17,25},{10,2},{2,... | collective-permute-start | bytes 27656 | tf_op jit(solution)/shard_map/ppermute | solution.py:54
  25.6 2.5 %collective-permute-start.11 = (bf16[128,512]{1,0:T(8,128)(2,1)S(1)}, bf16[128,512]{1,0:T(8,128)(2,1)S(1)}, u32[]{:S(2)}, u32[]{:S(2)}) collective-permute-start(bf16[128,512]{1,0:T(8,128)(2,1)S(1)} %get-tuple-element.49), channel_id=1, source_target_pairs={{0,6},{2,4},{4,2},{6,0},{1,7},{3,5},{5,3},{7,1},{8,14},{10,12},{12... | collective-permute-start | bytes 393224 | tf_op jit(solution)/shard_map/ppermute | solution.py:59
  28.1 0.0 collective-permute-done.5.refs_3_
  28.1 0.2 collective-permute-done.4.refs_2_
  28.3 0.5 %collective-permute-done.3.refs_1_ = f32[18,128]{1,0:T(8,128)S(1)} collective-permute-done((f32[18,128]{1,0:T(8,128)S(1)}, f32[18,128]{1,0:T(8,128)S(1)}, u32[]{:S(2)}, u32[]{:S(2)}) %collective-permute-start.3) | collective-permute-done | bytes 9248 | tf_op jit(solution)/shard_map/ppermute | solution.py:54
  28.8 4.3 %collective-permute-done.6.refs_4_ = bf16[128,512]{1,0:T(8,128)(2,1)S(1)} collective-permute-done((bf16[128,512]{1,0:T(8,128)(2,1)S(1)}, bf16[128,512]{1,0:T(8,128)(2,1)S(1)}, u32[]{:S(2)}, u32[]{:S(2)}) %collective-permute-start.6) | collective-permute-done | bytes 131104 | tf_op jit(solution)/shard_map/ppermute | solution.py:59
  33.1 0.0 collective-permute-start.10
  33.1 0.9 %collective-permute-start.9 = (f32[18,128]{1,0:T(8,128)S(1)}, f32[18,128]{1,0:T(8,128)S(1)}, u32[]{:S(2)}, u32[]{:S(2)}) collective-permute-start(f32[18,128]{1,0:T(8,128)S(1)} %get-tuple-element.45.refs_0_), channel_id=1, source_target_pairs={{6,0},{4,2},{2,4},{0,6},{7,1},{5,3},{3,5},{1,7},{14,8},{12,10},{10... | collective-permute-start | bytes 27656 | tf_op jit(solution)/shard_map/ppermute | solution.py:54
  33.9 2.6 %collective-permute-start.8 = (f32[18,128]{1,0:T(8,128)S(1)}, f32[18,128]{1,0:T(8,128)S(1)}, u32[]{:S(2)}, u32[]{:S(2)}) collective-permute-start(f32[18,128]{1,0:T(8,128)S(1)} %get-tuple-element.45.refs_0_), channel_id=1, source_target_pairs={{4,0},{6,2},{0,4},{2,6},{5,1},{7,3},{1,5},{3,7},{12,8},{14,10},{8,... | collective-permute-start | bytes 27656 | tf_op jit(solution)/shard_map/ppermute | solution.py:54
  36.6 1.0 %collective-permute-start.7 = (f32[18,128]{1,0:T(8,128)S(1)}, f32[18,128]{1,0:T(8,128)S(1)}, u32[]{:S(2)}, u32[]{:S(2)}) collective-permute-start(f32[18,128]{1,0:T(8,128)S(1)} %get-tuple-element.45.refs_0_), channel_id=1, source_target_pairs={{2,0},{0,2},{6,4},{4,6},{3,1},{1,3},{7,5},{5,7},{10,8},{8,10},{14,... | collective-permute-start | bytes 27656 | tf_op jit(solution)/shard_map/ppermute | solution.py:54
  37.5 1.8 %finish.1 = (bf16[128,2048]{1,0:T(8,128)(2,1)}, bf16[128,2048]{1,0:T(8,128)(2,1)}) custom-call(bf16[512,2048]{1,0:T(8,128)(2,1)S(1)} %get-tuple-element.36.probs_ref, bf16[512,2048]{1,0:T(8,128)(2,1)S(1)} %get-tuple-element.37.dscore_ref, bf16[512,256]{1,0:T(8,128)(2,1)S(1)} %get-tuple-element.38.keys_ref, bf16[512,256]{1,0:T(8,128)(2,1)S(1)} %get-tuple-element.39.values_ref), custom_call_target="tpu_custom_call" | custom-call | flops 536870912 | bytes 4194304 | tf_op jit(solution)/shard_map/finish/pallas_call | solution.py:296
  39.3 0.0 collective-permute-done.11.refs_7_
  39.3 0.0 collective-permute-done.9.refs_3_
  39.3 0.0 collective-permute-done.8.refs_2_
  39.3 0.9 %collective-permute-done.7.refs_1_ = f32[18,128]{1,0:T(8,128)S(1)} collective-permute-done((f32[18,128]{1,0:T(8,128)S(1)}, f32[18,128]{1,0:T(8,128)S(1)}, u32[]{:S(2)}, u32[]{:S(2)}) %collective-permute-start.7) | collective-permute-done | bytes 9248 | tf_op jit(solution)/shard_map/ppermute | solution.py:54
  40.3 0.0 collective-permute-done.10.refs_5_
  40.3 0.7 %collect.1 = (bf16[128,256]{1,0:T(8,128)(2,1)}, bf16[128,256]{1,0:T(8,128)(2,1)}, f32[16,128]{1,0:T(8,128)}, f32[2,128]{1,0:T(2,128)}) custom-call(f32[18,128]{1,0:T(8,128)S(1)} %get-tuple-element.45.refs_0_, f32[18,128]{1,0:T(8,128)S(1)} %collective-permute-done.7.refs_1_, f32[18,128]{1,0:T(8,128)S(1)} %collective-permute-done.8.refs_2_, ...), custom_call_target="tpu_custom_call" | custom-call | flops 262144 | bytes 524288 | tf_op jit(solution)/shard_map/collect/pallas_call | solution.py:318
  (1 shorter events, 0.0 us)
Async XLA Ops:
  1.5 11.0 %collective-permute-start.2 = (bf16[128,512]{1,0:T(8,128)(2,1)S(1)}, bf16[128,512]{1,0:T(8,128)(2,1)S(1)}, u32[]{:S(2)}, u32[]{:S(2)}) collective-permute-start(bf16[128,512]{1,0:T(8,128)(2,1)S(1)} %pad_maximum_fusion.pair_ref.refs_6_), channel_id=1, source_target_pairs={{6,0},{4,2},{2,4},{0,6},{7,1},{5,3},{3,5},{1,7},{14,8},{12,10},{10... | collective-permute-start | bytes 393224 | tf_op jit(solution)/shard_map/ppermute | solution.py:54
  6.6 11.1 %collective-permute-start.1 = (bf16[128,512]{1,0:T(8,128)(2,1)S(1)}, bf16[128,512]{1,0:T(8,128)(2,1)S(1)}, u32[]{:S(2)}, u32[]{:S(2)}) collective-permute-start(bf16[128,512]{1,0:T(8,128)(2,1)S(1)} %pad_maximum_fusion.pair_ref.refs_6_), channel_id=1, source_target_pairs={{4,0},{6,2},{0,4},{2,6},{5,1},{7,3},{1,5},{3,7},{12,8},{14,10},{8,... | collective-permute-start | bytes 393224 | tf_op jit(solution)/shard_map/ppermute | solution.py:54
  6.6 11.1 %collective-permute-start = (bf16[128,512]{1,0:T(8,128)(2,1)S(1)}, bf16[128,512]{1,0:T(8,128)(2,1)S(1)}, u32[]{:S(2)}, u32[]{:S(2)}) collective-permute-start(bf16[128,512]{1,0:T(8,128)(2,1)S(1)} %pad_maximum_fusion.pair_ref.refs_6_), channel_id=1, source_target_pairs={{2,0},{0,2},{6,4},{4,6},{3,1},{1,3},{7,5},{5,7},{10,8},{8,10},{14,... | collective-permute-start | bytes 393224 | tf_op jit(solution)/shard_map/ppermute | solution.py:54
  7.3 1.0 %copy-start = (bf16[1,128,2048]{2,1,0:T(8,128)(2,1)S(1)}, bf16[1,128,2048]{2,1,0:T(8,128)(2,1)}, u32[]{:S(2)}) copy-start(bf16[1,128,2048]{2,1,0:T(8,128)(2,1)} %param.7) | copy-start | bytes 1572868
  8.3 1.0 %copy-start.1 = (bf16[1,128,2048]{2,1,0:T(8,128)(2,1)S(1)}, bf16[1,128,2048]{2,1,0:T(8,128)(2,1)}, u32[]{:S(2)}) copy-start(bf16[1,128,2048]{2,1,0:T(8,128)(2,1)} %param.12) | copy-start | bytes 1572868
  9.4 0.7 %copy-start.2 = (bf16[2048]{0:T(1024)(128)(2,1)S(1)}, bf16[2048]{0:T(1024)(128)(2,1)}, u32[]{:S(2)}) copy-start(bf16[2048]{0:T(1024)(128)(2,1)} %param.8) | copy-start | bytes 12292
  10.0 0.7 %copy-start.3 = (s32[1,8]{1,0:T(1,128)S(1)}, s32[1,8]{1,0:T(1,128)}, u32[]{:S(2)}) copy-start(s32[1,8]{1,0:T(1,128)} %len_ref.1) | copy-start | bytes 100
  10.7 0.7 %copy-start.4 = (bf16[256]{0:T(256)(128)(2,1)S(1)}, bf16[256]{0:T(256)(128)(2,1)}, u32[]{:S(2)}) copy-start(bf16[256]{0:T(256)(128)(2,1)} %param.11) | copy-start | bytes 1540
  22.0 11.1 %collective-permute-start.6 = (bf16[128,512]{1,0:T(8,128)(2,1)S(1)}, bf16[128,512]{1,0:T(8,128)(2,1)S(1)}, u32[]{:S(2)}, u32[]{:S(2)}) collective-permute-start(bf16[128,512]{1,0:T(8,128)(2,1)S(1)} %get-tuple-element.43), channel_id=1, source_target_pairs={{0,4},{2,6},{4,0},{6,2},{1,5},{3,7},{5,1},{7,3},{8,12},{10,14},{12... | collective-permute-start | bytes 393224 | tf_op jit(solution)/shard_map/ppermute | solution.py:59
  22.0 6.0 %collective-permute-start.5 = (f32[18,128]{1,0:T(8,128)S(1)}, f32[18,128]{1,0:T(8,128)S(1)}, u32[]{:S(2)}, u32[]{:S(2)}) collective-permute-start(f32[18,128]{1,0:T(8,128)S(1)} %get-tuple-element.42.refs_0_), channel_id=1, source_target_pairs={{24,0},{16,8},{8,16},{0,24},{25,1},{17,9},{9,17},{1,25},{26,2},{18... | collective-permute-start | bytes 27656 | tf_op jit(solution)/shard_map/ppermute | solution.py:54
  24.6 3.7 %collective-permute-start.4 = (f32[18,128]{1,0:T(8,128)S(1)}, f32[18,128]{1,0:T(8,128)S(1)}, u32[]{:S(2)}, u32[]{:S(2)}) collective-permute-start(f32[18,128]{1,0:T(8,128)S(1)} %get-tuple-element.42.refs_0_), channel_id=1, source_target_pairs={{16,0},{24,8},{0,16},{8,24},{17,1},{25,9},{1,17},{9,25},{18,2},{26... | collective-permute-start | bytes 27656 | tf_op jit(solution)/shard_map/ppermute | solution.py:54
  25.1 3.7 %collective-permute-start.3 = (f32[18,128]{1,0:T(8,128)S(1)}, f32[18,128]{1,0:T(8,128)S(1)}, u32[]{:S(2)}, u32[]{:S(2)}) collective-permute-start(f32[18,128]{1,0:T(8,128)S(1)} %get-tuple-element.42.refs_0_), channel_id=1, source_target_pairs={{8,0},{0,8},{24,16},{16,24},{9,1},{1,9},{25,17},{17,25},{10,2},{2,... | collective-permute-start | bytes 27656 | tf_op jit(solution)/shard_map/ppermute | solution.py:54
  25.6 13.7 %collective-permute-start.11 = (bf16[128,512]{1,0:T(8,128)(2,1)S(1)}, bf16[128,512]{1,0:T(8,128)(2,1)S(1)}, u32[]{:S(2)}, u32[]{:S(2)}) collective-permute-start(bf16[128,512]{1,0:T(8,128)(2,1)S(1)} %get-tuple-element.49), channel_id=1, source_target_pairs={{0,6},{2,4},{4,2},{6,0},{1,7},{3,5},{5,3},{7,1},{8,14},{10,12},{12... | collective-permute-start | bytes 393224 | tf_op jit(solution)/shard_map/ppermute | solution.py:59
  33.1 7.2 %collective-permute-start.10 = (bf16[128,512]{1,0:T(8,128)(2,1)S(1)}, bf16[128,512]{1,0:T(8,128)(2,1)S(1)}, u32[]{:S(2)}, u32[]{:S(2)}) collective-permute-start(bf16[128,512]{1,0:T(8,128)(2,1)S(1)} %get-tuple-element.47), channel_id=1, source_target_pairs={{0,2},{2,0},{4,6},{6,4},{1,3},{3,1},{5,7},{7,5},{8,10},{10,8},{12,... | collective-permute-start | bytes 393224 | tf_op jit(solution)/shard_map/ppermute | solution.py:59
  33.1 6.3 %collective-permute-start.9 = (f32[18,128]{1,0:T(8,128)S(1)}, f32[18,128]{1,0:T(8,128)S(1)}, u32[]{:S(2)}, u32[]{:S(2)}) collective-permute-start(f32[18,128]{1,0:T(8,128)S(1)} %get-tuple-element.45.refs_0_), channel_id=1, source_target_pairs={{6,0},{4,2},{2,4},{0,6},{7,1},{5,3},{3,5},{1,7},{14,8},{12,10},{10... | collective-permute-start | bytes 27656 | tf_op jit(solution)/shard_map/ppermute | solution.py:54
  33.9 5.4 %collective-permute-start.8 = (f32[18,128]{1,0:T(8,128)S(1)}, f32[18,128]{1,0:T(8,128)S(1)}, u32[]{:S(2)}, u32[]{:S(2)}) collective-permute-start(f32[18,128]{1,0:T(8,128)S(1)} %get-tuple-element.45.refs_0_), channel_id=1, source_target_pairs={{4,0},{6,2},{0,4},{2,6},{5,1},{7,3},{1,5},{3,7},{12,8},{14,10},{8,... | collective-permute-start | bytes 27656 | tf_op jit(solution)/shard_map/ppermute | solution.py:54
  36.6 3.7 %collective-permute-start.7 = (f32[18,128]{1,0:T(8,128)S(1)}, f32[18,128]{1,0:T(8,128)S(1)}, u32[]{:S(2)}, u32[]{:S(2)}) collective-permute-start(f32[18,128]{1,0:T(8,128)S(1)} %get-tuple-element.45.refs_0_), channel_id=1, source_target_pairs={{2,0},{0,2},{6,4},{4,6},{3,1},{1,3},{7,5},{5,7},{10,8},{8,10},{14,... | collective-permute-start | bytes 27656 | tf_op jit(solution)/shard_map/ppermute | solution.py:54

commit v14 on v12

--- a/solution.py
+++ b/solution.py
@@ -47,6 +47,10 @@
     if size & (size - 1):
         return (rank + size - slot) % size
     return rank ^ slot
+
+
+def slot_order(size):
+    return [slot for slot in range(size) if slot != size // 2] + [size // 2]
 
 
 def fetch(array, axis, slot):
@@ -74,10 +78,10 @@
         end = end + length
         start = start + jnp.where(query_pos >= end, length, 0)
     offsets = lax.broadcasted_iota(jnp.int32, (tok, tok), 0)
-    for slot in range(slots):
+    for index, slot in enumerate(slot_order(slots)):
         key_pos = source_of(rank, slot, slots) * tok + offsets
         live = (key_pos >= start) & (key_pos <= query_pos)
-        live_ref[slot * tok : (slot + 1) * tok, :] = jnp.where(live, 0.0, NEGATIVE)
+        live_ref[index * tok : (index + 1) * tok, :] = jnp.where(live, 0.0, NEGATIVE)
     bias_ref[...] = vb_ref[...]
     column = lax.broadcasted_iota(jnp.int32, (tok, HEAD_DIM), 1)
     for kv_head in range(kv_heads):
@@ -93,56 +97,113 @@
         dprob_ref[:, rows] = dot(values, grads_ref[rows, :], 1, 1)
 
 
-def attend_kernel(slots, *refs):
-    bias_ref, queries_ref, grads_ref, score_ref, dprob_ref, live_ref = refs[:6]
-    pair_refs = refs[6 : 6 + slots]
-    refs = refs[6 + slots :]
-    probs_ref, dscore_ref, keys_ref, values_ref, sums_ref, own_ref = refs[:6]
-    out_refs = refs[6 : 6 + slots - 1]
-    weights_ref, all_dprob_ref = refs[6 + slots - 1 :]
+def over_rows(array, reduce):
+    return reduce(array.reshape(-1, 8, array.shape[-1]), axis=0)
+
+
+def unpack(pair_ref, bias_ref, keys_ref, values_ref, rows):
+    kv_heads = bias_ref.shape[0]
+    keys_ref[rows, :] = pair_ref[:, : kv_heads * HEAD_DIM]
+    for kv_head in range(kv_heads):
+        values_ref[rows, head_cols(kv_head)] = biased(
+            pair_ref[:, head_cols(kv_heads + kv_head)], bias_ref[kv_head : kv_head + 1, :]
+        )
+
+
+def near_kernel(
+    bias_ref, queries_ref, grads_ref, score_ref, own_dprob_ref, live_ref, *refs
+):
+    pair_refs, (weights_ref, dprob_ref, stats_ref, keys_ref, values_ref) = refs[:-5], refs[-5:]
     tok = pair_refs[0].shape[0]
-    kv_heads = bias_ref.shape[0]
-    kv_width = kv_heads * HEAD_DIM
-    heads = kv_heads * GROUP
-    for slot in range(slots):
-        rows = slice(slot * tok, (slot + 1) * tok)
-        keys_ref[rows, :] = pair_refs[slot][:, :kv_width]
-        for kv_head in range(kv_heads):
-            values_ref[rows, head_cols(kv_head)] = biased(
-                pair_refs[slot][:, head_cols(kv_heads + kv_head)], bias_ref[kv_head : kv_head + 1, :]
-            )
-    blocks = [slice(row, row + BLOCK) for row in range(0, slots * tok, BLOCK)]
-    for kv_head in range(kv_heads):
+    for index, pair_ref in enumerate(pair_refs):
+        unpack(pair_ref, bias_ref, keys_ref, values_ref, slice(index * tok, (index + 1) * tok))
+    blocks = [slice(row, row + BLOCK) for row in range(0, len(pair_refs) * tok, BLOCK)]
+    for kv_head in range(bias_ref.shape[0]):
         cols = head_cols(kv_head)
         group = slice(kv_head * GROUP * tok, (kv_head + 1) * GROUP * tok)
         weights_ref[tok:, group] = dot(keys_ref[tok:, cols], queries_ref[group, :HEAD_DIM], 1, 1)
-        all_dprob_ref[tok:, group] = dot(values_ref[tok:, cols], grads_ref[group, :], 1, 1)
-        for pair in range(GROUP // PAIR):
-            first = kv_head * GROUP + pair * PAIR
-            at = slice(first * tok, (first + PAIR) * tok)
+        dprob_ref[tok:, group] = dot(values_ref[tok:, cols], grads_ref[group, :], 1, 1)
+        for first in range(group.start, group.stop, PAIR * tok):
+            at = slice(first, first + PAIR * tok)
             row_max = None
             for block in blocks:
                 score = (score_ref if block.start < tok else weights_ref)[block, at]
                 score = score + jnp.concatenate([live_ref[block, :]] * PAIR, axis=1)
                 weights_ref[block, at] = score
-                part = jnp.max(score.reshape(-1, 8, PAIR * tok), axis=0)
+                part = over_rows(score, jnp.max)
                 row_max = part if row_max is None else jnp.maximum(row_max, part)
             row_max = jnp.max(row_max, axis=0, keepdims=True)
             total = jnp.zeros((8, PAIR * tok), jnp.float32)
             delta = jnp.zeros((8, PAIR * tok), jnp.float32)
             for block in blocks:
-                dprob = (dprob_ref if block.start < tok else all_dprob_ref)[block, at]
+                dprob = (own_dprob_ref if block.start < tok else dprob_ref)[block, at]
                 weights = jnp.exp2((weights_ref[block, at] - row_max) * (SCALE * LOG2E))
                 weights_ref[block, at] = weights
-                total = total + jnp.sum(weights.reshape(-1, 8, PAIR * tok), axis=0)
-                delta = delta + jnp.sum((weights * dprob).reshape(-1, 8, PAIR * tok), axis=0)
-            inverse = 1.0 / jnp.sum(total, axis=0, keepdims=True)
-            delta = jnp.sum(delta, axis=0, keepdims=True) * inverse
+                if block.start < tok:
+                    dprob_ref[block, at] = dprob
+                total = total + over_rows(weights, jnp.sum)
+                delta = delta + over_rows(weights * dprob, jnp.sum)
+            stats_ref[0:1, at] = row_max
+            stats_ref[1:2, at] = jnp.sum(total, axis=0, keepdims=True)
+            stats_ref[2:3, at] = jnp.sum(delta, axis=0, keepdims=True)
+
+
+def last_kernel(slots, first_head, *refs):
+    bias_ref, queries_ref, grads_ref, live_ref = refs[:4]
+    weights_ref, dprob_ref, stats_ref, near_keys_ref, near_values_ref, pair_ref = refs[4:10]
+    probs_ref, dscore_ref, keys_ref, values_ref, sums_ref, own_ref = refs[10:16]
+    out_refs = refs[16 : 16 + slots - 1]
+    last_weights_ref, last_dprob_ref = refs[16 + slots - 1 :]
+    tok = pair_ref.shape[0]
+    near = (slots - 1) * tok
+    kv_heads = bias_ref.shape[0]
+    kv_width = kv_heads * HEAD_DIM
+    heads = kv_heads * GROUP
+    keys_ref[:near, :] = near_keys_ref[...]
+    values_ref[:near, :] = near_values_ref[...]
+    unpack(pair_ref, bias_ref, keys_ref, values_ref, slice(near, near + tok))
+    near_blocks = [slice(row, row + BLOCK) for row in range(0, near, BLOCK)]
+    blocks = [slice(row, row + BLOCK) for row in range(0, tok, BLOCK)]
+    for kv_head in range(kv_heads):
+        cols = head_cols(kv_head)
+        group = slice(kv_head * GROUP * tok, (kv_head + 1) * GROUP * tok)
+        last_weights_ref[:, group] = dot(
+            keys_ref[near:, cols], queries_ref[group, :HEAD_DIM], 1, 1
+        )
+        last_dprob_ref[:, group] = dot(values_ref[near:, cols], grads_ref[group, :], 1, 1)
+        for first in range(group.start, group.stop, PAIR * tok):
+            at = slice(first, first + PAIR * tok)
+            near_max = stats_ref[0:1, at]
+            row_max = jnp.broadcast_to(near_max, (8, PAIR * tok))
             for block in blocks:
-                dprob = (dprob_ref if block.start < tok else all_dprob_ref)[block, at]
-                probs = weights_ref[block, at] * inverse
+                live = live_ref[near + block.start : near + block.stop, :]
+                score = last_weights_ref[block, at] + jnp.concatenate([live] * PAIR, axis=1)
+                last_weights_ref[block, at] = score
+                row_max = jnp.maximum(row_max, over_rows(score, jnp.max))
+            row_max = jnp.max(row_max, axis=0, keepdims=True)
+            total = jnp.zeros((8, PAIR * tok), jnp.float32)
+            delta = jnp.zeros((8, PAIR * tok), jnp.float32)
+            for block in blocks:
+                weights = jnp.exp2((last_weights_ref[block, at] - row_max) * (SCALE * LOG2E))
+                last_weights_ref[block, at] = weights
+                total = total + over_rows(weights, jnp.sum)
+                delta = delta + over_rows(weights * last_dprob_ref[block, at], jnp.sum)
+            factor = jnp.exp2((near_max - row_max) * (SCALE * LOG2E))
+            total = jnp.sum(total, axis=0, keepdims=True) + stats_ref[1:2, at] * factor
+            delta = jnp.sum(delta, axis=0, keepdims=True) + stats_ref[2:3, at] * factor
+            inverse = 1.0 / total
+            delta = delta * inverse
+            factor = factor * inverse
+            for block in near_blocks:
+                probs = weights_ref[block, at] * factor
                 probs_ref[block, at] = probs.astype(jnp.bfloat16)
-                dscore_ref[block, at] = (probs * (dprob - delta)).astype(jnp.bfloat16)
+                dscore_ref[block, at] = (probs * (dprob_ref[block, at] - delta)).astype(jnp.bfloat16)
+            for block in blocks:
+                to = slice(near + block.start, near + block.stop)
+                probs = last_weights_ref[block, at] * inverse
+                probs_ref[to, at] = probs.astype(jnp.bfloat16)
+                dscore = probs * (last_dprob_ref[block, at] - delta)
+                dscore_ref[to, at] = dscore.astype(jnp.bfloat16)
         value_term = dot(probs_ref[:, group], grads_ref[group, :], 1, 0)
         key_term = dot(dscore_ref[:, group], queries_ref[group, :], 1, 0)
         over_queries = key_term[:, HEAD_DIM:]
@@ -152,15 +213,17 @@
         all_keys = keys_ref[:, cols]
         query_sums = (dot(high, all_keys, 0, 0) + dot(low, all_keys, 0, 0)) * SCALE
         of_group = slice(kv_head * GROUP, (kv_head + 1) * GROUP)
-        sums_ref[of_group, :] = query_sums[of_group]
+        sums_ref[of_group, :] = query_sums[first_head + of_group.start : first_head + of_group.stop]
         sums_ref[heads + kv_head : heads + kv_head + 1, :] = jnp.sum(
             value_term, axis=0, keepdims=True
         )
         value_cols = head_cols(kv_heads + kv_head)
         own_ref[:, cols] = key_term[:tok]
         own_ref[:, value_cols] = value_term[:tok]
-        for slot in range(1, slots):
-            rows = slice(slot * tok, (slot + 1) * tok)
+        for index, slot in enumerate(slot_order(slots)):
+            if slot == 0:
+                continue
+            rows = slice(index * tok, (index + 1) * tok)
             out_refs[slot - 1][:, cols] = key_term[rows].astype(jnp.bfloat16)
             out_refs[slot - 1][:, value_cols] = value_term[rows].astype(jnp.bfloat16)
 
@@ -241,6 +304,66 @@
 
 def exchange(axis, part):
     return [part] + [fetch(part, axis, slot) for slot in range(1, lax.axis_size(axis))]
+
+
+def attend(first_head, bias, queries, grads, score, own_dprob, live, pairs):
+    ctx = len(pairs)
+    tok = pairs[0].shape[0]
+    kv_width = bias.shape[0] * HEAD_DIM
+    columns = queries.shape[0]
+    rows = ctx * tok
+    near = rows - tok
+    near_slots = slot_order(ctx)[:-1]
+    weights, dprob, stats, near_keys, near_values = pl.pallas_call(
+        near_kernel,
+        out_shape=[
+            shape((near, columns), jnp.float32),
+            shape((near, columns), jnp.float32),
+            shape((8, columns), jnp.float32),
+            shape((near, kv_width), jnp.bfloat16),
+            shape((near, kv_width), jnp.bfloat16),
+        ],
+        in_specs=[VMEM] * (6 + len(near_slots)),
+        out_specs=[VMEM] * 5,
+        compiler_params=params(20 if ctx < 8 else 48),
+        cost_estimate=pl.CostEstimate(
+            flops=4 * near * columns * HEAD_DIM,
+            bytes_accessed=8 * near * columns,
+            transcendentals=near * columns,
+        ),
+        name="near",
+    )(bias, queries, grads, score, own_dprob, live, *[pairs[slot] for slot in near_slots])
+    term = shape((tok, 2 * kv_width), jnp.bfloat16)
+    return pl.pallas_call(
+        functools.partial(last_kernel, ctx, first_head),
+        out_shape=[
+            shape((rows, columns), jnp.bfloat16),
+            shape((rows, columns), jnp.bfloat16),
+            shape((rows, kv_width), jnp.bfloat16),
+            shape((rows, kv_width), jnp.bfloat16),
+            shape((bias.shape[0] * (GROUP + 1), HEAD_DIM), jnp.float32),
+            shape((tok, 2 * kv_width), jnp.float32),
+        ]
+        + [term] * (ctx - 1),
+        in_specs=[VMEM] * 10,
+        out_specs=[VMEM] * (6 + ctx - 1),
+        scratch_shapes=[pltpu.VMEM((tok, columns), jnp.float32)] * 2,
+        compiler_params=params(24 if ctx < 8 else 48),
+        cost_estimate=pl.CostEstimate(
+            flops=4 * rows * columns * HEAD_DIM,
+            bytes_accessed=4 * rows * columns,
+            transcendentals=tok * columns,
+        ),
+        name="last",
+    )(bias, queries, grads, live, weights, dprob, stats, near_keys, near_values, pairs[ctx // 2])
+
+
+def joined(place, parts):
+    if place < 4:
+        return jnp.concatenate(parts, axis=1)
+    cut, axis = (GROUP, 0) if place == 4 else (HEAD_DIM, 1)
+    pieces = [jnp.split(part, [cut], axis=axis) for part in parts]
+    return jnp.concatenate([piece[n] for n in range(2) for piece in pieces], axis=axis)
 
 
 def shards(q_proj, q_bias, k_proj, v_proj, v_bias, dout, lengths):
@@ -279,32 +402,30 @@
         q_proj[0],
         dout[0],
     )
+    bias, queries, grads, score, own_dprob, live = prepared
+    if ctx < 8:
+        made = attend(0, bias, queries, grads, score, own_dprob, live, pairs)
+    else:
+        made = [
+            attend(
+                kv_head * GROUP,
+                bias[kv_head : kv_head + 1],
+                *(part[at] for part in (queries, grads)),
+                *(part[:, at] for part in (score, own_dprob)),
+                live,
+                [
+                    jnp.concatenate(
+                        [part[:, head_cols(kv_head)], part[:, head_cols(kv_heads + kv_head)]], axis=1
+                    )
+                    for part in pairs
+                ],
+            )
+            for kv_head in range(kv_heads)
+            for at in [slice(kv_head * GROUP * tok, (kv_head + 1) * GROUP * tok)]
+        ]
+        made = [joined(n, parts) for n, parts in enumerate(zip(*made))]
+    probs, dscore, all_keys, all_values, sums, own, *terms = made
     term = shape((tok, 2 * kv_width), jnp.bfloat16)
-    probs, dscore, all_keys, all_values, sums, own, *terms = pl.pallas_call(
-        functools.partial(attend_kernel, ctx),
-        out_shape=[
-            shape((rows, columns), jnp.bfloat16),
-            shape((rows, columns), jnp.bfloat16),
-            shape((rows, kv_width), jnp.bfloat16),
-            shape((rows, kv_width), jnp.bfloat16),
-            shape((heads + kv_heads, HEAD_DIM), jnp.float32),
-            shape((tok, 2 * kv_width), jnp.float32),
-        ]
-        + [term] * (ctx - 1),
-        in_specs=[VMEM] * (6 + ctx),
-        out_specs=[VMEM] * (6 + ctx - 1),
-        scratch_shapes=[
-            pltpu.VMEM((rows, columns), jnp.float32),
-            pltpu.VMEM((rows, columns), jnp.float32),
-        ],
-        compiler_params=params(24 if ctx < 8 else 48),
-        cost_estimate=pl.CostEstimate(
-            flops=8 * rows * tok * width,
-            bytes_accessed=4 * rows * columns,
-            transcendentals=rows * columns,
-        ),
-        name="attend",
-    )(*prepared, *pairs)
     half = ctx // 2
     early = send_back(terms.pop(half - 1), half)
     attn, q_grad, early = pl.pallas_call(

time: 39.5 us -> 38.2 us (0.967)
  waiting for transfers between devices: 11.8 us -> 9.45 us
  starting transfers between devices: 13.9 us -> 14.6 us
    ppermute x6, waiting for transfers between devices: 8.39 us -> 6.69 us  [fetch(): lax.ppermute(array, axis, [(source_of(i, slot, size), i) for i in range(s...]
    ppermute x4, starting transfers between devices: 4.56 us -> 5.35 us  [send_back(): lax.ppermute(array, 'ctx', [(i, source_of(i, slot, size)) for i in range(...]
    ppermute x4, waiting for transfers between devices: 3.37 us -> 2.76 us  [send_back(): lax.ppermute(array, 'ctx', [(i, source_of(i, slot, size)) for i in range(...]
    pallas_call x1 -> x2, Pallas kernels: 4.24 us -> 4.53 us  [the longest x1 2.84 us: attend(): pl.pallas_call(functools.partial(last_kernel, ctx, first_head), out_shape...]
  transfers between devices with their start and end apart: 10 -> 10, of which waited for: 5 -> 6; matrix products, arithmetic and copies ran while one was open for 0% -> 0% of each run, Pallas kernels for 8% -> 12%
where the time goes in v14:
time: 38.2 us; the launch traced here: 37.8 us
  starting transfers between devices  14.6 us (38%)
  waiting for transfers between devices  9.45 us (25%)
  Pallas kernels  8.16 us (21%)
  local copies, waits for them, and re-layouts  4.08 us (11%)
  other arithmetic  0.88 us (2%)
  between operations  0.68 us (2%)
    ppermute x6, starting transfers between devices, fetch(): lax.ppermute(array, axis, [(source_of(i, slot, size), i) for i in range(s...  9.24 us
    ppermute x6, waiting for transfers between devices, fetch(): lax.ppermute(array, axis, [(source_of(i, slot, size), i) for i in range(s...  6.69 us
    ppermute x4, starting transfers between devices, send_back(): lax.ppermute(array, 'ctx', [(i, source_of(i, slot, size)) for i in range(...  5.35 us
    unnamed x10, local copies, waits for them, and re-layouts  4.08 us
    pallas_call x1, Pallas kernels, attend(): pl.pallas_call(functools.partial(last_kernel, ctx, first_head), out_shape...  2.84 us
    ppermute x4, waiting for transfers between devices, send_back(): lax.ppermute(array, 'ctx', [(i, source_of(i, slot, size)) for i in range(...  2.76 us
    pallas_call x1, Pallas kernels, shards(): pl.pallas_call(finish_kernel, out_shape=[shape((tok, width), jnp.bfloat16...  1.8 us
    pallas_call x1, Pallas kernels, attend(): pl.pallas_call(near_kernel, out_shape=[shape((near, columns), jnp.float32...  1.69 us
  transfers between devices with their start and end apart: 10, of which 6 were waited for; matrix products, arithmetic and copies ran while one was open for 0% of the time, Pallas kernels for 12%

profile of v14, /device:TPU:0, one launch (start us, length us, event | category | flops | bytes accessed | tf_op | source)
XLA Modules:
  0.0 37.8 jit_solution(9912258469438407022)
XLA Ops:
  0.6 0.9 %pad_maximum_fusion.pair_ref.refs_0_ = bf16[128,512]{1,0:T(8,128)(2,1)S(1)} fusion(bf16[128,256]{1,0:T(8,128)(2,1)} %bitcast.16, bf16[128,256]{1,0:T(8,128)(2,1)} %bitcast.17), kind=kLoop, calls=%fused_computation | loop fusion | flops 262144 | bytes 262144 | tf_op jit(solution)/shard_map/concatenate | solution.py:378
  1.5 5.1 %collective-permute-start.1 = (bf16[128,512]{1,0:T(8,128)(2,1)S(1)}, bf16[128,512]{1,0:T(8,128)(2,1)S(1)}, u32[]{:S(2)}, u32[]{:S(2)}) collective-permute-start(bf16[128,512]{1,0:T(8,128)(2,1)S(1)} %pad_maximum_fusion.pair_ref.refs_0_), channel_id=1, source_target_pairs={{6,0},{4,2},{2,4},{0,6},{7,1},{5,3},{3,5},{1,7},{14,8},{12,10},{10... | collective-permute-start | bytes 393224 | tf_op jit(solution)/shard_map/ppermute | solution.py:58
  6.6 0.0 collective-permute-start
  6.6 0.6 %collective-permute-start.2 = (bf16[128,512]{1,0:T(8,128)(2,1)S(1)}, bf16[128,512]{1,0:T(8,128)(2,1)S(1)}, u32[]{:S(2)}, u32[]{:S(2)}) collective-permute-start(bf16[128,512]{1,0:T(8,128)(2,1)S(1)} %pad_maximum_fusion.pair_ref.refs_0_), channel_id=1, source_target_pairs={{4,0},{6,2},{0,4},{2,6},{5,1},{7,3},{1,5},{3,7},{12,8},{14,10},{8,... | collective-permute-start | bytes 393224 | tf_op jit(solution)/shard_map/ppermute | solution.py:58
  7.3 0.0 copy-start
  7.3 1.0 %copy-done = bf16[1,128,2048]{2,1,0:T(8,128)(2,1)S(1)} copy-done((bf16[1,128,2048]{2,1,0:T(8,128)(2,1)S(1)}, bf16[1,128,2048]{2,1,0:T(8,128)(2,1)}, u32[]{:S(2)}) %copy-start) | copy-done | bytes 524312
  8.3 0.0 copy-start.1
  8.3 1.0 %copy-done.1 = bf16[1,128,2048]{2,1,0:T(8,128)(2,1)S(1)} copy-done((bf16[1,128,2048]{2,1,0:T(8,128)(2,1)S(1)}, bf16[1,128,2048]{2,1,0:T(8,128)(2,1)}, u32[]{:S(2)}) %copy-start.1) | copy-done | bytes 524312
  9.4 0.0 copy-start.2
  9.4 0.7 %copy-done.2 = bf16[2048]{0:T(1024)(128)(2,1)S(1)} copy-done((bf16[2048]{0:T(1024)(128)(2,1)S(1)}, bf16[2048]{0:T(1024)(128)(2,1)}, u32[]{:S(2)}) %copy-start.2) | copy-done | bytes 4120
  10.0 0.0 copy-start.3
  10.0 0.7 %copy-done.3 = s32[1,8]{1,0:T(1,128)S(1)} copy-done((s32[1,8]{1,0:T(1,128)S(1)}, s32[1,8]{1,0:T(1,128)}, u32[]{:S(2)}) %copy-start.3) | copy-done | bytes 56
  10.7 0.0 copy-start.4
  10.7 0.7 %copy-done.4 = bf16[256]{0:T(256)(128)(2,1)S(1)} copy-done((bf16[256]{0:T(256)(128)(2,1)S(1)}, bf16[256]{0:T(256)(128)(2,1)}, u32[]{:S(2)}) %copy-start.4) | copy-done | bytes 536
  11.4 1.1 %prepare.1 = (bf16[2,128]{1,0:T(2,128)(2,1)S(1)}, bf16[2048,256]{1,0:T(8,128)(2,1)S(1)}, bf16[2048,128]{1,0:T(8,128)(2,1)S(1)}, f32[128,2048]{1,0:T(8,128)S(1)},...) custom-call(s32[1,8]{1,0:T(1,128)S(1)} %copy-done.3, bf16[128,512]{1,0:T(8,128)(2,1)S(1)} %pad_maximum_fusion.pair_ref.refs_0_, ...), custom_call_target="tpu_custom_call" | custom-call | flops 134217728 | bytes 4194304 | tf_op jit(solution)/shard_map/prepare/pallas_call | solution.py:380
  12.5 0.0 collective-permute-done.1.refs_2_
  12.5 1.5 %collective-permute-done.refs_1_ = bf16[128,512]{1,0:T(8,128)(2,1)S(1)} collective-permute-done((bf16[128,512]{1,0:T(8,128)(2,1)S(1)}, bf16[128,512]{1,0:T(8,128)(2,1)S(1)}, u32[]{:S(2)}, u32[]{:S(2)}) %collective-permute-start) | collective-permute-done | bytes 131104 | tf_op jit(solution)/shard_map/ppermute | solution.py:58
  14.0 1.7 %near.1 = (f32[384,2048]{1,0:T(8,128)S(1)}, f32[384,2048]{1,0:T(8,128)S(1)}, f32[8,2048]{1,0:T(8,128)S(1)}, bf16[384,256]{1,0:T(8,128)(2,1)S(1)}, bf16[384,256]{1,0:T(8,128)(2,1)S(1)}) custom-call(bf16[2,128]{1,0:T(2,128)(2,1)S(1)} %get-tuple-element.36.bias_ref.refs_0_, bf16[2048,256]{1,0:T(8,128)(2,1)S(1)} %get-tuple-element.37.queries_ref.refs_1_, ...), custom_call_target="tpu_custom_call" | custom-call | flops 402653184 | bytes 6291456 | tf_op jit(solution)/shard_map/near/pallas_call | solution.py:317
  15.7 2.0 %collective-permute-done.2.refs_9_ = bf16[128,512]{1,0:T(8,128)(2,1)S(1)} collective-permute-done((bf16[128,512]{1,0:T(8,128)(2,1)S(1)}, bf16[128,512]{1,0:T(8,128)(2,1)S(1)}, u32[]{:S(2)}, u32[]{:S(2)}) %collective-permute-start.2) | collective-permute-done | bytes 131104 | tf_op jit(solution)/shard_map/ppermute | solution.py:58
  17.7 2.8 %last.1 = (bf16[512,2048]{1,0:T(8,128)(2,1)S(1)}, bf16[512,2048]{1,0:T(8,128)(2,1)S(1)}, bf16[512,256]{1,0:T(8,128)(2,1)S(1)}, bf16[512,256]{1,0:T(8,128)(2,1)S(...) custom-call(bf16[2,128]{1,0:T(2,128)(2,1)S(1)} %get-tuple-element.36, ...), custom_call_target="tpu_custom_call" | custom-call | flops 536870912 | bytes 4194304 | tf_op jit(solution)/shard_map/last/pallas_call | solution.py:337
  20.6 0.9 %collective-permute-start.3 = (bf16[128,512]{1,0:T(8,128)(2,1)S(1)}, bf16[128,512]{1,0:T(8,128)(2,1)S(1)}, u32[]{:S(2)}, u32[]{:S(2)}) collective-permute-start(bf16[128,512]{1,0:T(8,128)(2,1)S(1)} %get-tuple-element.51), channel_id=1, source_target_pairs={{0,4},{2,6},{4,0},{6,2},{1,5},{3,7},{5,1},{7,3},{8,12},{10,14},{12... | collective-permute-start | bytes 393224 | tf_op jit(solution)/shard_map/ppermute | solution.py:63
  21.4 2.4 %collective-permute-start.6 = (f32[18,128]{1,0:T(8,128)S(1)}, f32[18,128]{1,0:T(8,128)S(1)}, u32[]{:S(2)}, u32[]{:S(2)}) collective-permute-start(f32[18,128]{1,0:T(8,128)S(1)} %get-tuple-element.54.refs_0_), channel_id=1, source_target_pairs={{24,0},{16,8},{8,16},{0,24},{25,1},{17,9},{9,17},{1,25},{26,2},{18... | collective-permute-start | bytes 27656 | tf_op jit(solution)/shard_map/ppermute | solution.py:58
  23.9 0.5 %collective-permute-start.5 = (f32[18,128]{1,0:T(8,128)S(1)}, f32[18,128]{1,0:T(8,128)S(1)}, u32[]{:S(2)}, u32[]{:S(2)}) collective-permute-start(f32[18,128]{1,0:T(8,128)S(1)} %get-tuple-element.54.refs_0_), channel_id=1, source_target_pairs={{16,0},{24,8},{0,16},{8,24},{17,1},{25,9},{1,17},{9,25},{18,2},{26... | collective-permute-start | bytes 27656 | tf_op jit(solution)/shard_map/ppermute | solution.py:58
  24.4 0.5 %collective-permute-start.4 = (f32[18,128]{1,0:T(8,128)S(1)}, f32[18,128]{1,0:T(8,128)S(1)}, u32[]{:S(2)}, u32[]{:S(2)}) collective-permute-start(f32[18,128]{1,0:T(8,128)S(1)} %get-tuple-element.54.refs_0_), channel_id=1, source_target_pairs={{8,0},{0,8},{24,16},{16,24},{9,1},{1,9},{25,17},{17,25},{10,2},{2,... | collective-permute-start | bytes 27656 | tf_op jit(solution)/shard_map/ppermute | solution.py:58
  24.9 1.1 %collective-permute-done.6.refs_3_ = f32[18,128]{1,0:T(8,128)S(1)} collective-permute-done((f32[18,128]{1,0:T(8,128)S(1)}, f32[18,128]{1,0:T(8,128)S(1)}, u32[]{:S(2)}, u32[]{:S(2)}) %collective-permute-start.6) | collective-permute-done | bytes 9248 | tf_op jit(solution)/shard_map/ppermute | solution.py:58
  26.1 1.5 %collective-permute-done.5.refs_2_ = f32[18,128]{1,0:T(8,128)S(1)} collective-permute-done((f32[18,128]{1,0:T(8,128)S(1)}, f32[18,128]{1,0:T(8,128)S(1)}, u32[]{:S(2)}, u32[]{:S(2)}) %collective-permute-start.5) | collective-permute-done | bytes 9248 | tf_op jit(solution)/shard_map/ppermute | solution.py:58
  27.6 0.5 %collective-permute-done.4.refs_1_ = f32[18,128]{1,0:T(8,128)S(1)} collective-permute-done((f32[18,128]{1,0:T(8,128)S(1)}, f32[18,128]{1,0:T(8,128)S(1)}, u32[]{:S(2)}, u32[]{:S(2)}) %collective-permute-start.4) | collective-permute-done | bytes 9248 | tf_op jit(solution)/shard_map/ppermute | solution.py:58
  28.1 1.8 %collective-permute-start.8 = (bf16[160,512]{1,0:T(8,128)(2,1)S(1)}, bf16[160,512]{1,0:T(8,128)(2,1)S(1)}, u32[]{:S(2)}, u32[]{:S(2)}) collective-permute-start(bf16[160,512]{1,0:T(8,128)(2,1)S(1)} %get-tuple-element.60), channel_id=1, source_target_pairs={{0,6},{2,4},{4,2},{6,0},{1,7},{3,5},{5,3},{7,1},{8,14},{10,12},{12... | collective-permute-start | bytes 491528 | tf_op jit(solution)/shard_map/ppermute | solution.py:63
  29.9 0.9 %collective-permute-start.9 = (bf16[160,512]{1,0:T(8,128)(2,1)S(1)}, bf16[160,512]{1,0:T(8,128)(2,1)S(1)}, u32[]{:S(2)}, u32[]{:S(2)}) collective-permute-start(bf16[160,512]{1,0:T(8,128)(2,1)S(1)} %get-tuple-element.61), channel_id=1, source_target_pairs={{0,2},{2,0},{4,6},{6,4},{1,3},{3,1},{5,7},{7,5},{8,10},{10,8},{12,... | collective-permute-start | bytes 491528 | tf_op jit(solution)/shard_map/ppermute | solution.py:63
  30.9 1.7 %collective-permute-start.7 = (f32[18,128]{1,0:T(8,128)S(1)}, f32[18,128]{1,0:T(8,128)S(1)}, u32[]{:S(2)}, u32[]{:S(2)}) collective-permute-start(f32[18,128]{1,0:T(8,128)S(1)} %get-tuple-element.57.refs_0_), channel_id=1, source_target_pairs={{0,4},{2,6},{4,0},{6,2},{1,5},{3,7},{5,1},{7,3},{8,12},{10,14},{12... | collective-permute-start | bytes 27656 | tf_op jit(solution)/shard_map/ppermute | solution.py:63
  32.6 0.0 collective-permute-done.3._
  32.6 1.8 %finish.1 = (bf16[128,2048]{1,0:T(8,128)(2,1)}, bf16[128,2048]{1,0:T(8,128)(2,1)}, bf16[128,512]{1,0:T(8,128)(2,1)S(1)}) custom-call(bf16[512,2048]{1,0:T(8,128)(2,1)S(1)} %get-tuple-element.47.probs_ref, bf16[512,2048]{1,0:T(8,128)(2,1)S(1)} %get-tuple-element.48.dscore_ref, ...), custom_call_target="tpu_custom_call", output_to_operand_aliasing={{2}: (4, {})} | custom-call | flops 536870912 | bytes 4194304 | tf_op jit(solution)/shard_map/finish/pallas_call | solution.py:431
  34.4 2.8 %collective-permute-done.7.refs_1_ = f32[18,128]{1,0:T(8,128)S(1)} collective-permute-done((f32[18,128]{1,0:T(8,128)S(1)}, f32[18,128]{1,0:T(8,128)S(1)}, u32[]{:S(2)}, u32[]{:S(2)}) %collective-permute-start.7) | collective-permute-done | bytes 9248 | tf_op jit(solution)/shard_map/ppermute | solution.py:63
  37.1 0.0 collective-permute-done.8.refs_4_
  37.1 0.0 collective-permute-done.9.refs_5_
  37.1 0.7 %collect.1 = (bf16[128,256]{1,0:T(8,128)(2,1)}, bf16[128,256]{1,0:T(8,128)(2,1)}, f32[16,128]{1,0:T(8,128)}, f32[2,128]{1,0:T(2,128)}) custom-call(f32[18,128]{1,0:T(8,128)S(1)} %get-tuple-element.57.refs_0_, f32[18,128]{1,0:T(8,128)S(1)} %collective-permute-done.7.refs_1_, f32[128,512]{1,0:T(8,128)S(1)} %get-tuple-element.58.refs_2_, ...), custom_call_target="tpu_custom_call" | custom-call | flops 262144 | bytes 524288 | tf_op jit(solution)/shard_map/collect/pallas_call | solution.py:451
  (1 shorter events, 0.0 us)
Async XLA Ops:
  1.5 11.0 %collective-permute-start.1 = (bf16[128,512]{1,0:T(8,128)(2,1)S(1)}, bf16[128,512]{1,0:T(8,128)(2,1)S(1)}, u32[]{:S(2)}, u32[]{:S(2)}) collective-permute-start(bf16[128,512]{1,0:T(8,128)(2,1)S(1)} %pad_maximum_fusion.pair_ref.refs_0_), channel_id=1, source_target_pairs={{6,0},{4,2},{2,4},{0,6},{7,1},{5,3},{3,5},{1,7},{14,8},{12,10},{10... | collective-permute-start | bytes 393224 | tf_op jit(solution)/shard_map/ppermute | solution.py:58
  6.6 7.4 %collective-permute-start = (bf16[128,512]{1,0:T(8,128)(2,1)S(1)}, bf16[128,512]{1,0:T(8,128)(2,1)S(1)}, u32[]{:S(2)}, u32[]{:S(2)}) collective-permute-start(bf16[128,512]{1,0:T(8,128)(2,1)S(1)} %pad_maximum_fusion.pair_ref.refs_0_), channel_id=1, source_target_pairs={{2,0},{0,2},{6,4},{4,6},{3,1},{1,3},{7,5},{5,7},{10,8},{8,10},{14,... | collective-permute-start | bytes 393224 | tf_op jit(solution)/shard_map/ppermute | solution.py:58
  6.6 11.1 %collective-permute-start.2 = (bf16[128,512]{1,0:T(8,128)(2,1)S(1)}, bf16[128,512]{1,0:T(8,128)(2,1)S(1)}, u32[]{:S(2)}, u32[]{:S(2)}) collective-permute-start(bf16[128,512]{1,0:T(8,128)(2,1)S(1)} %pad_maximum_fusion.pair_ref.refs_0_), channel_id=1, source_target_pairs={{4,0},{6,2},{0,4},{2,6},{5,1},{7,3},{1,5},{3,7},{12,8},{14,10},{8,... | collective-permute-start | bytes 393224 | tf_op jit(solution)/shard_map/ppermute | solution.py:58
  7.3 1.0 %copy-start = (bf16[1,128,2048]{2,1,0:T(8,128)(2,1)S(1)}, bf16[1,128,2048]{2,1,0:T(8,128)(2,1)}, u32[]{:S(2)}) copy-start(bf16[1,128,2048]{2,1,0:T(8,128)(2,1)} %param.7) | copy-start | bytes 1572868
  8.3 1.0 %copy-start.1 = (bf16[1,128,2048]{2,1,0:T(8,128)(2,1)S(1)}, bf16[1,128,2048]{2,1,0:T(8,128)(2,1)}, u32[]{:S(2)}) copy-start(bf16[1,128,2048]{2,1,0:T(8,128)(2,1)} %param.12) | copy-start | bytes 1572868
  9.4 0.7 %copy-start.2 = (bf16[2048]{0:T(1024)(128)(2,1)S(1)}, bf16[2048]{0:T(1024)(128)(2,1)}, u32[]{:S(2)}) copy-start(bf16[2048]{0:T(1024)(128)(2,1)} %param.8) | copy-start | bytes 12292
  10.0 0.7 %copy-start.3 = (s32[1,8]{1,0:T(1,128)S(1)}, s32[1,8]{1,0:T(1,128)}, u32[]{:S(2)}) copy-start(s32[1,8]{1,0:T(1,128)} %len_ref.1) | copy-start | bytes 100
  10.7 0.7 %copy-start.4 = (bf16[256]{0:T(256)(128)(2,1)S(1)}, bf16[256]{0:T(256)(128)(2,1)}, u32[]{:S(2)}) copy-start(bf16[256]{0:T(256)(128)(2,1)} %param.11) | copy-start | bytes 1540
  20.6 12.0 %collective-permute-start.3 = (bf16[128,512]{1,0:T(8,128)(2,1)S(1)}, bf16[128,512]{1,0:T(8,128)(2,1)S(1)}, u32[]{:S(2)}, u32[]{:S(2)}) collective-permute-start(bf16[128,512]{1,0:T(8,128)(2,1)S(1)} %get-tuple-element.51), channel_id=1, source_target_pairs={{0,4},{2,6},{4,0},{6,2},{1,5},{3,7},{5,1},{7,3},{8,12},{10,14},{12... | collective-permute-start | bytes 393224 | tf_op jit(solution)/shard_map/ppermute | solution.py:63
  21.4 4.6 %collective-permute-start.6 = (f32[18,128]{1,0:T(8,128)S(1)}, f32[18,128]{1,0:T(8,128)S(1)}, u32[]{:S(2)}, u32[]{:S(2)}) collective-permute-start(f32[18,128]{1,0:T(8,128)S(1)} %get-tuple-element.54.refs_0_), channel_id=1, source_target_pairs={{24,0},{16,8},{8,16},{0,24},{25,1},{17,9},{9,17},{1,25},{26,2},{18... | collective-permute-start | bytes 27656 | tf_op jit(solution)/shard_map/ppermute | solution.py:58
  23.9 3.7 %collective-permute-start.5 = (f32[18,128]{1,0:T(8,128)S(1)}, f32[18,128]{1,0:T(8,128)S(1)}, u32[]{:S(2)}, u32[]{:S(2)}) collective-permute-start(f32[18,128]{1,0:T(8,128)S(1)} %get-tuple-element.54.refs_0_), channel_id=1, source_target_pairs={{16,0},{24,8},{0,16},{8,24},{17,1},{25,9},{1,17},{9,25},{18,2},{26... | collective-permute-start | bytes 27656 | tf_op jit(solution)/shard_map/ppermute | solution.py:58
  24.4 3.7 %collective-permute-start.4 = (f32[18,128]{1,0:T(8,128)S(1)}, f32[18,128]{1,0:T(8,128)S(1)}, u32[]{:S(2)}, u32[]{:S(2)}) collective-permute-start(f32[18,128]{1,0:T(8,128)S(1)} %get-tuple-element.54.refs_0_), channel_id=1, source_target_pairs={{8,0},{0,8},{24,16},{16,24},{9,1},{1,9},{25,17},{17,25},{10,2},{2,... | collective-permute-start | bytes 27656 | tf_op jit(solution)/shard_map/ppermute | solution.py:58
  28.1 9.0 %collective-permute-start.8 = (bf16[160,512]{1,0:T(8,128)(2,1)S(1)}, bf16[160,512]{1,0:T(8,128)(2,1)S(1)}, u32[]{:S(2)}, u32[]{:S(2)}) collective-permute-start(bf16[160,512]{1,0:T(8,128)(2,1)S(1)} %get-tuple-element.60), channel_id=1, source_target_pairs={{0,6},{2,4},{4,2},{6,0},{1,7},{3,5},{5,3},{7,1},{8,14},{10,12},{12... | collective-permute-start | bytes 491528 | tf_op jit(solution)/shard_map/ppermute | solution.py:63
  29.9 7.2 %collective-permute-start.9 = (bf16[160,512]{1,0:T(8,128)(2,1)S(1)}, bf16[160,512]{1,0:T(8,128)(2,1)S(1)}, u32[]{:S(2)}, u32[]{:S(2)}) collective-permute-start(bf16[160,512]{1,0:T(8,128)(2,1)S(1)} %get-tuple-element.61), channel_id=1, source_target_pairs={{0,2},{2,0},{4,6},{6,4},{1,3},{3,1},{5,7},{7,5},{8,10},{10,8},{12,... | collective-permute-start | bytes 491528 | tf_op jit(solution)/shard_map/ppermute | solution.py:63
  30.9 6.3 %collective-permute-start.7 = (f32[18,128]{1,0:T(8,128)S(1)}, f32[18,128]{1,0:T(8,128)S(1)}, u32[]{:S(2)}, u32[]{:S(2)}) collective-permute-start(f32[18,128]{1,0:T(8,128)S(1)} %get-tuple-element.57.refs_0_), channel_id=1, source_target_pairs={{0,4},{2,6},{4,0},{6,2},{1,5},{3,7},{5,1},{7,3},{8,12},{10,14},{12... | collective-permute-start | bytes 27656 | tf_op jit(solution)/shard_map/ppermute | solution.py:63

commit v15 on v14

--- a/solution.py
+++ b/solution.py
@@ -17,6 +17,7 @@
 LOG2E = 1.4426950408889634
 NEGATIVE = -1e30
 VMEM = pl.BlockSpec(memory_space=pltpu.VMEM)
+HBM = pl.BlockSpec(memory_space=pltpu.HBM)
 ANY = pl.BlockSpec(memory_space=pl.ANY)
 SMEM = pl.BlockSpec(memory_space=pltpu.SMEM)
 
@@ -61,6 +62,20 @@
 def send_back(array, slot):
     size = lax.axis_size("ctx")
     return lax.ppermute(array, "ctx", [(i, source_of(i, slot, size)) for i in range(size)])
+
+
+def pack_kernel(k_ref, v_ref, pair_ref, sems):
+    kv_width = k_ref.shape[1]
+    copies = [
+        pltpu.make_async_copy(
+            part_ref, pair_ref.at[:, pl.ds(n * kv_width, kv_width)], sems.at[n]
+        )
+        for n, part_ref in enumerate([k_ref, v_ref])
+    ]
+    for copy in copies:
+        copy.start()
+    for copy in copies:
+        copy.wait()
 
 
 def prepare_kernel(
@@ -152,8 +167,7 @@
     bias_ref, queries_ref, grads_ref, live_ref = refs[:4]
     weights_ref, dprob_ref, stats_ref, near_keys_ref, near_values_ref, pair_ref = refs[4:10]
     probs_ref, dscore_ref, keys_ref, values_ref, sums_ref, own_ref = refs[10:16]
-    out_refs = refs[16 : 16 + slots - 1]
-    last_weights_ref, last_dprob_ref = refs[16 + slots - 1 :]
+    out_refs, (last_weights_ref, last_dprob_ref) = refs[16:-2], refs[-2:]
     tok = pair_ref.shape[0]
     near = (slots - 1) * tok
     kv_heads = bias_ref.shape[0]
@@ -221,14 +235,15 @@
         own_ref[:, cols] = key_term[:tok]
         own_ref[:, value_cols] = value_term[:tok]
         for index, slot in enumerate(slot_order(slots)):
-            if slot == 0:
-                continue
             rows = slice(index * tok, (index + 1) * tok)
-            out_refs[slot - 1][:, cols] = key_term[rows].astype(jnp.bfloat16)
-            out_refs[slot - 1][:, value_cols] = value_term[rows].astype(jnp.bfloat16)
-
-
-def finish_kernel(probs_ref, dscore_ref, keys_ref, values_ref, _, attn_ref, qg_ref, __):
+            if slot:
+                out_refs[slot - 1][:, cols] = key_term[rows].astype(jnp.bfloat16)
+                out_refs[slot - 1][:, value_cols] = value_term[rows].astype(jnp.bfloat16)
+
+
+def finish_kernel(probs_ref, dscore_ref, keys_ref, values_ref, *refs):
+    passed = (len(refs) - 2) // 2
+    attn_ref, qg_ref = refs[passed : passed + 2]
     tok = attn_ref.shape[0]
     kv_heads = keys_ref.shape[1] // HEAD_DIM
     for kv_head in range(kv_heads):
@@ -247,22 +262,31 @@
                 qg_ref[:, head_cols(head)] = query_grad[rows].astype(jnp.bfloat16)
 
 
-def collect_kernel(batches, messages, *refs):
-    sum_refs, refs = refs[:2], refs[2:]
-    own_ref, early_ref, refs = refs[0], refs[1], refs[2:]
-    message_refs, (kg_ref, vg_ref, qb_ref, vb_ref) = refs[:messages], refs[messages:]
+def collect_kernel(batches, parts, whole, *refs):
+    sum_refs, own_ref, refs = refs[:parts], refs[parts], refs[parts + 1 :]
+    whole_refs, message_refs, (kg_ref, vg_ref, qb_ref, vb_ref) = (
+        refs[:whole],
+        refs[whole:-4],
+        refs[-4:],
+    )
     heads, kv_heads = qb_ref.shape[0], vb_ref.shape[0]
     tok, kv_width = kg_ref.shape
-    total = sum_refs[0][...] + sum_refs[1][...]
-    term = own_ref[...] + early_ref[...].astype(jnp.float32)
+    total = sum_refs[0][...]
+    for ref in sum_refs[1:]:
+        total = total + ref[...]
+    query_sums, value_sums = total[:heads], total[heads:]
+    term = own_ref[...]
+    for ref in whole_refs:
+        term = term + ref[...].astype(jnp.float32)
     for ref in message_refs:
-        sums = ref[tok:, :].astype(jnp.float32)
-        sums = sums[:, :HEAD_DIM] + sums[:, HEAD_DIM : 2 * HEAD_DIM]
-        total = total + sums[: heads + kv_heads]
+        added = ref[tok:, :].astype(jnp.float32)
+        high_and_low = added[:, : 2 * HEAD_DIM], added[:, 2 * HEAD_DIM : 4 * HEAD_DIM]
+        of_queries, of_values = (both[:, :HEAD_DIM] + both[:, HEAD_DIM:] for both in high_and_low)
+        query_sums = query_sums + of_queries[:heads]
+        value_sums = value_sums + of_values[:kv_heads]
         term = term + ref[:tok, :].astype(jnp.float32)
-    total = total * (1.0 / batches)
-    qb_ref[...] = total[:heads]
-    vb_ref[...] = total[heads:]
+    qb_ref[...] = query_sums * (1.0 / batches)
+    vb_ref[...] = value_sums * (1.0 / batches)
     term = term.astype(jnp.bfloat16)
     kg_ref[...] = term[:, :kv_width]
     vg_ref[...] = term[:, kv_width:]
@@ -278,17 +302,27 @@
     total_ref[...] = total
     for term_ref, message_ref in zip(term_refs, message_refs):
         tok = term_ref.shape[0]
+        kv_heads = term_ref.shape[1] // (2 * HEAD_DIM)
         rows = message_ref.shape[0] - tok
-        high = jnp.concatenate([total, jnp.zeros((rows - total.shape[0], HEAD_DIM), jnp.float32)])
         message_ref[:tok, :] = term_ref[...]
-        message_ref[tok:, :] = jnp.zeros((rows, term_ref.shape[1]), jnp.bfloat16)
-        message_ref[tok:, :HEAD_DIM] = high.astype(jnp.bfloat16)
-        low = high - high.astype(jnp.bfloat16).astype(jnp.float32)
-        message_ref[tok:, HEAD_DIM : 2 * HEAD_DIM] = low.astype(jnp.bfloat16)
+        message_ref[tok:, : 4 * HEAD_DIM] = added_rows(total, total.shape[0] - kv_heads, rows)
+
+
+def added_rows(total, heads, rows):
+    high = total.astype(jnp.bfloat16).astype(jnp.float32)
+    both = jnp.concatenate([high, total - high], axis=1)
+    blocks = [both[:heads], both[heads:]]
+    blocks = [
+        jnp.concatenate([block, jnp.zeros((rows - block.shape[0], 2 * HEAD_DIM), jnp.float32)])
+        if block.shape[0] < rows
+        else block
+        for block in blocks
+    ]
+    return jnp.concatenate(blocks, axis=1).astype(jnp.bfloat16)
 
 
 def total_with(parts, terms):
-    rows = -(-parts[0].shape[0] // 16) * 16
+    rows = -(-parts[0].shape[0] * GROUP // (GROUP + 1) // 16) * 16
     total, *messages = pl.pallas_call(
         functools.partial(total_kernel, len(parts)),
         out_shape=[shape(parts[0].shape, parts[0].dtype)]
@@ -333,7 +367,7 @@
         ),
         name="near",
     )(bias, queries, grads, score, own_dprob, live, *[pairs[slot] for slot in near_slots])
-    term = shape((tok, 2 * kv_width), jnp.bfloat16)
+    terms = [shape((tok, 2 * kv_width), jnp.bfloat16)] * (ctx - 1)
     return pl.pallas_call(
         functools.partial(last_kernel, ctx, first_head),
         out_shape=[
@@ -344,9 +378,9 @@
             shape((bias.shape[0] * (GROUP + 1), HEAD_DIM), jnp.float32),
             shape((tok, 2 * kv_width), jnp.float32),
         ]
-        + [term] * (ctx - 1),
+        + terms,
         in_specs=[VMEM] * 10,
-        out_specs=[VMEM] * (6 + ctx - 1),
+        out_specs=[VMEM] * (6 + len(terms)),
         scratch_shapes=[pltpu.VMEM((tok, columns), jnp.float32)] * 2,
         compiler_params=params(24 if ctx < 8 else 48),
         cost_estimate=pl.CostEstimate(
@@ -375,7 +409,18 @@
     batches = lax.axis_size("dp")
     rows = ctx * tok
     columns = heads * tok
-    pair = jnp.concatenate([k_proj[0], v_proj[0]], axis=1)
+    pair = pl.pallas_call(
+        pack_kernel,
+        out_shape=shape((tok, 2 * kv_width), jnp.bfloat16),
+        in_specs=[HBM] * 2,
+        out_specs=VMEM,
+        scratch_shapes=[pltpu.SemaphoreType.DMA((2,))],
+        compiler_params=params(2),
+        cost_estimate=pl.CostEstimate(
+            flops=0, bytes_accessed=8 * tok * kv_width, transcendentals=0
+        ),
+        name="pack",
+    )(*[pltpu.with_memory_space_constraint(part[0], pltpu.HBM) for part in (k_proj, v_proj)])
     pairs = [pair] + [fetch(pair, "ctx", slot) for slot in range(1, ctx)]
     prepared = pl.pallas_call(
         functools.partial(prepare_kernel, ctx),
@@ -425,45 +470,44 @@
         ]
         made = [joined(n, parts) for n, parts in enumerate(zip(*made))]
     probs, dscore, all_keys, all_values, sums, own, *terms = made
-    term = shape((tok, 2 * kv_width), jnp.bfloat16)
     half = ctx // 2
-    early = send_back(terms.pop(half - 1), half)
-    attn, q_grad, early = pl.pallas_call(
+    far = range(half, ctx)
+    early = [send_back(terms[slot - 1], slot) for slot in far]
+    attn, q_grad, *early = pl.pallas_call(
         finish_kernel,
         out_shape=[
             shape((tok, width), jnp.bfloat16),
             shape((tok, width), jnp.bfloat16),
-            shape(early.shape, early.dtype),
-        ],
-        in_specs=[VMEM] * 4 + [ANY],
-        out_specs=[VMEM] * 2 + [ANY],
-        input_output_aliases={4: 2},
+        ]
+        + [shape(part.shape, part.dtype) for part in early],
+        in_specs=[VMEM] * 4 + [ANY] * len(early),
+        out_specs=[VMEM] * 2 + [ANY] * len(early),
+        input_output_aliases={4 + n: 2 + n for n in range(len(early))},
         compiler_params=params(24),
         cost_estimate=pl.CostEstimate(
             flops=4 * rows * tok * width, bytes_accessed=4 * rows * columns, transcendentals=0
         ),
         name="finish",
-    )(probs, dscore, all_keys, all_values, early)
-    sums, messages = total_with(exchange("dp", sums), terms)
-    slots = [slot for slot in range(1, ctx) if slot != half]
-    back = [send_back(message, slot) for slot, message in zip(slots, messages)][::-1]
-    sums = [sums, send_back(sums, half)]
+    )(probs, dscore, all_keys, all_values, *early)
+    sums, messages = total_with(exchange("dp", sums), terms[: half - 1])
+    late = [send_back(message, slot) for slot, message in enumerate(messages, 1)]
+    sums = [sums] + [send_back(sums, slot) for slot in far]
     k_grad, v_grad, q_sum, v_sum = pl.pallas_call(
-        functools.partial(collect_kernel, batches, len(back)),
+        functools.partial(collect_kernel, batches, len(sums), len(early)),
         out_shape=[
             shape((tok, kv_width), jnp.bfloat16),
             shape((tok, kv_width), jnp.bfloat16),
             shape((heads, HEAD_DIM), jnp.float32),
             shape((kv_heads, HEAD_DIM), jnp.float32),
         ],
-        in_specs=[VMEM] * (4 + len(back)),
+        in_specs=[VMEM] * (len(sums) + 1 + len(early) + len(late)),
         out_specs=[VMEM] * 4,
         compiler_params=params(8),
         cost_estimate=pl.CostEstimate(
             flops=8 * tok * kv_width, bytes_accessed=16 * tok * kv_width, transcendentals=0
         ),
         name="collect",
-    )(*sums, own, early, *back)
+    )(*sums, own, *early, *late)
     return (
         attn[None],
         q_grad[None],

time: 38.2 us -> 38.9 us (1.018)
  other arithmetic: 0.88 us -> 0 us
  Pallas kernels: 8.16 us -> 9.04 us
  starting transfers between devices: 14.6 us -> 15.4 us
    pallas_call x1 -> x2, Pallas kernels: 0.7 us -> 1.59 us  [the longest x1 0.89 us: shards(): pl.pallas_call(pack_kernel, out_shape=shape((tok, 2 * kv_width), jnp.bflo...]
    concatenate x1 -> x0, other arithmetic: 0.88 us -> none  [shards(): pair = jnp.concatenate([k_proj[0], v_proj[0]], axis=1)]
    ppermute x4 -> x5, starting transfers between devices: 5.35 us -> 6.18 us  [send_back(): lax.ppermute(array, 'ctx', [(i, source_of(i, slot, size)) for i in range(...]
    ppermute x4 -> x5, waiting for transfers between devices: 2.76 us -> 2.71 us  [send_back(): lax.ppermute(array, 'ctx', [(i, source_of(i, slot, size)) for i in range(...]
  transfers between devices with their start and end apart: 10 -> 11, of which waited for: 6 -> 7; matrix products, arithmetic and copies ran while one was open for 0% -> 0% of each run, Pallas kernels for 12% -> 12%
where the time goes in v15:
time: 38.9 us; the launch traced here: 38.6 us
  starting transfers between devices  15.4 us (40%)
  waiting for transfers between devices  9.39 us (24%)
  Pallas kernels  9.04 us (23%)
  local copies, waits for them, and re-layouts  4.08 us (10%)
  between operations  0.69 us (2%)
    ppermute x6, starting transfers between devices, fetch(): lax.ppermute(array, axis, [(source_of(i, slot, size), i) for i in range(s...  9.24 us
    ppermute x6, waiting for transfers between devices, fetch(): lax.ppermute(array, axis, [(source_of(i, slot, size), i) for i in range(s...  6.68 us
    ppermute x5, starting transfers between devices, send_back(): lax.ppermute(array, 'ctx', [(i, source_of(i, slot, size)) for i in range(...  6.18 us
    unnamed x10, local copies, waits for them, and re-layouts  4.08 us
    pallas_call x1, Pallas kernels, attend(): pl.pallas_call(functools.partial(last_kernel, ctx, first_head), out_shape...  2.83 us
    ppermute x5, waiting for transfers between devices, send_back(): lax.ppermute(array, 'ctx', [(i, source_of(i, slot, size)) for i in range(...  2.71 us
    pallas_call x1, Pallas kernels, shards(): pl.pallas_call(finish_kernel, out_shape=[shape((tok, width), jnp.bfloat16...  1.81 us
    pallas_call x1, Pallas kernels, attend(): pl.pallas_call(near_kernel, out_shape=[shape((near, columns), jnp.float32...  1.68 us
  transfers between devices with their start and end apart: 11, of which 7 were waited for; matrix products, arithmetic and copies ran while one was open for 0% of the time, Pallas kernels for 12%

profile of v15, /device:TPU:0, one launch (start us, length us, event | category | flops | bytes accessed | tf_op | source)
XLA Modules:
  0.0 38.6 jit_solution(2035479529261050863)
XLA Ops:
  0.6 0.9 %pack.1.pair_ref.refs_0_ = bf16[128,512]{1,0:T(8,128)(2,1)S(1)} custom-call(bf16[128,256]{1,0:T(8,128)(2,1)} %bitcast.16, bf16[128,256]{1,0:T(8,128)(2,1)} %bitcast.17), custom_call_target="tpu_custom_call" | custom-call | bytes 262144 | tf_op jit(solution)/shard_map/pack/pallas_call | solution.py:412
  1.5 5.1 %collective-permute-start.1 = (bf16[128,512]{1,0:T(8,128)(2,1)S(1)}, bf16[128,512]{1,0:T(8,128)(2,1)S(1)}, u32[]{:S(2)}, u32[]{:S(2)}) collective-permute-start(bf16[128,512]{1,0:T(8,128)(2,1)S(1)} %pack.1.pair_ref.refs_0_), channel_id=1, source_target_pairs={{6,0},{4,2},{2,4},{0,6},{7,1},{5,3},{3,5},{1,7},{14,8},{12,10},{10... | collective-permute-start | bytes 393224 | tf_op jit(solution)/shard_map/ppermute | solution.py:59
  6.6 0.0 collective-permute-start
  6.6 0.6 %collective-permute-start.2 = (bf16[128,512]{1,0:T(8,128)(2,1)S(1)}, bf16[128,512]{1,0:T(8,128)(2,1)S(1)}, u32[]{:S(2)}, u32[]{:S(2)}) collective-permute-start(bf16[128,512]{1,0:T(8,128)(2,1)S(1)} %pack.1.pair_ref.refs_0_), channel_id=1, source_target_pairs={{4,0},{6,2},{0,4},{2,6},{5,1},{7,3},{1,5},{3,7},{12,8},{14,10},{8,... | collective-permute-start | bytes 393224 | tf_op jit(solution)/shard_map/ppermute | solution.py:59
  7.3 0.0 copy-start
  7.3 1.0 %copy-done = bf16[1,128,2048]{2,1,0:T(8,128)(2,1)S(1)} copy-done((bf16[1,128,2048]{2,1,0:T(8,128)(2,1)S(1)}, bf16[1,128,2048]{2,1,0:T(8,128)(2,1)}, u32[]{:S(2)}) %copy-start) | copy-done | bytes 524312
  8.3 0.0 copy-start.1
  8.3 1.0 %copy-done.1 = bf16[1,128,2048]{2,1,0:T(8,128)(2,1)S(1)} copy-done((bf16[1,128,2048]{2,1,0:T(8,128)(2,1)S(1)}, bf16[1,128,2048]{2,1,0:T(8,128)(2,1)}, u32[]{:S(2)}) %copy-start.1) | copy-done | bytes 524312
  9.4 0.0 copy-start.2
  9.4 0.7 %copy-done.2 = bf16[2048]{0:T(1024)(128)(2,1)S(1)} copy-done((bf16[2048]{0:T(1024)(128)(2,1)S(1)}, bf16[2048]{0:T(1024)(128)(2,1)}, u32[]{:S(2)}) %copy-start.2) | copy-done | bytes 4120
  10.1 0.0 copy-start.3
  10.1 0.7 %copy-done.3 = s32[1,8]{1,0:T(1,128)S(1)} copy-done((s32[1,8]{1,0:T(1,128)S(1)}, s32[1,8]{1,0:T(1,128)}, u32[]{:S(2)}) %copy-start.3) | copy-done | bytes 56
  10.7 0.0 copy-start.4
  10.7 0.7 %copy-done.4 = bf16[256]{0:T(256)(128)(2,1)S(1)} copy-done((bf16[256]{0:T(256)(128)(2,1)S(1)}, bf16[256]{0:T(256)(128)(2,1)}, u32[]{:S(2)}) %copy-start.4) | copy-done | bytes 536
  11.4 1.1 %prepare.1 = (bf16[2,128]{1,0:T(2,128)(2,1)S(1)}, bf16[2048,256]{1,0:T(8,128)(2,1)S(1)}, bf16[2048,128]{1,0:T(8,128)(2,1)S(1)}, f32[128,2048]{1,0:T(8,128)S(1)},...) custom-call(s32[1,8]{1,0:T(1,128)S(1)} %copy-done.3, bf16[128,512]{1,0:T(8,128)(2,1)S(1)} %pack.1.pair_ref.refs_0_, ...), custom_call_target="tpu_custom_call" | custom-call | flops 134217728 | bytes 4194304 | tf_op jit(solution)/shard_map/prepare/pallas_call | solution.py:425
  12.5 0.0 collective-permute-done.1.refs_2_
  12.5 1.5 %collective-permute-done.refs_1_ = bf16[128,512]{1,0:T(8,128)(2,1)S(1)} collective-permute-done((bf16[128,512]{1,0:T(8,128)(2,1)S(1)}, bf16[128,512]{1,0:T(8,128)(2,1)S(1)}, u32[]{:S(2)}, u32[]{:S(2)}) %collective-permute-start) | collective-permute-done | bytes 131104 | tf_op jit(solution)/shard_map/ppermute | solution.py:59
  14.0 1.7 %near.1 = (f32[384,2048]{1,0:T(8,128)S(1)}, f32[384,2048]{1,0:T(8,128)S(1)}, f32[8,2048]{1,0:T(8,128)S(1)}, bf16[384,256]{1,0:T(8,128)(2,1)S(1)}, bf16[384,256]{1,0:T(8,128)(2,1)S(1)}) custom-call(bf16[2,128]{1,0:T(2,128)(2,1)S(1)} %get-tuple-element.36.bias_ref.refs_0_, bf16[2048,256]{1,0:T(8,128)(2,1)S(1)} %get-tuple-element.37.queries_ref.refs_1_, ...), custom_call_target="tpu_custom_call" | custom-call | flops 402653184 | bytes 6291456 | tf_op jit(solution)/shard_map/near/pallas_call | solution.py:351
  15.7 2.0 %collective-permute-done.2.refs_9_ = bf16[128,512]{1,0:T(8,128)(2,1)S(1)} collective-permute-done((bf16[128,512]{1,0:T(8,128)(2,1)S(1)}, bf16[128,512]{1,0:T(8,128)(2,1)S(1)}, u32[]{:S(2)}, u32[]{:S(2)}) %collective-permute-start.2) | collective-permute-done | bytes 131104 | tf_op jit(solution)/shard_map/ppermute | solution.py:59
  17.7 2.8 %last.1 = (bf16[512,2048]{1,0:T(8,128)(2,1)S(1)}, bf16[512,2048]{1,0:T(8,128)(2,1)S(1)}, bf16[512,256]{1,0:T(8,128)(2,1)S(1)}, bf16[512,256]{1,0:T(8,128)(2,1)S(...) custom-call(bf16[2,128]{1,0:T(2,128)(2,1)S(1)} %get-tuple-element.36, ...), custom_call_target="tpu_custom_call" | custom-call | flops 536870912 | bytes 4194304 | tf_op jit(solution)/shard_map/last/pallas_call | solution.py:371
  20.6 0.9 %collective-permute-start.3 = (bf16[128,512]{1,0:T(8,128)(2,1)S(1)}, bf16[128,512]{1,0:T(8,128)(2,1)S(1)}, u32[]{:S(2)}, u32[]{:S(2)}) collective-permute-start(bf16[128,512]{1,0:T(8,128)(2,1)S(1)} %get-tuple-element.51), channel_id=1, source_target_pairs={{0,4},{2,6},{4,0},{6,2},{1,5},{3,7},{5,1},{7,3},{8,12},{10,14},{12... | collective-permute-start | bytes 393224 | tf_op jit(solution)/shard_map/ppermute | solution.py:64
  21.5 1.7 %collective-permute-start.4 = (bf16[128,512]{1,0:T(8,128)(2,1)S(1)}, bf16[128,512]{1,0:T(8,128)(2,1)S(1)}, u32[]{:S(2)}, u32[]{:S(2)}) collective-permute-start(bf16[128,512]{1,0:T(8,128)(2,1)S(1)} %get-tuple-element.52), channel_id=1, source_target_pairs={{0,6},{2,4},{4,2},{6,0},{1,7},{3,5},{5,3},{7,1},{8,14},{10,12},{12... | collective-permute-start | bytes 393224 | tf_op jit(solution)/shard_map/ppermute | solution.py:64
  23.2 2.4 %collective-permute-start.7 = (f32[18,128]{1,0:T(8,128)S(1)}, f32[18,128]{1,0:T(8,128)S(1)}, u32[]{:S(2)}, u32[]{:S(2)}) collective-permute-start(f32[18,128]{1,0:T(8,128)S(1)} %get-tuple-element.55.refs_0_), channel_id=1, source_target_pairs={{24,0},{16,8},{8,16},{0,24},{25,1},{17,9},{9,17},{1,25},{26,2},{18... | collective-permute-start | bytes 27656 | tf_op jit(solution)/shard_map/ppermute | solution.py:59
  25.6 0.5 %collective-permute-start.6 = (f32[18,128]{1,0:T(8,128)S(1)}, f32[18,128]{1,0:T(8,128)S(1)}, u32[]{:S(2)}, u32[]{:S(2)}) collective-permute-start(f32[18,128]{1,0:T(8,128)S(1)} %get-tuple-element.55.refs_0_), channel_id=1, source_target_pairs={{16,0},{24,8},{0,16},{8,24},{17,1},{25,9},{1,17},{9,25},{18,2},{26... | collective-permute-start | bytes 27656 | tf_op jit(solution)/shard_map/ppermute | solution.py:59
  26.1 0.5 %collective-permute-start.5 = (f32[18,128]{1,0:T(8,128)S(1)}, f32[18,128]{1,0:T(8,128)S(1)}, u32[]{:S(2)}, u32[]{:S(2)}) collective-permute-start(f32[18,128]{1,0:T(8,128)S(1)} %get-tuple-element.55.refs_0_), channel_id=1, source_target_pairs={{8,0},{0,8},{24,16},{16,24},{9,1},{1,9},{25,17},{17,25},{10,2},{2,... | collective-permute-start | bytes 27656 | tf_op jit(solution)/shard_map/ppermute | solution.py:59
  26.7 1.1 %collective-permute-done.7.refs_3_ = f32[18,128]{1,0:T(8,128)S(1)} collective-permute-done((f32[18,128]{1,0:T(8,128)S(1)}, f32[18,128]{1,0:T(8,128)S(1)}, u32[]{:S(2)}, u32[]{:S(2)}) %collective-permute-start.7) | collective-permute-done | bytes 9248 | tf_op jit(solution)/shard_map/ppermute | solution.py:59
  27.8 1.5 %collective-permute-done.6.refs_2_ = f32[18,128]{1,0:T(8,128)S(1)} collective-permute-done((f32[18,128]{1,0:T(8,128)S(1)}, f32[18,128]{1,0:T(8,128)S(1)}, u32[]{:S(2)}, u32[]{:S(2)}) %collective-permute-start.6) | collective-permute-done | bytes 9248 | tf_op jit(solution)/shard_map/ppermute | solution.py:59
  29.3 0.5 %collective-permute-done.5.refs_1_ = f32[18,128]{1,0:T(8,128)S(1)} collective-permute-done((f32[18,128]{1,0:T(8,128)S(1)}, f32[18,128]{1,0:T(8,128)S(1)}, u32[]{:S(2)}, u32[]{:S(2)}) %collective-permute-start.5) | collective-permute-done | bytes 9248 | tf_op jit(solution)/shard_map/ppermute | solution.py:59
  29.9 1.0 %collective-permute-start.10 = (bf16[144,512]{1,0:T(8,128)(2,1)S(1)}, bf16[144,512]{1,0:T(8,128)(2,1)S(1)}, u32[]{:S(2)}, u32[]{:S(2)}) collective-permute-start(bf16[144,512]{1,0:T(8,128)(2,1)S(1)} %get-tuple-element.61), channel_id=1, source_target_pairs={{0,2},{2,0},{4,6},{6,4},{1,3},{3,1},{5,7},{7,5},{8,10},{10,8},{12,... | collective-permute-start | bytes 442376 | tf_op jit(solution)/shard_map/ppermute | solution.py:64
  30.9 2.5 %collective-permute-start.9 = (f32[18,128]{1,0:T(8,128)S(1)}, f32[18,128]{1,0:T(8,128)S(1)}, u32[]{:S(2)}, u32[]{:S(2)}) collective-permute-start(f32[18,128]{1,0:T(8,128)S(1)} %get-tuple-element.57.refs_0_), channel_id=1, source_target_pairs={{0,6},{2,4},{4,2},{6,0},{1,7},{3,5},{5,3},{7,1},{8,14},{10,12},{12... | collective-permute-start | bytes 27656 | tf_op jit(solution)/shard_map/ppermute | solution.py:64
  33.3 0.1 collective-permute-start.8
  33.4 0.0 collective-permute-done.3.refs_0_
  33.4 0.0 collective-permute-done.4.refs_1_
  33.4 1.8 %finish.1 = (bf16[128,2048]{1,0:T(8,128)(2,1)}, bf16[128,2048]{1,0:T(8,128)(2,1)}, bf16[128,512]{1,0:T(8,128)(2,1)S(1)}, bf16[128,512]{1,0:T(8,128)(2,1)S(1)}) custom-call(bf16[512,2048]{1,0:T(8,128)(2,1)S(1)} %get-tuple-element.47.probs_ref, bf16[512,2048]{1,0:T(8,128)(2,1)S(1)} %get-tuple-element.48.dscore_ref, ...), custom_call_target="tpu_custom_call", output_to_operand_aliasing={{2}: (4, {}), {3}: (5, {})} | custom-call | flops 536870912 | bytes 4194304 | tf_op jit(solution)/shard_map/finish/pallas_call | solution.py:476
  35.2 1.4 %collective-permute-done.9.refs_2_ = f32[18,128]{1,0:T(8,128)S(1)} collective-permute-done((f32[18,128]{1,0:T(8,128)S(1)}, f32[18,128]{1,0:T(8,128)S(1)}, u32[]{:S(2)}, u32[]{:S(2)}) %collective-permute-start.9) | collective-permute-done | bytes 9248 | tf_op jit(solution)/shard_map/ppermute | solution.py:64
  36.6 1.3 %collective-permute-done.8.refs_1_ = f32[18,128]{1,0:T(8,128)S(1)} collective-permute-done((f32[18,128]{1,0:T(8,128)S(1)}, f32[18,128]{1,0:T(8,128)S(1)}, u32[]{:S(2)}, u32[]{:S(2)}) %collective-permute-start.8) | collective-permute-done | bytes 9248 | tf_op jit(solution)/shard_map/ppermute | solution.py:64
  37.9 0.0 collective-permute-done.10.refs_6_
  37.9 0.7 %collect.1 = (bf16[128,256]{1,0:T(8,128)(2,1)}, bf16[128,256]{1,0:T(8,128)(2,1)}, f32[16,128]{1,0:T(8,128)}, f32[2,128]{1,0:T(2,128)}) custom-call(f32[18,128]{1,0:T(8,128)S(1)} %get-tuple-element.57.refs_0_, f32[18,128]{1,0:T(8,128)S(1)} %collective-permute-done.8.refs_1_, f32[18,128]{1,0:T(8,128)S(1)} %collective-permute-done.9.refs_2_, ...), custom_call_target="tpu_custom_call" | custom-call | flops 262144 | bytes 524288 | tf_op jit(solution)/shard_map/collect/pallas_call | solution.py:495
  (1 shorter events, 0.0 us)
Async XLA Ops:
  1.5 11.0 %collective-permute-start.1 = (bf16[128,512]{1,0:T(8,128)(2,1)S(1)}, bf16[128,512]{1,0:T(8,128)(2,1)S(1)}, u32[]{:S(2)}, u32[]{:S(2)}) collective-permute-start(bf16[128,512]{1,0:T(8,128)(2,1)S(1)} %pack.1.pair_ref.refs_0_), channel_id=1, source_target_pairs={{6,0},{4,2},{2,4},{0,6},{7,1},{5,3},{3,5},{1,7},{14,8},{12,10},{10... | collective-permute-start | bytes 393224 | tf_op jit(solution)/shard_map/ppermute | solution.py:59
  6.6 7.4 %collective-permute-start = (bf16[128,512]{1,0:T(8,128)(2,1)S(1)}, bf16[128,512]{1,0:T(8,128)(2,1)S(1)}, u32[]{:S(2)}, u32[]{:S(2)}) collective-permute-start(bf16[128,512]{1,0:T(8,128)(2,1)S(1)} %pack.1.pair_ref.refs_0_), channel_id=1, source_target_pairs={{2,0},{0,2},{6,4},{4,6},{3,1},{1,3},{7,5},{5,7},{10,8},{8,10},{14,... | collective-permute-start | bytes 393224 | tf_op jit(solution)/shard_map/ppermute | solution.py:59
  6.6 11.1 %collective-permute-start.2 = (bf16[128,512]{1,0:T(8,128)(2,1)S(1)}, bf16[128,512]{1,0:T(8,128)(2,1)S(1)}, u32[]{:S(2)}, u32[]{:S(2)}) collective-permute-start(bf16[128,512]{1,0:T(8,128)(2,1)S(1)} %pack.1.pair_ref.refs_0_), channel_id=1, source_target_pairs={{4,0},{6,2},{0,4},{2,6},{5,1},{7,3},{1,5},{3,7},{12,8},{14,10},{8,... | collective-permute-start | bytes 393224 | tf_op jit(solution)/shard_map/ppermute | solution.py:59
  7.3 1.0 %copy-start = (bf16[1,128,2048]{2,1,0:T(8,128)(2,1)S(1)}, bf16[1,128,2048]{2,1,0:T(8,128)(2,1)}, u32[]{:S(2)}) copy-start(bf16[1,128,2048]{2,1,0:T(8,128)(2,1)} %param.7) | copy-start | bytes 1572868
  8.3 1.0 %copy-start.1 = (bf16[1,128,2048]{2,1,0:T(8,128)(2,1)S(1)}, bf16[1,128,2048]{2,1,0:T(8,128)(2,1)}, u32[]{:S(2)}) copy-start(bf16[1,128,2048]{2,1,0:T(8,128)(2,1)} %param.12) | copy-start | bytes 1572868
  9.4 0.7 %copy-start.2 = (bf16[2048]{0:T(1024)(128)(2,1)S(1)}, bf16[2048]{0:T(1024)(128)(2,1)}, u32[]{:S(2)}) copy-start(bf16[2048]{0:T(1024)(128)(2,1)} %param.8) | copy-start | bytes 12292
  10.1 0.7 %copy-start.3 = (s32[1,8]{1,0:T(1,128)S(1)}, s32[1,8]{1,0:T(1,128)}, u32[]{:S(2)}) copy-start(s32[1,8]{1,0:T(1,128)} %len_ref.1) | copy-start | bytes 100
  10.7 0.7 %copy-start.4 = (bf16[256]{0:T(256)(128)(2,1)S(1)}, bf16[256]{0:T(256)(128)(2,1)}, u32[]{:S(2)}) copy-start(bf16[256]{0:T(256)(128)(2,1)} %param.11) | copy-start | bytes 1540
  20.6 12.9 %collective-permute-start.3 = (bf16[128,512]{1,0:T(8,128)(2,1)S(1)}, bf16[128,512]{1,0:T(8,128)(2,1)S(1)}, u32[]{:S(2)}, u32[]{:S(2)}) collective-permute-start(bf16[128,512]{1,0:T(8,128)(2,1)S(1)} %get-tuple-element.51), channel_id=1, source_target_pairs={{0,4},{2,6},{4,0},{6,2},{1,5},{3,7},{5,1},{7,3},{8,12},{10,14},{12... | collective-permute-start | bytes 393224 | tf_op jit(solution)/shard_map/ppermute | solution.py:64
  21.5 12.0 %collective-permute-start.4 = (bf16[128,512]{1,0:T(8,128)(2,1)S(1)}, bf16[128,512]{1,0:T(8,128)(2,1)S(1)}, u32[]{:S(2)}, u32[]{:S(2)}) collective-permute-start(bf16[128,512]{1,0:T(8,128)(2,1)S(1)} %get-tuple-element.52), channel_id=1, source_target_pairs={{0,6},{2,4},{4,2},{6,0},{1,7},{3,5},{5,3},{7,1},{8,14},{10,12},{12... | collective-permute-start | bytes 393224 | tf_op jit(solution)/shard_map/ppermute | solution.py:64
  23.2 4.6 %collective-permute-start.7 = (f32[18,128]{1,0:T(8,128)S(1)}, f32[18,128]{1,0:T(8,128)S(1)}, u32[]{:S(2)}, u32[]{:S(2)}) collective-permute-start(f32[18,128]{1,0:T(8,128)S(1)} %get-tuple-element.55.refs_0_), channel_id=1, source_target_pairs={{24,0},{16,8},{8,16},{0,24},{25,1},{17,9},{9,17},{1,25},{26,2},{18... | collective-permute-start | bytes 27656 | tf_op jit(solution)/shard_map/ppermute | solution.py:59
  25.6 3.7 %collective-permute-start.6 = (f32[18,128]{1,0:T(8,128)S(1)}, f32[18,128]{1,0:T(8,128)S(1)}, u32[]{:S(2)}, u32[]{:S(2)}) collective-permute-start(f32[18,128]{1,0:T(8,128)S(1)} %get-tuple-element.55.refs_0_), channel_id=1, source_target_pairs={{16,0},{24,8},{0,16},{8,24},{17,1},{25,9},{1,17},{9,25},{18,2},{26... | collective-permute-start | bytes 27656 | tf_op jit(solution)/shard_map/ppermute | solution.py:59
  26.1 3.7 %collective-permute-start.5 = (f32[18,128]{1,0:T(8,128)S(1)}, f32[18,128]{1,0:T(8,128)S(1)}, u32[]{:S(2)}, u32[]{:S(2)}) collective-permute-start(f32[18,128]{1,0:T(8,128)S(1)} %get-tuple-element.55.refs_0_), channel_id=1, source_target_pairs={{8,0},{0,8},{24,16},{16,24},{9,1},{1,9},{25,17},{17,25},{10,2},{2,... | collective-permute-start | bytes 27656 | tf_op jit(solution)/shard_map/ppermute | solution.py:59
  29.9 8.1 %collective-permute-start.10 = (bf16[144,512]{1,0:T(8,128)(2,1)S(1)}, bf16[144,512]{1,0:T(8,128)(2,1)S(1)}, u32[]{:S(2)}, u32[]{:S(2)}) collective-permute-start(bf16[144,512]{1,0:T(8,128)(2,1)S(1)} %get-tuple-element.61), channel_id=1, source_target_pairs={{0,2},{2,0},{4,6},{6,4},{1,3},{3,1},{5,7},{7,5},{8,10},{10,8},{12,... | collective-permute-start | bytes 442376 | tf_op jit(solution)/shard_map/ppermute | solution.py:64
  30.9 5.7 %collective-permute-start.9 = (f32[18,128]{1,0:T(8,128)S(1)}, f32[18,128]{1,0:T(8,128)S(1)}, u32[]{:S(2)}, u32[]{:S(2)}) collective-permute-start(f32[18,128]{1,0:T(8,128)S(1)} %get-tuple-element.57.refs_0_), channel_id=1, source_target_pairs={{0,6},{2,4},{4,2},{6,0},{1,7},{3,5},{5,3},{7,1},{8,14},{10,12},{12... | collective-permute-start | bytes 27656 | tf_op jit(solution)/shard_map/ppermute | solution.py:64
  33.3 4.6 %collective-permute-start.8 = (f32[18,128]{1,0:T(8,128)S(1)}, f32[18,128]{1,0:T(8,128)S(1)}, u32[]{:S(2)}, u32[]{:S(2)}) collective-permute-start(f32[18,128]{1,0:T(8,128)S(1)} %get-tuple-element.57.refs_0_), channel_id=1, source_target_pairs={{0,4},{2,6},{4,0},{6,2},{1,5},{3,7},{5,1},{7,3},{8,12},{10,14},{12... | collective-permute-start | bytes 27656 | tf_op jit(solution)/shard_map/ppermute | solution.py:64

commit v16 on v14

--- a/solution.py
+++ b/solution.py
@@ -12,7 +12,7 @@
 KV_HEADS = 4
 GROUP = HEADS // KV_HEADS
 PAIR = 2
-BLOCK = 64
+BLOCK = 32
 SCALE = HEAD_DIM ** (-0.5)
 LOG2E = 1.4426950408889634
 NEGATIVE = -1e30
@@ -248,21 +248,22 @@
 
 
 def collect_kernel(batches, messages, *refs):
-    sum_refs, refs = refs[:2], refs[2:]
-    own_ref, early_ref, refs = refs[0], refs[1], refs[2:]
+    sum_refs, (own_ref, early_ref), refs = refs[:2], refs[2:4], refs[4:]
     message_refs, (kg_ref, vg_ref, qb_ref, vb_ref) = refs[:messages], refs[messages:]
     heads, kv_heads = qb_ref.shape[0], vb_ref.shape[0]
     tok, kv_width = kg_ref.shape
     total = sum_refs[0][...] + sum_refs[1][...]
+    query_sums, value_sums = total[:heads], total[heads:]
     term = own_ref[...] + early_ref[...].astype(jnp.float32)
     for ref in message_refs:
-        sums = ref[tok:, :].astype(jnp.float32)
-        sums = sums[:, :HEAD_DIM] + sums[:, HEAD_DIM : 2 * HEAD_DIM]
-        total = total + sums[: heads + kv_heads]
+        added = ref[tok:, :].astype(jnp.float32)
+        high_and_low = added[:, : 2 * HEAD_DIM], added[:, 2 * HEAD_DIM : 4 * HEAD_DIM]
+        of_queries, of_values = (both[:, :HEAD_DIM] + both[:, HEAD_DIM:] for both in high_and_low)
+        query_sums = query_sums + of_queries[:heads]
+        value_sums = value_sums + of_values[:kv_heads]
         term = term + ref[:tok, :].astype(jnp.float32)
-    total = total * (1.0 / batches)
-    qb_ref[...] = total[:heads]
-    vb_ref[...] = total[heads:]
+    qb_ref[...] = query_sums * (1.0 / batches)
+    vb_ref[...] = value_sums * (1.0 / batches)
     term = term.astype(jnp.bfloat16)
     kg_ref[...] = term[:, :kv_width]
     vg_ref[...] = term[:, kv_width:]
@@ -277,18 +278,27 @@
         total = total + ref[...]
     total_ref[...] = total
     for term_ref, message_ref in zip(term_refs, message_refs):
-        tok = term_ref.shape[0]
-        rows = message_ref.shape[0] - tok
-        high = jnp.concatenate([total, jnp.zeros((rows - total.shape[0], HEAD_DIM), jnp.float32)])
+        tok, kv_heads = term_ref.shape[0], term_ref.shape[1] // (2 * HEAD_DIM)
         message_ref[:tok, :] = term_ref[...]
-        message_ref[tok:, :] = jnp.zeros((rows, term_ref.shape[1]), jnp.bfloat16)
-        message_ref[tok:, :HEAD_DIM] = high.astype(jnp.bfloat16)
-        low = high - high.astype(jnp.bfloat16).astype(jnp.float32)
-        message_ref[tok:, HEAD_DIM : 2 * HEAD_DIM] = low.astype(jnp.bfloat16)
+        message_ref[tok:, : 4 * HEAD_DIM] = added_rows(
+            total, total.shape[0] - kv_heads, message_ref.shape[0] - tok
+        )
+
+
+def added_rows(total, heads, rows):
+    high = total.astype(jnp.bfloat16).astype(jnp.float32)
+    both = jnp.concatenate([high, total - high], axis=1)
+    blocks = [
+        jnp.concatenate([block, jnp.zeros((rows - block.shape[0], 2 * HEAD_DIM), jnp.float32)])
+        if block.shape[0] < rows
+        else block
+        for block in (both[:heads], both[heads:])
+    ]
+    return jnp.concatenate(blocks, axis=1).astype(jnp.bfloat16)
 
 
 def total_with(parts, terms):
-    rows = -(-parts[0].shape[0] // 16) * 16
+    rows = -(-parts[0].shape[0] * GROUP // (GROUP + 1) // 16) * 16
     total, *messages = pl.pallas_call(
         functools.partial(total_kernel, len(parts)),
         out_shape=[shape(parts[0].shape, parts[0].dtype)]

time: 38.2 us -> 37.8 us (0.990)
  no operation moved by 1% of the time
where the time goes in v16:
time: 37.8 us; the launch traced here: 37.5 us
  starting transfers between devices  14.6 us (39%)
  waiting for transfers between devices  9.11 us (24%)
  Pallas kernels  8.12 us (21%)
  local copies, waits for them, and re-layouts  4.08 us (11%)
  other arithmetic  0.88 us (2%)
  between operations  0.68 us (2%)
    ppermute x6, starting transfers between devices, fetch(): lax.ppermute(array, axis, [(source_of(i, slot, size), i) for i in range(s...  9.24 us
    ppermute x6, waiting for transfers between devices, fetch(): lax.ppermute(array, axis, [(source_of(i, slot, size), i) for i in range(s...  6.71 us
    ppermute x4, starting transfers between devices, send_back(): lax.ppermute(array, 'ctx', [(i, source_of(i, slot, size)) for i in range(...  5.35 us
    unnamed x10, local copies, waits for them, and re-layouts  4.08 us
    pallas_call x1, Pallas kernels, attend(): pl.pallas_call(functools.partial(last_kernel, ctx, first_head), out_shape...  2.82 us
    ppermute x4, waiting for transfers between devices, send_back(): lax.ppermute(array, 'ctx', [(i, source_of(i, slot, size)) for i in range(...  2.41 us
    pallas_call x1, Pallas kernels, shards(): pl.pallas_call(finish_kernel, out_shape=[shape((tok, width), jnp.bfloat16...  1.8 us
    pallas_call x1, Pallas kernels, attend(): pl.pallas_call(near_kernel, out_shape=[shape((near, columns), jnp.float32...  1.67 us
  transfers between devices with their start and end apart: 10, of which 6 were waited for; matrix products, arithmetic and copies ran while one was open for 0% of the time, Pallas kernels for 12%

profile of v16, /device:TPU:0, one launch (start us, length us, event | category | flops | bytes accessed | tf_op | source)
XLA Modules:
  0.0 37.5 jit_solution(2668468864188518920)
XLA Ops:
  0.6 0.9 %pad_maximum_fusion.pair_ref.refs_0_ = bf16[128,512]{1,0:T(8,128)(2,1)S(1)} fusion(bf16[128,256]{1,0:T(8,128)(2,1)} %bitcast.16, bf16[128,256]{1,0:T(8,128)(2,1)} %bitcast.17), kind=kLoop, calls=%fused_computation | loop fusion | flops 262144 | bytes 262144 | tf_op jit(solution)/shard_map/concatenate | solution.py:388
  1.5 5.1 %collective-permute-start.1 = (bf16[128,512]{1,0:T(8,128)(2,1)S(1)}, bf16[128,512]{1,0:T(8,128)(2,1)S(1)}, u32[]{:S(2)}, u32[]{:S(2)}) collective-permute-start(bf16[128,512]{1,0:T(8,128)(2,1)S(1)} %pad_maximum_fusion.pair_ref.refs_0_), channel_id=1, source_target_pairs={{6,0},{4,2},{2,4},{0,6},{7,1},{5,3},{3,5},{1,7},{14,8},{12,10},{10... | collective-permute-start | bytes 393224 | tf_op jit(solution)/shard_map/ppermute | solution.py:58
  6.6 0.0 collective-permute-start
  6.6 0.6 %collective-permute-start.2 = (bf16[128,512]{1,0:T(8,128)(2,1)S(1)}, bf16[128,512]{1,0:T(8,128)(2,1)S(1)}, u32[]{:S(2)}, u32[]{:S(2)}) collective-permute-start(bf16[128,512]{1,0:T(8,128)(2,1)S(1)} %pad_maximum_fusion.pair_ref.refs_0_), channel_id=1, source_target_pairs={{4,0},{6,2},{0,4},{2,6},{5,1},{7,3},{1,5},{3,7},{12,8},{14,10},{8,... | collective-permute-start | bytes 393224 | tf_op jit(solution)/shard_map/ppermute | solution.py:58
  7.3 0.0 copy-start
  7.3 1.0 %copy-done = bf16[1,128,2048]{2,1,0:T(8,128)(2,1)S(1)} copy-done((bf16[1,128,2048]{2,1,0:T(8,128)(2,1)S(1)}, bf16[1,128,2048]{2,1,0:T(8,128)(2,1)}, u32[]{:S(2)}) %copy-start) | copy-done | bytes 524312
  8.3 0.0 copy-start.1
  8.3 1.0 %copy-done.1 = bf16[1,128,2048]{2,1,0:T(8,128)(2,1)S(1)} copy-done((bf16[1,128,2048]{2,1,0:T(8,128)(2,1)S(1)}, bf16[1,128,2048]{2,1,0:T(8,128)(2,1)}, u32[]{:S(2)}) %copy-start.1) | copy-done | bytes 524312
  9.4 0.0 copy-start.2
  9.4 0.7 %copy-done.2 = bf16[2048]{0:T(1024)(128)(2,1)S(1)} copy-done((bf16[2048]{0:T(1024)(128)(2,1)S(1)}, bf16[2048]{0:T(1024)(128)(2,1)}, u32[]{:S(2)}) %copy-start.2) | copy-done | bytes 4120
  10.0 0.0 copy-start.3
  10.0 0.7 %copy-done.3 = s32[1,8]{1,0:T(1,128)S(1)} copy-done((s32[1,8]{1,0:T(1,128)S(1)}, s32[1,8]{1,0:T(1,128)}, u32[]{:S(2)}) %copy-start.3) | copy-done | bytes 56
  10.7 0.0 copy-start.4
  10.7 0.7 %copy-done.4 = bf16[256]{0:T(256)(128)(2,1)S(1)} copy-done((bf16[256]{0:T(256)(128)(2,1)S(1)}, bf16[256]{0:T(256)(128)(2,1)}, u32[]{:S(2)}) %copy-start.4) | copy-done | bytes 536
  11.4 1.1 %prepare.1 = (bf16[2,128]{1,0:T(2,128)(2,1)S(1)}, bf16[2048,256]{1,0:T(8,128)(2,1)S(1)}, bf16[2048,128]{1,0:T(8,128)(2,1)S(1)}, f32[128,2048]{1,0:T(8,128)S(1)},...) custom-call(s32[1,8]{1,0:T(1,128)S(1)} %copy-done.3, bf16[128,512]{1,0:T(8,128)(2,1)S(1)} %pad_maximum_fusion.pair_ref.refs_0_, ...), custom_call_target="tpu_custom_call" | custom-call | flops 134217728 | bytes 4194304 | tf_op jit(solution)/shard_map/prepare/pallas_call | solution.py:390
  12.5 0.0 collective-permute-done.1.refs_2_
  12.5 1.5 %collective-permute-done.refs_1_ = bf16[128,512]{1,0:T(8,128)(2,1)S(1)} collective-permute-done((bf16[128,512]{1,0:T(8,128)(2,1)S(1)}, bf16[128,512]{1,0:T(8,128)(2,1)S(1)}, u32[]{:S(2)}, u32[]{:S(2)}) %collective-permute-start) | collective-permute-done | bytes 131104 | tf_op jit(solution)/shard_map/ppermute | solution.py:58
  14.0 1.7 %near.1 = (f32[384,2048]{1,0:T(8,128)S(1)}, f32[384,2048]{1,0:T(8,128)S(1)}, f32[8,2048]{1,0:T(8,128)S(1)}, bf16[384,256]{1,0:T(8,128)(2,1)S(1)}, bf16[384,256]{1,0:T(8,128)(2,1)S(1)}) custom-call(bf16[2,128]{1,0:T(2,128)(2,1)S(1)} %get-tuple-element.36.bias_ref.refs_0_, bf16[2048,256]{1,0:T(8,128)(2,1)S(1)} %get-tuple-element.37.queries_ref.refs_1_, ...), custom_call_target="tpu_custom_call" | custom-call | flops 402653184 | bytes 6291456 | tf_op jit(solution)/shard_map/near/pallas_call | solution.py:327
  15.7 2.0 %collective-permute-done.2.refs_9_ = bf16[128,512]{1,0:T(8,128)(2,1)S(1)} collective-permute-done((bf16[128,512]{1,0:T(8,128)(2,1)S(1)}, bf16[128,512]{1,0:T(8,128)(2,1)S(1)}, u32[]{:S(2)}, u32[]{:S(2)}) %collective-permute-start.2) | collective-permute-done | bytes 131104 | tf_op jit(solution)/shard_map/ppermute | solution.py:58
  17.7 2.8 %last.1 = (bf16[512,2048]{1,0:T(8,128)(2,1)S(1)}, bf16[512,2048]{1,0:T(8,128)(2,1)S(1)}, bf16[512,256]{1,0:T(8,128)(2,1)S(1)}, bf16[512,256]{1,0:T(8,128)(2,1)S(...) custom-call(bf16[2,128]{1,0:T(2,128)(2,1)S(1)} %get-tuple-element.36, ...), custom_call_target="tpu_custom_call" | custom-call | flops 536870912 | bytes 4194304 | tf_op jit(solution)/shard_map/last/pallas_call | solution.py:347
  20.5 0.9 %collective-permute-start.3 = (bf16[128,512]{1,0:T(8,128)(2,1)S(1)}, bf16[128,512]{1,0:T(8,128)(2,1)S(1)}, u32[]{:S(2)}, u32[]{:S(2)}) collective-permute-start(bf16[128,512]{1,0:T(8,128)(2,1)S(1)} %get-tuple-element.51), channel_id=1, source_target_pairs={{0,4},{2,6},{4,0},{6,2},{1,5},{3,7},{5,1},{7,3},{8,12},{10,14},{12... | collective-permute-start | bytes 393224 | tf_op jit(solution)/shard_map/ppermute | solution.py:63
  21.4 2.4 %collective-permute-start.6 = (f32[18,128]{1,0:T(8,128)S(1)}, f32[18,128]{1,0:T(8,128)S(1)}, u32[]{:S(2)}, u32[]{:S(2)}) collective-permute-start(f32[18,128]{1,0:T(8,128)S(1)} %get-tuple-element.54.refs_0_), channel_id=1, source_target_pairs={{24,0},{16,8},{8,16},{0,24},{25,1},{17,9},{9,17},{1,25},{26,2},{18... | collective-permute-start | bytes 27656 | tf_op jit(solution)/shard_map/ppermute | solution.py:58
  23.9 0.5 %collective-permute-start.5 = (f32[18,128]{1,0:T(8,128)S(1)}, f32[18,128]{1,0:T(8,128)S(1)}, u32[]{:S(2)}, u32[]{:S(2)}) collective-permute-start(f32[18,128]{1,0:T(8,128)S(1)} %get-tuple-element.54.refs_0_), channel_id=1, source_target_pairs={{16,0},{24,8},{0,16},{8,24},{17,1},{25,9},{1,17},{9,25},{18,2},{26... | collective-permute-start | bytes 27656 | tf_op jit(solution)/shard_map/ppermute | solution.py:58
  24.4 0.5 %collective-permute-start.4 = (f32[18,128]{1,0:T(8,128)S(1)}, f32[18,128]{1,0:T(8,128)S(1)}, u32[]{:S(2)}, u32[]{:S(2)}) collective-permute-start(f32[18,128]{1,0:T(8,128)S(1)} %get-tuple-element.54.refs_0_), channel_id=1, source_target_pairs={{8,0},{0,8},{24,16},{16,24},{9,1},{1,9},{25,17},{17,25},{10,2},{2,... | collective-permute-start | bytes 27656 | tf_op jit(solution)/shard_map/ppermute | solution.py:58
  24.9 1.1 %collective-permute-done.6.refs_3_ = f32[18,128]{1,0:T(8,128)S(1)} collective-permute-done((f32[18,128]{1,0:T(8,128)S(1)}, f32[18,128]{1,0:T(8,128)S(1)}, u32[]{:S(2)}, u32[]{:S(2)}) %collective-permute-start.6) | collective-permute-done | bytes 9248 | tf_op jit(solution)/shard_map/ppermute | solution.py:58
  26.0 1.5 %collective-permute-done.5.refs_2_ = f32[18,128]{1,0:T(8,128)S(1)} collective-permute-done((f32[18,128]{1,0:T(8,128)S(1)}, f32[18,128]{1,0:T(8,128)S(1)}, u32[]{:S(2)}, u32[]{:S(2)}) %collective-permute-start.5) | collective-permute-done | bytes 9248 | tf_op jit(solution)/shard_map/ppermute | solution.py:58
  27.6 0.5 %collective-permute-done.4.refs_1_ = f32[18,128]{1,0:T(8,128)S(1)} collective-permute-done((f32[18,128]{1,0:T(8,128)S(1)}, f32[18,128]{1,0:T(8,128)S(1)}, u32[]{:S(2)}, u32[]{:S(2)}) %collective-permute-start.4) | collective-permute-done | bytes 9248 | tf_op jit(solution)/shard_map/ppermute | solution.py:58
  28.1 1.8 %collective-permute-start.8 = (bf16[144,512]{1,0:T(8,128)(2,1)S(1)}, bf16[144,512]{1,0:T(8,128)(2,1)S(1)}, u32[]{:S(2)}, u32[]{:S(2)}) collective-permute-start(bf16[144,512]{1,0:T(8,128)(2,1)S(1)} %get-tuple-element.60), channel_id=1, source_target_pairs={{0,6},{2,4},{4,2},{6,0},{1,7},{3,5},{5,3},{7,1},{8,14},{10,12},{12... | collective-permute-start | bytes 442376 | tf_op jit(solution)/shard_map/ppermute | solution.py:63
  29.9 0.9 %collective-permute-start.9 = (bf16[144,512]{1,0:T(8,128)(2,1)S(1)}, bf16[144,512]{1,0:T(8,128)(2,1)S(1)}, u32[]{:S(2)}, u32[]{:S(2)}) collective-permute-start(bf16[144,512]{1,0:T(8,128)(2,1)S(1)} %get-tuple-element.61), channel_id=1, source_target_pairs={{0,2},{2,0},{4,6},{6,4},{1,3},{3,1},{5,7},{7,5},{8,10},{10,8},{12,... | collective-permute-start | bytes 442376 | tf_op jit(solution)/shard_map/ppermute | solution.py:63
  30.8 1.7 %collective-permute-start.7 = (f32[18,128]{1,0:T(8,128)S(1)}, f32[18,128]{1,0:T(8,128)S(1)}, u32[]{:S(2)}, u32[]{:S(2)}) collective-permute-start(f32[18,128]{1,0:T(8,128)S(1)} %get-tuple-element.57.refs_0_), channel_id=1, source_target_pairs={{0,4},{2,6},{4,0},{6,2},{1,5},{3,7},{5,1},{7,3},{8,12},{10,14},{12... | collective-permute-start | bytes 27656 | tf_op jit(solution)/shard_map/ppermute | solution.py:63
  32.6 0.0 collective-permute-done.3._
  32.6 1.8 %finish.1 = (bf16[128,2048]{1,0:T(8,128)(2,1)}, bf16[128,2048]{1,0:T(8,128)(2,1)}, bf16[128,512]{1,0:T(8,128)(2,1)S(1)}) custom-call(bf16[512,2048]{1,0:T(8,128)(2,1)S(1)} %get-tuple-element.47.probs_ref, bf16[512,2048]{1,0:T(8,128)(2,1)S(1)} %get-tuple-element.48.dscore_ref, ...), custom_call_target="tpu_custom_call", output_to_operand_aliasing={{2}: (4, {})} | custom-call | flops 536870912 | bytes 4194304 | tf_op jit(solution)/shard_map/finish/pallas_call | solution.py:441
  34.4 2.4 %collective-permute-done.7.refs_1_ = f32[18,128]{1,0:T(8,128)S(1)} collective-permute-done((f32[18,128]{1,0:T(8,128)S(1)}, f32[18,128]{1,0:T(8,128)S(1)}, u32[]{:S(2)}, u32[]{:S(2)}) %collective-permute-start.7) | collective-permute-done | bytes 9248 | tf_op jit(solution)/shard_map/ppermute | solution.py:63
  36.8 0.0 collective-permute-done.8.refs_4_
  36.8 0.0 collective-permute-done.9.refs_5_
  36.8 0.7 %collect.1 = (bf16[128,256]{1,0:T(8,128)(2,1)}, bf16[128,256]{1,0:T(8,128)(2,1)}, f32[16,128]{1,0:T(8,128)}, f32[2,128]{1,0:T(2,128)}) custom-call(f32[18,128]{1,0:T(8,128)S(1)} %get-tuple-element.57.refs_0_, f32[18,128]{1,0:T(8,128)S(1)} %collective-permute-done.7.refs_1_, f32[128,512]{1,0:T(8,128)S(1)} %get-tuple-element.58.refs_2_, ...), custom_call_target="tpu_custom_call" | custom-call | flops 262144 | bytes 524288 | tf_op jit(solution)/shard_map/collect/pallas_call | solution.py:461
  (1 shorter events, 0.0 us)
Async XLA Ops:
  1.5 11.0 %collective-permute-start.1 = (bf16[128,512]{1,0:T(8,128)(2,1)S(1)}, bf16[128,512]{1,0:T(8,128)(2,1)S(1)}, u32[]{:S(2)}, u32[]{:S(2)}) collective-permute-start(bf16[128,512]{1,0:T(8,128)(2,1)S(1)} %pad_maximum_fusion.pair_ref.refs_0_), channel_id=1, source_target_pairs={{6,0},{4,2},{2,4},{0,6},{7,1},{5,3},{3,5},{1,7},{14,8},{12,10},{10... | collective-permute-start | bytes 393224 | tf_op jit(solution)/shard_map/ppermute | solution.py:58
  6.6 7.4 %collective-permute-start = (bf16[128,512]{1,0:T(8,128)(2,1)S(1)}, bf16[128,512]{1,0:T(8,128)(2,1)S(1)}, u32[]{:S(2)}, u32[]{:S(2)}) collective-permute-start(bf16[128,512]{1,0:T(8,128)(2,1)S(1)} %pad_maximum_fusion.pair_ref.refs_0_), channel_id=1, source_target_pairs={{2,0},{0,2},{6,4},{4,6},{3,1},{1,3},{7,5},{5,7},{10,8},{8,10},{14,... | collective-permute-start | bytes 393224 | tf_op jit(solution)/shard_map/ppermute | solution.py:58
  6.6 11.1 %collective-permute-start.2 = (bf16[128,512]{1,0:T(8,128)(2,1)S(1)}, bf16[128,512]{1,0:T(8,128)(2,1)S(1)}, u32[]{:S(2)}, u32[]{:S(2)}) collective-permute-start(bf16[128,512]{1,0:T(8,128)(2,1)S(1)} %pad_maximum_fusion.pair_ref.refs_0_), channel_id=1, source_target_pairs={{4,0},{6,2},{0,4},{2,6},{5,1},{7,3},{1,5},{3,7},{12,8},{14,10},{8,... | collective-permute-start | bytes 393224 | tf_op jit(solution)/shard_map/ppermute | solution.py:58
  7.3 1.0 %copy-start = (bf16[1,128,2048]{2,1,0:T(8,128)(2,1)S(1)}, bf16[1,128,2048]{2,1,0:T(8,128)(2,1)}, u32[]{:S(2)}) copy-start(bf16[1,128,2048]{2,1,0:T(8,128)(2,1)} %param.7) | copy-start | bytes 1572868
  8.3 1.0 %copy-start.1 = (bf16[1,128,2048]{2,1,0:T(8,128)(2,1)S(1)}, bf16[1,128,2048]{2,1,0:T(8,128)(2,1)}, u32[]{:S(2)}) copy-start(bf16[1,128,2048]{2,1,0:T(8,128)(2,1)} %param.12) | copy-start | bytes 1572868
  9.4 0.7 %copy-start.2 = (bf16[2048]{0:T(1024)(128)(2,1)S(1)}, bf16[2048]{0:T(1024)(128)(2,1)}, u32[]{:S(2)}) copy-start(bf16[2048]{0:T(1024)(128)(2,1)} %param.8) | copy-start | bytes 12292
  10.0 0.7 %copy-start.3 = (s32[1,8]{1,0:T(1,128)S(1)}, s32[1,8]{1,0:T(1,128)}, u32[]{:S(2)}) copy-start(s32[1,8]{1,0:T(1,128)} %len_ref.1) | copy-start | bytes 100
  10.7 0.7 %copy-start.4 = (bf16[256]{0:T(256)(128)(2,1)S(1)}, bf16[256]{0:T(256)(128)(2,1)}, u32[]{:S(2)}) copy-start(bf16[256]{0:T(256)(128)(2,1)} %param.11) | copy-start | bytes 1540
  20.5 12.0 %collective-permute-start.3 = (bf16[128,512]{1,0:T(8,128)(2,1)S(1)}, bf16[128,512]{1,0:T(8,128)(2,1)S(1)}, u32[]{:S(2)}, u32[]{:S(2)}) collective-permute-start(bf16[128,512]{1,0:T(8,128)(2,1)S(1)} %get-tuple-element.51), channel_id=1, source_target_pairs={{0,4},{2,6},{4,0},{6,2},{1,5},{3,7},{5,1},{7,3},{8,12},{10,14},{12... | collective-permute-start | bytes 393224 | tf_op jit(solution)/shard_map/ppermute | solution.py:63
  21.4 4.6 %collective-permute-start.6 = (f32[18,128]{1,0:T(8,128)S(1)}, f32[18,128]{1,0:T(8,128)S(1)}, u32[]{:S(2)}, u32[]{:S(2)}) collective-permute-start(f32[18,128]{1,0:T(8,128)S(1)} %get-tuple-element.54.refs_0_), channel_id=1, source_target_pairs={{24,0},{16,8},{8,16},{0,24},{25,1},{17,9},{9,17},{1,25},{26,2},{18... | collective-permute-start | bytes 27656 | tf_op jit(solution)/shard_map/ppermute | solution.py:58
  23.9 3.7 %collective-permute-start.5 = (f32[18,128]{1,0:T(8,128)S(1)}, f32[18,128]{1,0:T(8,128)S(1)}, u32[]{:S(2)}, u32[]{:S(2)}) collective-permute-start(f32[18,128]{1,0:T(8,128)S(1)} %get-tuple-element.54.refs_0_), channel_id=1, source_target_pairs={{16,0},{24,8},{0,16},{8,24},{17,1},{25,9},{1,17},{9,25},{18,2},{26... | collective-permute-start | bytes 27656 | tf_op jit(solution)/shard_map/ppermute | solution.py:58
  24.4 3.7 %collective-permute-start.4 = (f32[18,128]{1,0:T(8,128)S(1)}, f32[18,128]{1,0:T(8,128)S(1)}, u32[]{:S(2)}, u32[]{:S(2)}) collective-permute-start(f32[18,128]{1,0:T(8,128)S(1)} %get-tuple-element.54.refs_0_), channel_id=1, source_target_pairs={{8,0},{0,8},{24,16},{16,24},{9,1},{1,9},{25,17},{17,25},{10,2},{2,... | collective-permute-start | bytes 27656 | tf_op jit(solution)/shard_map/ppermute | solution.py:58
  28.1 8.7 %collective-permute-start.8 = (bf16[144,512]{1,0:T(8,128)(2,1)S(1)}, bf16[144,512]{1,0:T(8,128)(2,1)S(1)}, u32[]{:S(2)}, u32[]{:S(2)}) collective-permute-start(bf16[144,512]{1,0:T(8,128)(2,1)S(1)} %get-tuple-element.60), channel_id=1, source_target_pairs={{0,6},{2,4},{4,2},{6,0},{1,7},{3,5},{5,3},{7,1},{8,14},{10,12},{12... | collective-permute-start | bytes 442376 | tf_op jit(solution)/shard_map/ppermute | solution.py:63
  29.9 6.9 %collective-permute-start.9 = (bf16[144,512]{1,0:T(8,128)(2,1)S(1)}, bf16[144,512]{1,0:T(8,128)(2,1)S(1)}, u32[]{:S(2)}, u32[]{:S(2)}) collective-permute-start(bf16[144,512]{1,0:T(8,128)(2,1)S(1)} %get-tuple-element.61), channel_id=1, source_target_pairs={{0,2},{2,0},{4,6},{6,4},{1,3},{3,1},{5,7},{7,5},{8,10},{10,8},{12,... | collective-permute-start | bytes 442376 | tf_op jit(solution)/shard_map/ppermute | solution.py:63
  30.8 5.9 %collective-permute-start.7 = (f32[18,128]{1,0:T(8,128)S(1)}, f32[18,128]{1,0:T(8,128)S(1)}, u32[]{:S(2)}, u32[]{:S(2)}) collective-permute-start(f32[18,128]{1,0:T(8,128)S(1)} %get-tuple-element.57.refs_0_), channel_id=1, source_target_pairs={{0,4},{2,6},{4,0},{6,2},{1,5},{3,7},{5,1},{7,3},{8,12},{10,14},{12... | collective-permute-start | bytes 27656 | tf_op jit(solution)/shard_map/ppermute | solution.py:63

commit v17 on v14

--- a/solution.py
+++ b/solution.py
@@ -12,7 +12,7 @@
 KV_HEADS = 4
 GROUP = HEADS // KV_HEADS
 PAIR = 2
-BLOCK = 64
+BLOCK = 32
 SCALE = HEAD_DIM ** (-0.5)
 LOG2E = 1.4426950408889634
 NEGATIVE = -1e30
@@ -247,59 +247,22 @@
                 qg_ref[:, head_cols(head)] = query_grad[rows].astype(jnp.bfloat16)
 
 
-def collect_kernel(batches, messages, *refs):
-    sum_refs, refs = refs[:2], refs[2:]
-    own_ref, early_ref, refs = refs[0], refs[1], refs[2:]
-    message_refs, (kg_ref, vg_ref, qb_ref, vb_ref) = refs[:messages], refs[messages:]
-    heads, kv_heads = qb_ref.shape[0], vb_ref.shape[0]
-    tok, kv_width = kg_ref.shape
-    total = sum_refs[0][...] + sum_refs[1][...]
-    term = own_ref[...] + early_ref[...].astype(jnp.float32)
-    for ref in message_refs:
-        sums = ref[tok:, :].astype(jnp.float32)
-        sums = sums[:, :HEAD_DIM] + sums[:, HEAD_DIM : 2 * HEAD_DIM]
-        total = total + sums[: heads + kv_heads]
-        term = term + ref[:tok, :].astype(jnp.float32)
+def collect_kernel(batches, parts, *refs):
+    sum_refs, term_refs, (kg_ref, vg_ref, qb_ref, vb_ref) = refs[:parts], refs[parts:-4], refs[-4:]
+    heads = qb_ref.shape[0]
+    kv_width = kg_ref.shape[1]
+    total = sum_refs[0][...]
+    for ref in sum_refs[1:]:
+        total = total + ref[...]
     total = total * (1.0 / batches)
     qb_ref[...] = total[:heads]
     vb_ref[...] = total[heads:]
+    term = term_refs[0][...]
+    for ref in term_refs[1:]:
+        term = term + ref[...].astype(jnp.float32)
     term = term.astype(jnp.bfloat16)
     kg_ref[...] = term[:, :kv_width]
     vg_ref[...] = term[:, kv_width:]
-
-
-def total_kernel(count, *refs):
-    parts, refs = refs[:count], refs[count:]
-    sent = (len(refs) - 1) // 2
-    term_refs, total_ref, message_refs = refs[:sent], refs[sent], refs[sent + 1 :]
-    total = parts[0][...]
-    for ref in parts[1:]:
-        total = total + ref[...]
-    total_ref[...] = total
-    for term_ref, message_ref in zip(term_refs, message_refs):
-        tok = term_ref.shape[0]
-        rows = message_ref.shape[0] - tok
-        high = jnp.concatenate([total, jnp.zeros((rows - total.shape[0], HEAD_DIM), jnp.float32)])
-        message_ref[:tok, :] = term_ref[...]
-        message_ref[tok:, :] = jnp.zeros((rows, term_ref.shape[1]), jnp.bfloat16)
-        message_ref[tok:, :HEAD_DIM] = high.astype(jnp.bfloat16)
-        low = high - high.astype(jnp.bfloat16).astype(jnp.float32)
-        message_ref[tok:, HEAD_DIM : 2 * HEAD_DIM] = low.astype(jnp.bfloat16)
-
-
-def total_with(parts, terms):
-    rows = -(-parts[0].shape[0] // 16) * 16
-    total, *messages = pl.pallas_call(
-        functools.partial(total_kernel, len(parts)),
-        out_shape=[shape(parts[0].shape, parts[0].dtype)]
-        + [shape((term.shape[0] + rows, term.shape[1]), term.dtype) for term in terms],
-        in_specs=[VMEM] * (len(parts) + len(terms)),
-        out_specs=[VMEM] * (1 + len(terms)),
-        compiler_params=params(8),
-        cost_estimate=pl.CostEstimate(flops=parts[0].size, bytes_accessed=0, transcendentals=0),
-        name="total",
-    )(*parts, *terms)
-    return total, messages
 
 
 def exchange(axis, part):
@@ -427,7 +390,7 @@
     probs, dscore, all_keys, all_values, sums, own, *terms = made
     term = shape((tok, 2 * kv_width), jnp.bfloat16)
     half = ctx // 2
-    early = send_back(terms.pop(half - 1), half)
+    early = send_back(terms[half - 1], half)
     attn, q_grad, early = pl.pallas_call(
         finish_kernel,
         out_shape=[
@@ -444,19 +407,18 @@
         ),
         name="finish",
     )(probs, dscore, all_keys, all_values, early)
-    sums, messages = total_with(exchange("dp", sums), terms)
-    slots = [slot for slot in range(1, ctx) if slot != half]
-    back = [send_back(message, slot) for slot, message in zip(slots, messages)][::-1]
-    sums = [sums, send_back(sums, half)]
+    sums = functools.reduce(lambda left, right: left + right, exchange("dp", sums))
+    sums = exchange("ctx", sums)
+    back = [send_back(terms[slot - 1], slot) for slot in range(ctx - 1, 0, -1) if slot != half]
     k_grad, v_grad, q_sum, v_sum = pl.pallas_call(
-        functools.partial(collect_kernel, batches, len(back)),
+        functools.partial(collect_kernel, batches, len(sums)),
         out_shape=[
             shape((tok, kv_width), jnp.bfloat16),
             shape((tok, kv_width), jnp.bfloat16),
             shape((heads, HEAD_DIM), jnp.float32),
             shape((kv_heads, HEAD_DIM), jnp.float32),
         ],
-        in_specs=[VMEM] * (4 + len(back)),
+        in_specs=[VMEM] * (len(sums) + 2 + len(back)),
         out_specs=[VMEM] * 4,
         compiler_params=params(8),
         cost_estimate=pl.CostEstimate(

time: 38.2 us -> 39.3 us (1.029)
  starting transfers between devices: 14.6 us -> 15.3 us
  waiting for transfers between devices: 9.45 us -> 9.89 us
    ppermute x6 -> x9, starting transfers between devices: 9.24 us -> 11.9 us  [fetch(): lax.ppermute(array, axis, [(source_of(i, slot, size), i) for i in range(s...]
    ppermute x4 -> x3, starting transfers between devices: 5.35 us -> 3.49 us  [send_back(): lax.ppermute(array, 'ctx', [(i, source_of(i, slot, size)) for i in range(...]
    ppermute x4 -> x3, waiting for transfers between devices: 2.76 us -> 4.45 us  [send_back(): lax.ppermute(array, 'ctx', [(i, source_of(i, slot, size)) for i in range(...]
    ppermute x6 -> x9, waiting for transfers between devices: 6.69 us -> 5.44 us  [fetch(): lax.ppermute(array, axis, [(source_of(i, slot, size), i) for i in range(s...]
  transfers between devices with their start and end apart: 10 -> 12, of which waited for: 6 -> 5; matrix products, arithmetic and copies ran while one was open for 0% -> 0% of each run, Pallas kernels for 12% -> 12%
where the time goes in v17:
time: 39.3 us; the launch traced here: 39 us
  starting transfers between devices  15.3 us (39%)
  waiting for transfers between devices  9.89 us (25%)
  Pallas kernels  8.1 us (21%)
  local copies, waits for them, and re-layouts  4.08 us (10%)
  other arithmetic  0.89 us (2%)
  between operations  0.68 us (2%)
    ppermute x9, starting transfers between devices, fetch(): lax.ppermute(array, axis, [(source_of(i, slot, size), i) for i in range(s...  11.9 us
    ppermute x9, waiting for transfers between devices, fetch(): lax.ppermute(array, axis, [(source_of(i, slot, size), i) for i in range(s...  5.44 us
    ppermute x3, waiting for transfers between devices, send_back(): lax.ppermute(array, 'ctx', [(i, source_of(i, slot, size)) for i in range(...  4.45 us
    unnamed x10, local copies, waits for them, and re-layouts  4.08 us
    ppermute x3, starting transfers between devices, send_back(): lax.ppermute(array, 'ctx', [(i, source_of(i, slot, size)) for i in range(...  3.49 us
    pallas_call x1, Pallas kernels, attend(): pl.pallas_call(functools.partial(last_kernel, ctx, first_head), out_shape...  2.82 us
    pallas_call x1, Pallas kernels, shards(): pl.pallas_call(finish_kernel, out_shape=[shape((tok, width), jnp.bfloat16...  1.8 us
    pallas_call x1, Pallas kernels, attend(): pl.pallas_call(near_kernel, out_shape=[shape((near, columns), jnp.float32...  1.67 us
  transfers between devices with their start and end apart: 12, of which 5 were waited for; matrix products, arithmetic and copies ran while one was open for 0% of the time, Pallas kernels for 12%

profile of v17, /device:TPU:0, one launch (start us, length us, event | category | flops | bytes accessed | tf_op | source)
XLA Modules:
  0.0 39.0 jit_solution(5926946369338578435)
XLA Ops:
  0.6 0.9 %pad_maximum_fusion.pair_ref.refs_0_ = bf16[128,512]{1,0:T(8,128)(2,1)S(1)} fusion(bf16[128,256]{1,0:T(8,128)(2,1)} %bitcast.16, bf16[128,256]{1,0:T(8,128)(2,1)} %bitcast.17), kind=kLoop, calls=%fused_computation | loop fusion | flops 262144 | bytes 262144 | tf_op jit(solution)/shard_map/concatenate | solution.py:341
  1.5 5.1 %collective-permute-start.1 = (bf16[128,512]{1,0:T(8,128)(2,1)S(1)}, bf16[128,512]{1,0:T(8,128)(2,1)S(1)}, u32[]{:S(2)}, u32[]{:S(2)}) collective-permute-start(bf16[128,512]{1,0:T(8,128)(2,1)S(1)} %pad_maximum_fusion.pair_ref.refs_0_), channel_id=1, source_target_pairs={{6,0},{4,2},{2,4},{0,6},{7,1},{5,3},{3,5},{1,7},{14,8},{12,10},{10... | collective-permute-start | bytes 393224 | tf_op jit(solution)/shard_map/ppermute | solution.py:58
  6.6 0.0 collective-permute-start
  6.6 0.6 %collective-permute-start.2 = (bf16[128,512]{1,0:T(8,128)(2,1)S(1)}, bf16[128,512]{1,0:T(8,128)(2,1)S(1)}, u32[]{:S(2)}, u32[]{:S(2)}) collective-permute-start(bf16[128,512]{1,0:T(8,128)(2,1)S(1)} %pad_maximum_fusion.pair_ref.refs_0_), channel_id=1, source_target_pairs={{4,0},{6,2},{0,4},{2,6},{5,1},{7,3},{1,5},{3,7},{12,8},{14,10},{8,... | collective-permute-start | bytes 393224 | tf_op jit(solution)/shard_map/ppermute | solution.py:58
  7.3 0.0 copy-start
  7.3 1.0 %copy-done = bf16[1,128,2048]{2,1,0:T(8,128)(2,1)S(1)} copy-done((bf16[1,128,2048]{2,1,0:T(8,128)(2,1)S(1)}, bf16[1,128,2048]{2,1,0:T(8,128)(2,1)}, u32[]{:S(2)}) %copy-start) | copy-done | bytes 524312
  8.3 0.0 copy-start.1
  8.3 1.0 %copy-done.1 = bf16[1,128,2048]{2,1,0:T(8,128)(2,1)S(1)} copy-done((bf16[1,128,2048]{2,1,0:T(8,128)(2,1)S(1)}, bf16[1,128,2048]{2,1,0:T(8,128)(2,1)}, u32[]{:S(2)}) %copy-start.1) | copy-done | bytes 524312
  9.4 0.0 copy-start.2
  9.4 0.7 %copy-done.2 = bf16[2048]{0:T(1024)(128)(2,1)S(1)} copy-done((bf16[2048]{0:T(1024)(128)(2,1)S(1)}, bf16[2048]{0:T(1024)(128)(2,1)}, u32[]{:S(2)}) %copy-start.2) | copy-done | bytes 4120
  10.0 0.0 copy-start.3
  10.0 0.7 %copy-done.3 = s32[1,8]{1,0:T(1,128)S(1)} copy-done((s32[1,8]{1,0:T(1,128)S(1)}, s32[1,8]{1,0:T(1,128)}, u32[]{:S(2)}) %copy-start.3) | copy-done | bytes 56
  10.7 0.0 copy-start.4
  10.7 0.7 %copy-done.4 = bf16[256]{0:T(256)(128)(2,1)S(1)} copy-done((bf16[256]{0:T(256)(128)(2,1)S(1)}, bf16[256]{0:T(256)(128)(2,1)}, u32[]{:S(2)}) %copy-start.4) | copy-done | bytes 536
  11.4 1.1 %prepare.1 = (bf16[2,128]{1,0:T(2,128)(2,1)S(1)}, bf16[2048,256]{1,0:T(8,128)(2,1)S(1)}, bf16[2048,128]{1,0:T(8,128)(2,1)S(1)}, f32[128,2048]{1,0:T(8,128)S(1)},...) custom-call(s32[1,8]{1,0:T(1,128)S(1)} %copy-done.3, bf16[128,512]{1,0:T(8,128)(2,1)S(1)} %pad_maximum_fusion.pair_ref.refs_0_, ...), custom_call_target="tpu_custom_call" | custom-call | flops 134217728 | bytes 4194304 | tf_op jit(solution)/shard_map/prepare/pallas_call | solution.py:343
  12.5 0.0 collective-permute-done.1.refs_2_
  12.5 1.5 %collective-permute-done.refs_1_ = bf16[128,512]{1,0:T(8,128)(2,1)S(1)} collective-permute-done((bf16[128,512]{1,0:T(8,128)(2,1)S(1)}, bf16[128,512]{1,0:T(8,128)(2,1)S(1)}, u32[]{:S(2)}, u32[]{:S(2)}) %collective-permute-start) | collective-permute-done | bytes 131104 | tf_op jit(solution)/shard_map/ppermute | solution.py:58
  14.0 1.7 %near.1 = (f32[384,2048]{1,0:T(8,128)S(1)}, f32[384,2048]{1,0:T(8,128)S(1)}, f32[8,2048]{1,0:T(8,128)S(1)}, bf16[384,256]{1,0:T(8,128)(2,1)S(1)}, bf16[384,256]{1,0:T(8,128)(2,1)S(1)}) custom-call(bf16[2,128]{1,0:T(2,128)(2,1)S(1)} %get-tuple-element.33.bias_ref.refs_0_, bf16[2048,256]{1,0:T(8,128)(2,1)S(1)} %get-tuple-element.34.queries_ref.refs_1_, ...), custom_call_target="tpu_custom_call" | custom-call | flops 402653184 | bytes 6291456 | tf_op jit(solution)/shard_map/near/pallas_call | solution.py:280
  15.7 2.0 %collective-permute-done.2.refs_9_ = bf16[128,512]{1,0:T(8,128)(2,1)S(1)} collective-permute-done((bf16[128,512]{1,0:T(8,128)(2,1)S(1)}, bf16[128,512]{1,0:T(8,128)(2,1)S(1)}, u32[]{:S(2)}, u32[]{:S(2)}) %collective-permute-start.2) | collective-permute-done | bytes 131104 | tf_op jit(solution)/shard_map/ppermute | solution.py:58
  17.7 2.8 %last.1 = (bf16[512,2048]{1,0:T(8,128)(2,1)S(1)}, bf16[512,2048]{1,0:T(8,128)(2,1)S(1)}, bf16[512,256]{1,0:T(8,128)(2,1)S(1)}, bf16[512,256]{1,0:T(8,128)(2,1)S(...) custom-call(bf16[2,128]{1,0:T(2,128)(2,1)S(1)} %get-tuple-element.33, ...), custom_call_target="tpu_custom_call" | custom-call | flops 536870912 | bytes 4194304 | tf_op jit(solution)/shard_map/last/pallas_call | solution.py:300
  20.5 2.5 %collective-permute-start.6 = (f32[18,128]{1,0:T(8,128)S(1)}, f32[18,128]{1,0:T(8,128)S(1)}, u32[]{:S(2)}, u32[]{:S(2)}) collective-permute-start(f32[18,128]{1,0:T(8,128)S(1)} %get-tuple-element.51), channel_id=1, source_target_pairs={{24,0},{16,8},{8,16},{0,24},{25,1},{17,9},{9,17},{1,25},{26,2},{18... | collective-permute-start | bytes 27656 | tf_op jit(solution)/shard_map/ppermute | solution.py:58
  23.0 0.5 %collective-permute-start.5 = (f32[18,128]{1,0:T(8,128)S(1)}, f32[18,128]{1,0:T(8,128)S(1)}, u32[]{:S(2)}, u32[]{:S(2)}) collective-permute-start(f32[18,128]{1,0:T(8,128)S(1)} %get-tuple-element.51), channel_id=1, source_target_pairs={{16,0},{24,8},{0,16},{8,24},{17,1},{25,9},{1,17},{9,25},{18,2},{26... | collective-permute-start | bytes 27656 | tf_op jit(solution)/shard_map/ppermute | solution.py:58
  23.6 0.5 %collective-permute-start.4 = (f32[18,128]{1,0:T(8,128)S(1)}, f32[18,128]{1,0:T(8,128)S(1)}, u32[]{:S(2)}, u32[]{:S(2)}) collective-permute-start(f32[18,128]{1,0:T(8,128)S(1)} %get-tuple-element.51), channel_id=1, source_target_pairs={{8,0},{0,8},{24,16},{16,24},{9,1},{1,9},{25,17},{17,25},{10,2},{2,... | collective-permute-start | bytes 27656 | tf_op jit(solution)/shard_map/ppermute | solution.py:58
  24.1 0.8 %collective-permute-start.3 = (bf16[128,512]{1,0:T(8,128)(2,1)S(1)}, bf16[128,512]{1,0:T(8,128)(2,1)S(1)}, u32[]{:S(2)}, u32[]{:S(2)}) collective-permute-start(bf16[128,512]{1,0:T(8,128)(2,1)S(1)} %get-tuple-element.48), channel_id=1, source_target_pairs={{0,4},{2,6},{4,0},{6,2},{1,5},{3,7},{5,1},{7,3},{8,12},{10,14},{12... | collective-permute-start | bytes 393224 | tf_op jit(solution)/shard_map/ppermute | solution.py:63
  24.9 1.6 %collective-permute-start.10 = (bf16[128,512]{1,0:T(8,128)(2,1)S(1)}, bf16[128,512]{1,0:T(8,128)(2,1)S(1)}, u32[]{:S(2)}, u32[]{:S(2)}) collective-permute-start(bf16[128,512]{1,0:T(8,128)(2,1)S(1)} %get-tuple-element.54), channel_id=1, source_target_pairs={{0,6},{2,4},{4,2},{6,0},{1,7},{3,5},{5,3},{7,1},{8,14},{10,12},{12... | collective-permute-start | bytes 393224 | tf_op jit(solution)/shard_map/ppermute | solution.py:63
  26.6 0.0 collective-permute-done.6
  26.6 1.0 %collective-permute-start.11 = (bf16[128,512]{1,0:T(8,128)(2,1)S(1)}, bf16[128,512]{1,0:T(8,128)(2,1)S(1)}, u32[]{:S(2)}, u32[]{:S(2)}) collective-permute-start(bf16[128,512]{1,0:T(8,128)(2,1)S(1)} %get-tuple-element.55), channel_id=1, source_target_pairs={{0,2},{2,0},{4,6},{6,4},{1,3},{3,1},{5,7},{7,5},{8,10},{10,8},{12,... | collective-permute-start | bytes 393224 | tf_op jit(solution)/shard_map/ppermute | solution.py:63
  27.6 0.0 collective-permute-done.5
  27.6 0.0 collective-permute-done.4
  27.6 2.5 %collective-permute-start.9 = (f32[18,128]{1,0:T(8,128)S(1)}, f32[18,128]{1,0:T(8,128)S(1)}, u32[]{:S(2)}, u32[]{:S(2)}) collective-permute-start(f32[18,128]{1,0:T(8,128)S(1)} %add_add_fusion.refs_0_), channel_id=1, source_target_pairs={{6,0},{4,2},{2,4},{0,6},{7,1},{5,3},{3,5},{1,7},{14,8},{12,10},{10... | collective-permute-start | bytes 27656 | tf_op jit(solution)/shard_map/ppermute | solution.py:58
  30.1 0.0 collective-permute-start.8
  30.1 4.4 %collective-permute-done.3._ = bf16[128,512]{1,0:T(8,128)(2,1)S(1)} collective-permute-done((bf16[128,512]{1,0:T(8,128)(2,1)S(1)}, bf16[128,512]{1,0:T(8,128)(2,1)S(1)}, u32[]{:S(2)}, u32[]{:S(2)}) %collective-permute-start.3) | collective-permute-done | bytes 131104 | tf_op jit(solution)/shard_map/ppermute | solution.py:63
  34.6 0.0 collective-permute-start.7
  34.6 1.8 %finish.1 = (bf16[128,2048]{1,0:T(8,128)(2,1)}, bf16[128,2048]{1,0:T(8,128)(2,1)}, bf16[128,512]{1,0:T(8,128)(2,1)S(1)}) custom-call(bf16[512,2048]{1,0:T(8,128)(2,1)S(1)} %get-tuple-element.44.probs_ref, bf16[512,2048]{1,0:T(8,128)(2,1)S(1)} %get-tuple-element.45.dscore_ref, ...), custom_call_target="tpu_custom_call", output_to_operand_aliasing={{2}: (4, {})} | custom-call | flops 536870912 | bytes 4194304 | tf_op jit(solution)/shard_map/finish/pallas_call | solution.py:394
  36.4 0.0 collective-permute-done.9.refs_3_
  36.4 0.4 %collective-permute-done.8.refs_2_ = f32[18,128]{1,0:T(8,128)S(1)} collective-permute-done((f32[18,128]{1,0:T(8,128)S(1)}, f32[18,128]{1,0:T(8,128)S(1)}, u32[]{:S(2)}, u32[]{:S(2)}) %collective-permute-start.8) | collective-permute-done | bytes 9248 | tf_op jit(solution)/shard_map/ppermute | solution.py:58
  36.8 1.5 %collective-permute-done.7.refs_1_ = f32[18,128]{1,0:T(8,128)S(1)} collective-permute-done((f32[18,128]{1,0:T(8,128)S(1)}, f32[18,128]{1,0:T(8,128)S(1)}, u32[]{:S(2)}, u32[]{:S(2)}) %collective-permute-start.7) | collective-permute-done | bytes 9248 | tf_op jit(solution)/shard_map/ppermute | solution.py:58
  38.3 0.0 collective-permute-done.10.refs_6_
  38.3 0.0 collective-permute-done.11.refs_7_
  38.3 0.7 %collect.1 = (bf16[128,256]{1,0:T(8,128)(2,1)}, bf16[128,256]{1,0:T(8,128)(2,1)}, f32[16,128]{1,0:T(8,128)}, f32[2,128]{1,0:T(2,128)}) custom-call(f32[18,128]{1,0:T(8,128)S(1)} %add_add_fusion.refs_0_, f32[18,128]{1,0:T(8,128)S(1)} %collective-permute-done.7.refs_1_, f32[18,128]{1,0:T(8,128)S(1)} %collective-permute-done.8.refs_2_, ...), custom_call_target="tpu_custom_call" | custom-call | flops 262144 | bytes 524288 | tf_op jit(solution)/shard_map/collect/pallas_call | solution.py:413
  (1 shorter events, 0.0 us)
Async XLA Ops:
  1.5 11.0 %collective-permute-start.1 = (bf16[128,512]{1,0:T(8,128)(2,1)S(1)}, bf16[128,512]{1,0:T(8,128)(2,1)S(1)}, u32[]{:S(2)}, u32[]{:S(2)}) collective-permute-start(bf16[128,512]{1,0:T(8,128)(2,1)S(1)} %pad_maximum_fusion.pair_ref.refs_0_), channel_id=1, source_target_pairs={{6,0},{4,2},{2,4},{0,6},{7,1},{5,3},{3,5},{1,7},{14,8},{12,10},{10... | collective-permute-start | bytes 393224 | tf_op jit(solution)/shard_map/ppermute | solution.py:58
  6.6 7.4 %collective-permute-start = (bf16[128,512]{1,0:T(8,128)(2,1)S(1)}, bf16[128,512]{1,0:T(8,128)(2,1)S(1)}, u32[]{:S(2)}, u32[]{:S(2)}) collective-permute-start(bf16[128,512]{1,0:T(8,128)(2,1)S(1)} %pad_maximum_fusion.pair_ref.refs_0_), channel_id=1, source_target_pairs={{2,0},{0,2},{6,4},{4,6},{3,1},{1,3},{7,5},{5,7},{10,8},{8,10},{14,... | collective-permute-start | bytes 393224 | tf_op jit(solution)/shard_map/ppermute | solution.py:58
  6.6 11.1 %collective-permute-start.2 = (bf16[128,512]{1,0:T(8,128)(2,1)S(1)}, bf16[128,512]{1,0:T(8,128)(2,1)S(1)}, u32[]{:S(2)}, u32[]{:S(2)}) collective-permute-start(bf16[128,512]{1,0:T(8,128)(2,1)S(1)} %pad_maximum_fusion.pair_ref.refs_0_), channel_id=1, source_target_pairs={{4,0},{6,2},{0,4},{2,6},{5,1},{7,3},{1,5},{3,7},{12,8},{14,10},{8,... | collective-permute-start | bytes 393224 | tf_op jit(solution)/shard_map/ppermute | solution.py:58
  7.3 1.0 %copy-start = (bf16[1,128,2048]{2,1,0:T(8,128)(2,1)S(1)}, bf16[1,128,2048]{2,1,0:T(8,128)(2,1)}, u32[]{:S(2)}) copy-start(bf16[1,128,2048]{2,1,0:T(8,128)(2,1)} %param.7) | copy-start | bytes 1572868
  8.3 1.0 %copy-start.1 = (bf16[1,128,2048]{2,1,0:T(8,128)(2,1)S(1)}, bf16[1,128,2048]{2,1,0:T(8,128)(2,1)}, u32[]{:S(2)}) copy-start(bf16[1,128,2048]{2,1,0:T(8,128)(2,1)} %param.12) | copy-start | bytes 1572868
  9.4 0.7 %copy-start.2 = (bf16[2048]{0:T(1024)(128)(2,1)S(1)}, bf16[2048]{0:T(1024)(128)(2,1)}, u32[]{:S(2)}) copy-start(bf16[2048]{0:T(1024)(128)(2,1)} %param.8) | copy-start | bytes 12292
  10.0 0.7 %copy-start.3 = (s32[1,8]{1,0:T(1,128)S(1)}, s32[1,8]{1,0:T(1,128)}, u32[]{:S(2)}) copy-start(s32[1,8]{1,0:T(1,128)} %len_ref.1) | copy-start | bytes 100
  10.7 0.7 %copy-start.4 = (bf16[256]{0:T(256)(128)(2,1)S(1)}, bf16[256]{0:T(256)(128)(2,1)}, u32[]{:S(2)}) copy-start(bf16[256]{0:T(256)(128)(2,1)} %param.11) | copy-start | bytes 1540
  20.5 6.0 %collective-permute-start.6 = (f32[18,128]{1,0:T(8,128)S(1)}, f32[18,128]{1,0:T(8,128)S(1)}, u32[]{:S(2)}, u32[]{:S(2)}) collective-permute-start(f32[18,128]{1,0:T(8,128)S(1)} %get-tuple-element.51), channel_id=1, source_target_pairs={{24,0},{16,8},{8,16},{0,24},{25,1},{17,9},{9,17},{1,25},{26,2},{18... | collective-permute-start | bytes 27656 | tf_op jit(solution)/shard_map/ppermute | solution.py:58
  23.0 4.5 %collective-permute-start.5 = (f32[18,128]{1,0:T(8,128)S(1)}, f32[18,128]{1,0:T(8,128)S(1)}, u32[]{:S(2)}, u32[]{:S(2)}) collective-permute-start(f32[18,128]{1,0:T(8,128)S(1)} %get-tuple-element.51), channel_id=1, source_target_pairs={{16,0},{24,8},{0,16},{8,24},{17,1},{25,9},{1,17},{9,25},{18,2},{26... | collective-permute-start | bytes 27656 | tf_op jit(solution)/shard_map/ppermute | solution.py:58
  23.6 4.0 %collective-permute-start.4 = (f32[18,128]{1,0:T(8,128)S(1)}, f32[18,128]{1,0:T(8,128)S(1)}, u32[]{:S(2)}, u32[]{:S(2)}) collective-permute-start(f32[18,128]{1,0:T(8,128)S(1)} %get-tuple-element.51), channel_id=1, source_target_pairs={{8,0},{0,8},{24,16},{16,24},{9,1},{1,9},{25,17},{17,25},{10,2},{2,... | collective-permute-start | bytes 27656 | tf_op jit(solution)/shard_map/ppermute | solution.py:58
  24.1 10.5 %collective-permute-start.3 = (bf16[128,512]{1,0:T(8,128)(2,1)S(1)}, bf16[128,512]{1,0:T(8,128)(2,1)S(1)}, u32[]{:S(2)}, u32[]{:S(2)}) collective-permute-start(bf16[128,512]{1,0:T(8,128)(2,1)S(1)} %get-tuple-element.48), channel_id=1, source_target_pairs={{0,4},{2,6},{4,0},{6,2},{1,5},{3,7},{5,1},{7,3},{8,12},{10,14},{12... | collective-permute-start | bytes 393224 | tf_op jit(solution)/shard_map/ppermute | solution.py:63
  24.9 13.4 %collective-permute-start.10 = (bf16[128,512]{1,0:T(8,128)(2,1)S(1)}, bf16[128,512]{1,0:T(8,128)(2,1)S(1)}, u32[]{:S(2)}, u32[]{:S(2)}) collective-permute-start(bf16[128,512]{1,0:T(8,128)(2,1)S(1)} %get-tuple-element.54), channel_id=1, source_target_pairs={{0,6},{2,4},{4,2},{6,0},{1,7},{3,5},{5,3},{7,1},{8,14},{10,12},{12... | collective-permute-start | bytes 393224 | tf_op jit(solution)/shard_map/ppermute | solution.py:63
  26.6 11.7 %collective-permute-start.11 = (bf16[128,512]{1,0:T(8,128)(2,1)S(1)}, bf16[128,512]{1,0:T(8,128)(2,1)S(1)}, u32[]{:S(2)}, u32[]{:S(2)}) collective-permute-start(bf16[128,512]{1,0:T(8,128)(2,1)S(1)} %get-tuple-element.55), channel_id=1, source_target_pairs={{0,2},{2,0},{4,6},{6,4},{1,3},{3,1},{5,7},{7,5},{8,10},{10,8},{12,... | collective-permute-start | bytes 393224 | tf_op jit(solution)/shard_map/ppermute | solution.py:63
  27.6 8.8 %collective-permute-start.9 = (f32[18,128]{1,0:T(8,128)S(1)}, f32[18,128]{1,0:T(8,128)S(1)}, u32[]{:S(2)}, u32[]{:S(2)}) collective-permute-start(f32[18,128]{1,0:T(8,128)S(1)} %add_add_fusion.refs_0_), channel_id=1, source_target_pairs={{6,0},{4,2},{2,4},{0,6},{7,1},{5,3},{3,5},{1,7},{14,8},{12,10},{10... | collective-permute-start | bytes 27656 | tf_op jit(solution)/shard_map/ppermute | solution.py:58
  30.1 6.7 %collective-permute-start.8 = (f32[18,128]{1,0:T(8,128)S(1)}, f32[18,128]{1,0:T(8,128)S(1)}, u32[]{:S(2)}, u32[]{:S(2)}) collective-permute-start(f32[18,128]{1,0:T(8,128)S(1)} %add_add_fusion.refs_0_), channel_id=1, source_target_pairs={{4,0},{6,2},{0,4},{2,6},{5,1},{7,3},{1,5},{3,7},{12,8},{14,10},{8,... | collective-permute-start | bytes 27656 | tf_op jit(solution)/shard_map/ppermute | solution.py:58
  34.6 3.7 %collective-permute-start.7 = (f32[18,128]{1,0:T(8,128)S(1)}, f32[18,128]{1,0:T(8,128)S(1)}, u32[]{:S(2)}, u32[]{:S(2)}) collective-permute-start(f32[18,128]{1,0:T(8,128)S(1)} %add_add_fusion.refs_0_), channel_id=1, source_target_pairs={{2,0},{0,2},{6,4},{4,6},{3,1},{1,3},{7,5},{5,7},{10,8},{8,10},{14,... | collective-permute-start | bytes 27656 | tf_op jit(solution)/shard_map/ppermute | solution.py:58

commit v18 on v15

--- a/solution.py
+++ b/solution.py
@@ -12,12 +12,11 @@
 KV_HEADS = 4
 GROUP = HEADS // KV_HEADS
 PAIR = 2
-BLOCK = 64
+BLOCK = 32
 SCALE = HEAD_DIM ** (-0.5)
 LOG2E = 1.4426950408889634
 NEGATIVE = -1e30
 VMEM = pl.BlockSpec(memory_space=pltpu.VMEM)
-HBM = pl.BlockSpec(memory_space=pltpu.HBM)
 ANY = pl.BlockSpec(memory_space=pl.ANY)
 SMEM = pl.BlockSpec(memory_space=pltpu.SMEM)
 
@@ -62,20 +61,6 @@
 def send_back(array, slot):
     size = lax.axis_size("ctx")
     return lax.ppermute(array, "ctx", [(i, source_of(i, slot, size)) for i in range(size)])
-
-
-def pack_kernel(k_ref, v_ref, pair_ref, sems):
-    kv_width = k_ref.shape[1]
-    copies = [
-        pltpu.make_async_copy(
-            part_ref, pair_ref.at[:, pl.ds(n * kv_width, kv_width)], sems.at[n]
-        )
-        for n, part_ref in enumerate([k_ref, v_ref])
-    ]
-    for copy in copies:
-        copy.start()
-    for copy in copies:
-        copy.wait()
 
 
 def prepare_kernel(
@@ -409,18 +394,7 @@
     batches = lax.axis_size("dp")
     rows = ctx * tok
     columns = heads * tok
-    pair = pl.pallas_call(
-        pack_kernel,
-        out_shape=shape((tok, 2 * kv_width), jnp.bfloat16),
-        in_specs=[HBM] * 2,
-        out_specs=VMEM,
-        scratch_shapes=[pltpu.SemaphoreType.DMA((2,))],
-        compiler_params=params(2),
-        cost_estimate=pl.CostEstimate(
-            flops=0, bytes_accessed=8 * tok * kv_width, transcendentals=0
-        ),
-        name="pack",
-    )(*[pltpu.with_memory_space_constraint(part[0], pltpu.HBM) for part in (k_proj, v_proj)])
+    pair = jnp.concatenate([k_proj[0], v_proj[0]], axis=1)
     pairs = [pair] + [fetch(pair, "ctx", slot) for slot in range(1, ctx)]
     prepared = pl.pallas_call(
         functools.partial(prepare_kernel, ctx),
@@ -473,22 +447,22 @@
     half = ctx // 2
     far = range(half, ctx)
     early = [send_back(terms[slot - 1], slot) for slot in far]
-    attn, q_grad, *early = pl.pallas_call(
+    attn, q_grad, early[0] = pl.pallas_call(
         finish_kernel,
         out_shape=[
             shape((tok, width), jnp.bfloat16),
             shape((tok, width), jnp.bfloat16),
         ]
-        + [shape(part.shape, part.dtype) for part in early],
-        in_specs=[VMEM] * 4 + [ANY] * len(early),
-        out_specs=[VMEM] * 2 + [ANY] * len(early),
-        input_output_aliases={4 + n: 2 + n for n in range(len(early))},
+        + [shape(early[0].shape, early[0].dtype)],
+        in_specs=[VMEM] * 4 + [ANY],
+        out_specs=[VMEM] * 2 + [ANY],
+        input_output_aliases={4: 2},
         compiler_params=params(24),
         cost_estimate=pl.CostEstimate(
-            flops=4 * rows * tok * width, bytes_accessed=4 * rows * columns, transcendentals=0
+            flops=16 * rows * tok * width, bytes_accessed=0, transcendentals=0
         ),
         name="finish",
-    )(probs, dscore, all_keys, all_values, *early)
+    )(probs, dscore, all_keys, all_values, early[0])
     sums, messages = total_with(exchange("dp", sums), terms[: half - 1])
     late = [send_back(message, slot) for slot, message in enumerate(messages, 1)]
     sums = [sums] + [send_back(sums, slot) for slot in far]

time: 38.9 us -> 38 us (0.977)
  waiting for transfers between devices: 9.39 us -> 7.6 us
  Pallas kernels: 9.04 us -> 8.11 us
  starting transfers between devices: 15.4 us -> 16.3 us
  other arithmetic: 0 us -> 0.88 us
    ppermute x6, waiting for transfers between devices: 6.68 us -> 4.97 us  [fetch(): lax.ppermute(array, axis, [(source_of(i, slot, size), i) for i in range(s...]
    ppermute x5, starting transfers between devices: 6.18 us -> 7.07 us  [send_back(): lax.ppermute(array, 'ctx', [(i, source_of(i, slot, size)) for i in range(...]
    pallas_call x1 -> x0, Pallas kernels: 0.89 us -> none  [shards(): pl.pallas_call(pack_kernel, out_shape=shape((tok, 2 * kv_width), jnp.bflo...]
    concatenate x0 -> x1, other arithmetic: none -> 0.88 us  [shards(): pair = jnp.concatenate([k_proj[0], v_proj[0]], axis=1)]
  transfers between devices with their start and end apart: 11 -> 11, of which waited for: 7 -> 6; matrix products, arithmetic and copies ran while one was open for 0% -> 0% of each run, Pallas kernels for 12% -> 12%
where the time goes in v18:
time: 38 us; the launch traced here: 37.7 us
  starting transfers between devices  16.3 us (43%)
  Pallas kernels  8.11 us (21%)
  waiting for transfers between devices  7.6 us (20%)
  local copies, waits for them, and re-layouts  4.08 us (11%)
  other arithmetic  0.88 us (2%)
  between operations  0.68 us (2%)
    ppermute x6, starting transfers between devices, fetch(): lax.ppermute(array, axis, [(source_of(i, slot, size), i) for i in range(s...  9.24 us
    ppermute x5, starting transfers between devices, send_back(): lax.ppermute(array, 'ctx', [(i, source_of(i, slot, size)) for i in range(...  7.07 us
    ppermute x6, waiting for transfers between devices, fetch(): lax.ppermute(array, axis, [(source_of(i, slot, size), i) for i in range(s...  4.97 us
    unnamed x10, local copies, waits for them, and re-layouts  4.08 us
    pallas_call x1, Pallas kernels, attend(): pl.pallas_call(functools.partial(last_kernel, ctx, first_head), out_shape...  2.82 us
    ppermute x5, waiting for transfers between devices, send_back(): lax.ppermute(array, 'ctx', [(i, source_of(i, slot, size)) for i in range(...  2.63 us
    pallas_call x1, Pallas kernels, shards(): pl.pallas_call(finish_kernel, out_shape=[shape((tok, width), jnp.bfloat16...  1.8 us
    pallas_call x1, Pallas kernels, attend(): pl.pallas_call(near_kernel, out_shape=[shape((near, columns), jnp.float32...  1.67 us
  transfers between devices with their start and end apart: 11, of which 6 were waited for; matrix products, arithmetic and copies ran while one was open for 0% of the time, Pallas kernels for 12%

profile of v18, /device:TPU:0, one launch (start us, length us, event | category | flops | bytes accessed | tf_op | source)
XLA Modules:
  0.0 37.7 jit_solution(16216353877703506019)
XLA Ops:
  0.6 0.9 %pad_maximum_fusion.pair_ref.refs_0_ = bf16[128,512]{1,0:T(8,128)(2,1)S(1)} fusion(bf16[128,256]{1,0:T(8,128)(2,1)} %bitcast.16, bf16[128,256]{1,0:T(8,128)(2,1)} %bitcast.17), kind=kLoop, calls=%fused_computation | loop fusion | flops 262144 | bytes 262144 | tf_op jit(solution)/shard_map/concatenate | solution.py:397
  1.5 5.1 %collective-permute-start.1 = (bf16[128,512]{1,0:T(8,128)(2,1)S(1)}, bf16[128,512]{1,0:T(8,128)(2,1)S(1)}, u32[]{:S(2)}, u32[]{:S(2)}) collective-permute-start(bf16[128,512]{1,0:T(8,128)(2,1)S(1)} %pad_maximum_fusion.pair_ref.refs_0_), channel_id=1, source_target_pairs={{6,0},{4,2},{2,4},{0,6},{7,1},{5,3},{3,5},{1,7},{14,8},{12,10},{10... | collective-permute-start | bytes 393224 | tf_op jit(solution)/shard_map/ppermute | solution.py:58
  6.6 0.0 collective-permute-start
  6.6 0.6 %collective-permute-start.2 = (bf16[128,512]{1,0:T(8,128)(2,1)S(1)}, bf16[128,512]{1,0:T(8,128)(2,1)S(1)}, u32[]{:S(2)}, u32[]{:S(2)}) collective-permute-start(bf16[128,512]{1,0:T(8,128)(2,1)S(1)} %pad_maximum_fusion.pair_ref.refs_0_), channel_id=1, source_target_pairs={{4,0},{6,2},{0,4},{2,6},{5,1},{7,3},{1,5},{3,7},{12,8},{14,10},{8,... | collective-permute-start | bytes 393224 | tf_op jit(solution)/shard_map/ppermute | solution.py:58
  7.3 0.0 copy-start
  7.3 1.0 %copy-done = bf16[1,128,2048]{2,1,0:T(8,128)(2,1)S(1)} copy-done((bf16[1,128,2048]{2,1,0:T(8,128)(2,1)S(1)}, bf16[1,128,2048]{2,1,0:T(8,128)(2,1)}, u32[]{:S(2)}) %copy-start) | copy-done | bytes 524312
  8.3 0.0 copy-start.1
  8.3 1.0 %copy-done.1 = bf16[1,128,2048]{2,1,0:T(8,128)(2,1)S(1)} copy-done((bf16[1,128,2048]{2,1,0:T(8,128)(2,1)S(1)}, bf16[1,128,2048]{2,1,0:T(8,128)(2,1)}, u32[]{:S(2)}) %copy-start.1) | copy-done | bytes 524312
  9.4 0.0 copy-start.2
  9.4 0.7 %copy-done.2 = bf16[2048]{0:T(1024)(128)(2,1)S(1)} copy-done((bf16[2048]{0:T(1024)(128)(2,1)S(1)}, bf16[2048]{0:T(1024)(128)(2,1)}, u32[]{:S(2)}) %copy-start.2) | copy-done | bytes 4120
  10.0 0.0 copy-start.3
  10.0 0.7 %copy-done.3 = s32[1,8]{1,0:T(1,128)S(1)} copy-done((s32[1,8]{1,0:T(1,128)S(1)}, s32[1,8]{1,0:T(1,128)}, u32[]{:S(2)}) %copy-start.3) | copy-done | bytes 56
  10.7 0.0 copy-start.4
  10.7 0.7 %copy-done.4 = bf16[256]{0:T(256)(128)(2,1)S(1)} copy-done((bf16[256]{0:T(256)(128)(2,1)S(1)}, bf16[256]{0:T(256)(128)(2,1)}, u32[]{:S(2)}) %copy-start.4) | copy-done | bytes 536
  11.4 1.1 %prepare.1 = (bf16[2,128]{1,0:T(2,128)(2,1)S(1)}, bf16[2048,256]{1,0:T(8,128)(2,1)S(1)}, bf16[2048,128]{1,0:T(8,128)(2,1)S(1)}, f32[128,2048]{1,0:T(8,128)S(1)},...) custom-call(s32[1,8]{1,0:T(1,128)S(1)} %copy-done.3, bf16[128,512]{1,0:T(8,128)(2,1)S(1)} %pad_maximum_fusion.pair_ref.refs_0_, ...), custom_call_target="tpu_custom_call" | custom-call | flops 134217728 | bytes 4194304 | tf_op jit(solution)/shard_map/prepare/pallas_call | solution.py:399
  12.5 0.0 collective-permute-done.1.refs_2_
  12.5 1.5 %collective-permute-done.refs_1_ = bf16[128,512]{1,0:T(8,128)(2,1)S(1)} collective-permute-done((bf16[128,512]{1,0:T(8,128)(2,1)S(1)}, bf16[128,512]{1,0:T(8,128)(2,1)S(1)}, u32[]{:S(2)}, u32[]{:S(2)}) %collective-permute-start) | collective-permute-done | bytes 131104 | tf_op jit(solution)/shard_map/ppermute | solution.py:58
  14.0 1.7 %near.1 = (f32[384,2048]{1,0:T(8,128)S(1)}, f32[384,2048]{1,0:T(8,128)S(1)}, f32[8,2048]{1,0:T(8,128)S(1)}, bf16[384,256]{1,0:T(8,128)(2,1)S(1)}, bf16[384,256]{1,0:T(8,128)(2,1)S(1)}) custom-call(bf16[2,128]{1,0:T(2,128)(2,1)S(1)} %get-tuple-element.35.bias_ref.refs_0_, bf16[2048,256]{1,0:T(8,128)(2,1)S(1)} %get-tuple-element.36.queries_ref.refs_1_, ...), custom_call_target="tpu_custom_call" | custom-call | flops 402653184 | bytes 6291456 | tf_op jit(solution)/shard_map/near/pallas_call | solution.py:336
  15.7 2.0 %collective-permute-done.2.refs_9_ = bf16[128,512]{1,0:T(8,128)(2,1)S(1)} collective-permute-done((bf16[128,512]{1,0:T(8,128)(2,1)S(1)}, bf16[128,512]{1,0:T(8,128)(2,1)S(1)}, u32[]{:S(2)}, u32[]{:S(2)}) %collective-permute-start.2) | collective-permute-done | bytes 131104 | tf_op jit(solution)/shard_map/ppermute | solution.py:58
  17.7 2.8 %last.1 = (bf16[512,2048]{1,0:T(8,128)(2,1)S(1)}, bf16[512,2048]{1,0:T(8,128)(2,1)S(1)}, bf16[512,256]{1,0:T(8,128)(2,1)S(1)}, bf16[512,256]{1,0:T(8,128)(2,1)S(...) custom-call(bf16[2,128]{1,0:T(2,128)(2,1)S(1)} %get-tuple-element.35, ...), custom_call_target="tpu_custom_call" | custom-call | flops 536870912 | bytes 4194304 | tf_op jit(solution)/shard_map/last/pallas_call | solution.py:356
  20.5 0.9 %collective-permute-start.3 = (bf16[128,512]{1,0:T(8,128)(2,1)S(1)}, bf16[128,512]{1,0:T(8,128)(2,1)S(1)}, u32[]{:S(2)}, u32[]{:S(2)}) collective-permute-start(bf16[128,512]{1,0:T(8,128)(2,1)S(1)} %get-tuple-element.50), channel_id=1, source_target_pairs={{0,4},{2,6},{4,0},{6,2},{1,5},{3,7},{5,1},{7,3},{8,12},{10,14},{12... | collective-permute-start | bytes 393224 | tf_op jit(solution)/shard_map/ppermute | solution.py:63
  21.4 2.4 %collective-permute-start.6 = (f32[18,128]{1,0:T(8,128)S(1)}, f32[18,128]{1,0:T(8,128)S(1)}, u32[]{:S(2)}, u32[]{:S(2)}) collective-permute-start(f32[18,128]{1,0:T(8,128)S(1)} %get-tuple-element.53.refs_0_), channel_id=1, source_target_pairs={{24,0},{16,8},{8,16},{0,24},{25,1},{17,9},{9,17},{1,25},{26,2},{18... | collective-permute-start | bytes 27656 | tf_op jit(solution)/shard_map/ppermute | solution.py:58
  23.9 0.5 %collective-permute-start.5 = (f32[18,128]{1,0:T(8,128)S(1)}, f32[18,128]{1,0:T(8,128)S(1)}, u32[]{:S(2)}, u32[]{:S(2)}) collective-permute-start(f32[18,128]{1,0:T(8,128)S(1)} %get-tuple-element.53.refs_0_), channel_id=1, source_target_pairs={{16,0},{24,8},{0,16},{8,24},{17,1},{25,9},{1,17},{9,25},{18,2},{26... | collective-permute-start | bytes 27656 | tf_op jit(solution)/shard_map/ppermute | solution.py:58
  24.4 0.5 %collective-permute-start.4 = (f32[18,128]{1,0:T(8,128)S(1)}, f32[18,128]{1,0:T(8,128)S(1)}, u32[]{:S(2)}, u32[]{:S(2)}) collective-permute-start(f32[18,128]{1,0:T(8,128)S(1)} %get-tuple-element.53.refs_0_), channel_id=1, source_target_pairs={{8,0},{0,8},{24,16},{16,24},{9,1},{1,9},{25,17},{17,25},{10,2},{2,... | collective-permute-start | bytes 27656 | tf_op jit(solution)/shard_map/ppermute | solution.py:58
  24.9 1.7 %collective-permute-start.9 = (bf16[128,512]{1,0:T(8,128)(2,1)S(1)}, bf16[128,512]{1,0:T(8,128)(2,1)S(1)}, u32[]{:S(2)}, u32[]{:S(2)}) collective-permute-start(bf16[128,512]{1,0:T(8,128)(2,1)S(1)} %get-tuple-element.58), channel_id=1, source_target_pairs={{0,6},{2,4},{4,2},{6,0},{1,7},{3,5},{5,3},{7,1},{8,14},{10,12},{12... | collective-permute-start | bytes 393224 | tf_op jit(solution)/shard_map/ppermute | solution.py:63
  26.6 0.0 collective-permute-done.6.refs_3_
  26.6 0.9 %collective-permute-done.5.refs_2_ = f32[18,128]{1,0:T(8,128)S(1)} collective-permute-done((f32[18,128]{1,0:T(8,128)S(1)}, f32[18,128]{1,0:T(8,128)S(1)}, u32[]{:S(2)}, u32[]{:S(2)}) %collective-permute-start.5) | collective-permute-done | bytes 9248 | tf_op jit(solution)/shard_map/ppermute | solution.py:58
  27.6 0.5 %collective-permute-done.4.refs_1_ = f32[18,128]{1,0:T(8,128)S(1)} collective-permute-done((f32[18,128]{1,0:T(8,128)S(1)}, f32[18,128]{1,0:T(8,128)S(1)}, u32[]{:S(2)}, u32[]{:S(2)}) %collective-permute-start.4) | collective-permute-done | bytes 9248 | tf_op jit(solution)/shard_map/ppermute | solution.py:58
  28.1 1.8 %collective-permute-start.8 = (f32[18,128]{1,0:T(8,128)S(1)}, f32[18,128]{1,0:T(8,128)S(1)}, u32[]{:S(2)}, u32[]{:S(2)}) collective-permute-start(f32[18,128]{1,0:T(8,128)S(1)} %get-tuple-element.55.refs_0_), channel_id=1, source_target_pairs={{0,6},{2,4},{4,2},{6,0},{1,7},{3,5},{5,3},{7,1},{8,14},{10,12},{12... | collective-permute-start | bytes 27656 | tf_op jit(solution)/shard_map/ppermute | solution.py:63
  29.9 1.9 %collective-permute-start.7 = (f32[18,128]{1,0:T(8,128)S(1)}, f32[18,128]{1,0:T(8,128)S(1)}, u32[]{:S(2)}, u32[]{:S(2)}) collective-permute-start(f32[18,128]{1,0:T(8,128)S(1)} %get-tuple-element.55.refs_0_), channel_id=1, source_target_pairs={{0,4},{2,6},{4,0},{6,2},{1,5},{3,7},{5,1},{7,3},{8,12},{10,14},{12... | collective-permute-start | bytes 27656 | tf_op jit(solution)/shard_map/ppermute | solution.py:63
  31.8 0.7 %collective-permute-start.10 = (bf16[144,512]{1,0:T(8,128)(2,1)S(1)}, bf16[144,512]{1,0:T(8,128)(2,1)S(1)}, u32[]{:S(2)}, u32[]{:S(2)}) collective-permute-start(bf16[144,512]{1,0:T(8,128)(2,1)S(1)} %get-tuple-element.59), channel_id=1, source_target_pairs={{0,2},{2,0},{4,6},{6,4},{1,3},{3,1},{5,7},{7,5},{8,10},{10,8},{12,... | collective-permute-start | bytes 442376 | tf_op jit(solution)/shard_map/ppermute | solution.py:63
  32.5 0.0 collective-permute-done.3.refs_0_
  32.5 1.8 %finish.1 = (bf16[128,2048]{1,0:T(8,128)(2,1)}, bf16[128,2048]{1,0:T(8,128)(2,1)}, bf16[128,512]{1,0:T(8,128)(2,1)S(1)}) custom-call(bf16[512,2048]{1,0:T(8,128)(2,1)S(1)} %get-tuple-element.46.probs_ref, bf16[512,2048]{1,0:T(8,128)(2,1)S(1)} %get-tuple-element.47.dscore_ref, ...), custom_call_target="tpu_custom_call", output_to_operand_aliasing={{2}: (4, {})} | custom-call | flops 2147483648 | tf_op jit(solution)/shard_map/finish/pallas_call | solution.py:450
  34.3 0.0 collective-permute-done.8.refs_2_
  34.4 0.1 collective-permute-done.7.refs_1_
  34.5 0.0 collective-permute-done.9.refs_5_
  34.5 2.5 %collective-permute-done.10.refs_6_ = bf16[144,512]{1,0:T(8,128)(2,1)S(1)} collective-permute-done((bf16[144,512]{1,0:T(8,128)(2,1)S(1)}, bf16[144,512]{1,0:T(8,128)(2,1)S(1)}, u32[]{:S(2)}, u32[]{:S(2)}) %collective-permute-start.10) | collective-permute-done | bytes 147488 | tf_op jit(solution)/shard_map/ppermute | solution.py:63
  37.0 0.7 %collect.1 = (bf16[128,256]{1,0:T(8,128)(2,1)}, bf16[128,256]{1,0:T(8,128)(2,1)}, f32[16,128]{1,0:T(8,128)}, f32[2,128]{1,0:T(2,128)}) custom-call(f32[18,128]{1,0:T(8,128)S(1)} %get-tuple-element.55.refs_0_, f32[18,128]{1,0:T(8,128)S(1)} %collective-permute-done.7.refs_1_, f32[18,128]{1,0:T(8,128)S(1)} %collective-permute-done.8.refs_2_, ...), custom_call_target="tpu_custom_call" | custom-call | flops 262144 | bytes 524288 | tf_op jit(solution)/shard_map/collect/pallas_call | solution.py:469
  (1 shorter events, 0.0 us)
Async XLA Ops:
  1.5 11.0 %collective-permute-start.1 = (bf16[128,512]{1,0:T(8,128)(2,1)S(1)}, bf16[128,512]{1,0:T(8,128)(2,1)S(1)}, u32[]{:S(2)}, u32[]{:S(2)}) collective-permute-start(bf16[128,512]{1,0:T(8,128)(2,1)S(1)} %pad_maximum_fusion.pair_ref.refs_0_), channel_id=1, source_target_pairs={{6,0},{4,2},{2,4},{0,6},{7,1},{5,3},{3,5},{1,7},{14,8},{12,10},{10... | collective-permute-start | bytes 393224 | tf_op jit(solution)/shard_map/ppermute | solution.py:58
  6.6 7.4 %collective-permute-start = (bf16[128,512]{1,0:T(8,128)(2,1)S(1)}, bf16[128,512]{1,0:T(8,128)(2,1)S(1)}, u32[]{:S(2)}, u32[]{:S(2)}) collective-permute-start(bf16[128,512]{1,0:T(8,128)(2,1)S(1)} %pad_maximum_fusion.pair_ref.refs_0_), channel_id=1, source_target_pairs={{2,0},{0,2},{6,4},{4,6},{3,1},{1,3},{7,5},{5,7},{10,8},{8,10},{14,... | collective-permute-start | bytes 393224 | tf_op jit(solution)/shard_map/ppermute | solution.py:58
  6.6 11.1 %collective-permute-start.2 = (bf16[128,512]{1,0:T(8,128)(2,1)S(1)}, bf16[128,512]{1,0:T(8,128)(2,1)S(1)}, u32[]{:S(2)}, u32[]{:S(2)}) collective-permute-start(bf16[128,512]{1,0:T(8,128)(2,1)S(1)} %pad_maximum_fusion.pair_ref.refs_0_), channel_id=1, source_target_pairs={{4,0},{6,2},{0,4},{2,6},{5,1},{7,3},{1,5},{3,7},{12,8},{14,10},{8,... | collective-permute-start | bytes 393224 | tf_op jit(solution)/shard_map/ppermute | solution.py:58
  7.3 1.0 %copy-start = (bf16[1,128,2048]{2,1,0:T(8,128)(2,1)S(1)}, bf16[1,128,2048]{2,1,0:T(8,128)(2,1)}, u32[]{:S(2)}) copy-start(bf16[1,128,2048]{2,1,0:T(8,128)(2,1)} %param.7) | copy-start | bytes 1572868
  8.3 1.0 %copy-start.1 = (bf16[1,128,2048]{2,1,0:T(8,128)(2,1)S(1)}, bf16[1,128,2048]{2,1,0:T(8,128)(2,1)}, u32[]{:S(2)}) copy-start(bf16[1,128,2048]{2,1,0:T(8,128)(2,1)} %param.12) | copy-start | bytes 1572868
  9.4 0.7 %copy-start.2 = (bf16[2048]{0:T(1024)(128)(2,1)S(1)}, bf16[2048]{0:T(1024)(128)(2,1)}, u32[]{:S(2)}) copy-start(bf16[2048]{0:T(1024)(128)(2,1)} %param.8) | copy-start | bytes 12292
  10.0 0.7 %copy-start.3 = (s32[1,8]{1,0:T(1,128)S(1)}, s32[1,8]{1,0:T(1,128)}, u32[]{:S(2)}) copy-start(s32[1,8]{1,0:T(1,128)} %len_ref.1) | copy-start | bytes 100
  10.7 0.7 %copy-start.4 = (bf16[256]{0:T(256)(128)(2,1)S(1)}, bf16[256]{0:T(256)(128)(2,1)}, u32[]{:S(2)}) copy-start(bf16[256]{0:T(256)(128)(2,1)} %param.11) | copy-start | bytes 1540
  20.5 12.0 %collective-permute-start.3 = (bf16[128,512]{1,0:T(8,128)(2,1)S(1)}, bf16[128,512]{1,0:T(8,128)(2,1)S(1)}, u32[]{:S(2)}, u32[]{:S(2)}) collective-permute-start(bf16[128,512]{1,0:T(8,128)(2,1)S(1)} %get-tuple-element.50), channel_id=1, source_target_pairs={{0,4},{2,6},{4,0},{6,2},{1,5},{3,7},{5,1},{7,3},{8,12},{10,14},{12... | collective-permute-start | bytes 393224 | tf_op jit(solution)/shard_map/ppermute | solution.py:63
  21.4 5.2 %collective-permute-start.6 = (f32[18,128]{1,0:T(8,128)S(1)}, f32[18,128]{1,0:T(8,128)S(1)}, u32[]{:S(2)}, u32[]{:S(2)}) collective-permute-start(f32[18,128]{1,0:T(8,128)S(1)} %get-tuple-element.53.refs_0_), channel_id=1, source_target_pairs={{24,0},{16,8},{8,16},{0,24},{25,1},{17,9},{9,17},{1,25},{26,2},{18... | collective-permute-start | bytes 27656 | tf_op jit(solution)/shard_map/ppermute | solution.py:58
  23.9 3.7 %collective-permute-start.5 = (f32[18,128]{1,0:T(8,128)S(1)}, f32[18,128]{1,0:T(8,128)S(1)}, u32[]{:S(2)}, u32[]{:S(2)}) collective-permute-start(f32[18,128]{1,0:T(8,128)S(1)} %get-tuple-element.53.refs_0_), channel_id=1, source_target_pairs={{16,0},{24,8},{0,16},{8,24},{17,1},{25,9},{1,17},{9,25},{18,2},{26... | collective-permute-start | bytes 27656 | tf_op jit(solution)/shard_map/ppermute | solution.py:58
  24.4 3.7 %collective-permute-start.4 = (f32[18,128]{1,0:T(8,128)S(1)}, f32[18,128]{1,0:T(8,128)S(1)}, u32[]{:S(2)}, u32[]{:S(2)}) collective-permute-start(f32[18,128]{1,0:T(8,128)S(1)} %get-tuple-element.53.refs_0_), channel_id=1, source_target_pairs={{8,0},{0,8},{24,16},{16,24},{9,1},{1,9},{25,17},{17,25},{10,2},{2,... | collective-permute-start | bytes 27656 | tf_op jit(solution)/shard_map/ppermute | solution.py:58
  24.9 9.6 %collective-permute-start.9 = (bf16[128,512]{1,0:T(8,128)(2,1)S(1)}, bf16[128,512]{1,0:T(8,128)(2,1)S(1)}, u32[]{:S(2)}, u32[]{:S(2)}) collective-permute-start(bf16[128,512]{1,0:T(8,128)(2,1)S(1)} %get-tuple-element.58), channel_id=1, source_target_pairs={{0,6},{2,4},{4,2},{6,0},{1,7},{3,5},{5,3},{7,1},{8,14},{10,12},{12... | collective-permute-start | bytes 393224 | tf_op jit(solution)/shard_map/ppermute | solution.py:63
  28.1 6.3 %collective-permute-start.8 = (f32[18,128]{1,0:T(8,128)S(1)}, f32[18,128]{1,0:T(8,128)S(1)}, u32[]{:S(2)}, u32[]{:S(2)}) collective-permute-start(f32[18,128]{1,0:T(8,128)S(1)} %get-tuple-element.55.refs_0_), channel_id=1, source_target_pairs={{0,6},{2,4},{4,2},{6,0},{1,7},{3,5},{5,3},{7,1},{8,14},{10,12},{12... | collective-permute-start | bytes 27656 | tf_op jit(solution)/shard_map/ppermute | solution.py:63
  29.9 4.6 %collective-permute-start.7 = (f32[18,128]{1,0:T(8,128)S(1)}, f32[18,128]{1,0:T(8,128)S(1)}, u32[]{:S(2)}, u32[]{:S(2)}) collective-permute-start(f32[18,128]{1,0:T(8,128)S(1)} %get-tuple-element.55.refs_0_), channel_id=1, source_target_pairs={{0,4},{2,6},{4,0},{6,2},{1,5},{3,7},{5,1},{7,3},{8,12},{10,14},{12... | collective-permute-start | bytes 27656 | tf_op jit(solution)/shard_map/ppermute | solution.py:63
  31.8 5.1 %collective-permute-start.10 = (bf16[144,512]{1,0:T(8,128)(2,1)S(1)}, bf16[144,512]{1,0:T(8,128)(2,1)S(1)}, u32[]{:S(2)}, u32[]{:S(2)}) collective-permute-start(bf16[144,512]{1,0:T(8,128)(2,1)S(1)} %get-tuple-element.59), channel_id=1, source_target_pairs={{0,2},{2,0},{4,6},{6,4},{1,3},{3,1},{5,7},{7,5},{8,10},{10,8},{12,... | collective-permute-start | bytes 442376 | tf_op jit(solution)/shard_map/ppermute | solution.py:63

commit v19 on v17

--- a/solution.py
+++ b/solution.py
@@ -228,7 +228,9 @@
             out_refs[slot - 1][:, value_cols] = value_term[rows].astype(jnp.bfloat16)
 
 
-def finish_kernel(probs_ref, dscore_ref, keys_ref, values_ref, _, attn_ref, qg_ref, __):
+def finish_kernel(probs_ref, dscore_ref, keys_ref, values_ref, *refs):
+    passed = (len(refs) - 2) // 2
+    attn_ref, qg_ref = refs[passed : passed + 2]
     tok = attn_ref.shape[0]
     kv_heads = keys_ref.shape[1] // HEAD_DIM
     for kv_head in range(kv_heads):
@@ -263,6 +265,13 @@
     term = term.astype(jnp.bfloat16)
     kg_ref[...] = term[:, :kv_width]
     vg_ref[...] = term[:, kv_width:]
+
+
+def total_kernel(*refs):
+    total = refs[0][...]
+    for ref in refs[1:-1]:
+        total = total + ref[...]
+    refs[-1][...] = total
 
 
 def exchange(axis, part):
@@ -390,26 +399,36 @@
     probs, dscore, all_keys, all_values, sums, own, *terms = made
     term = shape((tok, 2 * kv_width), jnp.bfloat16)
     half = ctx // 2
-    early = send_back(terms[half - 1], half)
-    attn, q_grad, early = pl.pallas_call(
+    back = {slot: send_back(terms[slot - 1], slot) for slot in range(1, ctx)}
+    tied = [half]
+    attn, q_grad, *passed = pl.pallas_call(
         finish_kernel,
         out_shape=[
             shape((tok, width), jnp.bfloat16),
             shape((tok, width), jnp.bfloat16),
-            shape(early.shape, early.dtype),
-        ],
-        in_specs=[VMEM] * 4 + [ANY],
-        out_specs=[VMEM] * 2 + [ANY],
-        input_output_aliases={4: 2},
+        ]
+        + [shape((tok, 2 * kv_width), jnp.bfloat16)] * len(tied),
+        in_specs=[VMEM] * 4 + [ANY] * len(tied),
+        out_specs=[VMEM] * 2 + [ANY] * len(tied),
+        input_output_aliases={4 + n: 2 + n for n in range(len(tied))},
         compiler_params=params(24),
         cost_estimate=pl.CostEstimate(
-            flops=4 * rows * tok * width, bytes_accessed=4 * rows * columns, transcendentals=0
+            flops=16 * rows * tok * width, bytes_accessed=0, transcendentals=0
         ),
         name="finish",
-    )(probs, dscore, all_keys, all_values, early)
-    sums = functools.reduce(lambda left, right: left + right, exchange("dp", sums))
+    )(probs, dscore, all_keys, all_values, *[back[slot] for slot in tied])
+    parts = exchange("dp", sums)
+    sums = pl.pallas_call(
+        total_kernel,
+        out_shape=shape(sums.shape, sums.dtype),
+        in_specs=[VMEM] * len(parts),
+        out_specs=VMEM,
+        compiler_params=params(4),
+        cost_estimate=pl.CostEstimate(flops=sums.size, bytes_accessed=0, transcendentals=0),
+        name="total",
+    )(*parts)
     sums = exchange("ctx", sums)
-    back = [send_back(terms[slot - 1], slot) for slot in range(ctx - 1, 0, -1) if slot != half]
+    back.update(zip(tied, passed))
     k_grad, v_grad, q_sum, v_sum = pl.pallas_call(
         functools.partial(collect_kernel, batches, len(sums)),
         out_shape=[
@@ -418,14 +437,14 @@
             shape((heads, HEAD_DIM), jnp.float32),
             shape((kv_heads, HEAD_DIM), jnp.float32),
         ],
-        in_specs=[VMEM] * (len(sums) + 2 + len(back)),
+        in_specs=[VMEM] * (len(sums) + 1 + len(back)),
         out_specs=[VMEM] * 4,
         compiler_params=params(8),
         cost_estimate=pl.CostEstimate(
             flops=8 * tok * kv_width, bytes_accessed=16 * tok * kv_width, transcendentals=0
         ),
         name="collect",
-    )(*sums, own, early, *back)
+    )(*sums, own, *[back[slot] for slot in sorted(back, reverse=True)])
     return (
         attn[None],
         q_grad[None],

time: 39.3 us -> 36.6 us (0.931)
  waiting for transfers between devices: 9.89 us -> 4.79 us
  starting transfers between devices: 15.3 us -> 17.8 us
    ppermute x3, waiting for transfers between devices: 4.45 us -> 0.15 us  [send_back(): lax.ppermute(array, 'ctx', [(i, source_of(i, slot, size)) for i in range(...]
    ppermute x9, starting transfers between devices: 11.9 us -> 13.6 us  [fetch(): lax.ppermute(array, axis, [(source_of(i, slot, size), i) for i in range(s...]
    ppermute x9, waiting for transfers between devices: 5.44 us -> 4.64 us  [fetch(): lax.ppermute(array, axis, [(source_of(i, slot, size), i) for i in range(s...]
    ppermute x3, starting transfers between devices: 3.49 us -> 4.21 us  [send_back(): lax.ppermute(array, 'ctx', [(i, source_of(i, slot, size)) for i in range(...]
  transfers between devices with their start and end apart: 12 -> 12, of which waited for: 5 -> 5; matrix products, arithmetic and copies ran while one was open for 0% -> 0% of each run, Pallas kernels for 12% -> 13%
where the time goes in v19:
time: 36.6 us; the launch traced here: 36.3 us
  starting transfers between devices  17.8 us (49%)
  Pallas kernels  8.11 us (22%)
  waiting for transfers between devices  4.79 us (13%)
  local copies, waits for them, and re-layouts  4.08 us (11%)
  other arithmetic  0.88 us (2%)
  between operations  0.68 us (2%)
    ppermute x9, starting transfers between devices, fetch(): lax.ppermute(array, axis, [(source_of(i, slot, size), i) for i in range(s...  13.6 us
    ppermute x9, waiting for transfers between devices, fetch(): lax.ppermute(array, axis, [(source_of(i, slot, size), i) for i in range(s...  4.64 us
    ppermute x3, starting transfers between devices, send_back(): lax.ppermute(array, 'ctx', [(i, source_of(i, slot, size)) for i in range(...  4.21 us
    unnamed x10, local copies, waits for them, and re-layouts  4.08 us
    pallas_call x1, Pallas kernels, attend(): pl.pallas_call(functools.partial(last_kernel, ctx, first_head), out_shape...  2.82 us
    pallas_call x1, Pallas kernels, shards(): pl.pallas_call(finish_kernel, out_shape=[shape((tok, width), jnp.bfloat16...  1.8 us
    pallas_call x1, Pallas kernels, attend(): pl.pallas_call(near_kernel, out_shape=[shape((near, columns), jnp.float32...  1.67 us
    pallas_call x1, Pallas kernels, shards(): pl.pallas_call(functools.partial(prepare_kernel, ctx), out_shape=[shape((...  1.11 us
  transfers between devices with their start and end apart: 12, of which 5 were waited for; matrix products, arithmetic and copies ran while one was open for 0% of the time, Pallas kernels for 13%

profile of v19, /device:TPU:0, one launch (start us, length us, event | category | flops | bytes accessed | tf_op | source)
XLA Modules:
  0.0 36.3 jit_solution(7133616032610376376)
XLA Ops:
  0.6 0.9 %pad_maximum_fusion.pair_ref.refs_0_ = bf16[128,512]{1,0:T(8,128)(2,1)S(1)} fusion(bf16[128,256]{1,0:T(8,128)(2,1)} %bitcast.16, bf16[128,256]{1,0:T(8,128)(2,1)} %bitcast.17), kind=kLoop, calls=%fused_computation | loop fusion | flops 262144 | bytes 262144 | tf_op jit(solution)/shard_map/concatenate | solution.py:350
  1.5 5.1 %collective-permute-start.1 = (bf16[128,512]{1,0:T(8,128)(2,1)S(1)}, bf16[128,512]{1,0:T(8,128)(2,1)S(1)}, u32[]{:S(2)}, u32[]{:S(2)}) collective-permute-start(bf16[128,512]{1,0:T(8,128)(2,1)S(1)} %pad_maximum_fusion.pair_ref.refs_0_), channel_id=1, source_target_pairs={{6,0},{4,2},{2,4},{0,6},{7,1},{5,3},{3,5},{1,7},{14,8},{12,10},{10... | collective-permute-start | bytes 393224 | tf_op jit(solution)/shard_map/ppermute | solution.py:58
  6.6 0.0 collective-permute-start
  6.6 0.6 %collective-permute-start.2 = (bf16[128,512]{1,0:T(8,128)(2,1)S(1)}, bf16[128,512]{1,0:T(8,128)(2,1)S(1)}, u32[]{:S(2)}, u32[]{:S(2)}) collective-permute-start(bf16[128,512]{1,0:T(8,128)(2,1)S(1)} %pad_maximum_fusion.pair_ref.refs_0_), channel_id=1, source_target_pairs={{4,0},{6,2},{0,4},{2,6},{5,1},{7,3},{1,5},{3,7},{12,8},{14,10},{8,... | collective-permute-start | bytes 393224 | tf_op jit(solution)/shard_map/ppermute | solution.py:58
  7.3 0.0 copy-start
  7.3 1.0 %copy-done = bf16[1,128,2048]{2,1,0:T(8,128)(2,1)S(1)} copy-done((bf16[1,128,2048]{2,1,0:T(8,128)(2,1)S(1)}, bf16[1,128,2048]{2,1,0:T(8,128)(2,1)}, u32[]{:S(2)}) %copy-start) | copy-done | bytes 524312
  8.3 0.0 copy-start.1
  8.3 1.0 %copy-done.1 = bf16[1,128,2048]{2,1,0:T(8,128)(2,1)S(1)} copy-done((bf16[1,128,2048]{2,1,0:T(8,128)(2,1)S(1)}, bf16[1,128,2048]{2,1,0:T(8,128)(2,1)}, u32[]{:S(2)}) %copy-start.1) | copy-done | bytes 524312
  9.4 0.0 copy-start.2
  9.4 0.7 %copy-done.2 = bf16[2048]{0:T(1024)(128)(2,1)S(1)} copy-done((bf16[2048]{0:T(1024)(128)(2,1)S(1)}, bf16[2048]{0:T(1024)(128)(2,1)}, u32[]{:S(2)}) %copy-start.2) | copy-done | bytes 4120
  10.0 0.0 copy-start.3
  10.0 0.7 %copy-done.3 = s32[1,8]{1,0:T(1,128)S(1)} copy-done((s32[1,8]{1,0:T(1,128)S(1)}, s32[1,8]{1,0:T(1,128)}, u32[]{:S(2)}) %copy-start.3) | copy-done | bytes 56
  10.7 0.0 copy-start.4
  10.7 0.7 %copy-done.4 = bf16[256]{0:T(256)(128)(2,1)S(1)} copy-done((bf16[256]{0:T(256)(128)(2,1)S(1)}, bf16[256]{0:T(256)(128)(2,1)}, u32[]{:S(2)}) %copy-start.4) | copy-done | bytes 536
  11.4 1.1 %prepare.1 = (bf16[2,128]{1,0:T(2,128)(2,1)S(1)}, bf16[2048,256]{1,0:T(8,128)(2,1)S(1)}, bf16[2048,128]{1,0:T(8,128)(2,1)S(1)}, f32[128,2048]{1,0:T(8,128)S(1)},...) custom-call(s32[1,8]{1,0:T(1,128)S(1)} %copy-done.3, bf16[128,512]{1,0:T(8,128)(2,1)S(1)} %pad_maximum_fusion.pair_ref.refs_0_, ...), custom_call_target="tpu_custom_call" | custom-call | flops 134217728 | bytes 4194304 | tf_op jit(solution)/shard_map/prepare/pallas_call | solution.py:352
  12.5 0.0 collective-permute-done.1.refs_2_
  12.5 1.5 %collective-permute-done.refs_1_ = bf16[128,512]{1,0:T(8,128)(2,1)S(1)} collective-permute-done((bf16[128,512]{1,0:T(8,128)(2,1)S(1)}, bf16[128,512]{1,0:T(8,128)(2,1)S(1)}, u32[]{:S(2)}, u32[]{:S(2)}) %collective-permute-start) | collective-permute-done | bytes 131104 | tf_op jit(solution)/shard_map/ppermute | solution.py:58
  14.0 1.7 %near.1 = (f32[384,2048]{1,0:T(8,128)S(1)}, f32[384,2048]{1,0:T(8,128)S(1)}, f32[8,2048]{1,0:T(8,128)S(1)}, bf16[384,256]{1,0:T(8,128)(2,1)S(1)}, bf16[384,256]{1,0:T(8,128)(2,1)S(1)}) custom-call(bf16[2,128]{1,0:T(2,128)(2,1)S(1)} %get-tuple-element.33.bias_ref.refs_0_, bf16[2048,256]{1,0:T(8,128)(2,1)S(1)} %get-tuple-element.34.queries_ref.refs_1_, ...), custom_call_target="tpu_custom_call" | custom-call | flops 402653184 | bytes 6291456 | tf_op jit(solution)/shard_map/near/pallas_call | solution.py:289
  15.7 2.0 %collective-permute-done.2.refs_9_ = bf16[128,512]{1,0:T(8,128)(2,1)S(1)} collective-permute-done((bf16[128,512]{1,0:T(8,128)(2,1)S(1)}, bf16[128,512]{1,0:T(8,128)(2,1)S(1)}, u32[]{:S(2)}, u32[]{:S(2)}) %collective-permute-start.2) | collective-permute-done | bytes 131104 | tf_op jit(solution)/shard_map/ppermute | solution.py:58
  17.7 2.8 %last.1 = (bf16[512,2048]{1,0:T(8,128)(2,1)S(1)}, bf16[512,2048]{1,0:T(8,128)(2,1)S(1)}, bf16[512,256]{1,0:T(8,128)(2,1)S(1)}, bf16[512,256]{1,0:T(8,128)(2,1)S(...) custom-call(bf16[2,128]{1,0:T(2,128)(2,1)S(1)} %get-tuple-element.33, ...), custom_call_target="tpu_custom_call" | custom-call | flops 536870912 | bytes 4194304 | tf_op jit(solution)/shard_map/last/pallas_call | solution.py:309
  20.5 0.9 %collective-permute-start.3 = (bf16[128,512]{1,0:T(8,128)(2,1)S(1)}, bf16[128,512]{1,0:T(8,128)(2,1)S(1)}, u32[]{:S(2)}, u32[]{:S(2)}) collective-permute-start(bf16[128,512]{1,0:T(8,128)(2,1)S(1)} %get-tuple-element.48), channel_id=1, source_target_pairs={{0,4},{2,6},{4,0},{6,2},{1,5},{3,7},{5,1},{7,3},{8,12},{10,14},{12... | collective-permute-start | bytes 393224 | tf_op jit(solution)/shard_map/ppermute | solution.py:63
  21.4 2.4 %collective-permute-start.6 = (f32[18,128]{1,0:T(8,128)S(1)}, f32[18,128]{1,0:T(8,128)S(1)}, u32[]{:S(2)}, u32[]{:S(2)}) collective-permute-start(f32[18,128]{1,0:T(8,128)S(1)} %get-tuple-element.51.refs_0_), channel_id=1, source_target_pairs={{24,0},{16,8},{8,16},{0,24},{25,1},{17,9},{9,17},{1,25},{26,2},{18... | collective-permute-start | bytes 27656 | tf_op jit(solution)/shard_map/ppermute | solution.py:58
  23.9 0.5 %collective-permute-start.5 = (f32[18,128]{1,0:T(8,128)S(1)}, f32[18,128]{1,0:T(8,128)S(1)}, u32[]{:S(2)}, u32[]{:S(2)}) collective-permute-start(f32[18,128]{1,0:T(8,128)S(1)} %get-tuple-element.51.refs_0_), channel_id=1, source_target_pairs={{16,0},{24,8},{0,16},{8,24},{17,1},{25,9},{1,17},{9,25},{18,2},{26... | collective-permute-start | bytes 27656 | tf_op jit(solution)/shard_map/ppermute | solution.py:58
  24.4 0.5 %collective-permute-start.4 = (f32[18,128]{1,0:T(8,128)S(1)}, f32[18,128]{1,0:T(8,128)S(1)}, u32[]{:S(2)}, u32[]{:S(2)}) collective-permute-start(f32[18,128]{1,0:T(8,128)S(1)} %get-tuple-element.51.refs_0_), channel_id=1, source_target_pairs={{8,0},{0,8},{24,16},{16,24},{9,1},{1,9},{25,17},{17,25},{10,2},{2,... | collective-permute-start | bytes 27656 | tf_op jit(solution)/shard_map/ppermute | solution.py:58
  24.9 1.7 %collective-permute-start.10 = (bf16[128,512]{1,0:T(8,128)(2,1)S(1)}, bf16[128,512]{1,0:T(8,128)(2,1)S(1)}, u32[]{:S(2)}, u32[]{:S(2)}) collective-permute-start(bf16[128,512]{1,0:T(8,128)(2,1)S(1)} %get-tuple-element.53), channel_id=1, source_target_pairs={{0,6},{2,4},{4,2},{6,0},{1,7},{3,5},{5,3},{7,1},{8,14},{10,12},{12... | collective-permute-start | bytes 393224 | tf_op jit(solution)/shard_map/ppermute | solution.py:63
  26.6 0.0 collective-permute-done.6.refs_3_
  26.6 1.6 %collective-permute-start.11 = (bf16[128,512]{1,0:T(8,128)(2,1)S(1)}, bf16[128,512]{1,0:T(8,128)(2,1)S(1)}, u32[]{:S(2)}, u32[]{:S(2)}) collective-permute-start(bf16[128,512]{1,0:T(8,128)(2,1)S(1)} %get-tuple-element.55), channel_id=1, source_target_pairs={{0,2},{2,0},{4,6},{6,4},{1,3},{3,1},{5,7},{7,5},{8,10},{10,8},{12,... | collective-permute-start | bytes 393224 | tf_op jit(solution)/shard_map/ppermute | solution.py:63
  28.2 0.0 collective-permute-done.5.refs_2_
  28.2 0.0 collective-permute-done.4.refs_1_
  28.2 1.9 %collective-permute-start.9 = (f32[18,128]{1,0:T(8,128)S(1)}, f32[18,128]{1,0:T(8,128)S(1)}, u32[]{:S(2)}, u32[]{:S(2)}) collective-permute-start(f32[18,128]{1,0:T(8,128)S(1)} %total.1.refs_0_), channel_id=1, source_target_pairs={{6,0},{4,2},{2,4},{0,6},{7,1},{5,3},{3,5},{1,7},{14,8},{12,10},{10... | collective-permute-start | bytes 27656 | tf_op jit(solution)/shard_map/ppermute | solution.py:58
  30.1 1.6 %collective-permute-start.8 = (f32[18,128]{1,0:T(8,128)S(1)}, f32[18,128]{1,0:T(8,128)S(1)}, u32[]{:S(2)}, u32[]{:S(2)}) collective-permute-start(f32[18,128]{1,0:T(8,128)S(1)} %total.1.refs_0_), channel_id=1, source_target_pairs={{4,0},{6,2},{0,4},{2,6},{5,1},{7,3},{1,5},{3,7},{12,8},{14,10},{8,... | collective-permute-start | bytes 27656 | tf_op jit(solution)/shard_map/ppermute | solution.py:58
  31.8 0.1 collective-permute-done.3.refs_0_
  31.9 0.8 %collective-permute-start.7 = (f32[18,128]{1,0:T(8,128)S(1)}, f32[18,128]{1,0:T(8,128)S(1)}, u32[]{:S(2)}, u32[]{:S(2)}) collective-permute-start(f32[18,128]{1,0:T(8,128)S(1)} %total.1.refs_0_), channel_id=1, source_target_pairs={{2,0},{0,2},{6,4},{4,6},{3,1},{1,3},{7,5},{5,7},{10,8},{8,10},{14,... | collective-permute-start | bytes 27656 | tf_op jit(solution)/shard_map/ppermute | solution.py:58
  32.7 1.8 %finish.1 = (bf16[128,2048]{1,0:T(8,128)(2,1)}, bf16[128,2048]{1,0:T(8,128)(2,1)}, bf16[128,512]{1,0:T(8,128)(2,1)S(1)}) custom-call(bf16[512,2048]{1,0:T(8,128)(2,1)S(1)} %get-tuple-element.44.probs_ref, bf16[512,2048]{1,0:T(8,128)(2,1)S(1)} %get-tuple-element.45.dscore_ref, ...), custom_call_target="tpu_custom_call", output_to_operand_aliasing={{2}: (4, {})} | custom-call | flops 2147483648 | tf_op jit(solution)/shard_map/finish/pallas_call | solution.py:404
  34.5 0.0 collective-permute-done.9.refs_3_
  34.5 0.2 collective-permute-done.8.refs_2_
  34.7 0.9 %collective-permute-done.7.refs_1_ = f32[18,128]{1,0:T(8,128)S(1)} collective-permute-done((f32[18,128]{1,0:T(8,128)S(1)}, f32[18,128]{1,0:T(8,128)S(1)}, u32[]{:S(2)}, u32[]{:S(2)}) %collective-permute-start.7) | collective-permute-done | bytes 9248 | tf_op jit(solution)/shard_map/ppermute | solution.py:58
  35.6 0.0 collective-permute-done.10.refs_5_
  35.6 0.0 collective-permute-done.11.refs_7_
  35.6 0.7 %collect.1 = (bf16[128,256]{1,0:T(8,128)(2,1)}, bf16[128,256]{1,0:T(8,128)(2,1)}, f32[16,128]{1,0:T(8,128)}, f32[2,128]{1,0:T(2,128)}) custom-call(f32[18,128]{1,0:T(8,128)S(1)} %total.1.refs_0_, f32[18,128]{1,0:T(8,128)S(1)} %collective-permute-done.7.refs_1_, f32[18,128]{1,0:T(8,128)S(1)} %collective-permute-done.8.refs_2_, ...), custom_call_target="tpu_custom_call" | custom-call | flops 262144 | bytes 524288 | tf_op jit(solution)/shard_map/collect/pallas_call | solution.py:432
  (1 shorter events, 0.0 us)
Async XLA Ops:
  1.5 11.0 %collective-permute-start.1 = (bf16[128,512]{1,0:T(8,128)(2,1)S(1)}, bf16[128,512]{1,0:T(8,128)(2,1)S(1)}, u32[]{:S(2)}, u32[]{:S(2)}) collective-permute-start(bf16[128,512]{1,0:T(8,128)(2,1)S(1)} %pad_maximum_fusion.pair_ref.refs_0_), channel_id=1, source_target_pairs={{6,0},{4,2},{2,4},{0,6},{7,1},{5,3},{3,5},{1,7},{14,8},{12,10},{10... | collective-permute-start | bytes 393224 | tf_op jit(solution)/shard_map/ppermute | solution.py:58
  6.6 7.4 %collective-permute-start = (bf16[128,512]{1,0:T(8,128)(2,1)S(1)}, bf16[128,512]{1,0:T(8,128)(2,1)S(1)}, u32[]{:S(2)}, u32[]{:S(2)}) collective-permute-start(bf16[128,512]{1,0:T(8,128)(2,1)S(1)} %pad_maximum_fusion.pair_ref.refs_0_), channel_id=1, source_target_pairs={{2,0},{0,2},{6,4},{4,6},{3,1},{1,3},{7,5},{5,7},{10,8},{8,10},{14,... | collective-permute-start | bytes 393224 | tf_op jit(solution)/shard_map/ppermute | solution.py:58
  6.6 11.1 %collective-permute-start.2 = (bf16[128,512]{1,0:T(8,128)(2,1)S(1)}, bf16[128,512]{1,0:T(8,128)(2,1)S(1)}, u32[]{:S(2)}, u32[]{:S(2)}) collective-permute-start(bf16[128,512]{1,0:T(8,128)(2,1)S(1)} %pad_maximum_fusion.pair_ref.refs_0_), channel_id=1, source_target_pairs={{4,0},{6,2},{0,4},{2,6},{5,1},{7,3},{1,5},{3,7},{12,8},{14,10},{8,... | collective-permute-start | bytes 393224 | tf_op jit(solution)/shard_map/ppermute | solution.py:58
  7.3 1.0 %copy-start = (bf16[1,128,2048]{2,1,0:T(8,128)(2,1)S(1)}, bf16[1,128,2048]{2,1,0:T(8,128)(2,1)}, u32[]{:S(2)}) copy-start(bf16[1,128,2048]{2,1,0:T(8,128)(2,1)} %param.7) | copy-start | bytes 1572868
  8.3 1.0 %copy-start.1 = (bf16[1,128,2048]{2,1,0:T(8,128)(2,1)S(1)}, bf16[1,128,2048]{2,1,0:T(8,128)(2,1)}, u32[]{:S(2)}) copy-start(bf16[1,128,2048]{2,1,0:T(8,128)(2,1)} %param.12) | copy-start | bytes 1572868
  9.4 0.7 %copy-start.2 = (bf16[2048]{0:T(1024)(128)(2,1)S(1)}, bf16[2048]{0:T(1024)(128)(2,1)}, u32[]{:S(2)}) copy-start(bf16[2048]{0:T(1024)(128)(2,1)} %param.8) | copy-start | bytes 12292
  10.0 0.7 %copy-start.3 = (s32[1,8]{1,0:T(1,128)S(1)}, s32[1,8]{1,0:T(1,128)}, u32[]{:S(2)}) copy-start(s32[1,8]{1,0:T(1,128)} %len_ref.1) | copy-start | bytes 100
  10.7 0.7 %copy-start.4 = (bf16[256]{0:T(256)(128)(2,1)S(1)}, bf16[256]{0:T(256)(128)(2,1)}, u32[]{:S(2)}) copy-start(bf16[256]{0:T(256)(128)(2,1)} %param.11) | copy-start | bytes 1540
  20.5 11.4 %collective-permute-start.3 = (bf16[128,512]{1,0:T(8,128)(2,1)S(1)}, bf16[128,512]{1,0:T(8,128)(2,1)S(1)}, u32[]{:S(2)}, u32[]{:S(2)}) collective-permute-start(bf16[128,512]{1,0:T(8,128)(2,1)S(1)} %get-tuple-element.48), channel_id=1, source_target_pairs={{0,4},{2,6},{4,0},{6,2},{1,5},{3,7},{5,1},{7,3},{8,12},{10,14},{12... | collective-permute-start | bytes 393224 | tf_op jit(solution)/shard_map/ppermute | solution.py:63
  21.4 5.2 %collective-permute-start.6 = (f32[18,128]{1,0:T(8,128)S(1)}, f32[18,128]{1,0:T(8,128)S(1)}, u32[]{:S(2)}, u32[]{:S(2)}) collective-permute-start(f32[18,128]{1,0:T(8,128)S(1)} %get-tuple-element.51.refs_0_), channel_id=1, source_target_pairs={{24,0},{16,8},{8,16},{0,24},{25,1},{17,9},{9,17},{1,25},{26,2},{18... | collective-permute-start | bytes 27656 | tf_op jit(solution)/shard_map/ppermute | solution.py:58
  23.9 4.4 %collective-permute-start.5 = (f32[18,128]{1,0:T(8,128)S(1)}, f32[18,128]{1,0:T(8,128)S(1)}, u32[]{:S(2)}, u32[]{:S(2)}) collective-permute-start(f32[18,128]{1,0:T(8,128)S(1)} %get-tuple-element.51.refs_0_), channel_id=1, source_target_pairs={{16,0},{24,8},{0,16},{8,24},{17,1},{25,9},{1,17},{9,25},{18,2},{26... | collective-permute-start | bytes 27656 | tf_op jit(solution)/shard_map/ppermute | solution.py:58
  24.4 3.9 %collective-permute-start.4 = (f32[18,128]{1,0:T(8,128)S(1)}, f32[18,128]{1,0:T(8,128)S(1)}, u32[]{:S(2)}, u32[]{:S(2)}) collective-permute-start(f32[18,128]{1,0:T(8,128)S(1)} %get-tuple-element.51.refs_0_), channel_id=1, source_target_pairs={{8,0},{0,8},{24,16},{16,24},{9,1},{1,9},{25,17},{17,25},{10,2},{2,... | collective-permute-start | bytes 27656 | tf_op jit(solution)/shard_map/ppermute | solution.py:58
  24.9 10.7 %collective-permute-start.10 = (bf16[128,512]{1,0:T(8,128)(2,1)S(1)}, bf16[128,512]{1,0:T(8,128)(2,1)S(1)}, u32[]{:S(2)}, u32[]{:S(2)}) collective-permute-start(bf16[128,512]{1,0:T(8,128)(2,1)S(1)} %get-tuple-element.53), channel_id=1, source_target_pairs={{0,6},{2,4},{4,2},{6,0},{1,7},{3,5},{5,3},{7,1},{8,14},{10,12},{12... | collective-permute-start | bytes 393224 | tf_op jit(solution)/shard_map/ppermute | solution.py:63
  26.6 9.0 %collective-permute-start.11 = (bf16[128,512]{1,0:T(8,128)(2,1)S(1)}, bf16[128,512]{1,0:T(8,128)(2,1)S(1)}, u32[]{:S(2)}, u32[]{:S(2)}) collective-permute-start(bf16[128,512]{1,0:T(8,128)(2,1)S(1)} %get-tuple-element.55), channel_id=1, source_target_pairs={{0,2},{2,0},{4,6},{6,4},{1,3},{3,1},{5,7},{7,5},{8,10},{10,8},{12,... | collective-permute-start | bytes 393224 | tf_op jit(solution)/shard_map/ppermute | solution.py:63
  28.2 6.3 %collective-permute-start.9 = (f32[18,128]{1,0:T(8,128)S(1)}, f32[18,128]{1,0:T(8,128)S(1)}, u32[]{:S(2)}, u32[]{:S(2)}) collective-permute-start(f32[18,128]{1,0:T(8,128)S(1)} %total.1.refs_0_), channel_id=1, source_target_pairs={{6,0},{4,2},{2,4},{0,6},{7,1},{5,3},{3,5},{1,7},{14,8},{12,10},{10... | collective-permute-start | bytes 27656 | tf_op jit(solution)/shard_map/ppermute | solution.py:58
  30.1 4.6 %collective-permute-start.8 = (f32[18,128]{1,0:T(8,128)S(1)}, f32[18,128]{1,0:T(8,128)S(1)}, u32[]{:S(2)}, u32[]{:S(2)}) collective-permute-start(f32[18,128]{1,0:T(8,128)S(1)} %total.1.refs_0_), channel_id=1, source_target_pairs={{4,0},{6,2},{0,4},{2,6},{5,1},{7,3},{1,5},{3,7},{12,8},{14,10},{8,... | collective-permute-start | bytes 27656 | tf_op jit(solution)/shard_map/ppermute | solution.py:58
  31.9 3.7 %collective-permute-start.7 = (f32[18,128]{1,0:T(8,128)S(1)}, f32[18,128]{1,0:T(8,128)S(1)}, u32[]{:S(2)}, u32[]{:S(2)}) collective-permute-start(f32[18,128]{1,0:T(8,128)S(1)} %total.1.refs_0_), channel_id=1, source_target_pairs={{2,0},{0,2},{6,4},{4,6},{3,1},{1,3},{7,5},{5,7},{10,8},{8,10},{14,... | collective-permute-start | bytes 27656 | tf_op jit(solution)/shard_map/ppermute | solution.py:58

commit v20 on v19

--- a/solution.py
+++ b/solution.py
@@ -417,7 +417,7 @@
         ),
         name="finish",
     )(probs, dscore, all_keys, all_values, *[back[slot] for slot in tied])
-    parts = exchange("dp", sums)
+    parts = exchange("dp", sums)[::-1]
     sums = pl.pallas_call(
         total_kernel,
         out_shape=shape(sums.shape, sums.dtype),

time: 36.6 us -> 37.4 us (1.022)
  waiting for transfers between devices: 4.79 us -> 6.19 us
  starting transfers between devices: 17.8 us -> 17.2 us
    ppermute x9, waiting for transfers between devices: 4.64 us -> 6.18 us  [fetch(): lax.ppermute(array, axis, [(source_of(i, slot, size), i) for i in range(s...]
    ppermute x3, starting transfers between devices: 4.21 us -> 3.55 us  [send_back(): lax.ppermute(array, 'ctx', [(i, source_of(i, slot, size)) for i in range(...]
  transfers between devices with their start and end apart: 12 -> 12, of which waited for: 5 -> 5; matrix products, arithmetic and copies ran while one was open for 0% -> 0% of each run, Pallas kernels for 13% -> 12%
where the time goes in v20:
time: 37.4 us; the launch traced here: 37.1 us
  starting transfers between devices  17.2 us (46%)
  Pallas kernels  8.1 us (22%)
  waiting for transfers between devices  6.19 us (17%)
  local copies, waits for them, and re-layouts  4.08 us (11%)
  other arithmetic  0.88 us (2%)
  between operations  0.68 us (2%)
    ppermute x9, starting transfers between devices, fetch(): lax.ppermute(array, axis, [(source_of(i, slot, size), i) for i in range(s...  13.6 us
    ppermute x9, waiting for transfers between devices, fetch(): lax.ppermute(array, axis, [(source_of(i, slot, size), i) for i in range(s...  6.18 us
    unnamed x10, local copies, waits for them, and re-layouts  4.08 us
    ppermute x3, starting transfers between devices, send_back(): lax.ppermute(array, 'ctx', [(i, source_of(i, slot, size)) for i in range(...  3.55 us
    pallas_call x1, Pallas kernels, attend(): pl.pallas_call(functools.partial(last_kernel, ctx, first_head), out_shape...  2.82 us
    pallas_call x1, Pallas kernels, shards(): pl.pallas_call(finish_kernel, out_shape=[shape((tok, width), jnp.bfloat16...  1.8 us
    pallas_call x1, Pallas kernels, attend(): pl.pallas_call(near_kernel, out_shape=[shape((near, columns), jnp.float32...  1.67 us
    pallas_call x1, Pallas kernels, shards(): pl.pallas_call(functools.partial(prepare_kernel, ctx), out_shape=[shape((...  1.11 us
  transfers between devices with their start and end apart: 12, of which 5 were waited for; matrix products, arithmetic and copies ran while one was open for 0% of the time, Pallas kernels for 12%

profile of v20, /device:TPU:0, one launch (start us, length us, event | category | flops | bytes accessed | tf_op | source)
XLA Modules:
  0.0 37.1 jit_solution(2979177669653251124)
XLA Ops:
  0.6 0.9 %pad_maximum_fusion.pair_ref.refs_0_ = bf16[128,512]{1,0:T(8,128)(2,1)S(1)} fusion(bf16[128,256]{1,0:T(8,128)(2,1)} %bitcast.16, bf16[128,256]{1,0:T(8,128)(2,1)} %bitcast.17), kind=kLoop, calls=%fused_computation | loop fusion | flops 262144 | bytes 262144 | tf_op jit(solution)/shard_map/concatenate | solution.py:350
  1.5 5.1 %collective-permute-start.1 = (bf16[128,512]{1,0:T(8,128)(2,1)S(1)}, bf16[128,512]{1,0:T(8,128)(2,1)S(1)}, u32[]{:S(2)}, u32[]{:S(2)}) collective-permute-start(bf16[128,512]{1,0:T(8,128)(2,1)S(1)} %pad_maximum_fusion.pair_ref.refs_0_), channel_id=1, source_target_pairs={{6,0},{4,2},{2,4},{0,6},{7,1},{5,3},{3,5},{1,7},{14,8},{12,10},{10... | collective-permute-start | bytes 393224 | tf_op jit(solution)/shard_map/ppermute | solution.py:58
  6.6 0.0 collective-permute-start
  6.6 0.6 %collective-permute-start.2 = (bf16[128,512]{1,0:T(8,128)(2,1)S(1)}, bf16[128,512]{1,0:T(8,128)(2,1)S(1)}, u32[]{:S(2)}, u32[]{:S(2)}) collective-permute-start(bf16[128,512]{1,0:T(8,128)(2,1)S(1)} %pad_maximum_fusion.pair_ref.refs_0_), channel_id=1, source_target_pairs={{4,0},{6,2},{0,4},{2,6},{5,1},{7,3},{1,5},{3,7},{12,8},{14,10},{8,... | collective-permute-start | bytes 393224 | tf_op jit(solution)/shard_map/ppermute | solution.py:58
  7.3 0.0 copy-start
  7.3 1.0 %copy-done = bf16[1,128,2048]{2,1,0:T(8,128)(2,1)S(1)} copy-done((bf16[1,128,2048]{2,1,0:T(8,128)(2,1)S(1)}, bf16[1,128,2048]{2,1,0:T(8,128)(2,1)}, u32[]{:S(2)}) %copy-start) | copy-done | bytes 524312
  8.3 0.0 copy-start.1
  8.3 1.0 %copy-done.1 = bf16[1,128,2048]{2,1,0:T(8,128)(2,1)S(1)} copy-done((bf16[1,128,2048]{2,1,0:T(8,128)(2,1)S(1)}, bf16[1,128,2048]{2,1,0:T(8,128)(2,1)}, u32[]{:S(2)}) %copy-start.1) | copy-done | bytes 524312
  9.4 0.0 copy-start.2
  9.4 0.7 %copy-done.2 = bf16[2048]{0:T(1024)(128)(2,1)S(1)} copy-done((bf16[2048]{0:T(1024)(128)(2,1)S(1)}, bf16[2048]{0:T(1024)(128)(2,1)}, u32[]{:S(2)}) %copy-start.2) | copy-done | bytes 4120
  10.0 0.0 copy-start.3
  10.0 0.7 %copy-done.3 = s32[1,8]{1,0:T(1,128)S(1)} copy-done((s32[1,8]{1,0:T(1,128)S(1)}, s32[1,8]{1,0:T(1,128)}, u32[]{:S(2)}) %copy-start.3) | copy-done | bytes 56
  10.7 0.0 copy-start.4
  10.7 0.7 %copy-done.4 = bf16[256]{0:T(256)(128)(2,1)S(1)} copy-done((bf16[256]{0:T(256)(128)(2,1)S(1)}, bf16[256]{0:T(256)(128)(2,1)}, u32[]{:S(2)}) %copy-start.4) | copy-done | bytes 536
  11.4 1.1 %prepare.1 = (bf16[2,128]{1,0:T(2,128)(2,1)S(1)}, bf16[2048,256]{1,0:T(8,128)(2,1)S(1)}, bf16[2048,128]{1,0:T(8,128)(2,1)S(1)}, f32[128,2048]{1,0:T(8,128)S(1)},...) custom-call(s32[1,8]{1,0:T(1,128)S(1)} %copy-done.3, bf16[128,512]{1,0:T(8,128)(2,1)S(1)} %pad_maximum_fusion.pair_ref.refs_0_, ...), custom_call_target="tpu_custom_call" | custom-call | flops 134217728 | bytes 4194304 | tf_op jit(solution)/shard_map/prepare/pallas_call | solution.py:352
  12.5 0.0 collective-permute-done.1.refs_2_
  12.5 1.5 %collective-permute-done.refs_1_ = bf16[128,512]{1,0:T(8,128)(2,1)S(1)} collective-permute-done((bf16[128,512]{1,0:T(8,128)(2,1)S(1)}, bf16[128,512]{1,0:T(8,128)(2,1)S(1)}, u32[]{:S(2)}, u32[]{:S(2)}) %collective-permute-start) | collective-permute-done | bytes 131104 | tf_op jit(solution)/shard_map/ppermute | solution.py:58
  14.0 1.7 %near.1 = (f32[384,2048]{1,0:T(8,128)S(1)}, f32[384,2048]{1,0:T(8,128)S(1)}, f32[8,2048]{1,0:T(8,128)S(1)}, bf16[384,256]{1,0:T(8,128)(2,1)S(1)}, bf16[384,256]{1,0:T(8,128)(2,1)S(1)}) custom-call(bf16[2,128]{1,0:T(2,128)(2,1)S(1)} %get-tuple-element.33.bias_ref.refs_0_, bf16[2048,256]{1,0:T(8,128)(2,1)S(1)} %get-tuple-element.34.queries_ref.refs_1_, ...), custom_call_target="tpu_custom_call" | custom-call | flops 402653184 | bytes 6291456 | tf_op jit(solution)/shard_map/near/pallas_call | solution.py:289
  15.7 2.0 %collective-permute-done.2.refs_9_ = bf16[128,512]{1,0:T(8,128)(2,1)S(1)} collective-permute-done((bf16[128,512]{1,0:T(8,128)(2,1)S(1)}, bf16[128,512]{1,0:T(8,128)(2,1)S(1)}, u32[]{:S(2)}, u32[]{:S(2)}) %collective-permute-start.2) | collective-permute-done | bytes 131104 | tf_op jit(solution)/shard_map/ppermute | solution.py:58
  17.7 2.8 %last.1 = (bf16[512,2048]{1,0:T(8,128)(2,1)S(1)}, bf16[512,2048]{1,0:T(8,128)(2,1)S(1)}, bf16[512,256]{1,0:T(8,128)(2,1)S(1)}, bf16[512,256]{1,0:T(8,128)(2,1)S(...) custom-call(bf16[2,128]{1,0:T(2,128)(2,1)S(1)} %get-tuple-element.33, ...), custom_call_target="tpu_custom_call" | custom-call | flops 536870912 | bytes 4194304 | tf_op jit(solution)/shard_map/last/pallas_call | solution.py:309
  20.5 0.9 %collective-permute-start.3 = (bf16[128,512]{1,0:T(8,128)(2,1)S(1)}, bf16[128,512]{1,0:T(8,128)(2,1)S(1)}, u32[]{:S(2)}, u32[]{:S(2)}) collective-permute-start(bf16[128,512]{1,0:T(8,128)(2,1)S(1)} %get-tuple-element.48), channel_id=1, source_target_pairs={{0,4},{2,6},{4,0},{6,2},{1,5},{3,7},{5,1},{7,3},{8,12},{10,14},{12... | collective-permute-start | bytes 393224 | tf_op jit(solution)/shard_map/ppermute | solution.py:63
  21.4 1.5 %collective-permute-start.6 = (f32[18,128]{1,0:T(8,128)S(1)}, f32[18,128]{1,0:T(8,128)S(1)}, u32[]{:S(2)}, u32[]{:S(2)}) collective-permute-start(f32[18,128]{1,0:T(8,128)S(1)} %get-tuple-element.51.refs_3_), channel_id=1, source_target_pairs={{8,0},{0,8},{24,16},{16,24},{9,1},{1,9},{25,17},{17,25},{10,2},{2,... | collective-permute-start | bytes 27656 | tf_op jit(solution)/shard_map/ppermute | solution.py:58
  22.9 1.5 %collective-permute-start.5 = (f32[18,128]{1,0:T(8,128)S(1)}, f32[18,128]{1,0:T(8,128)S(1)}, u32[]{:S(2)}, u32[]{:S(2)}) collective-permute-start(f32[18,128]{1,0:T(8,128)S(1)} %get-tuple-element.51.refs_3_), channel_id=1, source_target_pairs={{16,0},{24,8},{0,16},{8,24},{17,1},{25,9},{1,17},{9,25},{18,2},{26... | collective-permute-start | bytes 27656 | tf_op jit(solution)/shard_map/ppermute | solution.py:58
  24.4 0.5 %collective-permute-start.4 = (f32[18,128]{1,0:T(8,128)S(1)}, f32[18,128]{1,0:T(8,128)S(1)}, u32[]{:S(2)}, u32[]{:S(2)}) collective-permute-start(f32[18,128]{1,0:T(8,128)S(1)} %get-tuple-element.51.refs_3_), channel_id=1, source_target_pairs={{24,0},{16,8},{8,16},{0,24},{25,1},{17,9},{9,17},{1,25},{26,2},{18... | collective-permute-start | bytes 27656 | tf_op jit(solution)/shard_map/ppermute | solution.py:58
  24.9 1.7 %collective-permute-start.10 = (bf16[128,512]{1,0:T(8,128)(2,1)S(1)}, bf16[128,512]{1,0:T(8,128)(2,1)S(1)}, u32[]{:S(2)}, u32[]{:S(2)}) collective-permute-start(bf16[128,512]{1,0:T(8,128)(2,1)S(1)} %get-tuple-element.53), channel_id=1, source_target_pairs={{0,6},{2,4},{4,2},{6,0},{1,7},{3,5},{5,3},{7,1},{8,14},{10,12},{12... | collective-permute-start | bytes 393224 | tf_op jit(solution)/shard_map/ppermute | solution.py:63
  26.6 0.0 collective-permute-done.6.refs_2_
  26.6 0.9 %collective-permute-start.11 = (bf16[128,512]{1,0:T(8,128)(2,1)S(1)}, bf16[128,512]{1,0:T(8,128)(2,1)S(1)}, u32[]{:S(2)}, u32[]{:S(2)}) collective-permute-start(bf16[128,512]{1,0:T(8,128)(2,1)S(1)} %get-tuple-element.55), channel_id=1, source_target_pairs={{0,2},{2,0},{4,6},{6,4},{1,3},{3,1},{5,7},{7,5},{8,10},{10,8},{12,... | collective-permute-start | bytes 393224 | tf_op jit(solution)/shard_map/ppermute | solution.py:63
  27.6 0.0 collective-permute-done.5.refs_1_
  27.6 1.5 %collective-permute-done.4.refs_0_ = f32[18,128]{1,0:T(8,128)S(1)} collective-permute-done((f32[18,128]{1,0:T(8,128)S(1)}, f32[18,128]{1,0:T(8,128)S(1)}, u32[]{:S(2)}, u32[]{:S(2)}) %collective-permute-start.4) | collective-permute-done | bytes 9248 | tf_op jit(solution)/shard_map/ppermute | solution.py:58
  29.0 1.7 %collective-permute-start.9 = (f32[18,128]{1,0:T(8,128)S(1)}, f32[18,128]{1,0:T(8,128)S(1)}, u32[]{:S(2)}, u32[]{:S(2)}) collective-permute-start(f32[18,128]{1,0:T(8,128)S(1)} %total.1.refs_0_), channel_id=1, source_target_pairs={{6,0},{4,2},{2,4},{0,6},{7,1},{5,3},{3,5},{1,7},{14,8},{12,10},{10... | collective-permute-start | bytes 27656 | tf_op jit(solution)/shard_map/ppermute | solution.py:58
  30.8 1.9 %collective-permute-start.8 = (f32[18,128]{1,0:T(8,128)S(1)}, f32[18,128]{1,0:T(8,128)S(1)}, u32[]{:S(2)}, u32[]{:S(2)}) collective-permute-start(f32[18,128]{1,0:T(8,128)S(1)} %total.1.refs_0_), channel_id=1, source_target_pairs={{4,0},{6,2},{0,4},{2,6},{5,1},{7,3},{1,5},{3,7},{12,8},{14,10},{8,... | collective-permute-start | bytes 27656 | tf_op jit(solution)/shard_map/ppermute | solution.py:58
  32.7 0.0 collective-permute-done.3.refs_0_
  32.7 0.7 %collective-permute-start.7 = (f32[18,128]{1,0:T(8,128)S(1)}, f32[18,128]{1,0:T(8,128)S(1)}, u32[]{:S(2)}, u32[]{:S(2)}) collective-permute-start(f32[18,128]{1,0:T(8,128)S(1)} %total.1.refs_0_), channel_id=1, source_target_pairs={{2,0},{0,2},{6,4},{4,6},{3,1},{1,3},{7,5},{5,7},{10,8},{8,10},{14,... | collective-permute-start | bytes 27656 | tf_op jit(solution)/shard_map/ppermute | solution.py:58
  33.4 1.8 %finish.1 = (bf16[128,2048]{1,0:T(8,128)(2,1)}, bf16[128,2048]{1,0:T(8,128)(2,1)}, bf16[128,512]{1,0:T(8,128)(2,1)S(1)}) custom-call(bf16[512,2048]{1,0:T(8,128)(2,1)S(1)} %get-tuple-element.44.probs_ref, bf16[512,2048]{1,0:T(8,128)(2,1)S(1)} %get-tuple-element.45.dscore_ref, ...), custom_call_target="tpu_custom_call", output_to_operand_aliasing={{2}: (4, {})} | custom-call | flops 2147483648 | tf_op jit(solution)/shard_map/finish/pallas_call | solution.py:404
  35.2 0.0 collective-permute-done.9.refs_3_
  35.2 0.1 collective-permute-done.8.refs_2_
  35.4 1.1 %collective-permute-done.7.refs_1_ = f32[18,128]{1,0:T(8,128)S(1)} collective-permute-done((f32[18,128]{1,0:T(8,128)S(1)}, f32[18,128]{1,0:T(8,128)S(1)}, u32[]{:S(2)}, u32[]{:S(2)}) %collective-permute-start.7) | collective-permute-done | bytes 9248 | tf_op jit(solution)/shard_map/ppermute | solution.py:58
  36.4 0.0 collective-permute-done.10.refs_5_
  36.4 0.0 collective-permute-done.11.refs_7_
  36.4 0.7 %collect.1 = (bf16[128,256]{1,0:T(8,128)(2,1)}, bf16[128,256]{1,0:T(8,128)(2,1)}, f32[16,128]{1,0:T(8,128)}, f32[2,128]{1,0:T(2,128)}) custom-call(f32[18,128]{1,0:T(8,128)S(1)} %total.1.refs_0_, f32[18,128]{1,0:T(8,128)S(1)} %collective-permute-done.7.refs_1_, f32[18,128]{1,0:T(8,128)S(1)} %collective-permute-done.8.refs_2_, ...), custom_call_target="tpu_custom_call" | custom-call | flops 262144 | bytes 524288 | tf_op jit(solution)/shard_map/collect/pallas_call | solution.py:432
  (1 shorter events, 0.0 us)
Async XLA Ops:
  1.5 11.0 %collective-permute-start.1 = (bf16[128,512]{1,0:T(8,128)(2,1)S(1)}, bf16[128,512]{1,0:T(8,128)(2,1)S(1)}, u32[]{:S(2)}, u32[]{:S(2)}) collective-permute-start(bf16[128,512]{1,0:T(8,128)(2,1)S(1)} %pad_maximum_fusion.pair_ref.refs_0_), channel_id=1, source_target_pairs={{6,0},{4,2},{2,4},{0,6},{7,1},{5,3},{3,5},{1,7},{14,8},{12,10},{10... | collective-permute-start | bytes 393224 | tf_op jit(solution)/shard_map/ppermute | solution.py:58
  6.6 7.4 %collective-permute-start = (bf16[128,512]{1,0:T(8,128)(2,1)S(1)}, bf16[128,512]{1,0:T(8,128)(2,1)S(1)}, u32[]{:S(2)}, u32[]{:S(2)}) collective-permute-start(bf16[128,512]{1,0:T(8,128)(2,1)S(1)} %pad_maximum_fusion.pair_ref.refs_0_), channel_id=1, source_target_pairs={{2,0},{0,2},{6,4},{4,6},{3,1},{1,3},{7,5},{5,7},{10,8},{8,10},{14,... | collective-permute-start | bytes 393224 | tf_op jit(solution)/shard_map/ppermute | solution.py:58
  6.6 11.1 %collective-permute-start.2 = (bf16[128,512]{1,0:T(8,128)(2,1)S(1)}, bf16[128,512]{1,0:T(8,128)(2,1)S(1)}, u32[]{:S(2)}, u32[]{:S(2)}) collective-permute-start(bf16[128,512]{1,0:T(8,128)(2,1)S(1)} %pad_maximum_fusion.pair_ref.refs_0_), channel_id=1, source_target_pairs={{4,0},{6,2},{0,4},{2,6},{5,1},{7,3},{1,5},{3,7},{12,8},{14,10},{8,... | collective-permute-start | bytes 393224 | tf_op jit(solution)/shard_map/ppermute | solution.py:58
  7.3 1.0 %copy-start = (bf16[1,128,2048]{2,1,0:T(8,128)(2,1)S(1)}, bf16[1,128,2048]{2,1,0:T(8,128)(2,1)}, u32[]{:S(2)}) copy-start(bf16[1,128,2048]{2,1,0:T(8,128)(2,1)} %param.7) | copy-start | bytes 1572868
  8.3 1.0 %copy-start.1 = (bf16[1,128,2048]{2,1,0:T(8,128)(2,1)S(1)}, bf16[1,128,2048]{2,1,0:T(8,128)(2,1)}, u32[]{:S(2)}) copy-start(bf16[1,128,2048]{2,1,0:T(8,128)(2,1)} %param.12) | copy-start | bytes 1572868
  9.4 0.7 %copy-start.2 = (bf16[2048]{0:T(1024)(128)(2,1)S(1)}, bf16[2048]{0:T(1024)(128)(2,1)}, u32[]{:S(2)}) copy-start(bf16[2048]{0:T(1024)(128)(2,1)} %param.8) | copy-start | bytes 12292
  10.0 0.7 %copy-start.3 = (s32[1,8]{1,0:T(1,128)S(1)}, s32[1,8]{1,0:T(1,128)}, u32[]{:S(2)}) copy-start(s32[1,8]{1,0:T(1,128)} %len_ref.1) | copy-start | bytes 100
  10.7 0.7 %copy-start.4 = (bf16[256]{0:T(256)(128)(2,1)S(1)}, bf16[256]{0:T(256)(128)(2,1)}, u32[]{:S(2)}) copy-start(bf16[256]{0:T(256)(128)(2,1)} %param.11) | copy-start | bytes 1540
  20.5 12.2 %collective-permute-start.3 = (bf16[128,512]{1,0:T(8,128)(2,1)S(1)}, bf16[128,512]{1,0:T(8,128)(2,1)S(1)}, u32[]{:S(2)}, u32[]{:S(2)}) collective-permute-start(bf16[128,512]{1,0:T(8,128)(2,1)S(1)} %get-tuple-element.48), channel_id=1, source_target_pairs={{0,4},{2,6},{4,0},{6,2},{1,5},{3,7},{5,1},{7,3},{8,12},{10,14},{12... | collective-permute-start | bytes 393224 | tf_op jit(solution)/shard_map/ppermute | solution.py:63
  21.4 5.2 %collective-permute-start.6 = (f32[18,128]{1,0:T(8,128)S(1)}, f32[18,128]{1,0:T(8,128)S(1)}, u32[]{:S(2)}, u32[]{:S(2)}) collective-permute-start(f32[18,128]{1,0:T(8,128)S(1)} %get-tuple-element.51.refs_3_), channel_id=1, source_target_pairs={{8,0},{0,8},{24,16},{16,24},{9,1},{1,9},{25,17},{17,25},{10,2},{2,... | collective-permute-start | bytes 27656 | tf_op jit(solution)/shard_map/ppermute | solution.py:58
  22.9 4.7 %collective-permute-start.5 = (f32[18,128]{1,0:T(8,128)S(1)}, f32[18,128]{1,0:T(8,128)S(1)}, u32[]{:S(2)}, u32[]{:S(2)}) collective-permute-start(f32[18,128]{1,0:T(8,128)S(1)} %get-tuple-element.51.refs_3_), channel_id=1, source_target_pairs={{16,0},{24,8},{0,16},{8,24},{17,1},{25,9},{1,17},{9,25},{18,2},{26... | collective-permute-start | bytes 27656 | tf_op jit(solution)/shard_map/ppermute | solution.py:58
  24.4 4.6 %collective-permute-start.4 = (f32[18,128]{1,0:T(8,128)S(1)}, f32[18,128]{1,0:T(8,128)S(1)}, u32[]{:S(2)}, u32[]{:S(2)}) collective-permute-start(f32[18,128]{1,0:T(8,128)S(1)} %get-tuple-element.51.refs_3_), channel_id=1, source_target_pairs={{24,0},{16,8},{8,16},{0,24},{25,1},{17,9},{9,17},{1,25},{26,2},{18... | collective-permute-start | bytes 27656 | tf_op jit(solution)/shard_map/ppermute | solution.py:58
  24.9 11.5 %collective-permute-start.10 = (bf16[128,512]{1,0:T(8,128)(2,1)S(1)}, bf16[128,512]{1,0:T(8,128)(2,1)S(1)}, u32[]{:S(2)}, u32[]{:S(2)}) collective-permute-start(bf16[128,512]{1,0:T(8,128)(2,1)S(1)} %get-tuple-element.53), channel_id=1, source_target_pairs={{0,6},{2,4},{4,2},{6,0},{1,7},{3,5},{5,3},{7,1},{8,14},{10,12},{12... | collective-permute-start | bytes 393224 | tf_op jit(solution)/shard_map/ppermute | solution.py:63
  26.6 9.8 %collective-permute-start.11 = (bf16[128,512]{1,0:T(8,128)(2,1)S(1)}, bf16[128,512]{1,0:T(8,128)(2,1)S(1)}, u32[]{:S(2)}, u32[]{:S(2)}) collective-permute-start(bf16[128,512]{1,0:T(8,128)(2,1)S(1)} %get-tuple-element.55), channel_id=1, source_target_pairs={{0,2},{2,0},{4,6},{6,4},{1,3},{3,1},{5,7},{7,5},{8,10},{10,8},{12,... | collective-permute-start | bytes 393224 | tf_op jit(solution)/shard_map/ppermute | solution.py:63
  29.0 6.2 %collective-permute-start.9 = (f32[18,128]{1,0:T(8,128)S(1)}, f32[18,128]{1,0:T(8,128)S(1)}, u32[]{:S(2)}, u32[]{:S(2)}) collective-permute-start(f32[18,128]{1,0:T(8,128)S(1)} %total.1.refs_0_), channel_id=1, source_target_pairs={{6,0},{4,2},{2,4},{0,6},{7,1},{5,3},{3,5},{1,7},{14,8},{12,10},{10... | collective-permute-start | bytes 27656 | tf_op jit(solution)/shard_map/ppermute | solution.py:58
  30.8 4.6 %collective-permute-start.8 = (f32[18,128]{1,0:T(8,128)S(1)}, f32[18,128]{1,0:T(8,128)S(1)}, u32[]{:S(2)}, u32[]{:S(2)}) collective-permute-start(f32[18,128]{1,0:T(8,128)S(1)} %total.1.refs_0_), channel_id=1, source_target_pairs={{4,0},{6,2},{0,4},{2,6},{5,1},{7,3},{1,5},{3,7},{12,8},{14,10},{8,... | collective-permute-start | bytes 27656 | tf_op jit(solution)/shard_map/ppermute | solution.py:58
  32.7 3.7 %collective-permute-start.7 = (f32[18,128]{1,0:T(8,128)S(1)}, f32[18,128]{1,0:T(8,128)S(1)}, u32[]{:S(2)}, u32[]{:S(2)}) collective-permute-start(f32[18,128]{1,0:T(8,128)S(1)} %total.1.refs_0_), channel_id=1, source_target_pairs={{2,0},{0,2},{6,4},{4,6},{3,1},{1,3},{7,5},{5,7},{10,8},{8,10},{14,... | collective-permute-start | bytes 27656 | tf_op jit(solution)/shard_map/ppermute | solution.py:58

commit v21 on v19

--- a/solution.py
+++ b/solution.py
@@ -11,7 +11,7 @@
 HEADS = 32
 KV_HEADS = 4
 GROUP = HEADS // KV_HEADS
-PAIR = 2
+PAIR = 4
 BLOCK = 32
 SCALE = HEAD_DIM ** (-0.5)
 LOG2E = 1.4426950408889634

time: 36.6 us -> 36.6 us (level)
  no operation moved by 1% of the time
where the time goes in v21:
time: 36.6 us; the launch traced here: 36.3 us
  starting transfers between devices  17.8 us (49%)
  Pallas kernels  8.06 us (22%)
  waiting for transfers between devices  4.82 us (13%)
  local copies, waits for them, and re-layouts  4.08 us (11%)
  other arithmetic  0.88 us (2%)
  between operations  0.68 us (2%)
    ppermute x9, starting transfers between devices, fetch(): lax.ppermute(array, axis, [(source_of(i, slot, size), i) for i in range(s...  13.6 us
    ppermute x9, waiting for transfers between devices, fetch(): lax.ppermute(array, axis, [(source_of(i, slot, size), i) for i in range(s...  4.67 us
    ppermute x3, starting transfers between devices, send_back(): lax.ppermute(array, 'ctx', [(i, source_of(i, slot, size)) for i in range(...  4.21 us
    unnamed x10, local copies, waits for them, and re-layouts  4.08 us
    pallas_call x1, Pallas kernels, attend(): pl.pallas_call(functools.partial(last_kernel, ctx, first_head), out_shape...  2.81 us
    pallas_call x1, Pallas kernels, shards(): pl.pallas_call(finish_kernel, out_shape=[shape((tok, width), jnp.bfloat16...  1.74 us
    pallas_call x1, Pallas kernels, attend(): pl.pallas_call(near_kernel, out_shape=[shape((near, columns), jnp.float32...  1.7 us
    pallas_call x1, Pallas kernels, shards(): pl.pallas_call(functools.partial(prepare_kernel, ctx), out_shape=[shape((...  1.11 us
  transfers between devices with their start and end apart: 12, of which 5 were waited for; matrix products, arithmetic and copies ran while one was open for 0% of the time, Pallas kernels for 13%

profile of v21, /device:TPU:0, one launch (start us, length us, event | category | flops | bytes accessed | tf_op | source)
XLA Modules:
  0.0 36.3 jit_solution(13643730387746583876)
XLA Ops:
  0.6 0.9 %pad_maximum_fusion.pair_ref.refs_0_ = bf16[128,512]{1,0:T(8,128)(2,1)S(1)} fusion(bf16[128,256]{1,0:T(8,128)(2,1)} %bitcast.16, bf16[128,256]{1,0:T(8,128)(2,1)} %bitcast.17), kind=kLoop, calls=%fused_computation | loop fusion | flops 262144 | bytes 262144 | tf_op jit(solution)/shard_map/concatenate | solution.py:350
  1.5 5.1 %collective-permute-start.1 = (bf16[128,512]{1,0:T(8,128)(2,1)S(1)}, bf16[128,512]{1,0:T(8,128)(2,1)S(1)}, u32[]{:S(2)}, u32[]{:S(2)}) collective-permute-start(bf16[128,512]{1,0:T(8,128)(2,1)S(1)} %pad_maximum_fusion.pair_ref.refs_0_), channel_id=1, source_target_pairs={{6,0},{4,2},{2,4},{0,6},{7,1},{5,3},{3,5},{1,7},{14,8},{12,10},{10... | collective-permute-start | bytes 393224 | tf_op jit(solution)/shard_map/ppermute | solution.py:58
  6.6 0.0 collective-permute-start
  6.6 0.6 %collective-permute-start.2 = (bf16[128,512]{1,0:T(8,128)(2,1)S(1)}, bf16[128,512]{1,0:T(8,128)(2,1)S(1)}, u32[]{:S(2)}, u32[]{:S(2)}) collective-permute-start(bf16[128,512]{1,0:T(8,128)(2,1)S(1)} %pad_maximum_fusion.pair_ref.refs_0_), channel_id=1, source_target_pairs={{4,0},{6,2},{0,4},{2,6},{5,1},{7,3},{1,5},{3,7},{12,8},{14,10},{8,... | collective-permute-start | bytes 393224 | tf_op jit(solution)/shard_map/ppermute | solution.py:58
  7.3 0.0 copy-start
  7.3 1.0 %copy-done = bf16[1,128,2048]{2,1,0:T(8,128)(2,1)S(1)} copy-done((bf16[1,128,2048]{2,1,0:T(8,128)(2,1)S(1)}, bf16[1,128,2048]{2,1,0:T(8,128)(2,1)}, u32[]{:S(2)}) %copy-start) | copy-done | bytes 524312
  8.3 0.0 copy-start.1
  8.3 1.0 %copy-done.1 = bf16[1,128,2048]{2,1,0:T(8,128)(2,1)S(1)} copy-done((bf16[1,128,2048]{2,1,0:T(8,128)(2,1)S(1)}, bf16[1,128,2048]{2,1,0:T(8,128)(2,1)}, u32[]{:S(2)}) %copy-start.1) | copy-done | bytes 524312
  9.4 0.0 copy-start.2
  9.4 0.7 %copy-done.2 = bf16[2048]{0:T(1024)(128)(2,1)S(1)} copy-done((bf16[2048]{0:T(1024)(128)(2,1)S(1)}, bf16[2048]{0:T(1024)(128)(2,1)}, u32[]{:S(2)}) %copy-start.2) | copy-done | bytes 4120
  10.0 0.0 copy-start.3
  10.0 0.7 %copy-done.3 = s32[1,8]{1,0:T(1,128)S(1)} copy-done((s32[1,8]{1,0:T(1,128)S(1)}, s32[1,8]{1,0:T(1,128)}, u32[]{:S(2)}) %copy-start.3) | copy-done | bytes 56
  10.7 0.0 copy-start.4
  10.7 0.7 %copy-done.4 = bf16[256]{0:T(256)(128)(2,1)S(1)} copy-done((bf16[256]{0:T(256)(128)(2,1)S(1)}, bf16[256]{0:T(256)(128)(2,1)}, u32[]{:S(2)}) %copy-start.4) | copy-done | bytes 536
  11.4 1.1 %prepare.1 = (bf16[2,128]{1,0:T(2,128)(2,1)S(1)}, bf16[2048,256]{1,0:T(8,128)(2,1)S(1)}, bf16[2048,128]{1,0:T(8,128)(2,1)S(1)}, f32[128,2048]{1,0:T(8,128)S(1)},...) custom-call(s32[1,8]{1,0:T(1,128)S(1)} %copy-done.3, bf16[128,512]{1,0:T(8,128)(2,1)S(1)} %pad_maximum_fusion.pair_ref.refs_0_, ...), custom_call_target="tpu_custom_call" | custom-call | flops 134217728 | bytes 4194304 | tf_op jit(solution)/shard_map/prepare/pallas_call | solution.py:352
  12.5 0.0 collective-permute-done.1.refs_2_
  12.5 1.5 %collective-permute-done.refs_1_ = bf16[128,512]{1,0:T(8,128)(2,1)S(1)} collective-permute-done((bf16[128,512]{1,0:T(8,128)(2,1)S(1)}, bf16[128,512]{1,0:T(8,128)(2,1)S(1)}, u32[]{:S(2)}, u32[]{:S(2)}) %collective-permute-start) | collective-permute-done | bytes 131104 | tf_op jit(solution)/shard_map/ppermute | solution.py:58
  14.0 1.7 %near.1 = (f32[384,2048]{1,0:T(8,128)S(1)}, f32[384,2048]{1,0:T(8,128)S(1)}, f32[8,2048]{1,0:T(8,128)S(1)}, bf16[384,256]{1,0:T(8,128)(2,1)S(1)}, bf16[384,256]{1,0:T(8,128)(2,1)S(1)}) custom-call(bf16[2,128]{1,0:T(2,128)(2,1)S(1)} %get-tuple-element.33.bias_ref.refs_0_, bf16[2048,256]{1,0:T(8,128)(2,1)S(1)} %get-tuple-element.34.queries_ref.refs_1_, ...), custom_call_target="tpu_custom_call" | custom-call | flops 402653184 | bytes 6291456 | tf_op jit(solution)/shard_map/near/pallas_call | solution.py:289
  15.7 2.0 %collective-permute-done.2.refs_9_ = bf16[128,512]{1,0:T(8,128)(2,1)S(1)} collective-permute-done((bf16[128,512]{1,0:T(8,128)(2,1)S(1)}, bf16[128,512]{1,0:T(8,128)(2,1)S(1)}, u32[]{:S(2)}, u32[]{:S(2)}) %collective-permute-start.2) | collective-permute-done | bytes 131104 | tf_op jit(solution)/shard_map/ppermute | solution.py:58
  17.7 2.8 %last.1 = (bf16[512,2048]{1,0:T(8,128)(2,1)S(1)}, bf16[512,2048]{1,0:T(8,128)(2,1)S(1)}, bf16[512,256]{1,0:T(8,128)(2,1)S(1)}, bf16[512,256]{1,0:T(8,128)(2,1)S(...) custom-call(bf16[2,128]{1,0:T(2,128)(2,1)S(1)} %get-tuple-element.33, ...), custom_call_target="tpu_custom_call" | custom-call | flops 536870912 | bytes 4194304 | tf_op jit(solution)/shard_map/last/pallas_call | solution.py:309
  20.5 0.9 %collective-permute-start.3 = (bf16[128,512]{1,0:T(8,128)(2,1)S(1)}, bf16[128,512]{1,0:T(8,128)(2,1)S(1)}, u32[]{:S(2)}, u32[]{:S(2)}) collective-permute-start(bf16[128,512]{1,0:T(8,128)(2,1)S(1)} %get-tuple-element.48), channel_id=1, source_target_pairs={{0,4},{2,6},{4,0},{6,2},{1,5},{3,7},{5,1},{7,3},{8,12},{10,14},{12... | collective-permute-start | bytes 393224 | tf_op jit(solution)/shard_map/ppermute | solution.py:63
  21.4 2.5 %collective-permute-start.6 = (f32[18,128]{1,0:T(8,128)S(1)}, f32[18,128]{1,0:T(8,128)S(1)}, u32[]{:S(2)}, u32[]{:S(2)}) collective-permute-start(f32[18,128]{1,0:T(8,128)S(1)} %get-tuple-element.51.refs_0_), channel_id=1, source_target_pairs={{24,0},{16,8},{8,16},{0,24},{25,1},{17,9},{9,17},{1,25},{26,2},{18... | collective-permute-start | bytes 27656 | tf_op jit(solution)/shard_map/ppermute | solution.py:58
  23.9 0.5 %collective-permute-start.5 = (f32[18,128]{1,0:T(8,128)S(1)}, f32[18,128]{1,0:T(8,128)S(1)}, u32[]{:S(2)}, u32[]{:S(2)}) collective-permute-start(f32[18,128]{1,0:T(8,128)S(1)} %get-tuple-element.51.refs_0_), channel_id=1, source_target_pairs={{16,0},{24,8},{0,16},{8,24},{17,1},{25,9},{1,17},{9,25},{18,2},{26... | collective-permute-start | bytes 27656 | tf_op jit(solution)/shard_map/ppermute | solution.py:58
  24.4 0.5 %collective-permute-start.4 = (f32[18,128]{1,0:T(8,128)S(1)}, f32[18,128]{1,0:T(8,128)S(1)}, u32[]{:S(2)}, u32[]{:S(2)}) collective-permute-start(f32[18,128]{1,0:T(8,128)S(1)} %get-tuple-element.51.refs_0_), channel_id=1, source_target_pairs={{8,0},{0,8},{24,16},{16,24},{9,1},{1,9},{25,17},{17,25},{10,2},{2,... | collective-permute-start | bytes 27656 | tf_op jit(solution)/shard_map/ppermute | solution.py:58
  24.9 1.7 %collective-permute-start.10 = (bf16[128,512]{1,0:T(8,128)(2,1)S(1)}, bf16[128,512]{1,0:T(8,128)(2,1)S(1)}, u32[]{:S(2)}, u32[]{:S(2)}) collective-permute-start(bf16[128,512]{1,0:T(8,128)(2,1)S(1)} %get-tuple-element.53), channel_id=1, source_target_pairs={{0,6},{2,4},{4,2},{6,0},{1,7},{3,5},{5,3},{7,1},{8,14},{10,12},{12... | collective-permute-start | bytes 393224 | tf_op jit(solution)/shard_map/ppermute | solution.py:63
  26.6 0.0 collective-permute-done.6.refs_3_
  26.6 1.6 %collective-permute-start.11 = (bf16[128,512]{1,0:T(8,128)(2,1)S(1)}, bf16[128,512]{1,0:T(8,128)(2,1)S(1)}, u32[]{:S(2)}, u32[]{:S(2)}) collective-permute-start(bf16[128,512]{1,0:T(8,128)(2,1)S(1)} %get-tuple-element.55), channel_id=1, source_target_pairs={{0,2},{2,0},{4,6},{6,4},{1,3},{3,1},{5,7},{7,5},{8,10},{10,8},{12,... | collective-permute-start | bytes 393224 | tf_op jit(solution)/shard_map/ppermute | solution.py:63
  28.2 0.0 collective-permute-done.5.refs_2_
  28.2 0.0 collective-permute-done.4.refs_1_
  28.2 1.9 %collective-permute-start.9 = (f32[18,128]{1,0:T(8,128)S(1)}, f32[18,128]{1,0:T(8,128)S(1)}, u32[]{:S(2)}, u32[]{:S(2)}) collective-permute-start(f32[18,128]{1,0:T(8,128)S(1)} %total.1.refs_0_), channel_id=1, source_target_pairs={{6,0},{4,2},{2,4},{0,6},{7,1},{5,3},{3,5},{1,7},{14,8},{12,10},{10... | collective-permute-start | bytes 27656 | tf_op jit(solution)/shard_map/ppermute | solution.py:58
  30.1 1.6 %collective-permute-start.8 = (f32[18,128]{1,0:T(8,128)S(1)}, f32[18,128]{1,0:T(8,128)S(1)}, u32[]{:S(2)}, u32[]{:S(2)}) collective-permute-start(f32[18,128]{1,0:T(8,128)S(1)} %total.1.refs_0_), channel_id=1, source_target_pairs={{4,0},{6,2},{0,4},{2,6},{5,1},{7,3},{1,5},{3,7},{12,8},{14,10},{8,... | collective-permute-start | bytes 27656 | tf_op jit(solution)/shard_map/ppermute | solution.py:58
  31.7 0.1 collective-permute-done.3.refs_0_
  31.9 0.8 %collective-permute-start.7 = (f32[18,128]{1,0:T(8,128)S(1)}, f32[18,128]{1,0:T(8,128)S(1)}, u32[]{:S(2)}, u32[]{:S(2)}) collective-permute-start(f32[18,128]{1,0:T(8,128)S(1)} %total.1.refs_0_), channel_id=1, source_target_pairs={{2,0},{0,2},{6,4},{4,6},{3,1},{1,3},{7,5},{5,7},{10,8},{8,10},{14,... | collective-permute-start | bytes 27656 | tf_op jit(solution)/shard_map/ppermute | solution.py:58
  32.7 1.7 %finish.1 = (bf16[128,2048]{1,0:T(8,128)(2,1)}, bf16[128,2048]{1,0:T(8,128)(2,1)}, bf16[128,512]{1,0:T(8,128)(2,1)S(1)}) custom-call(bf16[512,2048]{1,0:T(8,128)(2,1)S(1)} %get-tuple-element.44.probs_ref, bf16[512,2048]{1,0:T(8,128)(2,1)S(1)} %get-tuple-element.45.dscore_ref, ...), custom_call_target="tpu_custom_call", output_to_operand_aliasing={{2}: (4, {})} | custom-call | flops 2147483648 | tf_op jit(solution)/shard_map/finish/pallas_call | solution.py:404
  34.4 0.0 collective-permute-done.9.refs_3_
  34.4 0.3 collective-permute-done.8.refs_2_
  34.7 0.9 %collective-permute-done.7.refs_1_ = f32[18,128]{1,0:T(8,128)S(1)} collective-permute-done((f32[18,128]{1,0:T(8,128)S(1)}, f32[18,128]{1,0:T(8,128)S(1)}, u32[]{:S(2)}, u32[]{:S(2)}) %collective-permute-start.7) | collective-permute-done | bytes 9248 | tf_op jit(solution)/shard_map/ppermute | solution.py:58
  35.6 0.0 collective-permute-done.10.refs_5_
  35.6 0.0 collective-permute-done.11.refs_7_
  35.6 0.7 %collect.1 = (bf16[128,256]{1,0:T(8,128)(2,1)}, bf16[128,256]{1,0:T(8,128)(2,1)}, f32[16,128]{1,0:T(8,128)}, f32[2,128]{1,0:T(2,128)}) custom-call(f32[18,128]{1,0:T(8,128)S(1)} %total.1.refs_0_, f32[18,128]{1,0:T(8,128)S(1)} %collective-permute-done.7.refs_1_, f32[18,128]{1,0:T(8,128)S(1)} %collective-permute-done.8.refs_2_, ...), custom_call_target="tpu_custom_call" | custom-call | flops 262144 | bytes 524288 | tf_op jit(solution)/shard_map/collect/pallas_call | solution.py:432
  (1 shorter events, 0.0 us)
Async XLA Ops:
  1.5 11.0 %collective-permute-start.1 = (bf16[128,512]{1,0:T(8,128)(2,1)S(1)}, bf16[128,512]{1,0:T(8,128)(2,1)S(1)}, u32[]{:S(2)}, u32[]{:S(2)}) collective-permute-start(bf16[128,512]{1,0:T(8,128)(2,1)S(1)} %pad_maximum_fusion.pair_ref.refs_0_), channel_id=1, source_target_pairs={{6,0},{4,2},{2,4},{0,6},{7,1},{5,3},{3,5},{1,7},{14,8},{12,10},{10... | collective-permute-start | bytes 393224 | tf_op jit(solution)/shard_map/ppermute | solution.py:58
  6.6 7.4 %collective-permute-start = (bf16[128,512]{1,0:T(8,128)(2,1)S(1)}, bf16[128,512]{1,0:T(8,128)(2,1)S(1)}, u32[]{:S(2)}, u32[]{:S(2)}) collective-permute-start(bf16[128,512]{1,0:T(8,128)(2,1)S(1)} %pad_maximum_fusion.pair_ref.refs_0_), channel_id=1, source_target_pairs={{2,0},{0,2},{6,4},{4,6},{3,1},{1,3},{7,5},{5,7},{10,8},{8,10},{14,... | collective-permute-start | bytes 393224 | tf_op jit(solution)/shard_map/ppermute | solution.py:58
  6.6 11.1 %collective-permute-start.2 = (bf16[128,512]{1,0:T(8,128)(2,1)S(1)}, bf16[128,512]{1,0:T(8,128)(2,1)S(1)}, u32[]{:S(2)}, u32[]{:S(2)}) collective-permute-start(bf16[128,512]{1,0:T(8,128)(2,1)S(1)} %pad_maximum_fusion.pair_ref.refs_0_), channel_id=1, source_target_pairs={{4,0},{6,2},{0,4},{2,6},{5,1},{7,3},{1,5},{3,7},{12,8},{14,10},{8,... | collective-permute-start | bytes 393224 | tf_op jit(solution)/shard_map/ppermute | solution.py:58
  7.3 1.0 %copy-start = (bf16[1,128,2048]{2,1,0:T(8,128)(2,1)S(1)}, bf16[1,128,2048]{2,1,0:T(8,128)(2,1)}, u32[]{:S(2)}) copy-start(bf16[1,128,2048]{2,1,0:T(8,128)(2,1)} %param.7) | copy-start | bytes 1572868
  8.3 1.0 %copy-start.1 = (bf16[1,128,2048]{2,1,0:T(8,128)(2,1)S(1)}, bf16[1,128,2048]{2,1,0:T(8,128)(2,1)}, u32[]{:S(2)}) copy-start(bf16[1,128,2048]{2,1,0:T(8,128)(2,1)} %param.12) | copy-start | bytes 1572868
  9.4 0.7 %copy-start.2 = (bf16[2048]{0:T(1024)(128)(2,1)S(1)}, bf16[2048]{0:T(1024)(128)(2,1)}, u32[]{:S(2)}) copy-start(bf16[2048]{0:T(1024)(128)(2,1)} %param.8) | copy-start | bytes 12292
  10.0 0.7 %copy-start.3 = (s32[1,8]{1,0:T(1,128)S(1)}, s32[1,8]{1,0:T(1,128)}, u32[]{:S(2)}) copy-start(s32[1,8]{1,0:T(1,128)} %len_ref.1) | copy-start | bytes 100
  10.7 0.7 %copy-start.4 = (bf16[256]{0:T(256)(128)(2,1)S(1)}, bf16[256]{0:T(256)(128)(2,1)}, u32[]{:S(2)}) copy-start(bf16[256]{0:T(256)(128)(2,1)} %param.11) | copy-start | bytes 1540
  20.5 11.4 %collective-permute-start.3 = (bf16[128,512]{1,0:T(8,128)(2,1)S(1)}, bf16[128,512]{1,0:T(8,128)(2,1)S(1)}, u32[]{:S(2)}, u32[]{:S(2)}) collective-permute-start(bf16[128,512]{1,0:T(8,128)(2,1)S(1)} %get-tuple-element.48), channel_id=1, source_target_pairs={{0,4},{2,6},{4,0},{6,2},{1,5},{3,7},{5,1},{7,3},{8,12},{10,14},{12... | collective-permute-start | bytes 393224 | tf_op jit(solution)/shard_map/ppermute | solution.py:63
  21.4 5.2 %collective-permute-start.6 = (f32[18,128]{1,0:T(8,128)S(1)}, f32[18,128]{1,0:T(8,128)S(1)}, u32[]{:S(2)}, u32[]{:S(2)}) collective-permute-start(f32[18,128]{1,0:T(8,128)S(1)} %get-tuple-element.51.refs_0_), channel_id=1, source_target_pairs={{24,0},{16,8},{8,16},{0,24},{25,1},{17,9},{9,17},{1,25},{26,2},{18... | collective-permute-start | bytes 27656 | tf_op jit(solution)/shard_map/ppermute | solution.py:58
  23.9 4.4 %collective-permute-start.5 = (f32[18,128]{1,0:T(8,128)S(1)}, f32[18,128]{1,0:T(8,128)S(1)}, u32[]{:S(2)}, u32[]{:S(2)}) collective-permute-start(f32[18,128]{1,0:T(8,128)S(1)} %get-tuple-element.51.refs_0_), channel_id=1, source_target_pairs={{16,0},{24,8},{0,16},{8,24},{17,1},{25,9},{1,17},{9,25},{18,2},{26... | collective-permute-start | bytes 27656 | tf_op jit(solution)/shard_map/ppermute | solution.py:58
  24.4 3.9 %collective-permute-start.4 = (f32[18,128]{1,0:T(8,128)S(1)}, f32[18,128]{1,0:T(8,128)S(1)}, u32[]{:S(2)}, u32[]{:S(2)}) collective-permute-start(f32[18,128]{1,0:T(8,128)S(1)} %get-tuple-element.51.refs_0_), channel_id=1, source_target_pairs={{8,0},{0,8},{24,16},{16,24},{9,1},{1,9},{25,17},{17,25},{10,2},{2,... | collective-permute-start | bytes 27656 | tf_op jit(solution)/shard_map/ppermute | solution.py:58
  24.9 10.7 %collective-permute-start.10 = (bf16[128,512]{1,0:T(8,128)(2,1)S(1)}, bf16[128,512]{1,0:T(8,128)(2,1)S(1)}, u32[]{:S(2)}, u32[]{:S(2)}) collective-permute-start(bf16[128,512]{1,0:T(8,128)(2,1)S(1)} %get-tuple-element.53), channel_id=1, source_target_pairs={{0,6},{2,4},{4,2},{6,0},{1,7},{3,5},{5,3},{7,1},{8,14},{10,12},{12... | collective-permute-start | bytes 393224 | tf_op jit(solution)/shard_map/ppermute | solution.py:63
  26.6 9.0 %collective-permute-start.11 = (bf16[128,512]{1,0:T(8,128)(2,1)S(1)}, bf16[128,512]{1,0:T(8,128)(2,1)S(1)}, u32[]{:S(2)}, u32[]{:S(2)}) collective-permute-start(bf16[128,512]{1,0:T(8,128)(2,1)S(1)} %get-tuple-element.55), channel_id=1, source_target_pairs={{0,2},{2,0},{4,6},{6,4},{1,3},{3,1},{5,7},{7,5},{8,10},{10,8},{12,... | collective-permute-start | bytes 393224 | tf_op jit(solution)/shard_map/ppermute | solution.py:63
  28.2 6.2 %collective-permute-start.9 = (f32[18,128]{1,0:T(8,128)S(1)}, f32[18,128]{1,0:T(8,128)S(1)}, u32[]{:S(2)}, u32[]{:S(2)}) collective-permute-start(f32[18,128]{1,0:T(8,128)S(1)} %total.1.refs_0_), channel_id=1, source_target_pairs={{6,0},{4,2},{2,4},{0,6},{7,1},{5,3},{3,5},{1,7},{14,8},{12,10},{10... | collective-permute-start | bytes 27656 | tf_op jit(solution)/shard_map/ppermute | solution.py:58
  30.1 4.6 %collective-permute-start.8 = (f32[18,128]{1,0:T(8,128)S(1)}, f32[18,128]{1,0:T(8,128)S(1)}, u32[]{:S(2)}, u32[]{:S(2)}) collective-permute-start(f32[18,128]{1,0:T(8,128)S(1)} %total.1.refs_0_), channel_id=1, source_target_pairs={{4,0},{6,2},{0,4},{2,6},{5,1},{7,3},{1,5},{3,7},{12,8},{14,10},{8,... | collective-permute-start | bytes 27656 | tf_op jit(solution)/shard_map/ppermute | solution.py:58
  31.9 3.7 %collective-permute-start.7 = (f32[18,128]{1,0:T(8,128)S(1)}, f32[18,128]{1,0:T(8,128)S(1)}, u32[]{:S(2)}, u32[]{:S(2)}) collective-permute-start(f32[18,128]{1,0:T(8,128)S(1)} %total.1.refs_0_), channel_id=1, source_target_pairs={{2,0},{0,2},{6,4},{4,6},{3,1},{1,3},{7,5},{5,7},{10,8},{8,10},{14,... | collective-permute-start | bytes 27656 | tf_op jit(solution)/shard_map/ppermute | solution.py:58

commit v22 on v21

--- a/solution.py
+++ b/solution.py
@@ -428,6 +428,7 @@
         name="total",
     )(*parts)
     sums = exchange("ctx", sums)
+    sums = [sums[0], *sums[2:], *sums[1:2]]
     back.update(zip(tied, passed))
     k_grad, v_grad, q_sum, v_sum = pl.pallas_call(
         functools.partial(collect_kernel, batches, len(sums)),

time: 36.6 us -> 37.2 us (1.016)
  waiting for transfers between devices: 4.82 us -> 6.2 us
  starting transfers between devices: 17.8 us -> 17 us
    ppermute x9, waiting for transfers between devices: 4.67 us -> 6.19 us  [fetch(): lax.ppermute(array, axis, [(source_of(i, slot, size), i) for i in range(s...]
    ppermute x9, starting transfers between devices: 13.6 us -> 12.8 us  [fetch(): lax.ppermute(array, axis, [(source_of(i, slot, size), i) for i in range(s...]
  transfers between devices with their start and end apart: 12 -> 12, of which waited for: 5 -> 4; matrix products, arithmetic and copies ran while one was open for 0% -> 0% of each run, Pallas kernels for 13% -> 12%
where the time goes in v22:
time: 37.2 us; the launch traced here: 36.9 us
  starting transfers between devices  17 us (46%)
  Pallas kernels  8.06 us (22%)
  waiting for transfers between devices  6.2 us (17%)
  local copies, waits for them, and re-layouts  4.08 us (11%)
  other arithmetic  0.88 us (2%)
  between operations  0.68 us (2%)
    ppermute x9, starting transfers between devices, fetch(): lax.ppermute(array, axis, [(source_of(i, slot, size), i) for i in range(s...  12.8 us
    ppermute x9, waiting for transfers between devices, fetch(): lax.ppermute(array, axis, [(source_of(i, slot, size), i) for i in range(s...  6.19 us
    ppermute x3, starting transfers between devices, send_back(): lax.ppermute(array, 'ctx', [(i, source_of(i, slot, size)) for i in range(...  4.21 us
    unnamed x10, local copies, waits for them, and re-layouts  4.08 us
    pallas_call x1, Pallas kernels, attend(): pl.pallas_call(functools.partial(last_kernel, ctx, first_head), out_shape...  2.81 us
    pallas_call x1, Pallas kernels, shards(): pl.pallas_call(finish_kernel, out_shape=[shape((tok, width), jnp.bfloat16...  1.74 us
    pallas_call x1, Pallas kernels, attend(): pl.pallas_call(near_kernel, out_shape=[shape((near, columns), jnp.float32...  1.7 us
    pallas_call x1, Pallas kernels, shards(): pl.pallas_call(functools.partial(prepare_kernel, ctx), out_shape=[shape((...  1.11 us
  transfers between devices with their start and end apart: 12, of which 4 were waited for; matrix products, arithmetic and copies ran while one was open for 0% of the time, Pallas kernels for 12%

profile of v22, /device:TPU:0, one launch (start us, length us, event | category | flops | bytes accessed | tf_op | source)
XLA Modules:
  0.0 36.9 jit_solution(5475274357380315676)
XLA Ops:
  0.6 0.9 %pad_maximum_fusion.pair_ref.refs_0_ = bf16[128,512]{1,0:T(8,128)(2,1)S(1)} fusion(bf16[128,256]{1,0:T(8,128)(2,1)} %bitcast.16, bf16[128,256]{1,0:T(8,128)(2,1)} %bitcast.17), kind=kLoop, calls=%fused_computation | loop fusion | flops 262144 | bytes 262144 | tf_op jit(solution)/shard_map/concatenate | solution.py:350
  1.5 5.1 %collective-permute-start.1 = (bf16[128,512]{1,0:T(8,128)(2,1)S(1)}, bf16[128,512]{1,0:T(8,128)(2,1)S(1)}, u32[]{:S(2)}, u32[]{:S(2)}) collective-permute-start(bf16[128,512]{1,0:T(8,128)(2,1)S(1)} %pad_maximum_fusion.pair_ref.refs_0_), channel_id=1, source_target_pairs={{6,0},{4,2},{2,4},{0,6},{7,1},{5,3},{3,5},{1,7},{14,8},{12,10},{10... | collective-permute-start | bytes 393224 | tf_op jit(solution)/shard_map/ppermute | solution.py:58
  6.6 0.0 collective-permute-start
  6.6 0.6 %collective-permute-start.2 = (bf16[128,512]{1,0:T(8,128)(2,1)S(1)}, bf16[128,512]{1,0:T(8,128)(2,1)S(1)}, u32[]{:S(2)}, u32[]{:S(2)}) collective-permute-start(bf16[128,512]{1,0:T(8,128)(2,1)S(1)} %pad_maximum_fusion.pair_ref.refs_0_), channel_id=1, source_target_pairs={{4,0},{6,2},{0,4},{2,6},{5,1},{7,3},{1,5},{3,7},{12,8},{14,10},{8,... | collective-permute-start | bytes 393224 | tf_op jit(solution)/shard_map/ppermute | solution.py:58
  7.3 0.0 copy-start
  7.3 1.0 %copy-done = bf16[1,128,2048]{2,1,0:T(8,128)(2,1)S(1)} copy-done((bf16[1,128,2048]{2,1,0:T(8,128)(2,1)S(1)}, bf16[1,128,2048]{2,1,0:T(8,128)(2,1)}, u32[]{:S(2)}) %copy-start) | copy-done | bytes 524312
  8.3 0.0 copy-start.1
  8.3 1.0 %copy-done.1 = bf16[1,128,2048]{2,1,0:T(8,128)(2,1)S(1)} copy-done((bf16[1,128,2048]{2,1,0:T(8,128)(2,1)S(1)}, bf16[1,128,2048]{2,1,0:T(8,128)(2,1)}, u32[]{:S(2)}) %copy-start.1) | copy-done | bytes 524312
  9.4 0.0 copy-start.2
  9.4 0.7 %copy-done.2 = bf16[2048]{0:T(1024)(128)(2,1)S(1)} copy-done((bf16[2048]{0:T(1024)(128)(2,1)S(1)}, bf16[2048]{0:T(1024)(128)(2,1)}, u32[]{:S(2)}) %copy-start.2) | copy-done | bytes 4120
  10.0 0.0 copy-start.3
  10.0 0.7 %copy-done.3 = s32[1,8]{1,0:T(1,128)S(1)} copy-done((s32[1,8]{1,0:T(1,128)S(1)}, s32[1,8]{1,0:T(1,128)}, u32[]{:S(2)}) %copy-start.3) | copy-done | bytes 56
  10.7 0.0 copy-start.4
  10.7 0.7 %copy-done.4 = bf16[256]{0:T(256)(128)(2,1)S(1)} copy-done((bf16[256]{0:T(256)(128)(2,1)S(1)}, bf16[256]{0:T(256)(128)(2,1)}, u32[]{:S(2)}) %copy-start.4) | copy-done | bytes 536
  11.4 1.1 %prepare.1 = (bf16[2,128]{1,0:T(2,128)(2,1)S(1)}, bf16[2048,256]{1,0:T(8,128)(2,1)S(1)}, bf16[2048,128]{1,0:T(8,128)(2,1)S(1)}, f32[128,2048]{1,0:T(8,128)S(1)},...) custom-call(s32[1,8]{1,0:T(1,128)S(1)} %copy-done.3, bf16[128,512]{1,0:T(8,128)(2,1)S(1)} %pad_maximum_fusion.pair_ref.refs_0_, ...), custom_call_target="tpu_custom_call" | custom-call | flops 134217728 | bytes 4194304 | tf_op jit(solution)/shard_map/prepare/pallas_call | solution.py:352
  12.5 0.0 collective-permute-done.1.refs_2_
  12.5 1.5 %collective-permute-done.refs_1_ = bf16[128,512]{1,0:T(8,128)(2,1)S(1)} collective-permute-done((bf16[128,512]{1,0:T(8,128)(2,1)S(1)}, bf16[128,512]{1,0:T(8,128)(2,1)S(1)}, u32[]{:S(2)}, u32[]{:S(2)}) %collective-permute-start) | collective-permute-done | bytes 131104 | tf_op jit(solution)/shard_map/ppermute | solution.py:58
  14.0 1.7 %near.1 = (f32[384,2048]{1,0:T(8,128)S(1)}, f32[384,2048]{1,0:T(8,128)S(1)}, f32[8,2048]{1,0:T(8,128)S(1)}, bf16[384,256]{1,0:T(8,128)(2,1)S(1)}, bf16[384,256]{1,0:T(8,128)(2,1)S(1)}) custom-call(bf16[2,128]{1,0:T(2,128)(2,1)S(1)} %get-tuple-element.33.bias_ref.refs_0_, bf16[2048,256]{1,0:T(8,128)(2,1)S(1)} %get-tuple-element.34.queries_ref.refs_1_, ...), custom_call_target="tpu_custom_call" | custom-call | flops 402653184 | bytes 6291456 | tf_op jit(solution)/shard_map/near/pallas_call | solution.py:289
  15.7 2.0 %collective-permute-done.2.refs_9_ = bf16[128,512]{1,0:T(8,128)(2,1)S(1)} collective-permute-done((bf16[128,512]{1,0:T(8,128)(2,1)S(1)}, bf16[128,512]{1,0:T(8,128)(2,1)S(1)}, u32[]{:S(2)}, u32[]{:S(2)}) %collective-permute-start.2) | collective-permute-done | bytes 131104 | tf_op jit(solution)/shard_map/ppermute | solution.py:58
  17.7 2.8 %last.1 = (bf16[512,2048]{1,0:T(8,128)(2,1)S(1)}, bf16[512,2048]{1,0:T(8,128)(2,1)S(1)}, bf16[512,256]{1,0:T(8,128)(2,1)S(1)}, bf16[512,256]{1,0:T(8,128)(2,1)S(...) custom-call(bf16[2,128]{1,0:T(2,128)(2,1)S(1)} %get-tuple-element.33, ...), custom_call_target="tpu_custom_call" | custom-call | flops 536870912 | bytes 4194304 | tf_op jit(solution)/shard_map/last/pallas_call | solution.py:309
  20.5 0.9 %collective-permute-start.3 = (bf16[128,512]{1,0:T(8,128)(2,1)S(1)}, bf16[128,512]{1,0:T(8,128)(2,1)S(1)}, u32[]{:S(2)}, u32[]{:S(2)}) collective-permute-start(bf16[128,512]{1,0:T(8,128)(2,1)S(1)} %get-tuple-element.48), channel_id=1, source_target_pairs={{0,4},{2,6},{4,0},{6,2},{1,5},{3,7},{5,1},{7,3},{8,12},{10,14},{12... | collective-permute-start | bytes 393224 | tf_op jit(solution)/shard_map/ppermute | solution.py:63
  21.4 2.5 %collective-permute-start.6 = (f32[18,128]{1,0:T(8,128)S(1)}, f32[18,128]{1,0:T(8,128)S(1)}, u32[]{:S(2)}, u32[]{:S(2)}) collective-permute-start(f32[18,128]{1,0:T(8,128)S(1)} %get-tuple-element.51.refs_0_), channel_id=1, source_target_pairs={{24,0},{16,8},{8,16},{0,24},{25,1},{17,9},{9,17},{1,25},{26,2},{18... | collective-permute-start | bytes 27656 | tf_op jit(solution)/shard_map/ppermute | solution.py:58
  23.9 0.5 %collective-permute-start.5 = (f32[18,128]{1,0:T(8,128)S(1)}, f32[18,128]{1,0:T(8,128)S(1)}, u32[]{:S(2)}, u32[]{:S(2)}) collective-permute-start(f32[18,128]{1,0:T(8,128)S(1)} %get-tuple-element.51.refs_0_), channel_id=1, source_target_pairs={{16,0},{24,8},{0,16},{8,24},{17,1},{25,9},{1,17},{9,25},{18,2},{26... | collective-permute-start | bytes 27656 | tf_op jit(solution)/shard_map/ppermute | solution.py:58
  24.4 0.5 %collective-permute-start.4 = (f32[18,128]{1,0:T(8,128)S(1)}, f32[18,128]{1,0:T(8,128)S(1)}, u32[]{:S(2)}, u32[]{:S(2)}) collective-permute-start(f32[18,128]{1,0:T(8,128)S(1)} %get-tuple-element.51.refs_0_), channel_id=1, source_target_pairs={{8,0},{0,8},{24,16},{16,24},{9,1},{1,9},{25,17},{17,25},{10,2},{2,... | collective-permute-start | bytes 27656 | tf_op jit(solution)/shard_map/ppermute | solution.py:58
  24.9 1.7 %collective-permute-start.10 = (bf16[128,512]{1,0:T(8,128)(2,1)S(1)}, bf16[128,512]{1,0:T(8,128)(2,1)S(1)}, u32[]{:S(2)}, u32[]{:S(2)}) collective-permute-start(bf16[128,512]{1,0:T(8,128)(2,1)S(1)} %get-tuple-element.53), channel_id=1, source_target_pairs={{0,6},{2,4},{4,2},{6,0},{1,7},{3,5},{5,3},{7,1},{8,14},{10,12},{12... | collective-permute-start | bytes 393224 | tf_op jit(solution)/shard_map/ppermute | solution.py:63
  26.6 0.0 collective-permute-done.6.refs_3_
  26.6 1.6 %collective-permute-start.11 = (bf16[128,512]{1,0:T(8,128)(2,1)S(1)}, bf16[128,512]{1,0:T(8,128)(2,1)S(1)}, u32[]{:S(2)}, u32[]{:S(2)}) collective-permute-start(bf16[128,512]{1,0:T(8,128)(2,1)S(1)} %get-tuple-element.55), channel_id=1, source_target_pairs={{0,2},{2,0},{4,6},{6,4},{1,3},{3,1},{5,7},{7,5},{8,10},{10,8},{12,... | collective-permute-start | bytes 393224 | tf_op jit(solution)/shard_map/ppermute | solution.py:63
  28.2 0.0 collective-permute-done.5.refs_2_
  28.2 0.0 collective-permute-done.4.refs_1_
  28.2 2.0 %collective-permute-start.9 = (f32[18,128]{1,0:T(8,128)S(1)}, f32[18,128]{1,0:T(8,128)S(1)}, u32[]{:S(2)}, u32[]{:S(2)}) collective-permute-start(f32[18,128]{1,0:T(8,128)S(1)} %total.1.refs_0_), channel_id=1, source_target_pairs={{2,0},{0,2},{6,4},{4,6},{3,1},{1,3},{7,5},{5,7},{10,8},{8,10},{14,... | collective-permute-start | bytes 27656 | tf_op jit(solution)/shard_map/ppermute | solution.py:58
  30.3 1.3 %collective-permute-start.8 = (f32[18,128]{1,0:T(8,128)S(1)}, f32[18,128]{1,0:T(8,128)S(1)}, u32[]{:S(2)}, u32[]{:S(2)}) collective-permute-start(f32[18,128]{1,0:T(8,128)S(1)} %total.1.refs_0_), channel_id=1, source_target_pairs={{6,0},{4,2},{2,4},{0,6},{7,1},{5,3},{3,5},{1,7},{14,8},{12,10},{10... | collective-permute-start | bytes 27656 | tf_op jit(solution)/shard_map/ppermute | solution.py:58
  31.6 0.0 collective-permute-done.3.refs_0_
  31.6 0.2 collective-permute-start.7
  31.8 1.7 %finish.1 = (bf16[128,2048]{1,0:T(8,128)(2,1)}, bf16[128,2048]{1,0:T(8,128)(2,1)}, bf16[128,512]{1,0:T(8,128)(2,1)S(1)}) custom-call(bf16[512,2048]{1,0:T(8,128)(2,1)S(1)} %get-tuple-element.44.probs_ref, bf16[512,2048]{1,0:T(8,128)(2,1)S(1)} %get-tuple-element.45.dscore_ref, ...), custom_call_target="tpu_custom_call", output_to_operand_aliasing={{2}: (4, {})} | custom-call | flops 2147483648 | tf_op jit(solution)/shard_map/finish/pallas_call | solution.py:404
  33.6 0.0 collective-permute-done.9.refs_3_
  33.6 2.2 %collective-permute-done.8.refs_2_ = f32[18,128]{1,0:T(8,128)S(1)} collective-permute-done((f32[18,128]{1,0:T(8,128)S(1)}, f32[18,128]{1,0:T(8,128)S(1)}, u32[]{:S(2)}, u32[]{:S(2)}) %collective-permute-start.8) | collective-permute-done | bytes 9248 | tf_op jit(solution)/shard_map/ppermute | solution.py:58
  35.8 0.5 %collective-permute-done.7.refs_1_ = f32[18,128]{1,0:T(8,128)S(1)} collective-permute-done((f32[18,128]{1,0:T(8,128)S(1)}, f32[18,128]{1,0:T(8,128)S(1)}, u32[]{:S(2)}, u32[]{:S(2)}) %collective-permute-start.7) | collective-permute-done | bytes 9248 | tf_op jit(solution)/shard_map/ppermute | solution.py:58
  36.2 0.0 collective-permute-done.10.refs_5_
  36.2 0.0 collective-permute-done.11.refs_7_
  36.2 0.7 %collect.1 = (bf16[128,256]{1,0:T(8,128)(2,1)}, bf16[128,256]{1,0:T(8,128)(2,1)}, f32[16,128]{1,0:T(8,128)}, f32[2,128]{1,0:T(2,128)}) custom-call(f32[18,128]{1,0:T(8,128)S(1)} %total.1.refs_0_, f32[18,128]{1,0:T(8,128)S(1)} %collective-permute-done.7.refs_1_, f32[18,128]{1,0:T(8,128)S(1)} %collective-permute-done.8.refs_2_, ...), custom_call_target="tpu_custom_call" | custom-call | flops 262144 | bytes 524288 | tf_op jit(solution)/shard_map/collect/pallas_call | solution.py:433
  (1 shorter events, 0.0 us)
Async XLA Ops:
  1.5 11.0 %collective-permute-start.1 = (bf16[128,512]{1,0:T(8,128)(2,1)S(1)}, bf16[128,512]{1,0:T(8,128)(2,1)S(1)}, u32[]{:S(2)}, u32[]{:S(2)}) collective-permute-start(bf16[128,512]{1,0:T(8,128)(2,1)S(1)} %pad_maximum_fusion.pair_ref.refs_0_), channel_id=1, source_target_pairs={{6,0},{4,2},{2,4},{0,6},{7,1},{5,3},{3,5},{1,7},{14,8},{12,10},{10... | collective-permute-start | bytes 393224 | tf_op jit(solution)/shard_map/ppermute | solution.py:58
  6.6 7.4 %collective-permute-start = (bf16[128,512]{1,0:T(8,128)(2,1)S(1)}, bf16[128,512]{1,0:T(8,128)(2,1)S(1)}, u32[]{:S(2)}, u32[]{:S(2)}) collective-permute-start(bf16[128,512]{1,0:T(8,128)(2,1)S(1)} %pad_maximum_fusion.pair_ref.refs_0_), channel_id=1, source_target_pairs={{2,0},{0,2},{6,4},{4,6},{3,1},{1,3},{7,5},{5,7},{10,8},{8,10},{14,... | collective-permute-start | bytes 393224 | tf_op jit(solution)/shard_map/ppermute | solution.py:58
  6.6 11.1 %collective-permute-start.2 = (bf16[128,512]{1,0:T(8,128)(2,1)S(1)}, bf16[128,512]{1,0:T(8,128)(2,1)S(1)}, u32[]{:S(2)}, u32[]{:S(2)}) collective-permute-start(bf16[128,512]{1,0:T(8,128)(2,1)S(1)} %pad_maximum_fusion.pair_ref.refs_0_), channel_id=1, source_target_pairs={{4,0},{6,2},{0,4},{2,6},{5,1},{7,3},{1,5},{3,7},{12,8},{14,10},{8,... | collective-permute-start | bytes 393224 | tf_op jit(solution)/shard_map/ppermute | solution.py:58
  7.3 1.0 %copy-start = (bf16[1,128,2048]{2,1,0:T(8,128)(2,1)S(1)}, bf16[1,128,2048]{2,1,0:T(8,128)(2,1)}, u32[]{:S(2)}) copy-start(bf16[1,128,2048]{2,1,0:T(8,128)(2,1)} %param.7) | copy-start | bytes 1572868
  8.3 1.0 %copy-start.1 = (bf16[1,128,2048]{2,1,0:T(8,128)(2,1)S(1)}, bf16[1,128,2048]{2,1,0:T(8,128)(2,1)}, u32[]{:S(2)}) copy-start(bf16[1,128,2048]{2,1,0:T(8,128)(2,1)} %param.12) | copy-start | bytes 1572868
  9.4 0.7 %copy-start.2 = (bf16[2048]{0:T(1024)(128)(2,1)S(1)}, bf16[2048]{0:T(1024)(128)(2,1)}, u32[]{:S(2)}) copy-start(bf16[2048]{0:T(1024)(128)(2,1)} %param.8) | copy-start | bytes 12292
  10.0 0.7 %copy-start.3 = (s32[1,8]{1,0:T(1,128)S(1)}, s32[1,8]{1,0:T(1,128)}, u32[]{:S(2)}) copy-start(s32[1,8]{1,0:T(1,128)} %len_ref.1) | copy-start | bytes 100
  10.7 0.7 %copy-start.4 = (bf16[256]{0:T(256)(128)(2,1)S(1)}, bf16[256]{0:T(256)(128)(2,1)}, u32[]{:S(2)}) copy-start(bf16[256]{0:T(256)(128)(2,1)} %param.11) | copy-start | bytes 1540
  20.5 11.1 %collective-permute-start.3 = (bf16[128,512]{1,0:T(8,128)(2,1)S(1)}, bf16[128,512]{1,0:T(8,128)(2,1)S(1)}, u32[]{:S(2)}, u32[]{:S(2)}) collective-permute-start(bf16[128,512]{1,0:T(8,128)(2,1)S(1)} %get-tuple-element.48), channel_id=1, source_target_pairs={{0,4},{2,6},{4,0},{6,2},{1,5},{3,7},{5,1},{7,3},{8,12},{10,14},{12... | collective-permute-start | bytes 393224 | tf_op jit(solution)/shard_map/ppermute | solution.py:63
  21.4 5.2 %collective-permute-start.6 = (f32[18,128]{1,0:T(8,128)S(1)}, f32[18,128]{1,0:T(8,128)S(1)}, u32[]{:S(2)}, u32[]{:S(2)}) collective-permute-start(f32[18,128]{1,0:T(8,128)S(1)} %get-tuple-element.51.refs_0_), channel_id=1, source_target_pairs={{24,0},{16,8},{8,16},{0,24},{25,1},{17,9},{9,17},{1,25},{26,2},{18... | collective-permute-start | bytes 27656 | tf_op jit(solution)/shard_map/ppermute | solution.py:58
  23.9 4.4 %collective-permute-start.5 = (f32[18,128]{1,0:T(8,128)S(1)}, f32[18,128]{1,0:T(8,128)S(1)}, u32[]{:S(2)}, u32[]{:S(2)}) collective-permute-start(f32[18,128]{1,0:T(8,128)S(1)} %get-tuple-element.51.refs_0_), channel_id=1, source_target_pairs={{16,0},{24,8},{0,16},{8,24},{17,1},{25,9},{1,17},{9,25},{18,2},{26... | collective-permute-start | bytes 27656 | tf_op jit(solution)/shard_map/ppermute | solution.py:58
  24.4 3.9 %collective-permute-start.4 = (f32[18,128]{1,0:T(8,128)S(1)}, f32[18,128]{1,0:T(8,128)S(1)}, u32[]{:S(2)}, u32[]{:S(2)}) collective-permute-start(f32[18,128]{1,0:T(8,128)S(1)} %get-tuple-element.51.refs_0_), channel_id=1, source_target_pairs={{8,0},{0,8},{24,16},{16,24},{9,1},{1,9},{25,17},{17,25},{10,2},{2,... | collective-permute-start | bytes 27656 | tf_op jit(solution)/shard_map/ppermute | solution.py:58
  24.9 11.3 %collective-permute-start.10 = (bf16[128,512]{1,0:T(8,128)(2,1)S(1)}, bf16[128,512]{1,0:T(8,128)(2,1)S(1)}, u32[]{:S(2)}, u32[]{:S(2)}) collective-permute-start(bf16[128,512]{1,0:T(8,128)(2,1)S(1)} %get-tuple-element.53), channel_id=1, source_target_pairs={{0,6},{2,4},{4,2},{6,0},{1,7},{3,5},{5,3},{7,1},{8,14},{10,12},{12... | collective-permute-start | bytes 393224 | tf_op jit(solution)/shard_map/ppermute | solution.py:63
  26.6 9.6 %collective-permute-start.11 = (bf16[128,512]{1,0:T(8,128)(2,1)S(1)}, bf16[128,512]{1,0:T(8,128)(2,1)S(1)}, u32[]{:S(2)}, u32[]{:S(2)}) collective-permute-start(bf16[128,512]{1,0:T(8,128)(2,1)S(1)} %get-tuple-element.55), channel_id=1, source_target_pairs={{0,2},{2,0},{4,6},{6,4},{1,3},{3,1},{5,7},{7,5},{8,10},{10,8},{12,... | collective-permute-start | bytes 393224 | tf_op jit(solution)/shard_map/ppermute | solution.py:63
  28.2 5.4 %collective-permute-start.9 = (f32[18,128]{1,0:T(8,128)S(1)}, f32[18,128]{1,0:T(8,128)S(1)}, u32[]{:S(2)}, u32[]{:S(2)}) collective-permute-start(f32[18,128]{1,0:T(8,128)S(1)} %total.1.refs_0_), channel_id=1, source_target_pairs={{2,0},{0,2},{6,4},{4,6},{3,1},{1,3},{7,5},{5,7},{10,8},{8,10},{14,... | collective-permute-start | bytes 27656 | tf_op jit(solution)/shard_map/ppermute | solution.py:58
  30.3 5.5 %collective-permute-start.8 = (f32[18,128]{1,0:T(8,128)S(1)}, f32[18,128]{1,0:T(8,128)S(1)}, u32[]{:S(2)}, u32[]{:S(2)}) collective-permute-start(f32[18,128]{1,0:T(8,128)S(1)} %total.1.refs_0_), channel_id=1, source_target_pairs={{6,0},{4,2},{2,4},{0,6},{7,1},{5,3},{3,5},{1,7},{14,8},{12,10},{10... | collective-permute-start | bytes 27656 | tf_op jit(solution)/shard_map/ppermute | solution.py:58
  31.6 4.6 %collective-permute-start.7 = (f32[18,128]{1,0:T(8,128)S(1)}, f32[18,128]{1,0:T(8,128)S(1)}, u32[]{:S(2)}, u32[]{:S(2)}) collective-permute-start(f32[18,128]{1,0:T(8,128)S(1)} %total.1.refs_0_), channel_id=1, source_target_pairs={{4,0},{6,2},{0,4},{2,6},{5,1},{7,3},{1,5},{3,7},{12,8},{14,10},{8,... | collective-permute-start | bytes 27656 | tf_op jit(solution)/shard_map/ppermute | solution.py:58

commit v23 on v21

--- a/solution.py
+++ b/solution.py
@@ -444,7 +444,7 @@
             flops=8 * tok * kv_width, bytes_accessed=16 * tok * kv_width, transcendentals=0
         ),
         name="collect",
-    )(*sums, own, *[back[slot] for slot in sorted(back, reverse=True)])
+    )(*sums, own, *[back[slot] for slot in sorted(back)])
     return (
         attn[None],
         q_grad[None],

time: 36.6 us -> 36.6 us (level)
  starting transfers between devices: 17.8 us -> 18.2 us
  transfers between devices with their start and end apart: 12 -> 12, of which waited for: 5 -> 3; matrix products, arithmetic and copies ran while one was open for 0% -> 0% of each run, Pallas kernels for 13% -> 13%
where the time goes in v23:
time: 36.6 us; the launch traced here: 36.3 us
  starting transfers between devices  18.2 us (50%)
  Pallas kernels  8.06 us (22%)
  waiting for transfers between devices  4.47 us (12%)
  local copies, waits for them, and re-layouts  4.08 us (11%)
  other arithmetic  0.88 us (2%)
  between operations  0.69 us (2%)
    ppermute x9, starting transfers between devices, fetch(): lax.ppermute(array, axis, [(source_of(i, slot, size), i) for i in range(s...  13.7 us
    ppermute x9, waiting for transfers between devices, fetch(): lax.ppermute(array, axis, [(source_of(i, slot, size), i) for i in range(s...  4.46 us
    ppermute x3, starting transfers between devices, send_back(): lax.ppermute(array, 'ctx', [(i, source_of(i, slot, size)) for i in range(...  4.45 us
    unnamed x10, local copies, waits for them, and re-layouts  4.08 us
    pallas_call x1, Pallas kernels, attend(): pl.pallas_call(functools.partial(last_kernel, ctx, first_head), out_shape...  2.81 us
    pallas_call x1, Pallas kernels, shards(): pl.pallas_call(finish_kernel, out_shape=[shape((tok, width), jnp.bfloat16...  1.74 us
    pallas_call x1, Pallas kernels, attend(): pl.pallas_call(near_kernel, out_shape=[shape((near, columns), jnp.float32...  1.7 us
    pallas_call x1, Pallas kernels, shards(): pl.pallas_call(functools.partial(prepare_kernel, ctx), out_shape=[shape((...  1.11 us
  transfers between devices with their start and end apart: 12, of which 3 were waited for; matrix products, arithmetic and copies ran while one was open for 0% of the time, Pallas kernels for 13%

profile of v23, /device:TPU:0, one launch (start us, length us, event | category | flops | bytes accessed | tf_op | source)
XLA Modules:
  0.0 36.3 jit_solution(15384143008297919417)
XLA Ops:
  0.6 0.9 %pad_maximum_fusion.pair_ref.refs_0_ = bf16[128,512]{1,0:T(8,128)(2,1)S(1)} fusion(bf16[128,256]{1,0:T(8,128)(2,1)} %bitcast.16, bf16[128,256]{1,0:T(8,128)(2,1)} %bitcast.17), kind=kLoop, calls=%fused_computation | loop fusion | flops 262144 | bytes 262144 | tf_op jit(solution)/shard_map/concatenate | solution.py:350
  1.5 5.1 %collective-permute-start.1 = (bf16[128,512]{1,0:T(8,128)(2,1)S(1)}, bf16[128,512]{1,0:T(8,128)(2,1)S(1)}, u32[]{:S(2)}, u32[]{:S(2)}) collective-permute-start(bf16[128,512]{1,0:T(8,128)(2,1)S(1)} %pad_maximum_fusion.pair_ref.refs_0_), channel_id=1, source_target_pairs={{6,0},{4,2},{2,4},{0,6},{7,1},{5,3},{3,5},{1,7},{14,8},{12,10},{10... | collective-permute-start | bytes 393224 | tf_op jit(solution)/shard_map/ppermute | solution.py:58
  6.6 0.0 collective-permute-start
  6.6 0.6 %collective-permute-start.2 = (bf16[128,512]{1,0:T(8,128)(2,1)S(1)}, bf16[128,512]{1,0:T(8,128)(2,1)S(1)}, u32[]{:S(2)}, u32[]{:S(2)}) collective-permute-start(bf16[128,512]{1,0:T(8,128)(2,1)S(1)} %pad_maximum_fusion.pair_ref.refs_0_), channel_id=1, source_target_pairs={{4,0},{6,2},{0,4},{2,6},{5,1},{7,3},{1,5},{3,7},{12,8},{14,10},{8,... | collective-permute-start | bytes 393224 | tf_op jit(solution)/shard_map/ppermute | solution.py:58
  7.3 0.0 copy-start
  7.3 1.0 %copy-done = bf16[1,128,2048]{2,1,0:T(8,128)(2,1)S(1)} copy-done((bf16[1,128,2048]{2,1,0:T(8,128)(2,1)S(1)}, bf16[1,128,2048]{2,1,0:T(8,128)(2,1)}, u32[]{:S(2)}) %copy-start) | copy-done | bytes 524312
  8.3 0.0 copy-start.1
  8.3 1.0 %copy-done.1 = bf16[1,128,2048]{2,1,0:T(8,128)(2,1)S(1)} copy-done((bf16[1,128,2048]{2,1,0:T(8,128)(2,1)S(1)}, bf16[1,128,2048]{2,1,0:T(8,128)(2,1)}, u32[]{:S(2)}) %copy-start.1) | copy-done | bytes 524312
  9.4 0.0 copy-start.2
  9.4 0.7 %copy-done.2 = bf16[2048]{0:T(1024)(128)(2,1)S(1)} copy-done((bf16[2048]{0:T(1024)(128)(2,1)S(1)}, bf16[2048]{0:T(1024)(128)(2,1)}, u32[]{:S(2)}) %copy-start.2) | copy-done | bytes 4120
  10.0 0.0 copy-start.3
  10.0 0.7 %copy-done.3 = s32[1,8]{1,0:T(1,128)S(1)} copy-done((s32[1,8]{1,0:T(1,128)S(1)}, s32[1,8]{1,0:T(1,128)}, u32[]{:S(2)}) %copy-start.3) | copy-done | bytes 56
  10.7 0.0 copy-start.4
  10.7 0.7 %copy-done.4 = bf16[256]{0:T(256)(128)(2,1)S(1)} copy-done((bf16[256]{0:T(256)(128)(2,1)S(1)}, bf16[256]{0:T(256)(128)(2,1)}, u32[]{:S(2)}) %copy-start.4) | copy-done | bytes 536
  11.4 1.1 %prepare.1 = (bf16[2,128]{1,0:T(2,128)(2,1)S(1)}, bf16[2048,256]{1,0:T(8,128)(2,1)S(1)}, bf16[2048,128]{1,0:T(8,128)(2,1)S(1)}, f32[128,2048]{1,0:T(8,128)S(1)},...) custom-call(s32[1,8]{1,0:T(1,128)S(1)} %copy-done.3, bf16[128,512]{1,0:T(8,128)(2,1)S(1)} %pad_maximum_fusion.pair_ref.refs_0_, ...), custom_call_target="tpu_custom_call" | custom-call | flops 134217728 | bytes 4194304 | tf_op jit(solution)/shard_map/prepare/pallas_call | solution.py:352
  12.5 0.0 collective-permute-done.1.refs_2_
  12.5 1.5 %collective-permute-done.refs_1_ = bf16[128,512]{1,0:T(8,128)(2,1)S(1)} collective-permute-done((bf16[128,512]{1,0:T(8,128)(2,1)S(1)}, bf16[128,512]{1,0:T(8,128)(2,1)S(1)}, u32[]{:S(2)}, u32[]{:S(2)}) %collective-permute-start) | collective-permute-done | bytes 131104 | tf_op jit(solution)/shard_map/ppermute | solution.py:58
  14.0 1.7 %near.1 = (f32[384,2048]{1,0:T(8,128)S(1)}, f32[384,2048]{1,0:T(8,128)S(1)}, f32[8,2048]{1,0:T(8,128)S(1)}, bf16[384,256]{1,0:T(8,128)(2,1)S(1)}, bf16[384,256]{1,0:T(8,128)(2,1)S(1)}) custom-call(bf16[2,128]{1,0:T(2,128)(2,1)S(1)} %get-tuple-element.33.bias_ref.refs_0_, bf16[2048,256]{1,0:T(8,128)(2,1)S(1)} %get-tuple-element.34.queries_ref.refs_1_, ...), custom_call_target="tpu_custom_call" | custom-call | flops 402653184 | bytes 6291456 | tf_op jit(solution)/shard_map/near/pallas_call | solution.py:289
  15.7 2.0 %collective-permute-done.2.refs_9_ = bf16[128,512]{1,0:T(8,128)(2,1)S(1)} collective-permute-done((bf16[128,512]{1,0:T(8,128)(2,1)S(1)}, bf16[128,512]{1,0:T(8,128)(2,1)S(1)}, u32[]{:S(2)}, u32[]{:S(2)}) %collective-permute-start.2) | collective-permute-done | bytes 131104 | tf_op jit(solution)/shard_map/ppermute | solution.py:58
  17.7 2.8 %last.1 = (bf16[512,2048]{1,0:T(8,128)(2,1)S(1)}, bf16[512,2048]{1,0:T(8,128)(2,1)S(1)}, bf16[512,256]{1,0:T(8,128)(2,1)S(1)}, bf16[512,256]{1,0:T(8,128)(2,1)S(...) custom-call(bf16[2,128]{1,0:T(2,128)(2,1)S(1)} %get-tuple-element.33, ...), custom_call_target="tpu_custom_call" | custom-call | flops 536870912 | bytes 4194304 | tf_op jit(solution)/shard_map/last/pallas_call | solution.py:309
  20.5 0.9 %collective-permute-start.3 = (bf16[128,512]{1,0:T(8,128)(2,1)S(1)}, bf16[128,512]{1,0:T(8,128)(2,1)S(1)}, u32[]{:S(2)}, u32[]{:S(2)}) collective-permute-start(bf16[128,512]{1,0:T(8,128)(2,1)S(1)} %get-tuple-element.48), channel_id=1, source_target_pairs={{0,4},{2,6},{4,0},{6,2},{1,5},{3,7},{5,1},{7,3},{8,12},{10,14},{12... | collective-permute-start | bytes 393224 | tf_op jit(solution)/shard_map/ppermute | solution.py:63
  21.4 2.5 %collective-permute-start.6 = (f32[18,128]{1,0:T(8,128)S(1)}, f32[18,128]{1,0:T(8,128)S(1)}, u32[]{:S(2)}, u32[]{:S(2)}) collective-permute-start(f32[18,128]{1,0:T(8,128)S(1)} %get-tuple-element.51.refs_0_), channel_id=1, source_target_pairs={{24,0},{16,8},{8,16},{0,24},{25,1},{17,9},{9,17},{1,25},{26,2},{18... | collective-permute-start | bytes 27656 | tf_op jit(solution)/shard_map/ppermute | solution.py:58
  23.9 0.5 %collective-permute-start.5 = (f32[18,128]{1,0:T(8,128)S(1)}, f32[18,128]{1,0:T(8,128)S(1)}, u32[]{:S(2)}, u32[]{:S(2)}) collective-permute-start(f32[18,128]{1,0:T(8,128)S(1)} %get-tuple-element.51.refs_0_), channel_id=1, source_target_pairs={{16,0},{24,8},{0,16},{8,24},{17,1},{25,9},{1,17},{9,25},{18,2},{26... | collective-permute-start | bytes 27656 | tf_op jit(solution)/shard_map/ppermute | solution.py:58
  24.4 0.5 %collective-permute-start.4 = (f32[18,128]{1,0:T(8,128)S(1)}, f32[18,128]{1,0:T(8,128)S(1)}, u32[]{:S(2)}, u32[]{:S(2)}) collective-permute-start(f32[18,128]{1,0:T(8,128)S(1)} %get-tuple-element.51.refs_0_), channel_id=1, source_target_pairs={{8,0},{0,8},{24,16},{16,24},{9,1},{1,9},{25,17},{17,25},{10,2},{2,... | collective-permute-start | bytes 27656 | tf_op jit(solution)/shard_map/ppermute | solution.py:58
  24.9 2.2 %collective-permute-start.10 = (bf16[128,512]{1,0:T(8,128)(2,1)S(1)}, bf16[128,512]{1,0:T(8,128)(2,1)S(1)}, u32[]{:S(2)}, u32[]{:S(2)}) collective-permute-start(bf16[128,512]{1,0:T(8,128)(2,1)S(1)} %get-tuple-element.53), channel_id=1, source_target_pairs={{0,2},{2,0},{4,6},{6,4},{1,3},{3,1},{5,7},{7,5},{8,10},{10,8},{12,... | collective-permute-start | bytes 393224 | tf_op jit(solution)/shard_map/ppermute | solution.py:63
  27.1 0.0 collective-permute-done.6.refs_3_
  27.1 1.3 %collective-permute-start.11 = (bf16[128,512]{1,0:T(8,128)(2,1)S(1)}, bf16[128,512]{1,0:T(8,128)(2,1)S(1)}, u32[]{:S(2)}, u32[]{:S(2)}) collective-permute-start(bf16[128,512]{1,0:T(8,128)(2,1)S(1)} %get-tuple-element.55), channel_id=1, source_target_pairs={{0,6},{2,4},{4,2},{6,0},{1,7},{3,5},{5,3},{7,1},{8,14},{10,12},{12... | collective-permute-start | bytes 393224 | tf_op jit(solution)/shard_map/ppermute | solution.py:63
  28.5 0.0 collective-permute-done.5.refs_2_
  28.5 0.0 collective-permute-done.4.refs_1_
  28.5 2.5 %collective-permute-start.9 = (f32[18,128]{1,0:T(8,128)S(1)}, f32[18,128]{1,0:T(8,128)S(1)}, u32[]{:S(2)}, u32[]{:S(2)}) collective-permute-start(f32[18,128]{1,0:T(8,128)S(1)} %total.1.refs_0_), channel_id=1, source_target_pairs={{6,0},{4,2},{2,4},{0,6},{7,1},{5,3},{3,5},{1,7},{14,8},{12,10},{10... | collective-permute-start | bytes 27656 | tf_op jit(solution)/shard_map/ppermute | solution.py:58
  31.0 0.7 %collective-permute-start.8 = (f32[18,128]{1,0:T(8,128)S(1)}, f32[18,128]{1,0:T(8,128)S(1)}, u32[]{:S(2)}, u32[]{:S(2)}) collective-permute-start(f32[18,128]{1,0:T(8,128)S(1)} %total.1.refs_0_), channel_id=1, source_target_pairs={{4,0},{6,2},{0,4},{2,6},{5,1},{7,3},{1,5},{3,7},{12,8},{14,10},{8,... | collective-permute-start | bytes 27656 | tf_op jit(solution)/shard_map/ppermute | solution.py:58
  31.7 0.0 collective-permute-done.3.refs_0_
  31.8 1.2 %collective-permute-start.7 = (f32[18,128]{1,0:T(8,128)S(1)}, f32[18,128]{1,0:T(8,128)S(1)}, u32[]{:S(2)}, u32[]{:S(2)}) collective-permute-start(f32[18,128]{1,0:T(8,128)S(1)} %total.1.refs_0_), channel_id=1, source_target_pairs={{2,0},{0,2},{6,4},{4,6},{3,1},{1,3},{7,5},{5,7},{10,8},{8,10},{14,... | collective-permute-start | bytes 27656 | tf_op jit(solution)/shard_map/ppermute | solution.py:58
  32.9 1.7 %finish.1 = (bf16[128,2048]{1,0:T(8,128)(2,1)}, bf16[128,2048]{1,0:T(8,128)(2,1)}, bf16[128,512]{1,0:T(8,128)(2,1)S(1)}) custom-call(bf16[512,2048]{1,0:T(8,128)(2,1)S(1)} %get-tuple-element.44.probs_ref, bf16[512,2048]{1,0:T(8,128)(2,1)S(1)} %get-tuple-element.45.dscore_ref, ...), custom_call_target="tpu_custom_call", output_to_operand_aliasing={{2}: (4, {})} | custom-call | flops 2147483648 | tf_op jit(solution)/shard_map/finish/pallas_call | solution.py:404
  34.7 0.0 collective-permute-done.9.refs_3_
  34.7 0.9 %collective-permute-done.8.refs_2_ = f32[18,128]{1,0:T(8,128)S(1)} collective-permute-done((f32[18,128]{1,0:T(8,128)S(1)}, f32[18,128]{1,0:T(8,128)S(1)}, u32[]{:S(2)}, u32[]{:S(2)}) %collective-permute-start.8) | collective-permute-done | bytes 9248 | tf_op jit(solution)/shard_map/ppermute | solution.py:58
  35.6 0.0 collective-permute-done.7.refs_1_
  35.6 0.0 collective-permute-done.10.refs_5_
  35.6 0.0 collective-permute-done.11.refs_7_
  35.6 0.7 %collect.1 = (bf16[128,256]{1,0:T(8,128)(2,1)}, bf16[128,256]{1,0:T(8,128)(2,1)}, f32[16,128]{1,0:T(8,128)}, f32[2,128]{1,0:T(2,128)}) custom-call(f32[18,128]{1,0:T(8,128)S(1)} %total.1.refs_0_, f32[18,128]{1,0:T(8,128)S(1)} %collective-permute-done.7.refs_1_, f32[18,128]{1,0:T(8,128)S(1)} %collective-permute-done.8.refs_2_, ...), custom_call_target="tpu_custom_call" | custom-call | flops 262144 | bytes 524288 | tf_op jit(solution)/shard_map/collect/pallas_call | solution.py:432
  (1 shorter events, 0.0 us)
Async XLA Ops:
  1.5 11.0 %collective-permute-start.1 = (bf16[128,512]{1,0:T(8,128)(2,1)S(1)}, bf16[128,512]{1,0:T(8,128)(2,1)S(1)}, u32[]{:S(2)}, u32[]{:S(2)}) collective-permute-start(bf16[128,512]{1,0:T(8,128)(2,1)S(1)} %pad_maximum_fusion.pair_ref.refs_0_), channel_id=1, source_target_pairs={{6,0},{4,2},{2,4},{0,6},{7,1},{5,3},{3,5},{1,7},{14,8},{12,10},{10... | collective-permute-start | bytes 393224 | tf_op jit(solution)/shard_map/ppermute | solution.py:58
  6.6 7.4 %collective-permute-start = (bf16[128,512]{1,0:T(8,128)(2,1)S(1)}, bf16[128,512]{1,0:T(8,128)(2,1)S(1)}, u32[]{:S(2)}, u32[]{:S(2)}) collective-permute-start(bf16[128,512]{1,0:T(8,128)(2,1)S(1)} %pad_maximum_fusion.pair_ref.refs_0_), channel_id=1, source_target_pairs={{2,0},{0,2},{6,4},{4,6},{3,1},{1,3},{7,5},{5,7},{10,8},{8,10},{14,... | collective-permute-start | bytes 393224 | tf_op jit(solution)/shard_map/ppermute | solution.py:58
  6.6 11.1 %collective-permute-start.2 = (bf16[128,512]{1,0:T(8,128)(2,1)S(1)}, bf16[128,512]{1,0:T(8,128)(2,1)S(1)}, u32[]{:S(2)}, u32[]{:S(2)}) collective-permute-start(bf16[128,512]{1,0:T(8,128)(2,1)S(1)} %pad_maximum_fusion.pair_ref.refs_0_), channel_id=1, source_target_pairs={{4,0},{6,2},{0,4},{2,6},{5,1},{7,3},{1,5},{3,7},{12,8},{14,10},{8,... | collective-permute-start | bytes 393224 | tf_op jit(solution)/shard_map/ppermute | solution.py:58
  7.3 1.0 %copy-start = (bf16[1,128,2048]{2,1,0:T(8,128)(2,1)S(1)}, bf16[1,128,2048]{2,1,0:T(8,128)(2,1)}, u32[]{:S(2)}) copy-start(bf16[1,128,2048]{2,1,0:T(8,128)(2,1)} %param.7) | copy-start | bytes 1572868
  8.3 1.0 %copy-start.1 = (bf16[1,128,2048]{2,1,0:T(8,128)(2,1)S(1)}, bf16[1,128,2048]{2,1,0:T(8,128)(2,1)}, u32[]{:S(2)}) copy-start(bf16[1,128,2048]{2,1,0:T(8,128)(2,1)} %param.12) | copy-start | bytes 1572868
  9.4 0.7 %copy-start.2 = (bf16[2048]{0:T(1024)(128)(2,1)S(1)}, bf16[2048]{0:T(1024)(128)(2,1)}, u32[]{:S(2)}) copy-start(bf16[2048]{0:T(1024)(128)(2,1)} %param.8) | copy-start | bytes 12292
  10.0 0.7 %copy-start.3 = (s32[1,8]{1,0:T(1,128)S(1)}, s32[1,8]{1,0:T(1,128)}, u32[]{:S(2)}) copy-start(s32[1,8]{1,0:T(1,128)} %len_ref.1) | copy-start | bytes 100
  10.7 0.7 %copy-start.4 = (bf16[256]{0:T(256)(128)(2,1)S(1)}, bf16[256]{0:T(256)(128)(2,1)}, u32[]{:S(2)}) copy-start(bf16[256]{0:T(256)(128)(2,1)} %param.11) | copy-start | bytes 1540
  20.5 11.2 %collective-permute-start.3 = (bf16[128,512]{1,0:T(8,128)(2,1)S(1)}, bf16[128,512]{1,0:T(8,128)(2,1)S(1)}, u32[]{:S(2)}, u32[]{:S(2)}) collective-permute-start(bf16[128,512]{1,0:T(8,128)(2,1)S(1)} %get-tuple-element.48), channel_id=1, source_target_pairs={{0,4},{2,6},{4,0},{6,2},{1,5},{3,7},{5,1},{7,3},{8,12},{10,14},{12... | collective-permute-start | bytes 393224 | tf_op jit(solution)/shard_map/ppermute | solution.py:63
  21.4 5.7 %collective-permute-start.6 = (f32[18,128]{1,0:T(8,128)S(1)}, f32[18,128]{1,0:T(8,128)S(1)}, u32[]{:S(2)}, u32[]{:S(2)}) collective-permute-start(f32[18,128]{1,0:T(8,128)S(1)} %get-tuple-element.51.refs_0_), channel_id=1, source_target_pairs={{24,0},{16,8},{8,16},{0,24},{25,1},{17,9},{9,17},{1,25},{26,2},{18... | collective-permute-start | bytes 27656 | tf_op jit(solution)/shard_map/ppermute | solution.py:58
  23.9 4.6 %collective-permute-start.5 = (f32[18,128]{1,0:T(8,128)S(1)}, f32[18,128]{1,0:T(8,128)S(1)}, u32[]{:S(2)}, u32[]{:S(2)}) collective-permute-start(f32[18,128]{1,0:T(8,128)S(1)} %get-tuple-element.51.refs_0_), channel_id=1, source_target_pairs={{16,0},{24,8},{0,16},{8,24},{17,1},{25,9},{1,17},{9,25},{18,2},{26... | collective-permute-start | bytes 27656 | tf_op jit(solution)/shard_map/ppermute | solution.py:58
  24.4 4.1 %collective-permute-start.4 = (f32[18,128]{1,0:T(8,128)S(1)}, f32[18,128]{1,0:T(8,128)S(1)}, u32[]{:S(2)}, u32[]{:S(2)}) collective-permute-start(f32[18,128]{1,0:T(8,128)S(1)} %get-tuple-element.51.refs_0_), channel_id=1, source_target_pairs={{8,0},{0,8},{24,16},{16,24},{9,1},{1,9},{25,17},{17,25},{10,2},{2,... | collective-permute-start | bytes 27656 | tf_op jit(solution)/shard_map/ppermute | solution.py:58
  24.9 10.7 %collective-permute-start.10 = (bf16[128,512]{1,0:T(8,128)(2,1)S(1)}, bf16[128,512]{1,0:T(8,128)(2,1)S(1)}, u32[]{:S(2)}, u32[]{:S(2)}) collective-permute-start(bf16[128,512]{1,0:T(8,128)(2,1)S(1)} %get-tuple-element.53), channel_id=1, source_target_pairs={{0,2},{2,0},{4,6},{6,4},{1,3},{3,1},{5,7},{7,5},{8,10},{10,8},{12,... | collective-permute-start | bytes 393224 | tf_op jit(solution)/shard_map/ppermute | solution.py:63
  27.1 8.5 %collective-permute-start.11 = (bf16[128,512]{1,0:T(8,128)(2,1)S(1)}, bf16[128,512]{1,0:T(8,128)(2,1)S(1)}, u32[]{:S(2)}, u32[]{:S(2)}) collective-permute-start(bf16[128,512]{1,0:T(8,128)(2,1)S(1)} %get-tuple-element.55), channel_id=1, source_target_pairs={{0,6},{2,4},{4,2},{6,0},{1,7},{3,5},{5,3},{7,1},{8,14},{10,12},{12... | collective-permute-start | bytes 393224 | tf_op jit(solution)/shard_map/ppermute | solution.py:63
  28.5 6.2 %collective-permute-start.9 = (f32[18,128]{1,0:T(8,128)S(1)}, f32[18,128]{1,0:T(8,128)S(1)}, u32[]{:S(2)}, u32[]{:S(2)}) collective-permute-start(f32[18,128]{1,0:T(8,128)S(1)} %total.1.refs_0_), channel_id=1, source_target_pairs={{6,0},{4,2},{2,4},{0,6},{7,1},{5,3},{3,5},{1,7},{14,8},{12,10},{10... | collective-permute-start | bytes 27656 | tf_op jit(solution)/shard_map/ppermute | solution.py:58
  31.0 4.6 %collective-permute-start.8 = (f32[18,128]{1,0:T(8,128)S(1)}, f32[18,128]{1,0:T(8,128)S(1)}, u32[]{:S(2)}, u32[]{:S(2)}) collective-permute-start(f32[18,128]{1,0:T(8,128)S(1)} %total.1.refs_0_), channel_id=1, source_target_pairs={{4,0},{6,2},{0,4},{2,6},{5,1},{7,3},{1,5},{3,7},{12,8},{14,10},{8,... | collective-permute-start | bytes 27656 | tf_op jit(solution)/shard_map/ppermute | solution.py:58
  31.8 3.9 %collective-permute-start.7 = (f32[18,128]{1,0:T(8,128)S(1)}, f32[18,128]{1,0:T(8,128)S(1)}, u32[]{:S(2)}, u32[]{:S(2)}) collective-permute-start(f32[18,128]{1,0:T(8,128)S(1)} %total.1.refs_0_), channel_id=1, source_target_pairs={{2,0},{0,2},{6,4},{4,6},{3,1},{1,3},{7,5},{5,7},{10,8},{8,10},{14,... | collective-permute-start | bytes 27656 | tf_op jit(solution)/shard_map/ppermute | solution.py:58
